TPU v7x, 32 devices: a whole 2x2x4 slice. The times are simulated.
32 devices in a mesh: expert: 8 (over y, x, core), hidden: 4 (over z).
Axes of the slice: x: 2, y: 2, z: 4, core: 2. Of those that a mesh axis runs over, the one named last changes fastest.
Arguments:
- tokens: bfloat16 [32, 196, 1024], P('expert'), may hold values from -32 to 32
- slot_keys: bfloat16 [1024, 16], replicated, may hold values from -1 to 1
- w_in: bfloat16 [16, 1024, 4096], P('expert', None, 'hidden'), may hold values from -0.1875 to 0.1875
- b_in: float32 [16, 4096], P('expert', 'hidden'), may hold values from -6 to 6
- w_out: bfloat16 [16, 4096, 1024], P('expert', 'hidden'), may hold values from -0.09375 to 0.09375
- b_out: float32 [16, 1024], replicated, may hold values from -6 to 6
- out_grad: bfloat16 [32, 196, 1024], P('expert'), may hold values from -6 to 6
Outputs:
- token_grad: bfloat16 [32, 196, 1024], P(('expert', 'hidden'))
All inputs are finite; a program needn't handle non-finite values.
Results may differ from a plain program's by a relative error of at most 0.028.
Values may be sent and summed in bfloat16 or wider, within the bound.
No kernel may reach another device: no remote copies, remote signals or barrier semaphores. Data moves between devices by JAX's collectives and lax.ppermute only.
A program may use at most 64 MiB of HBM per device.

v0:
```python
import jax
import jax.numpy as jnp
from jax import lax
from jax.sharding import PartitionSpec as P


def gelu_slope(pre_act):
    return (
        0.5 * (1.0 + lax.erf(pre_act * 0.7071067811865476))
        + pre_act * jnp.exp(-0.5 * pre_act * pre_act) * 0.3989422804014327
    )


def send_home(term_fn, row_total, n_expert, quarter, local_experts, width, full_bias):
    n_hidden = lax.axis_size("hidden")
    term = term_fn(0, row_total).astype(jnp.bfloat16)
    term = term.reshape(n_hidden, n_expert, quarter, local_experts, width)
    moved = lax.all_to_all(term, "expert", split_axis=1, concat_axis=3, tiled=True)
    summed = lax.psum_scatter(
        moved.astype(jnp.float32).astype(jnp.bfloat16), "hidden", scatter_dimension=0, tiled=True
    ).astype(jnp.float32)
    summed = summed.reshape(quarter, n_expert * local_experts, width)
    return (summed + full_bias[None]).astype(jnp.bfloat16)


def local(tokens, slot_keys, w_in, b_in, w_out, b_out, out_grad):
    n_expert = lax.axis_size("expert")
    n_hidden = lax.axis_size("hidden")
    image_count, positions, width = tokens.shape
    quarter = image_count // n_hidden
    slot_count = slot_keys.shape[1]
    local_experts = w_in.shape[0]
    logits = jnp.einsum("btd,ds->bts", tokens, slot_keys, preferred_element_type=jnp.float32)
    dispatch = jax.nn.softmax(logits, axis=1).astype(jnp.bfloat16)
    combine = jax.nn.softmax(logits, axis=2).astype(jnp.bfloat16)
    slot_in = jnp.einsum(
        "bts,btd->bsd", dispatch, tokens, preferred_element_type=jnp.float32
    ).astype(jnp.bfloat16)
    slot_grad = jnp.einsum(
        "bts,btd->bsd", combine, out_grad, preferred_element_type=jnp.float32
    ).astype(jnp.bfloat16)
    grouped = (n_hidden, quarter, slot_count, width)
    sent_in, sent_grad = (
        lax.all_to_all(slot_in.reshape(grouped), "expert", split_axis=2, concat_axis=1, tiled=True),
        lax.all_to_all(
            slot_grad.reshape(grouped), "expert", split_axis=2, concat_axis=1, tiled=True
        ),
    )
    row_total = n_hidden * n_expert * quarter
    rows_in = sent_in.reshape(row_total, local_experts, width)
    rows_grad = sent_grad.reshape(row_total, local_experts, width)
    pre_act = (
        jnp.einsum("rkd,kdf->rkf", rows_in, w_in, preferred_element_type=jnp.float32) + b_in[None]
    )
    hidden_act = jax.nn.gelu(pre_act, approximate=False).astype(jnp.bfloat16)

    def output_term(row_start, row_count):
        return jnp.einsum("rkf,kfd->rkd", hidden_act, w_out, preferred_element_type=jnp.float32)

    slot_out = send_home(output_term, row_total, n_expert, quarter, local_experts, width, b_out)
    act_grad = jnp.einsum("rkd,kfd->rkf", rows_grad, w_out, preferred_element_type=jnp.float32)
    pre_grad = (act_grad * gelu_slope(pre_act)).astype(jnp.bfloat16)

    def input_term(row_start, row_count):
        return jnp.einsum("rkf,kdf->rkd", pre_grad, w_in, preferred_element_type=jnp.float32)

    zero_full = jnp.zeros_like(b_out)
    slot_in_grad = send_home(
        input_term, row_total, n_expert, quarter, local_experts, width, zero_full
    )
    offset = lax.axis_index("hidden") * quarter
    mine_tokens = lax.dynamic_slice_in_dim(tokens, offset, quarter, 0)
    mine_grad = lax.dynamic_slice_in_dim(out_grad, offset, quarter, 0)
    mine_dispatch = lax.dynamic_slice_in_dim(dispatch, offset, quarter, 0)
    mine_combine = lax.dynamic_slice_in_dim(combine, offset, quarter, 0)
    comb_grad = jnp.einsum("btd,bsd->bts", mine_grad, slot_out, preferred_element_type=jnp.float32)
    disp_grad = jnp.einsum(
        "btd,bsd->bts", mine_tokens, slot_in_grad, preferred_element_type=jnp.float32
    )
    comb_wide = mine_combine.astype(jnp.float32)
    disp_wide = mine_dispatch.astype(jnp.float32)
    logit_grad = comb_wide * (comb_grad - jnp.sum(comb_wide * comb_grad, axis=2, keepdims=True))
    logit_grad = logit_grad + disp_wide * (
        disp_grad - jnp.sum(disp_wide * disp_grad, axis=1, keepdims=True)
    )
    logit_grad = logit_grad.astype(jnp.bfloat16)
    token_grad = jnp.einsum(
        "bts,bsd->btd", mine_dispatch, slot_in_grad, preferred_element_type=jnp.float32
    )
    token_grad = token_grad + jnp.einsum(
        "bts,ds->btd", logit_grad, slot_keys, preferred_element_type=jnp.float32
    )
    return token_grad.astype(jnp.bfloat16)


def solution(mesh):
    return jax.shard_map(
        local,
        mesh=mesh,
        in_specs=(
            P("expert", None, None),
            P(),
            P("expert", None, "hidden"),
            P("expert", "hidden"),
            P("expert", "hidden", None),
            P(),
            P("expert", None, None),
        ),
        out_specs=P(("expert", "hidden"), None, None),
        check_vma=False,
    )
```

profile of v0, /device:TPU:0, one launch (start us, length us, event | category | flops | bytes accessed | tf_op | source)
XLA Modules:
  0.0 98.7 jit_solution(15604105668320337525)
XLA Ops:
  6.5 0.0 copy-start
  6.5 0.0 copy-start.1
  6.5 0.8 copy-done
  7.3 2.2 %fusion.141 = (f32[4,16]{1,0:T(4,128)S(1)}, f32[4,196,16]{1,2,0:T(8,128)S(1)}) fusion(bf16[1024,16]{0,1:T(8,128)(2,1)S(1)} %copy-done, bf16[4,196,1024]{2,0,1:T(4,128)(2,1)} %param.7), kind=kOutput, calls=%fused_computation.160 | convolution fusion | flops 25715396 | bytes 1688832 | tf_op jit(solution)/shard_map/sub | solution.py:34
  9.5 0.1 divide_convert_fusion.1
  9.6 0.0 copy-done.1
  9.6 1.0 fusion.10
  10.5 0.0 copy-start.2
  10.6 0.8 copy.47
  11.3 5.2 %all-to-all-start.1 = ((bf16[4,1,16,1024]{3,0,1,2:T(4,128)(2,1)}), bf16[4,1,16,1024]{3,0,1,2:T(4,128)(2,1)S(1)}, u32[]{:S(2)}, u32[]{:S(2)}) async-start(bf16[4,1,16,1024]{3,0,1,2:T(4,128)(2,1)} %copy.47), calls=%async_computation.1 | async-start | bytes 262144 | tf_op jit(solution)/shard_map/all_to_all | solution.py:44
  16.5 0.6 fusion.142
  17.1 0.0 copy-done.2
  17.1 0.0 copy-start.3
  17.1 0.0 copy-start.6
  17.2 1.0 fusion.9
  18.1 0.8 copy.43
  18.9 3.1 %all-to-all-done.1 = bf16[4,1,16,1024]{3,0,1,2:T(4,128)(2,1)S(1)} async-done(((bf16[4,1,16,1024]{3,0,1,2:T(4,128)(2,1)}), bf16[4,1,16,1024]{3,0,1,2:T(4,128)(2,1)S(1)}, u32[]{:S(2)}, u32[]{:S(2)}) %all-to-all-start.1) | async-done | bytes 131104 | tf_op jit(solution)/shard_map/all_to_all | solution.py:44
  22.0 0.0 copy-done.3
  22.0 3.4 %all-to-all-start = ((bf16[4,1,16,1024]{3,0,1,2:T(4,128)(2,1)}), bf16[4,1,16,1024]{3,0,1,2:T(4,128)(2,1)S(1)}, u32[]{:S(2)}, u32[]{:S(2)}) async-start(bf16[4,1,16,1024]{3,0,1,2:T(4,128)(2,1)} %copy.43), calls=%async_computation | async-start | bytes 262144 | tf_op jit(solution)/shard_map/all_to_all | solution.py:45
  25.4 0.0 reduce-scatter.3.cloned.1.call-start
  25.4 0.7 copy.48
  26.1 1.6 %reshape.92 = bf16[32,2,1024]{2,1,0:T(2,128)(2,1)} reshape(bf16[4,1,16,1024]{3,2,0,1:T(8,128)(2,1)} %copy.48) | data formatting | bytes 262144 | tf_op jit(solution)/shard_map/reshape | solution.py:50
  27.7 3.1 %all-to-all-done = bf16[4,1,16,1024]{3,0,1,2:T(4,128)(2,1)S(1)} async-done(((bf16[4,1,16,1024]{3,0,1,2:T(4,128)(2,1)}), bf16[4,1,16,1024]{3,0,1,2:T(4,128)(2,1)S(1)}, u32[]{:S(2)}, u32[]{:S(2)}) %all-to-all-start) | async-done | bytes 131104 | tf_op jit(solution)/shard_map/all_to_all | solution.py:45
  30.9 0.7 reshape.90
  31.6 0.0 copy-done.6
  31.6 3.1 %fusion.4 = f32[32,2,1024]{2,0,1:T(8,128)S(1)} fusion(bf16[2,1024,1024]{2,1,0:T(8,128)(2,1)} %param.9, bf16[32,2,1024]{2,1,0:T(2,128)(2,1)} %reshape.92, f32[2,1024]{1,0:T(2,128)S(1)} %copy-done.6), kind=kOutput, calls=%fused_computation.6 | convolution fusion | flops 134283264 | bytes 4595712 | tf_op jit(solution)/shard_map/rkd,kdf->rkf/dot_general | solution.py:53
  34.7 6.7 %fusion.7 = bf16[4,8,1,2,1024]{4,1,0,3,2:T(8,128)(2,1)} fusion(bf16[2,1024,1024]{2,1,0:T(8,128)(2,1)} %param.9, bf16[2,1024,1024]{2,1,0:T(8,128)(2,1)} %param.11, f32[32,2,1024]{2,0,1:T(8,128)S(1)} %fusion.4, bf16[32,2,1024]{2,1,0:T(2,128)(2,1)} %reshape.90), kind=kOutput, calls=%fused_computation.14 | convolution fusion | flops 269156352 | bytes 8912896 | tf_op jit(solution)/shard_map/rkf,kdf->rkd/dot_general | solution.py:65
  41.4 1.0 %copy.50 = bf16[4,8,1,2,1024]{4,0,3,2,1:T(4,128)(2,1)S(1)} copy(bf16[4,8,1,2,1024]{4,1,0,3,2:T(8,128)(2,1)} %fusion.7) | data formatting | bytes 262144 | tf_op jit(solution)/shard_map/reshape | solution.py:17
  42.4 7.9 %all_to_all.42 = bf16[4,8,1,2,1024]{4,0,3,2,1:T(4,128)(2,1)S(1)} all-to-all(bf16[4,8,1,2,1024]{4,0,3,2,1:T(4,128)(2,1)S(1)} %copy.50), channel_id=1, replica_groups=mesh['expert'=8,'hidden'=4] {'expert'}, dimensions={1} | all-to-all | bytes 262144 | tf_op jit(solution)/shard_map/all_to_all | solution.py:18
  50.4 0.7 copy.51
  51.1 0.0 reduce-scatter.3.cloned.1.call-update
  51.1 3.4 %fusion.8 = bf16[4,8,1,2,1024]{4,1,0,3,2:T(8,128)(2,1)S(1)} fusion(bf16[2,1024,1024]{2,1,0:T(8,128)(2,1)} %param.11, f32[32,2,1024]{2,0,1:T(8,128)S(1)} %fusion.4), kind=kOutput, calls=%fused_computation.15 | convolution fusion | flops 138543104 | bytes 4587520 | tf_op jit(solution)/shard_map/rkf,kfd->rkd/dot_general | solution.py:58
  54.5 0.8 copy.53
  55.2 3.4 %all-to-all-start.3 = ((bf16[4,8,1,2,1024]{4,0,3,2,1:T(4,128)(2,1)}), bf16[4,8,1,2,1024]{4,0,3,2,1:T(4,128)(2,1)S(1)}, u32[]{:S(2)}, u32[]{:S(2)}) async-start(bf16[4,8,1,2,1024]{4,0,3,2,1:T(4,128)(2,1)} %copy.53), calls=%async_computation.4 | async-start | bytes 262144 | tf_op jit(solution)/shard_map/all_to_all | solution.py:18
  58.6 0.0 reduce-scatter.5.cloned.1.call-start
  58.7 1.7 %copy.41 = bf16[4,196,1024]{2,1,0:T(8,128)(2,1)} copy(bf16[4,196,1024]{2,0,1:T(4,128)(2,1)S(1)} %copy-done.1) | data formatting | bytes 3211264 | tf_op args[0]
  60.3 1.7 %copy.42 = bf16[4,196,1024]{2,1,0:T(8,128)(2,1)} copy(bf16[4,196,1024]{2,0,1:T(4,128)(2,1)S(1)} %copy-done.2) | data formatting | bytes 3211264 | tf_op args[6]
  62.0 0.0 copy-start.4
  62.0 0.0 copy-start.5
  62.0 2.1 %all-to-all-done.3 = bf16[4,8,1,2,1024]{4,0,3,2,1:T(4,128)(2,1)S(1)} async-done(((bf16[4,8,1,2,1024]{4,0,3,2,1:T(4,128)(2,1)}), bf16[4,8,1,2,1024]{4,0,3,2,1:T(4,128)(2,1)S(1)}, u32[]{:S(2)}, u32[]{:S(2)}) %all-to-all-start.3) | async-done | bytes 131104 | tf_op jit(solution)/shard_map/all_to_all | solution.py:18
  64.1 0.7 copy.54
  64.8 0.0 reduce-scatter.5.cloned.1.call-update
  64.8 5.0 %reduce-scatter.3.cloned.1.call-done = bf16[1,1,1,16,1024]{4,3,2,1,0:T(8,128)(2,1)} async-done(((bf16[4,1,1,16,1024]{4,3,2,1,0:T(8,128)(2,1)}), bf16[1,1,1,16,1024]{4,3,2,1,0:T(8,128)(2,1)}) %reduce-scatter.3.cloned.1.call-update) | async-done | bytes 32784 | tf_op jit(solution)/shard_map/reduce_scatter | solution.py:19
  69.8 1.3 %fusion.90 = (f32[16]{0:T(128)S(1)}, f32[196,16]{0,1:T(8,128)S(1)}) fusion(bf16[4,196,16]{1,2,0:T(8,128)(2,1)S(1)} %divide_convert_fusion.1, s32[]{:T(128)S(6)} %select_n.2, bf16[1,1,1,16,1024]{4,3,2,1,0:T(8,128)(2,1)} %reduce-scatter.3.cloned.1.call-done, bf16[4,196,1024]{2,1,0:T(8,128)(2,1)} %copy.41), kind=kOutput, calls=%fused_computation.110 | convolution fusion | flops 6431920 | bytes 462272 | tf_op jit(solution)/shard_map/btd,bsd->bts/dot_general | solution.py:77
  71.1 1.0 %fusion.83 = f32[196,1024]{1,0:T(8,128)S(1)} fusion(bf16[1,1,1,16,1024]{4,3,2,1,0:T(8,128)(2,1)} %reduce-scatter.3.cloned.1.call-done, bf16[4,196,16]{1,2,0:T(8,128)(2,1)S(1)} %divide_convert_fusion.1, s32[]{:T(128)S(6)} %select_n.2), kind=kOutput, calls=%fused_computation.99 | convolution fusion | flops 6422528 | bytes 843780 | tf_op jit(solution)/shard_map/bts,bsd->btd/dot_general | solution.py:87
  72.2 17.3 %reduce-scatter.5.cloned.1.call-done = bf16[1,1,1,16,1024]{4,3,2,1,0:T(8,128)(2,1)} async-done(((bf16[4,1,1,16,1024]{4,3,2,1,0:T(8,128)(2,1)}), bf16[1,1,1,16,1024]{4,3,2,1,0:T(8,128)(2,1)}) %reduce-scatter.5.cloned.1.call-update) | async-done | bytes 32784 | tf_op jit(solution)/shard_map/reduce_scatter | solution.py:19
  89.5 0.0 copy-done.4
  89.5 0.0 copy-done.5
  89.5 1.2 %fusion.87 = (f32[196]{0:T(256)S(1)}, f32[196,16]{0,1:T(8,128)S(1)}) fusion(bf16[4,196,16]{1,2,0:T(8,128)(2,1)S(1)} %copy-done.4, s32[]{:T(128)S(6)} %select_n.2, f32[16,1024]{1,0:T(8,128)S(1)} %copy-done.5, bf16[1,1,1,16,1024]{4,3,2,1,0:T(8,128)(2,1)} %reduce-scatter.5.cloned.1.call-done, bf16[4,196,1024]{2,1,0:T(8,128)(2,1)} %copy.42), kind=kOutput, calls=%fused_computation.107 | convolution fusion | flops 6480892 | bytes 528528 | tf_op jit(solution)/shard_map/btd,bsd->bts/dot_general | solution.py:76
  90.8 1.1 %fusion.3 = bf16[1,196,1024]{2,1,0:T(8,128)(2,1)} fusion(f32[196,1024]{1,0:T(8,128)S(1)} %fusion.83, bf16[1024,16]{0,1:T(8,128)(2,1)S(1)} %copy-done, f32[196,16]{0,1:T(8,128)S(1)} %get-tuple-element.10, f32[196,16]{0,1:T(8,128)S(1)} %get-tuple-element.12, f32[16]{0:T(128)S(1)} %get-tuple-element.9, f32[196]{0:T(256)S(1)} %get-tuple-element.11, ...), kind=kOutput, calls=%fused_computation.4 | convolution fusion | flops 6849024 | bytes 1304068 | tf_op jit(solution)/shard_map/bts,ds->btd/dot_general | solution.py:90
  (2 shorter events, 0.1 us)
Async XLA Ops:
  6.5 0.8 copy-start
  6.5 3.0 %copy-start.1 = (bf16[4,196,1024]{2,0,1:T(4,128)(2,1)S(1)}, bf16[4,196,1024]{2,0,1:T(4,128)(2,1)}, u32[]{:S(2)}) copy-start(bf16[4,196,1024]{2,0,1:T(4,128)(2,1)} %param.7) | copy-start | bytes 4816900
  10.5 6.6 %copy-start.2 = (bf16[4,196,1024]{2,0,1:T(4,128)(2,1)S(1)}, bf16[4,196,1024]{2,0,1:T(4,128)(2,1)}, u32[]{:S(2)}) copy-start(bf16[4,196,1024]{2,0,1:T(4,128)(2,1)} %param.13) | copy-start | bytes 4816900
  11.3 10.7 %all-to-all-start.1 = ((bf16[4,1,16,1024]{3,0,1,2:T(4,128)(2,1)}), bf16[4,1,16,1024]{3,0,1,2:T(4,128)(2,1)S(1)}, u32[]{:S(2)}, u32[]{:S(2)}) async-start(bf16[4,1,16,1024]{3,0,1,2:T(4,128)(2,1)} %copy.47), calls=%async_computation.1 | async-start | bytes 262144 | tf_op jit(solution)/shard_map/all_to_all | solution.py:44
  17.1 4.9 %copy-start.3 = (bf16[4,196,16]{1,2,0:T(8,128)(2,1)}, bf16[4,196,16]{1,2,0:T(8,128)(2,1)S(1)}, u32[]{:S(2)}) copy-start(bf16[4,196,16]{1,2,0:T(8,128)(2,1)S(1)} %divide_convert_fusion) | copy-start | bytes 75268
  17.1 14.5 %copy-start.6 = (f32[2,1024]{1,0:T(2,128)S(1)}, f32[2,1024]{1,0:T(2,128)}, u32[]{:S(2)}) copy-start(f32[2,1024]{1,0:T(2,128)} %param.10) | copy-start | bytes 24580
  22.0 8.8 %all-to-all-start = ((bf16[4,1,16,1024]{3,0,1,2:T(4,128)(2,1)}), bf16[4,1,16,1024]{3,0,1,2:T(4,128)(2,1)S(1)}, u32[]{:S(2)}, u32[]{:S(2)}) async-start(bf16[4,1,16,1024]{3,0,1,2:T(4,128)(2,1)} %copy.43), calls=%async_computation | async-start | bytes 262144 | tf_op jit(solution)/shard_map/all_to_all | solution.py:45
  25.4 44.4 %reduce-scatter.3.cloned.1.call-start = ((), (), s32[]{:S(2)}) async-start(), calls=%async_computation.6 | async-start | bytes 163840 | tf_op jit(solution)/shard_map/reduce_scatter | solution.py:19
  55.2 8.8 %all-to-all-start.3 = ((bf16[4,8,1,2,1024]{4,0,3,2,1:T(4,128)(2,1)}), bf16[4,8,1,2,1024]{4,0,3,2,1:T(4,128)(2,1)S(1)}, u32[]{:S(2)}, u32[]{:S(2)}) async-start(bf16[4,8,1,2,1024]{4,0,3,2,1:T(4,128)(2,1)} %copy.53), calls=%async_computation.4 | async-start | bytes 262144 | tf_op jit(solution)/shard_map/all_to_all | solution.py:18
  58.6 30.9 %reduce-scatter.5.cloned.1.call-start = ((), (), s32[]{:S(2)}) async-start(), calls=%async_computation.7 | async-start | bytes 163840 | tf_op jit(solution)/shard_map/reduce_scatter | solution.py:19
  62.0 27.5 %copy-start.4 = (bf16[4,196,16]{1,2,0:T(8,128)(2,1)S(1)}, bf16[4,196,16]{1,2,0:T(8,128)(2,1)}, u32[]{:S(2)}) copy-start(bf16[4,196,16]{1,2,0:T(8,128)(2,1)} %copy-done.3) | copy-start | bytes 75268
  62.0 27.5 %copy-start.5 = (f32[16,1024]{1,0:T(8,128)S(1)}, f32[16,1024]{1,0:T(8,128)}, u32[]{:S(2)}) copy-start(f32[16,1024]{1,0:T(8,128)} %param.12) | copy-start | bytes 196612
Sparse Core Ops, SparseCore 0:
  51.2 18.5 reduce-scatter.2
  72.1 17.3 reduce-scatter.4
where the time goes:
time: 99.4 us; the launch traced here: 98.7 us
  waiting for transfers between devices  30.7 us (31%)
  matrix products  22.7 us (23%)
  between operations  13.5 us (14%)
  starting transfers between devices  12 us (12%)
  local copies, waits for them, and re-layouts  11.8 us (12%)
  blocking collectives  7.92 us (8%)
    reduce_scatter x2, waiting for transfers between devices, send_home(): lax.psum_scatter(moved.astype(jnp.float32).astype(jnp.bfloat16), 'hidden'...  22.3 us
    all_to_all x1, blocking collectives, send_home(): lax.all_to_all(term, 'expert', split_axis=1, concat_axis=3, tiled=True)  7.92 us
    dot_general x1, matrix products, input_term(): jnp.einsum('rkf,kdf->rkd', pre_grad, w_in, preferred_element_type=jnp.flo...  6.73 us
    all_to_all x1, starting transfers between devices, local(): lax.all_to_all(slot_in.reshape(grouped), 'expert', split_axis=2, concat_a...  5.17 us
    unnamed x16, local copies, waits for them, and re-layouts  4.11 us
    dot_general x1, matrix products, output_term(): jnp.einsum('rkf,kfd->rkd', hidden_act, w_out, preferred_element_type=jnp....  3.38 us
    all_to_all x1, starting transfers between devices, local(): lax.all_to_all(slot_grad.reshape(grouped), 'expert', split_axis=2, concat...  3.37 us
    all_to_all x1, starting transfers between devices, send_home(): lax.all_to_all(term, 'expert', split_axis=1, concat_axis=3, tiled=True)  3.37 us
  transfers between devices with their start and end apart: 5, of which 5 were waited for; matrix products, arithmetic and copies ran while one was open for 15% of the time, Pallas kernels for 0%

commit v1 on v0

v1 whole, which is shorter than its diff:
```python
import jax
import jax.numpy as jnp
from jax import lax
from jax.sharding import PartitionSpec as P


def gelu_slope(pre_act):
    return (
        0.5 * (1.0 + lax.erf(pre_act * 0.7071067811865476))
        + pre_act * jnp.exp(-0.5 * pre_act * pre_act) * 0.3989422804014327
    )


def local(tokens, slot_keys, w_in, b_in, w_out, b_out, out_grad):
    n_expert = lax.axis_size("expert")
    n_hidden = lax.axis_size("hidden")
    n_all = n_expert * n_hidden
    images, positions, width = tokens.shape
    quarter = images // n_hidden
    slots = slot_keys.shape[1]
    k = w_in.shape[0]
    logits = jnp.einsum("btd,ds->bts", tokens, slot_keys, preferred_element_type=jnp.float32)
    dispatch = jax.nn.softmax(logits, axis=1).astype(jnp.bfloat16)
    combine = jax.nn.softmax(logits, axis=2).astype(jnp.bfloat16)
    slot_in = jnp.einsum(
        "bts,btd->sbd", dispatch, tokens, preferred_element_type=jnp.float32
    ).astype(jnp.bfloat16)
    slot_grad = jnp.einsum(
        "bts,btd->sbd", combine, out_grad, preferred_element_type=jnp.float32
    ).astype(jnp.bfloat16)
    sent = jnp.concatenate(
        [
            slot_in.reshape(n_expert, k * images, width),
            slot_grad.reshape(n_expert, k * images, width),
        ],
        axis=1,
    )
    got = lax.all_to_all(sent, "expert", split_axis=0, concat_axis=0, tiled=True)
    got = got.reshape(n_expert, 2, k, images, width)
    rows_in = got[:, 0].swapaxes(0, 1).reshape(k, n_expert * images, width)
    rows_grad = got[:, 1].swapaxes(0, 1).reshape(k, n_expert * images, width)
    pre_act = (
        jnp.einsum("krd,kdf->krf", rows_in, w_in, preferred_element_type=jnp.float32)
        + b_in[:, None]
    )
    hidden_act = jax.nn.gelu(pre_act, approximate=False).astype(jnp.bfloat16)
    out_part = jnp.einsum("krf,kfd->krd", hidden_act, w_out, preferred_element_type=jnp.float32)
    act_grad = jnp.einsum("krd,kfd->krf", rows_grad, w_out, preferred_element_type=jnp.float32)
    pre_grad = (act_grad * gelu_slope(pre_act)).astype(jnp.bfloat16)
    in_part = jnp.einsum("krf,kdf->krd", pre_grad, w_in, preferred_element_type=jnp.float32)

    def home(part):
        part = part.astype(jnp.bfloat16).reshape(k, n_all, quarter, width)
        part = part.swapaxes(0, 1).reshape(n_all, k * quarter, width)
        return part

    back = jnp.concatenate([home(out_part), home(in_part)], axis=1)
    back = lax.all_to_all(back, ("expert", "hidden"), split_axis=0, concat_axis=0, tiled=True)
    back = back.reshape(n_expert, n_hidden, 2, k, quarter, width).astype(jnp.float32)
    back = jnp.sum(back, axis=1)
    back = back.transpose(1, 3, 0, 2, 4).reshape(2, quarter, slots, width)
    slot_out = (back[0] + b_out[None]).astype(jnp.bfloat16)
    slot_in_grad = back[1].astype(jnp.bfloat16)
    offset = lax.axis_index("hidden") * quarter
    mine_tokens = lax.dynamic_slice_in_dim(tokens, offset, quarter, 0)
    mine_grad = lax.dynamic_slice_in_dim(out_grad, offset, quarter, 0)
    mine_dispatch = lax.dynamic_slice_in_dim(dispatch, offset, quarter, 0)
    mine_combine = lax.dynamic_slice_in_dim(combine, offset, quarter, 0)
    comb_grad = jnp.einsum("btd,bsd->bts", mine_grad, slot_out, preferred_element_type=jnp.float32)
    disp_grad = jnp.einsum(
        "btd,bsd->bts", mine_tokens, slot_in_grad, preferred_element_type=jnp.float32
    )
    comb_wide = mine_combine.astype(jnp.float32)
    disp_wide = mine_dispatch.astype(jnp.float32)
    logit_grad = comb_wide * (comb_grad - jnp.sum(comb_wide * comb_grad, axis=2, keepdims=True))
    logit_grad = logit_grad + disp_wide * (
        disp_grad - jnp.sum(disp_wide * disp_grad, axis=1, keepdims=True)
    )
    logit_grad = logit_grad.astype(jnp.bfloat16)
    token_grad = jnp.einsum(
        "bts,bsd->btd", mine_dispatch, slot_in_grad, preferred_element_type=jnp.float32
    )
    token_grad = token_grad + jnp.einsum(
        "bts,ds->btd", logit_grad, slot_keys, preferred_element_type=jnp.float32
    )
    return token_grad.astype(jnp.bfloat16)


def solution(mesh):
    return jax.shard_map(
        local,
        mesh=mesh,
        in_specs=(
            P("expert", None, None),
            P(),
            P("expert", None, "hidden"),
            P("expert", "hidden"),
            P("expert", "hidden", None),
            P(),
            P("expert", None, None),
        ),
        out_specs=P(("expert", "hidden"), None, None),
        check_vma=False,
    )
```

time: 99.4 us -> 56.9 us (0.57)
  waiting for transfers between devices: 30.7 us -> 6.86 us
  between operations: 13.5 us -> 0.2 us
  starting transfers between devices: 12 us -> 3.97 us
  blocking collectives: 7.92 us -> 11.9 us
  local copies, waits for them, and re-layouts: 11.8 us -> 8.2 us
  other arithmetic: 0.1 us -> 1.85 us
    reduce_scatter x2 -> x0, waiting for transfers between devices: 22.3 us -> none  [send_home(): lax.psum_scatter(moved.astype(jnp.float32).astype(jnp.bfloat16), 'hidden'...]
    all_to_all x3 -> x1, starting transfers between devices: 11.9 us -> 3.97 us  [local(): lax.all_to_all(back, ('expert', 'hidden'), split_axis=0, concat_axis=0, t...]
    reshape x6 -> x3, local copies, waits for them, and re-layouts: 5.6 us -> 1.41 us  [the longest x1 0.69 us: local(): rows_in = got[:, 0].swapaxes(0, 1).reshape(k, n_expert * images, width)]
    all_to_all x1, blocking collectives: 7.92 us -> 11.9 us  [local(): lax.all_to_all(sent, 'expert', split_axis=0, concat_axis=0, tiled=True)]
    all_to_all x4 -> x1, local copies, waits for them, and re-layouts: 2.13 us -> 0.15 us  [local(): lax.all_to_all(sent, 'expert', split_axis=0, concat_axis=0, tiled=True)]
    dot_general x5, matrix products: 15.2 us -> 16.7 us  [the longest x1 6.74 us: local(): jnp.einsum('krf,kdf->krd', pre_grad, w_in, preferred_element_type=jnp.flo...]
    all_to_all x3 -> x1, waiting for transfers between devices: 8.31 us -> 6.86 us  [local(): lax.all_to_all(back, ('expert', 'hidden'), split_axis=0, concat_axis=0, t...]
    sub x1, matrix products: 2.16 us -> 0.74 us  [local(): dispatch = jax.nn.softmax(logits, axis=1).astype(jnp.bfloat16)]
  transfers between devices with their start and end apart: 5 -> 1, of which waited for: 5 -> 1; matrix products, arithmetic and copies ran while one was open for 15% -> 6% of each run, Pallas kernels for 0% -> 0%
where the time goes in v1:
time: 56.9 us; the launch traced here: 56.5 us
  matrix products  23.5 us (41%)
  blocking collectives  11.9 us (21%)
  local copies, waits for them, and re-layouts  8.2 us (14%)
  waiting for transfers between devices  6.86 us (12%)
  starting transfers between devices  3.97 us (7%)
  other arithmetic  1.85 us (3%)
    all_to_all x1, blocking collectives, local(): lax.all_to_all(sent, 'expert', split_axis=0, concat_axis=0, tiled=True)  11.9 us
    all_to_all x1, waiting for transfers between devices, local(): lax.all_to_all(back, ('expert', 'hidden'), split_axis=0, concat_axis=0, t...  6.86 us
    dot_general x1, matrix products, local(): jnp.einsum('krf,kdf->krd', pre_grad, w_in, preferred_element_type=jnp.flo...  6.74 us
    unnamed x17, local copies, waits for them, and re-layouts  4.2 us
    all_to_all x1, starting transfers between devices, local(): lax.all_to_all(back, ('expert', 'hidden'), split_axis=0, concat_axis=0, t...  3.97 us
    dot_general x1, matrix products, local(): jnp.einsum('krd,kdf->krf', rows_in, w_in, preferred_element_type=jnp.floa...  3.78 us
    dot_general x1, matrix products, local(): jnp.einsum('krf,kfd->krd', hidden_act, w_out, preferred_element_type=jnp....  3.49 us
    sub x1, matrix products, local(): combine = jax.nn.softmax(logits, axis=2).astype(jnp.bfloat16)  2.03 us
  transfers between devices with their start and end apart: 1, of which 1 were waited for; matrix products, arithmetic and copies ran while one was open for 6% of the time, Pallas kernels for 0%

profile of v1, /device:TPU:0, one launch (start us, length us, event | category | flops | bytes accessed | tf_op | source)
XLA Modules:
  0.0 56.5 jit_solution(17512600660559361393)
XLA Ops:
  0.0 0.0 copy-start
  0.0 0.0 copy-start.2
  0.0 0.8 %copy-done = bf16[1024,16]{0,1:T(8,128)(2,1)S(1)} copy-done((bf16[1024,16]{0,1:T(8,128)(2,1)S(1)}, bf16[1024,16]{0,1:T(8,128)(2,1)}, u32[]{:S(2)}) %copy-start) | copy-done | bytes 32792
  0.8 2.0 %fusion.138 = (f32[4,196]{1,0:T(4,128)S(1)}, f32[4,196,16]{1,2,0:T(8,128)S(1)}) fusion(bf16[1024,16]{0,1:T(8,128)(2,1)S(1)} %copy-done, bf16[4,196,1024]{2,0,1:T(4,128)(2,1)} %param.7), kind=kOutput, calls=%fused_computation.168 | convolution fusion | flops 25715216 | bytes 1691712 | tf_op jit(solution)/shard_map/sub | solution.py:24
  2.8 0.0 copy-done.2
  2.8 0.7 %fusion.139 = (f32[4,16]{1,0:T(4,128)S(1)}, f32[4,196,16]{1,2,0:T(8,128)S(1)}) fusion(bf16[1024,16]{0,1:T(8,128)(2,1)S(1)} %copy-done, bf16[4,196,1024]{2,0,1:T(4,128)(2,1)S(1)} %copy-done.2), kind=kOutput, calls=%fused_computation.169 | convolution fusion | flops 25715396 | bytes 1688832 | tf_op jit(solution)/shard_map/sub | solution.py:23
  3.5 0.0 copy-start.1
  3.6 0.6 %divide_convert_fusion = (bf16[4,196,16]{1,2,0:T(8,128)(2,1)}, bf16[4,196,16]{1,2,0:T(8,128)(2,1)S(1)}) fusion(f32[4,196,16]{1,2,0:T(8,128)S(1)} %get-tuple-element.10, f32[4,196]{1,0:T(4,128)S(1)} %get-tuple-element.9, f32[4,196,16]{1,2,0:T(8,128)S(1)} %get-tuple-element.12, f32[4,16]{1,0:T(4,128)S(1)} %get-tuple-element.11), kind=kLoop, calls=%fused_computation.101 | loop fusion | flops 50176 | bytes 153920 | tf_op jit(solution)/shard_map/convert_element_type | solution.py:24
  4.2 1.0 %fusion.7 = bf16[16,4,1024]{2,0,1:T(8,128)(2,1)S(1)} fusion(bf16[4,196,16]{1,2,0:T(8,128)(2,1)S(1)} %get-tuple-element.19, bf16[4,196,1024]{2,0,1:T(4,128)(2,1)S(1)} %copy-done.2), kind=kOutput, calls=%fused_computation.14 | convolution fusion | flops 25755648 | bytes 1761792 | tf_op jit(solution)/shard_map/bts,btd->sbd/dot_general | solution.py:25
  5.2 0.1 copy.46
  5.3 0.0 copy-done.1
  5.3 1.7 %fusion.8 = bf16[16,4,1024]{2,0,1:T(8,128)(2,1)S(1)} fusion(bf16[4,196,16]{1,2,0:T(8,128)(2,1)} %get-tuple-element.18, bf16[4,196,1024]{2,0,1:T(4,128)(2,1)S(1)} %copy-done.1), kind=kOutput, calls=%fused_computation.15 | convolution fusion | flops 25755648 | bytes 1761792 | tf_op jit(solution)/shard_map/bts,btd->sbd/dot_general | solution.py:28
  7.1 0.1 copy.48
  7.2 0.0 copy-start.6
  7.2 0.7 %reshape.100 = bf16[8,8,1024]{2,1,0:T(8,128)(2,1)} reshape(bf16[16,4,1024]{2,1,0:T(4,128)(2,1)S(1)} %copy.48) | data formatting | bytes 262144 | tf_op jit(solution)/shard_map/reshape | solution.py:34
  7.9 0.9 %pad_maximum_fusion = bf16[8,16,1024]{2,1,0:T(8,128)(2,1)S(1)} fusion(bf16[8,8,1024]{2,1,0:T(8,128)(2,1)} %reshape.100, bf16[8,8,1024]{2,1,0:T(8,128)(2,1)S(1)} %reshape.99), kind=kLoop, calls=%fused_computation.40 | loop fusion | flops 524288 | bytes 524288 | tf_op jit(solution)/shard_map/concatenate | solution.py:31
  8.8 11.9 %all_to_all.10 = bf16[8,16,1024]{2,1,0:T(8,128)(2,1)S(1)} all-to-all(bf16[8,16,1024]{2,1,0:T(8,128)(2,1)S(1)} %pad_maximum_fusion), channel_id=1, replica_groups=mesh['expert'=8,'hidden'=4] {'expert'}, dimensions={0} | all-to-all | bytes 524288 | tf_op jit(solution)/shard_map/all_to_all | solution.py:38
  20.7 0.1 copy.49
  20.9 0.1 copy.50
  21.0 0.7 %reshape.102 = bf16[2,32,1024]{2,1,0:T(8,128)(2,1)} reshape(bf16[2,8,4,1024]{3,2,1,0:T(4,128)(2,1)S(1)} %copy.50) | data formatting | bytes 262144 | tf_op jit(solution)/shard_map/reshape | solution.py:40
  21.7 0.8 %copy.51 = bf16[2,8,4,1024]{3,0,2,1:T(2,128)(2,1)} copy(bf16[2,8,4,1024]{3,1,2,0:T(8,128)(2,1)S(1)} %get-tuple-element.7) | data formatting | bytes 262144 | tf_op jit(solution)/shard_map/transpose | solution.py:41
  22.5 0.0 copy-done.6
  22.5 3.8 %fusion.77 = (u8[32,1024]{1,0:T(8,128)(4,1)}, u8[32,1024]{1,0:T(8,128)(4,1)}, f32[2,32,1024]{2,1,0:T(8,128)S(1)}) fusion(f32[2,1024]{1,0:T(2,128)S(1)} %copy-done.6, bf16[2,32,1024]{2,1,0:T(8,128)(2,1)} %reshape.102, bf16[2,1024,1024]{2,1,0:T(8,128)(2,1)} %param.9), kind=kOutput, calls=%fused_computation.104 | convolution fusion | flops 135069696 | bytes 4661248 | tf_op jit(solution)/shard_map/krd,kdf->krf/dot_general | solution.py:43
  26.2 6.7 %fusion.6 = bf16[32,2,1024]{2,0,1:T(8,128)(2,1)} fusion(bf16[2,1024,1024]{2,1,0:T(8,128)(2,1)} %param.9, bf16[2,1024,1024]{2,1,0:T(8,128)(2,1)} %param.11, f32[2,32,1024]{2,1,0:T(8,128)S(1)} %get-tuple-element.13, bf16[2,32,1024]{2,0,1:T(2,128)(2,1)} %bitcast.81), kind=kOutput, calls=%fused_computation.13 | convolution fusion | flops 269156352 | bytes 8912896 | tf_op jit(solution)/shard_map/krf,kdf->krd/dot_general | solution.py:50
  33.0 0.0 copy-start.3
  33.0 3.5 %fusion.5 = bf16[32,2,1024]{2,0,1:T(8,128)(2,1)S(1)} fusion(bf16[2,1024,1024]{2,1,0:T(8,128)(2,1)} %param.11, f32[2,32,1024]{2,1,0:T(8,128)S(1)} %get-tuple-element.13, u8[32,1024]{1,0:T(8,128)(4,1)} %get-tuple-element.6, u8[32,1024]{1,0:T(8,128)(4,1)} %get-tuple-element.5), kind=kOutput, calls=%fused_computation.12 | convolution fusion | flops 138870784 | bytes 4653056 | tf_op jit(solution)/shard_map/krf,kfd->krd/dot_general | solution.py:47
  36.5 0.0 copy-done.3
  36.5 0.9 %copy.53 = bf16[32,4,1024]{2,1,0:T(4,128)(2,1)} copy(bf16[32,4,1024]{2,0,1:T(8,128)(2,1)S(1)} %pad_maximum_fusion.1) | data formatting | bytes 524288 | tf_op jit(solution)/shard_map/concatenate | solution.py:57
  37.4 4.0 %all-to-all-start.1 = ((bf16[32,4,1024]{2,1,0:T(4,128)(2,1)}), bf16[32,4,1024]{2,1,0:T(4,128)(2,1)S(1)}, u32[]{:S(2)}, u32[]{:S(2)}) async-start(bf16[32,4,1024]{2,1,0:T(4,128)(2,1)} %copy.53), calls=%async_computation.1 | async-start | bytes 524288 | tf_op jit(solution)/shard_map/all_to_all | solution.py:58
  41.4 1.7 %copy.47 = bf16[4,196,1024]{2,1,0:T(8,128)(2,1)} copy(bf16[4,196,1024]{2,0,1:T(4,128)(2,1)S(1)} %copy-done.1) | data formatting | bytes 3211264 | tf_op args[6]
  43.1 1.7 %copy.44 = bf16[4,196,1024]{2,1,0:T(8,128)(2,1)} copy(bf16[4,196,1024]{2,0,1:T(4,128)(2,1)S(1)} %copy-done.2) | data formatting | bytes 3211264 | tf_op args[0]
  44.7 0.0 copy-start.4
  44.8 0.0 copy-start.5
  44.8 6.9 %all-to-all-done.1 = bf16[32,4,1024]{2,1,0:T(4,128)(2,1)S(1)} async-done(((bf16[32,4,1024]{2,1,0:T(4,128)(2,1)}), bf16[32,4,1024]{2,1,0:T(4,128)(2,1)S(1)}, u32[]{:S(2)}, u32[]{:S(2)}) %all-to-all-start.1) | async-done | bytes 262176 | tf_op jit(solution)/shard_map/all_to_all | solution.py:58
  51.6 0.3 reshape.111
  51.9 0.3 reduce_sum.49
  52.2 0.1 copy.74
  52.3 0.1 copy.57
  52.5 0.3 fusion.88
  52.7 1.3 %fusion.85 = (f32[16]{0:T(128)S(1)}, f32[196,16]{0,1:T(8,128)S(1)}) fusion(bf16[4,196,16]{1,2,0:T(8,128)(2,1)S(1)} %get-tuple-element.19, s32[]{:T(128)S(6)} %select_n.2, bf16[16,1024]{1,0:T(8,128)(2,1)S(1)} %convert_element_type.84, bf16[4,196,1024]{2,1,0:T(8,128)(2,1)} %copy.44), kind=kOutput, calls=%fused_computation.116 | convolution fusion | flops 6431920 | bytes 462272 | tf_op jit(solution)/shard_map/btd,bsd->bts/dot_general | solution.py:70
  54.1 0.0 copy-done.4
  54.1 0.0 copy-done.5
  54.1 1.2 %fusion.82 = (f32[196]{0:T(256)S(1)}, f32[196,16]{0,1:T(8,128)S(1)}) fusion(bf16[4,196,16]{1,2,0:T(8,128)(2,1)S(1)} %copy-done.4, s32[]{:T(128)S(6)} %select_n.2, f32[16,1024]{1,0:T(8,128)S(1)} %squeeze.12, f32[16,1024]{1,0:T(8,128)S(1)} %copy-done.5, bf16[4,196,1024]{2,1,0:T(8,128)(2,1)} %copy.47), kind=kOutput, calls=%fused_computation.113 | convolution fusion | flops 6464508 | bytes 561296 | tf_op jit(solution)/shard_map/btd,bsd->bts/dot_general | solution.py:69
  55.4 1.1 %fusion.3 = bf16[1,196,1024]{2,1,0:T(8,128)(2,1)} fusion(f32[196,1024]{1,0:T(8,128)S(1)} %fusion.88, bf16[1024,16]{0,1:T(8,128)(2,1)S(1)} %copy-done, f32[196,16]{0,1:T(8,128)S(1)} %get-tuple-element.15, f32[196,16]{0,1:T(8,128)S(1)} %get-tuple-element.17, f32[16]{0:T(128)S(1)} %get-tuple-element.14, f32[196]{0:T(256)S(1)} %get-tuple-element.16, ...), kind=kOutput, calls=%fused_computation.4 | convolution fusion | flops 6849024 | bytes 1304068 | tf_op jit(solution)/shard_map/bts,ds->btd/dot_general | solution.py:83
  (8 shorter events, 0.2 us)
Async XLA Ops:
  0.0 0.8 %copy-start = (bf16[1024,16]{0,1:T(8,128)(2,1)S(1)}, bf16[1024,16]{0,1:T(8,128)(2,1)}, u32[]{:S(2)}) copy-start(bf16[1024,16]{0,1:T(8,128)(2,1)} %param.8) | copy-start | bytes 98308
  0.0 2.8 %copy-start.2 = (bf16[4,196,1024]{2,0,1:T(4,128)(2,1)S(1)}, bf16[4,196,1024]{2,0,1:T(4,128)(2,1)}, u32[]{:S(2)}) copy-start(bf16[4,196,1024]{2,0,1:T(4,128)(2,1)} %param.7) | copy-start | bytes 4816900
  3.5 1.8 %copy-start.1 = (bf16[4,196,1024]{2,0,1:T(4,128)(2,1)S(1)}, bf16[4,196,1024]{2,0,1:T(4,128)(2,1)}, u32[]{:S(2)}) copy-start(bf16[4,196,1024]{2,0,1:T(4,128)(2,1)} %param.13) | copy-start | bytes 4816900
  7.2 15.3 %copy-start.6 = (f32[2,1024]{1,0:T(2,128)S(1)}, f32[2,1024]{1,0:T(2,128)}, u32[]{:S(2)}) copy-start(f32[2,1024]{1,0:T(2,128)} %param.10) | copy-start | bytes 24580
  33.0 3.5 %copy-start.3 = (bf16[32,2,1024]{2,0,1:T(8,128)(2,1)S(1)}, bf16[32,2,1024]{2,0,1:T(8,128)(2,1)}, u32[]{:S(2)}) copy-start(bf16[32,2,1024]{2,0,1:T(8,128)(2,1)} %fusion.6) | copy-start | bytes 393220
  37.4 14.2 %all-to-all-start.1 = ((bf16[32,4,1024]{2,1,0:T(4,128)(2,1)}), bf16[32,4,1024]{2,1,0:T(4,128)(2,1)S(1)}, u32[]{:S(2)}, u32[]{:S(2)}) async-start(bf16[32,4,1024]{2,1,0:T(4,128)(2,1)} %copy.53), calls=%async_computation.1 | async-start | bytes 524288 | tf_op jit(solution)/shard_map/all_to_all | solution.py:58
  44.7 9.3 %copy-start.4 = (bf16[4,196,16]{1,2,0:T(8,128)(2,1)S(1)}, bf16[4,196,16]{1,2,0:T(8,128)(2,1)}, u32[]{:S(2)}) copy-start(bf16[4,196,16]{1,2,0:T(8,128)(2,1)} %get-tuple-element.18) | copy-start | bytes 75268
  44.8 9.4 %copy-start.5 = (f32[16,1024]{1,0:T(8,128)S(1)}, f32[16,1024]{1,0:T(8,128)}, u32[]{:S(2)}) copy-start(f32[16,1024]{1,0:T(8,128)} %param.12) | copy-start | bytes 196612

commit v2 on v1

--- a/solution.py
+++ b/solution.py
@@ -9,6 +9,14 @@
         0.5 * (1.0 + lax.erf(pre_act * 0.7071067811865476))
         + pre_act * jnp.exp(-0.5 * pre_act * pre_act) * 0.3989422804014327
     )
+
+
+def exchange(blocks, axis, sign):
+    n = lax.axis_size(axis)
+    got = [blocks[0]]
+    for j in range(1, n):
+        got.append(lax.ppermute(blocks[j], axis, [(i, (i + sign * j) % n) for i in range(n)]))
+    return got
 
 
 def local(tokens, slot_keys, w_in, b_in, w_out, b_out, out_grad):
@@ -35,10 +43,10 @@
         ],
         axis=1,
     )
-    got = lax.all_to_all(sent, "expert", split_axis=0, concat_axis=0, tiled=True)
-    got = got.reshape(n_expert, 2, k, images, width)
-    rows_in = got[:, 0].swapaxes(0, 1).reshape(k, n_expert * images, width)
-    rows_grad = got[:, 1].swapaxes(0, 1).reshape(k, n_expert * images, width)
+    sent = jnp.roll(sent, -lax.axis_index("expert"), 0)
+    got = exchange([sent[j] for j in range(n_expert)], "expert", 1)
+    rows_in = jnp.concatenate([g[: k * images].reshape(k, images, width) for g in got], axis=1)
+    rows_grad = jnp.concatenate([g[k * images :].reshape(k, images, width) for g in got], axis=1)
     pre_act = (
         jnp.einsum("krd,kdf->krf", rows_in, w_in, preferred_element_type=jnp.float32)
         + b_in[:, None]
@@ -49,18 +57,24 @@
     pre_grad = (act_grad * gelu_slope(pre_act)).astype(jnp.bfloat16)
     in_part = jnp.einsum("krf,kdf->krd", pre_grad, w_in, preferred_element_type=jnp.float32)
 
-    def home(part):
-        part = part.astype(jnp.bfloat16).reshape(k, n_all, quarter, width)
-        part = part.swapaxes(0, 1).reshape(n_all, k * quarter, width)
-        return part
+    def gather_quarters(part):
+        part = part.astype(jnp.bfloat16).reshape(k, n_expert, n_hidden, quarter, width)
+        part = part.transpose(2, 1, 0, 3, 4).reshape(n_hidden, n_expert * k * quarter, width)
+        return jnp.roll(part, -lax.axis_index("hidden"), 0)
 
-    back = jnp.concatenate([home(out_part), home(in_part)], axis=1)
-    back = lax.all_to_all(back, ("expert", "hidden"), split_axis=0, concat_axis=0, tiled=True)
-    back = back.reshape(n_expert, n_hidden, 2, k, quarter, width).astype(jnp.float32)
-    back = jnp.sum(back, axis=1)
+    parts = jnp.concatenate([gather_quarters(out_part), gather_quarters(in_part)], axis=1)
+    parts = exchange([parts[j] for j in range(n_hidden)], "hidden", 1)
+    total = sum(p.astype(jnp.float32) for p in parts)
+    total = total.reshape(2, n_expert, k, quarter, width)
+    bias = lax.dynamic_slice_in_dim(b_out, lax.axis_index("expert") * k, k, 0)
+    both = jnp.stack([total[0] + bias[None, :, None], total[1]], axis=1).astype(jnp.bfloat16)
+    both = both.reshape(n_expert, 2 * k * quarter, width)
+    back = exchange([both[j] for j in range(n_expert)], "expert", -1)
+    back = jnp.stack(back)
+    back = back.reshape(n_expert, 2, k, quarter, width)
+    back = jnp.roll(back, lax.axis_index("expert"), 0)
     back = back.transpose(1, 3, 0, 2, 4).reshape(2, quarter, slots, width)
-    slot_out = (back[0] + b_out[None]).astype(jnp.bfloat16)
-    slot_in_grad = back[1].astype(jnp.bfloat16)
+    slot_out, slot_in_grad = back[0], back[1]
     offset = lax.axis_index("hidden") * quarter
     mine_tokens = lax.dynamic_slice_in_dim(tokens, offset, quarter, 0)
     mine_grad = lax.dynamic_slice_in_dim(out_grad, offset, quarter, 0)

time: 56.9 us -> 61.1 us (1.074)
  starting transfers between devices: 3.97 us -> 21.3 us
  blocking collectives: 11.9 us -> 0 us
  matrix products: 23.5 us -> 19 us
  local copies, waits for them, and re-layouts: 8.2 us -> 10 us
    ppermute x0 -> x17, starting transfers between devices: none -> 21.3 us  [exchange(): lax.ppermute(blocks[j], axis, [(i, (i + sign * j) % n) for i in range(n)])]
    all_to_all x1 -> x0, blocking collectives: 11.9 us -> none  [local(): lax.all_to_all(sent, 'expert', split_axis=0, concat_axis=0, tiled=True)]
    ppermute x0 -> x17, waiting for transfers between devices: none -> 7.1 us  [exchange(): lax.ppermute(blocks[j], axis, [(i, (i + sign * j) % n) for i in range(n)])]
    all_to_all x1 -> x0, waiting for transfers between devices: 6.86 us -> none  [local(): lax.all_to_all(back, ('expert', 'hidden'), split_axis=0, concat_axis=0, t...]
    all_to_all x1 -> x0, starting transfers between devices: 3.97 us -> none  [local(): lax.all_to_all(back, ('expert', 'hidden'), split_axis=0, concat_axis=0, t...]
    slice x4 -> x11, local copies, waits for them, and re-layouts: 0.1 us -> 3.76 us  [the longest x8 3.7 us: local(): g[:k * images].reshape(k, images, width)]
    dot_general x1, matrix products: 3.49 us -> 1.27 us  [local(): jnp.einsum('krf,kfd->krd', hidden_act, w_out, preferred_element_type=jnp....]
    sub x1, matrix products: 0.74 us -> 2.28 us  [local(): dispatch = jax.nn.softmax(logits, axis=1).astype(jnp.bfloat16)]
  transfers between devices with their start and end apart: 1 -> 17, of which waited for: 1 -> 6; matrix products, arithmetic and copies ran while one was open for 6% -> 10% of each run, Pallas kernels for 0% -> 0%
where the time goes in v2:
time: 61.1 us; the launch traced here: 60.1 us
  starting transfers between devices  21.3 us (35%)
  matrix products  19 us (31%)
  local copies, waits for them, and re-layouts  10 us (16%)
  waiting for transfers between devices  7.1 us (12%)
  other arithmetic  2.13 us (3%)
    ppermute x17, starting transfers between devices, exchange(): lax.ppermute(blocks[j], axis, [(i, (i + sign * j) % n) for i in range(n)])  21.3 us
    ppermute x17, waiting for transfers between devices, exchange(): lax.ppermute(blocks[j], axis, [(i, (i + sign * j) % n) for i in range(n)])  7.1 us
    dot_general x1, matrix products, local(): jnp.einsum('krf,kdf->krd', pre_grad, w_in, preferred_element_type=jnp.flo...  6.03 us
    slice x8, local copies, waits for them, and re-layouts, local(): g[:k * images].reshape(k, images, width)  3.7 us
    dot_general x1, matrix products, local(): jnp.einsum('krd,kdf->krf', rows_in, w_in, preferred_element_type=jnp.floa...  3.22 us
    unnamed x40, local copies, waits for them, and re-layouts  2.69 us
    sub x1, matrix products, local(): dispatch = jax.nn.softmax(logits, axis=1).astype(jnp.bfloat16)  2.28 us
    dot_general x1, matrix products, local(): jnp.einsum('krf,kfd->krd', hidden_act, w_out, preferred_element_type=jnp....  1.27 us
  transfers between devices with their start and end apart: 17, of which 6 were waited for; matrix products, arithmetic and copies ran while one was open for 10% of the time, Pallas kernels for 0%

profile of v2, /device:TPU:0, one launch (start us, length us, event | category | flops | bytes accessed | tf_op | source)
XLA Modules:
  0.0 60.1 jit_solution(5051104196380985182)
XLA Ops:
  0.0 2.3 %fusion.155 = (f32[4,16]{1,0:T(4,128)S(1)}, f32[4,196,16]{1,2,0:T(8,128)S(1)}) fusion(bf16[1024,16]{0,1:T(8,128)(2,1)} %param.10, bf16[4,196,1024]{2,0,1:T(4,128)(2,1)} %param.9), kind=kOutput, calls=%fused_computation.233 | convolution fusion | flops 25715396 | bytes 1688832 | tf_op jit(solution)/shard_map/sub | solution.py:31
  2.3 1.2 %fusion.156 = (f32[4,196]{1,0:T(4,128)S(1)}, f32[4,196,16]{1,2,0:T(8,128)}) fusion(bf16[1024,16]{0,1:T(8,128)(2,1)S(1)} %copy-done.9, bf16[4,196,1024]{2,0,1:T(4,128)(2,1)S(1)} %copy-done.2), kind=kOutput, calls=%fused_computation.234 | convolution fusion | flops 25715216 | bytes 1691712 | tf_op jit(solution)/shard_map/sub | solution.py:32
  3.5 0.1 divide_convert_fusion.1
  3.6 1.0 %fusion.5 = bf16[16,4,1024]{2,0,1:T(8,128)(2,1)S(1)} fusion(bf16[4,196,16]{1,2,0:T(8,128)(2,1)S(1)} %divide_convert_fusion.1, bf16[4,196,1024]{2,0,1:T(4,128)(2,1)S(1)} %copy-done.2), kind=kOutput, calls=%fused_computation.12 | convolution fusion | flops 25755648 | bytes 1761792 | tf_op jit(solution)/shard_map/bts,btd->sbd/dot_general | solution.py:33
  4.6 0.1 copy.46
  4.8 0.9 %divide_convert_fusion = bf16[4,196,16]{1,2,0:T(8,128)(2,1)S(1)} fusion(f32[4,196,16]{1,2,0:T(8,128)} %get-tuple-element.48, f32[4,196]{1,0:T(4,128)S(1)} %get-tuple-element.47), kind=kLoop, calls=%fused_computation.124 | loop fusion | flops 25088 | bytes 78400 | tf_op jit(solution)/shard_map/convert_element_type | solution.py:32
  5.7 1.0 %fusion.6 = bf16[16,4,1024]{2,0,1:T(8,128)(2,1)S(1)} fusion(bf16[4,196,16]{1,2,0:T(8,128)(2,1)S(1)} %divide_convert_fusion, bf16[4,196,1024]{2,0,1:T(4,128)(2,1)S(1)} %copy-done.1), kind=kOutput, calls=%fused_computation.13 | convolution fusion | flops 25755648 | bytes 1761792 | tf_op jit(solution)/shard_map/bts,btd->sbd/dot_general | solution.py:36
  6.6 0.8 %copy.48 = bf16[16,4,1024]{2,1,0:T(4,128)(2,1)} copy(bf16[16,4,1024]{2,0,1:T(8,128)(2,1)S(1)} %fusion.6) | data formatting | bytes 262144 | tf_op jit(solution)/shard_map/convert_element_type | solution.py:38
  7.4 0.9 %reshape.215 = bf16[8,8,1024]{2,1,0:T(8,128)(2,1)S(1)} reshape(bf16[16,4,1024]{2,1,0:T(4,128)(2,1)} %copy.48) | data formatting | bytes 262144 | tf_op jit(solution)/shard_map/reshape | solution.py:42
  8.4 0.1 fusion.26
  8.5 0.6 %slice_bitcast_fusion = (bf16[16,1024]{1,0:T(8,128)(2,1)S(1)}, bf16[16,1024]{1,0:T(8,128)(2,1)S(1)}, bf16[16,1024]{1,0:T(8,128)(2,1)S(1)}, bf16[16,1024]{1,0:T(8...) fusion(bf16[8,16,1024]{2,1,0:T(8,128)(2,1)S(1)} %fusion.26), kind=kLoop, calls=%fused_computation.147 | loop fusion | bytes 458752 | tf_op jit(solution)/shard_map/squeeze | solution.py:47
  9.1 0.5 collective-permute-start
  9.6 2.5 %collective-permute-start.1 = (bf16[16,1024]{1,0:T(8,128)(2,1)S(1)}, bf16[16,1024]{1,0:T(8,128)(2,1)}, u32[]{:S(2)}, u32[]{:S(2)}) collective-permute-start(bf16[16,1024]{1,0:T(8,128)(2,1)S(1)} %get-tuple-element.19), channel_id=1, source_target_pairs={{0,8},{4,12},{8,16},{12,20},{16,24},{20,28},{24,0},{28,4},{1,9},{5... | collective-permute-start | bytes 98312 | tf_op jit(solution)/shard_map/ppermute | solution.py:18
  12.1 2.4 %collective-permute-start.2 = (bf16[16,1024]{1,0:T(8,128)(2,1)S(1)}, bf16[16,1024]{1,0:T(8,128)(2,1)}, u32[]{:S(2)}, u32[]{:S(2)}) collective-permute-start(bf16[16,1024]{1,0:T(8,128)(2,1)S(1)} %get-tuple-element.18), channel_id=1, source_target_pairs={{0,12},{4,16},{8,20},{12,24},{16,28},{20,0},{24,4},{28,8},{1,13},{... | collective-permute-start | bytes 98312 | tf_op jit(solution)/shard_map/ppermute | solution.py:18
  14.5 0.5 collective-permute-start.3
  15.0 0.1 collective-permute-start.4
  15.1 1.7 %copy.47 = bf16[4,196,1024]{2,1,0:T(8,128)(2,1)} copy(bf16[4,196,1024]{2,0,1:T(4,128)(2,1)S(1)} %copy-done.1) | data formatting | bytes 3211264 | tf_op args[6]
  16.8 0.5 copy.44
  17.3 1.5 %collective-permute-start.5 = (bf16[16,1024]{1,0:T(8,128)(2,1)S(1)}, bf16[16,1024]{1,0:T(8,128)(2,1)S(1)}, u32[]{:S(2)}, u32[]{:S(2)}) collective-permute-start(bf16[16,1024]{1,0:T(8,128)(2,1)S(1)} %get-tuple-element.15), channel_id=1, source_target_pairs={{0,24},{4,28},{8,0},{12,4},{16,8},{20,12},{24,16},{28,20},{1,25},{... | collective-permute-start | bytes 98312 | tf_op jit(solution)/shard_map/ppermute | solution.py:18
  18.8 0.7 %fusion.154 = (bf16[8,1024]{1,0:T(8,128)(2,1)S(1)}, bf16[8,1024]{1,0:T(8,128)(2,1)S(1)}) fusion(bf16[16,1024]{1,0:T(8,128)(2,1)} %collective-permute-done), kind=kLoop, calls=%fused_computation.232 | loop fusion | bytes 65536 | tf_op jit(solution)/shard_map/slice | solution.py:48
  19.6 0.0 collective-permute-done.1
  19.6 2.3 %collective-permute-start.6 = (bf16[16,1024]{1,0:T(8,128)(2,1)S(1)}, bf16[16,1024]{1,0:T(8,128)(2,1)S(1)}, u32[]{:S(2)}, u32[]{:S(2)}) collective-permute-start(bf16[16,1024]{1,0:T(8,128)(2,1)S(1)} %get-tuple-element.14), channel_id=1, source_target_pairs={{0,28},{4,0},{8,4},{12,8},{16,12},{20,16},{24,20},{28,24},{1,29},{... | collective-permute-start | bytes 98312 | tf_op jit(solution)/shard_map/ppermute | solution.py:18
  21.9 0.7 %fusion.153 = (bf16[8,1024]{1,0:T(8,128)(2,1)S(1)}, bf16[8,1024]{1,0:T(8,128)(2,1)S(1)}) fusion(bf16[16,1024]{1,0:T(8,128)(2,1)} %collective-permute-done.1), kind=kLoop, calls=%fused_computation.231 | loop fusion | bytes 65536 | tf_op jit(solution)/shard_map/slice | solution.py:48
  22.6 0.7 %fusion.152 = (bf16[8,1024]{1,0:T(8,128)(2,1)S(1)}, bf16[8,1024]{1,0:T(8,128)(2,1)S(1)}) fusion(bf16[16,1024]{1,0:T(8,128)(2,1)} %collective-permute-done.2), kind=kLoop, calls=%fused_computation.230 | loop fusion | bytes 65536 | tf_op jit(solution)/shard_map/slice | solution.py:48
  23.4 0.0 collective-permute-done.3
  23.4 0.7 %fusion.151 = (bf16[8,1024]{1,0:T(8,128)(2,1)S(1)}, bf16[8,1024]{1,0:T(8,128)(2,1)S(1)}) fusion(bf16[16,1024]{1,0:T(8,128)(2,1)} %collective-permute-done.3), kind=kLoop, calls=%fused_computation.229 | loop fusion | bytes 65536 | tf_op jit(solution)/shard_map/slice | solution.py:48
  24.1 0.0 collective-permute-done.4
  24.1 0.7 %fusion.150 = (bf16[8,1024]{1,0:T(8,128)(2,1)S(1)}, bf16[8,1024]{1,0:T(8,128)(2,1)S(1)}) fusion(bf16[16,1024]{1,0:T(8,128)(2,1)} %collective-permute-done.4), kind=kLoop, calls=%fused_computation.228 | loop fusion | bytes 65536 | tf_op jit(solution)/shard_map/slice | solution.py:48
  25.0 0.0 collective-permute-done.6
  25.1 0.1 concatenate.36
  25.2 0.0 copy-start.3
  25.2 3.2 %fusion.84 = (u8[32,1024]{1,0:T(8,128)(4,1)S(1)}, u8[32,1024]{1,0:T(8,128)(4,1)S(1)}, f32[2,32,1024]{2,1,0:T(8,128)S(1)}) fusion(f32[2,1024]{1,0:T(2,128)S(1)} %copy-done.8, bf16[2,32,1024]{2,1,0:T(8,128)(2,1)S(1)} %concatenate.36, bf16[2,1024,1024]{2,1,0:T(8,128)(2,1)} %param.11), kind=kOutput, calls=%fused_computation.127 | convolution fusion | flops 135069696 | bytes 4661248 | tf_op jit(solution)/shard_map/krd,kdf->krf/dot_general | solution.py:51
  28.4 0.2 copy-done.3
  28.7 1.3 %convolution_convert_fusion.1 = bf16[2,32,1024]{2,1,0:T(8,128)(2,1)S(1)} fusion(bf16[2,1024,1024]{2,1,0:T(8,128)(2,1)S(1)} %copy-done.3, f32[2,32,1024]{2,1,0:T(8,128)S(1)} %get-tuple-element.49, u8[32,1024]{1,0:T(8,128)(4,1)S(1)} %get-tuple-element.7, u8[32,1024]{1,0:T(8,128)(4,1)S(1)} %get-tuple-element.6), kind=kOutput, calls=%fused_computation.9 | convolution fusion | flops 138870784 | bytes 4653056 | tf_op jit(solution)/shard_map/krf,kfd->krd/dot_general | solution.py:55
  29.9 0.1 reshape.224
  30.2 0.1 concatenate.37
  30.3 6.0 %convolution_convert_fusion = bf16[2,32,1024]{2,1,0:T(8,128)(2,1)S(1)} fusion(bf16[2,1024,1024]{2,1,0:T(8,128)(2,1)} %param.11, bf16[2,32,1024]{2,1,0:T(8,128)(2,1)S(1)} %concatenate.37, bf16[2,1024,1024]{2,1,0:T(8,128)(2,1)} %param.13, f32[2,32,1024]{2,1,0:T(8,128)S(1)} %get-tuple-element.49), kind=kOutput, calls=%fused_computation.8 | convolution fusion | flops 269156352 | bytes 8912896 | tf_op jit(solution)/shard_map/krf,kdf->krd/dot_general | solution.py:58
  36.4 0.1 reshape.234
  36.5 0.5 fusion.39
  37.0 0.4 fusion.43
  37.5 1.6 %collective-permute-start.7 = (bf16[32,1024]{1,0:T(8,128)(2,1)S(1)}, bf16[32,1024]{1,0:T(8,128)(2,1)S(1)}, u32[]{:S(2)}, u32[]{:S(2)}) collective-permute-start(bf16[32,1024]{1,0:T(8,128)(2,1)S(1)} %bitcast.110), channel_id=1, source_target_pairs={{0,1},{1,2},{2,3},{3,0},{4,5},{5,6},{6,7},{7,4},{8,9},{9,10},{10,1... | collective-permute-start | bytes 196616 | tf_op jit(solution)/shard_map/ppermute | solution.py:18
  39.1 2.7 %collective-permute-start.8 = (bf16[32,1024]{1,0:T(8,128)(2,1)S(1)}, bf16[32,1024]{1,0:T(8,128)(2,1)S(1)}, u32[]{:S(2)}, u32[]{:S(2)}) collective-permute-start(bf16[32,1024]{1,0:T(8,128)(2,1)S(1)} %bitcast.111), channel_id=1, source_target_pairs={{0,2},{1,3},{2,0},{3,1},{4,6},{5,7},{6,4},{7,5},{8,10},{9,11},{10,... | collective-permute-start | bytes 196616 | tf_op jit(solution)/shard_map/ppermute | solution.py:18
  41.8 1.4 %collective-permute-start.9 = (bf16[32,1024]{1,0:T(8,128)(2,1)S(1)}, bf16[32,1024]{1,0:T(8,128)(2,1)S(1)}, u32[]{:S(2)}, u32[]{:S(2)}) collective-permute-start(bf16[32,1024]{1,0:T(8,128)(2,1)S(1)} %bitcast.112), channel_id=1, source_target_pairs={{0,3},{1,0},{2,1},{3,2},{4,7},{5,4},{6,5},{7,6},{8,11},{9,8},{10,9... | collective-permute-start | bytes 196616 | tf_op jit(solution)/shard_map/ppermute | solution.py:18
  43.2 1.1 %collective-permute-done.7 = bf16[32,1024]{1,0:T(8,128)(2,1)S(1)} collective-permute-done((bf16[32,1024]{1,0:T(8,128)(2,1)S(1)}, bf16[32,1024]{1,0:T(8,128)(2,1)S(1)}, u32[]{:S(2)}, u32[]{:S(2)}) %collective-permute-start.7) | collective-permute-done | bytes 65568 | tf_op jit(solution)/shard_map/ppermute | solution.py:18
  44.3 1.9 %collective-permute-done.8 = bf16[32,1024]{1,0:T(8,128)(2,1)S(1)} collective-permute-done((bf16[32,1024]{1,0:T(8,128)(2,1)S(1)}, bf16[32,1024]{1,0:T(8,128)(2,1)S(1)}, u32[]{:S(2)}, u32[]{:S(2)}) %collective-permute-start.8) | collective-permute-done | bytes 65568 | tf_op jit(solution)/shard_map/ppermute | solution.py:18
  46.2 0.3 collective-permute-done.9
  46.6 0.0 copy-start.10
  46.7 0.1 pad_maximum_fusion.1
  46.8 0.9 %collective-permute-start.10 = (bf16[4,1024]{1,0:T(4,128)(2,1)S(1)}, bf16[4,1024]{1,0:T(4,128)(2,1)S(1)}, u32[]{:S(2)}, u32[]{:S(2)}) collective-permute-start(bf16[4,1024]{1,0:T(4,128)(2,1)S(1)} %squeeze.69), channel_id=1, source_target_pairs={{0,28},{4,0},{8,4},{12,8},{16,12},{20,16},{24,20},{28,24},{1,29},{... | collective-permute-start | bytes 24584 | tf_op jit(solution)/shard_map/ppermute | solution.py:18
  47.7 0.8 %collective-permute-start.11 = (bf16[4,1024]{1,0:T(4,128)(2,1)S(1)}, bf16[4,1024]{1,0:T(4,128)(2,1)S(1)}, u32[]{:S(2)}, u32[]{:S(2)}) collective-permute-start(bf16[4,1024]{1,0:T(4,128)(2,1)S(1)} %squeeze.70), channel_id=1, source_target_pairs={{0,24},{4,28},{8,0},{12,4},{16,8},{20,12},{24,16},{28,20},{1,25},{... | collective-permute-start | bytes 24584 | tf_op jit(solution)/shard_map/ppermute | solution.py:18
  48.6 0.3 collective-permute-start.12
  48.9 1.5 %collective-permute-start.13 = (bf16[4,1024]{1,0:T(4,128)(2,1)S(1)}, bf16[4,1024]{1,0:T(4,128)(2,1)S(1)}, u32[]{:S(2)}, u32[]{:S(2)}) collective-permute-start(bf16[4,1024]{1,0:T(4,128)(2,1)S(1)} %squeeze.72), channel_id=1, source_target_pairs={{0,16},{4,20},{8,24},{12,28},{16,0},{20,4},{24,8},{28,12},{1,17},{... | collective-permute-start | bytes 24584 | tf_op jit(solution)/shard_map/ppermute | solution.py:18
  50.4 0.2 collective-permute-start.14
  50.6 0.0 collective-permute-done.10
  50.6 2.0 %collective-permute-start.15 = (bf16[4,1024]{1,0:T(4,128)(2,1)S(1)}, bf16[4,1024]{1,0:T(4,128)(2,1)S(1)}, u32[]{:S(2)}, u32[]{:S(2)}) collective-permute-start(bf16[4,1024]{1,0:T(4,128)(2,1)S(1)} %squeeze.74), channel_id=1, source_target_pairs={{0,8},{4,12},{8,16},{12,20},{16,24},{20,28},{24,0},{28,4},{1,9},{5... | collective-permute-start | bytes 24584 | tf_op jit(solution)/shard_map/ppermute | solution.py:18
  52.7 0.1 collective-permute-start.16
  52.9 0.6 %collective-permute-done.14 = bf16[4,1024]{1,0:T(4,128)(2,1)S(1)} collective-permute-done((bf16[4,1024]{1,0:T(4,128)(2,1)S(1)}, bf16[4,1024]{1,0:T(4,128)(2,1)S(1)}, u32[]{:S(2)}, u32[]{:S(2)}) %collective-permute-start.14) | collective-permute-done | bytes 8224 | tf_op jit(solution)/shard_map/ppermute | solution.py:18
  53.5 1.9 %collective-permute-done.15 = bf16[4,1024]{1,0:T(4,128)(2,1)S(1)} collective-permute-done((bf16[4,1024]{1,0:T(4,128)(2,1)S(1)}, bf16[4,1024]{1,0:T(4,128)(2,1)S(1)}, u32[]{:S(2)}, u32[]{:S(2)}) %collective-permute-start.15) | collective-permute-done | bytes 8224 | tf_op jit(solution)/shard_map/ppermute | solution.py:18
  55.4 1.3 %collective-permute-done.16 = bf16[4,1024]{1,0:T(4,128)(2,1)S(1)} collective-permute-done((bf16[4,1024]{1,0:T(4,128)(2,1)S(1)}, bf16[4,1024]{1,0:T(4,128)(2,1)S(1)}, u32[]{:S(2)}, u32[]{:S(2)}) %collective-permute-start.16) | collective-permute-done | bytes 8224 | tf_op jit(solution)/shard_map/ppermute | solution.py:18
  56.9 0.1 dynamic-slice_bitcast_fusion
  57.1 0.3 fusion.96
  57.4 0.3 fusion.93
  57.7 1.2 %fusion.90 = (f32[196]{0:T(256)S(1)}, f32[196,16]{0,1:T(8,128)S(1)}) fusion(bf16[4,196,16]{1,2,0:T(8,128)(2,1)S(1)} %copy-done.7, s32[]{:T(128)S(6)} %select_n.39, bf16[16,1024]{1,0:T(8,128)(2,1)S(1)} %reshape.238, bf16[4,196,1024]{2,1,0:T(8,128)(2,1)} %copy.47), kind=kOutput, calls=%fused_computation.160 | convolution fusion | flops 6431740 | bytes 462992 | tf_op jit(solution)/shard_map/btd,bsd->bts/dot_general | solution.py:83
  59.0 1.1 %fusion.3 = bf16[1,196,1024]{2,1,0:T(8,128)(2,1)} fusion(f32[196,1024]{1,0:T(8,128)S(1)} %fusion.96, bf16[1024,16]{0,1:T(8,128)(2,1)S(1)} %copy-done.10, f32[196,16]{0,1:T(8,128)S(1)} %get-tuple-element.51, f32[196,16]{0,1:T(8,128)S(1)} %get-tuple-element.53, f32[16]{0:T(128)S(1)} %get-tuple-element.50, f32[196]{0:T(256)S(1)} %get-tuple-element.52, ...), kind=kOutput, calls=%fused_computation.4 | convolution fusion | flops 6849024 | bytes 1304068 | tf_op jit(solution)/shard_map/bts,ds->btd/dot_general | solution.py:97
  (90 shorter events, 1.2 us)
Async XLA Ops:
  0.0 43.2 %copy-start = (f32[16,1024]{1,0:T(8,128)S(1)}, f32[16,1024]{1,0:T(8,128)}, u32[]{:S(2)}) copy-start(f32[16,1024]{1,0:T(8,128)} %param.14) | copy-start | bytes 196612
  0.0 2.3 %copy-start.9 = (bf16[1024,16]{0,1:T(8,128)(2,1)S(1)}, bf16[1024,16]{0,1:T(8,128)(2,1)}, u32[]{:S(2)}) copy-start(bf16[1024,16]{0,1:T(8,128)(2,1)} %param.10) | copy-start | bytes 98308
  0.0 2.3 %copy-start.2 = (bf16[4,196,1024]{2,0,1:T(4,128)(2,1)S(1)}, bf16[4,196,1024]{2,0,1:T(4,128)(2,1)}, u32[]{:S(2)}) copy-start(bf16[4,196,1024]{2,0,1:T(4,128)(2,1)} %param.9) | copy-start | bytes 4816900
  3.5 2.1 %copy-start.1 = (bf16[4,196,1024]{2,0,1:T(4,128)(2,1)S(1)}, bf16[4,196,1024]{2,0,1:T(4,128)(2,1)}, u32[]{:S(2)}) copy-start(bf16[4,196,1024]{2,0,1:T(4,128)(2,1)} %param.15) | copy-start | bytes 4816900
  3.6 1.0 %copy-start.4 = (bf16[4,196,16]{1,2,0:T(8,128)(2,1)}, bf16[4,196,16]{1,2,0:T(8,128)(2,1)S(1)}, u32[]{:S(2)}) copy-start(bf16[4,196,16]{1,2,0:T(8,128)(2,1)S(1)} %divide_convert_fusion.1) | copy-start | bytes 75268
  5.6 1.0 %copy-start.6 = (bf16[4,196,16]{1,2,0:T(8,128)(2,1)}, bf16[4,196,16]{1,2,0:T(8,128)(2,1)S(1)}, u32[]{:S(2)}) copy-start(bf16[4,196,16]{1,2,0:T(8,128)(2,1)S(1)} %divide_convert_fusion) | copy-start | bytes 75268
  9.1 8.2 %collective-permute-start = (bf16[16,1024]{1,0:T(8,128)(2,1)}, bf16[16,1024]{1,0:T(8,128)(2,1)}, u32[]{:S(2)}, u32[]{:S(2)}) collective-permute-start(bf16[16,1024]{1,0:T(8,128)(2,1)} %get-tuple-element.20), channel_id=1, source_target_pairs={{0,4},{4,8},{8,12},{12,16},{16,20},{20,24},{24,28},{28,0},{1,5},{5... | collective-permute-start | bytes 98312 | tf_op jit(solution)/shard_map/ppermute | solution.py:18
  9.6 10.0 %collective-permute-start.1 = (bf16[16,1024]{1,0:T(8,128)(2,1)S(1)}, bf16[16,1024]{1,0:T(8,128)(2,1)}, u32[]{:S(2)}, u32[]{:S(2)}) collective-permute-start(bf16[16,1024]{1,0:T(8,128)(2,1)S(1)} %get-tuple-element.19), channel_id=1, source_target_pairs={{0,8},{4,12},{8,16},{12,20},{16,24},{20,28},{24,0},{28,4},{1,9},{5... | collective-permute-start | bytes 98312 | tf_op jit(solution)/shard_map/ppermute | solution.py:18
  12.1 10.5 %collective-permute-start.2 = (bf16[16,1024]{1,0:T(8,128)(2,1)S(1)}, bf16[16,1024]{1,0:T(8,128)(2,1)}, u32[]{:S(2)}, u32[]{:S(2)}) collective-permute-start(bf16[16,1024]{1,0:T(8,128)(2,1)S(1)} %get-tuple-element.18), channel_id=1, source_target_pairs={{0,12},{4,16},{8,20},{12,24},{16,28},{20,0},{24,4},{28,8},{1,13},{... | collective-permute-start | bytes 98312 | tf_op jit(solution)/shard_map/ppermute | solution.py:18
  14.5 8.9 %collective-permute-start.3 = (bf16[16,1024]{1,0:T(8,128)(2,1)S(1)}, bf16[16,1024]{1,0:T(8,128)(2,1)}, u32[]{:S(2)}, u32[]{:S(2)}) collective-permute-start(bf16[16,1024]{1,0:T(8,128)(2,1)S(1)} %get-tuple-element.17), channel_id=1, source_target_pairs={{0,16},{4,20},{8,24},{12,28},{16,0},{20,4},{24,8},{28,12},{1,17},{... | collective-permute-start | bytes 98312 | tf_op jit(solution)/shard_map/ppermute | solution.py:18
  15.0 9.1 %collective-permute-start.4 = (bf16[16,1024]{1,0:T(8,128)(2,1)S(1)}, bf16[16,1024]{1,0:T(8,128)(2,1)}, u32[]{:S(2)}, u32[]{:S(2)}) collective-permute-start(bf16[16,1024]{1,0:T(8,128)(2,1)S(1)} %get-tuple-element.16), channel_id=1, source_target_pairs={{0,20},{4,24},{8,28},{12,0},{16,4},{20,8},{24,12},{28,16},{1,21},{... | collective-permute-start | bytes 98312 | tf_op jit(solution)/shard_map/ppermute | solution.py:18
  16.8 8.4 %copy-start.8 = (f32[2,1024]{1,0:T(2,128)S(1)}, f32[2,1024]{1,0:T(2,128)}, u32[]{:S(2)}) copy-start(f32[2,1024]{1,0:T(2,128)} %param.12) | copy-start | bytes 24580
  17.3 7.5 %collective-permute-start.5 = (bf16[16,1024]{1,0:T(8,128)(2,1)S(1)}, bf16[16,1024]{1,0:T(8,128)(2,1)S(1)}, u32[]{:S(2)}, u32[]{:S(2)}) collective-permute-start(bf16[16,1024]{1,0:T(8,128)(2,1)S(1)} %get-tuple-element.15), channel_id=1, source_target_pairs={{0,24},{4,28},{8,0},{12,4},{16,8},{20,12},{24,16},{28,20},{1,25},{... | collective-permute-start | bytes 98312 | tf_op jit(solution)/shard_map/ppermute | solution.py:18
  19.6 5.4 %collective-permute-start.6 = (bf16[16,1024]{1,0:T(8,128)(2,1)S(1)}, bf16[16,1024]{1,0:T(8,128)(2,1)S(1)}, u32[]{:S(2)}, u32[]{:S(2)}) collective-permute-start(bf16[16,1024]{1,0:T(8,128)(2,1)S(1)} %get-tuple-element.14), channel_id=1, source_target_pairs={{0,28},{4,0},{8,4},{12,8},{16,12},{20,16},{24,20},{28,24},{1,29},{... | collective-permute-start | bytes 98312 | tf_op jit(solution)/shard_map/ppermute | solution.py:18
  25.2 3.5 %copy-start.3 = (bf16[2,1024,1024]{2,1,0:T(8,128)(2,1)S(1)}, bf16[2,1024,1024]{2,1,0:T(8,128)(2,1)}, u32[]{:S(2)}) copy-start(bf16[2,1024,1024]{2,1,0:T(8,128)(2,1)} %param.13) | copy-start | bytes 12582916
  37.0 20.1 %copy-start.5 = (bf16[4,196,16]{1,2,0:T(8,128)(2,1)S(1)}, bf16[4,196,16]{1,2,0:T(8,128)(2,1)}, u32[]{:S(2)}) copy-start(bf16[4,196,16]{1,2,0:T(8,128)(2,1)} %copy-done.4) | copy-start | bytes 75268
  37.5 6.8 %collective-permute-start.7 = (bf16[32,1024]{1,0:T(8,128)(2,1)S(1)}, bf16[32,1024]{1,0:T(8,128)(2,1)S(1)}, u32[]{:S(2)}, u32[]{:S(2)}) collective-permute-start(bf16[32,1024]{1,0:T(8,128)(2,1)S(1)} %bitcast.110), channel_id=1, source_target_pairs={{0,1},{1,2},{2,3},{3,0},{4,5},{5,6},{6,7},{7,4},{8,9},{9,10},{10,1... | collective-permute-start | bytes 196616 | tf_op jit(solution)/shard_map/ppermute | solution.py:18
  39.1 7.1 %collective-permute-start.8 = (bf16[32,1024]{1,0:T(8,128)(2,1)S(1)}, bf16[32,1024]{1,0:T(8,128)(2,1)S(1)}, u32[]{:S(2)}, u32[]{:S(2)}) collective-permute-start(bf16[32,1024]{1,0:T(8,128)(2,1)S(1)} %bitcast.111), channel_id=1, source_target_pairs={{0,2},{1,3},{2,0},{3,1},{4,6},{5,7},{6,4},{7,5},{8,10},{9,11},{10,... | collective-permute-start | bytes 196616 | tf_op jit(solution)/shard_map/ppermute | solution.py:18
  41.8 4.7 %collective-permute-start.9 = (bf16[32,1024]{1,0:T(8,128)(2,1)S(1)}, bf16[32,1024]{1,0:T(8,128)(2,1)S(1)}, u32[]{:S(2)}, u32[]{:S(2)}) collective-permute-start(bf16[32,1024]{1,0:T(8,128)(2,1)S(1)} %bitcast.112), channel_id=1, source_target_pairs={{0,3},{1,0},{2,1},{3,2},{4,7},{5,4},{6,5},{7,6},{8,11},{9,8},{10,9... | collective-permute-start | bytes 196616 | tf_op jit(solution)/shard_map/ppermute | solution.py:18
  46.5 11.2 %copy-start.7 = (bf16[4,196,16]{1,2,0:T(8,128)(2,1)S(1)}, bf16[4,196,16]{1,2,0:T(8,128)(2,1)}, u32[]{:S(2)}) copy-start(bf16[4,196,16]{1,2,0:T(8,128)(2,1)} %copy-done.6) | copy-start | bytes 75268
  46.6 12.4 %copy-start.10 = (bf16[1024,16]{0,1:T(8,128)(2,1)S(1)}, bf16[1024,16]{0,1:T(8,128)(2,1)}, u32[]{:S(2)}) copy-start(bf16[1024,16]{0,1:T(8,128)(2,1)} %param.10) | copy-start | bytes 98308
  46.8 3.8 %collective-permute-start.10 = (bf16[4,1024]{1,0:T(4,128)(2,1)S(1)}, bf16[4,1024]{1,0:T(4,128)(2,1)S(1)}, u32[]{:S(2)}, u32[]{:S(2)}) collective-permute-start(bf16[4,1024]{1,0:T(4,128)(2,1)S(1)} %squeeze.69), channel_id=1, source_target_pairs={{0,28},{4,0},{8,4},{12,8},{16,12},{20,16},{24,20},{28,24},{1,29},{... | collective-permute-start | bytes 24584 | tf_op jit(solution)/shard_map/ppermute | solution.py:18
  47.7 4.9 %collective-permute-start.11 = (bf16[4,1024]{1,0:T(4,128)(2,1)S(1)}, bf16[4,1024]{1,0:T(4,128)(2,1)S(1)}, u32[]{:S(2)}, u32[]{:S(2)}) collective-permute-start(bf16[4,1024]{1,0:T(4,128)(2,1)S(1)} %squeeze.70), channel_id=1, source_target_pairs={{0,24},{4,28},{8,0},{12,4},{16,8},{20,12},{24,16},{28,20},{1,25},{... | collective-permute-start | bytes 24584 | tf_op jit(solution)/shard_map/ppermute | solution.py:18
  48.6 4.2 %collective-permute-start.12 = (bf16[4,1024]{1,0:T(4,128)(2,1)S(1)}, bf16[4,1024]{1,0:T(4,128)(2,1)S(1)}, u32[]{:S(2)}, u32[]{:S(2)}) collective-permute-start(bf16[4,1024]{1,0:T(4,128)(2,1)S(1)} %squeeze.71), channel_id=1, source_target_pairs={{0,20},{4,24},{8,28},{12,0},{16,4},{20,8},{24,12},{28,16},{1,21},{... | collective-permute-start | bytes 24584 | tf_op jit(solution)/shard_map/ppermute | solution.py:18
  48.9 3.9 %collective-permute-start.13 = (bf16[4,1024]{1,0:T(4,128)(2,1)S(1)}, bf16[4,1024]{1,0:T(4,128)(2,1)S(1)}, u32[]{:S(2)}, u32[]{:S(2)}) collective-permute-start(bf16[4,1024]{1,0:T(4,128)(2,1)S(1)} %squeeze.72), channel_id=1, source_target_pairs={{0,16},{4,20},{8,24},{12,28},{16,0},{20,4},{24,8},{28,12},{1,17},{... | collective-permute-start | bytes 24584 | tf_op jit(solution)/shard_map/ppermute | solution.py:18
  50.4 3.1 %collective-permute-start.14 = (bf16[4,1024]{1,0:T(4,128)(2,1)S(1)}, bf16[4,1024]{1,0:T(4,128)(2,1)S(1)}, u32[]{:S(2)}, u32[]{:S(2)}) collective-permute-start(bf16[4,1024]{1,0:T(4,128)(2,1)S(1)} %squeeze.73), channel_id=1, source_target_pairs={{0,12},{4,16},{8,20},{12,24},{16,28},{20,0},{24,4},{28,8},{1,13},{... | collective-permute-start | bytes 24584 | tf_op jit(solution)/shard_map/ppermute | solution.py:18
  50.6 4.8 %collective-permute-start.15 = (bf16[4,1024]{1,0:T(4,128)(2,1)S(1)}, bf16[4,1024]{1,0:T(4,128)(2,1)S(1)}, u32[]{:S(2)}, u32[]{:S(2)}) collective-permute-start(bf16[4,1024]{1,0:T(4,128)(2,1)S(1)} %squeeze.74), channel_id=1, source_target_pairs={{0,8},{4,12},{8,16},{12,20},{16,24},{20,28},{24,0},{28,4},{1,9},{5... | collective-permute-start | bytes 24584 | tf_op jit(solution)/shard_map/ppermute | solution.py:18
  52.7 4.0 %collective-permute-start.16 = (bf16[4,1024]{1,0:T(4,128)(2,1)S(1)}, bf16[4,1024]{1,0:T(4,128)(2,1)S(1)}, u32[]{:S(2)}, u32[]{:S(2)}) collective-permute-start(bf16[4,1024]{1,0:T(4,128)(2,1)S(1)} %squeeze.75), channel_id=1, source_target_pairs={{0,4},{4,8},{8,12},{12,16},{16,20},{20,24},{24,28},{28,0},{1,5},{5... | collective-permute-start | bytes 24584 | tf_op jit(solution)/shard_map/ppermute | solution.py:18

commit v3 on v1

v3 whole, which is shorter than its diff:
```python
import functools

import jax
import jax.numpy as jnp
import numpy as np
from jax import lax
from jax.experimental import pallas as pl
from jax.experimental.pallas import tpu as pltpu
from jax.sharding import PartitionSpec as P

BF = jnp.bfloat16
F32 = jnp.float32
NN = (((1,), (0,)), ((), ()))
NT = (((1,), (1,)), ((), ()))


def mm(a, b, dims=NN):
    return lax.dot_general(a, b, dims, preferred_element_type=F32)


def block_of(n_expert):
    return 8 if n_expert % 8 == 0 else n_expert


def one_hot_rows(source, count):
    return np.asarray(np.asarray(source).reshape(-1)[:, None] == np.arange(count)[None], BF)


def dispatch_kernel(images, k, gb, tok_ref, grad_ref, keys_ref, perm_ref, send_ref, disp_ref, comb_ref):
    slots = keys_ref.shape[0]
    keys = keys_ref[...]
    slot_rows = [[], []]
    for b in range(images):
        tok = tok_ref[b]
        logits = mm(keys, tok, NT)
        e = jnp.exp(logits - jnp.max(logits, axis=1, keepdims=True))
        disp = (e / jnp.sum(e, axis=1, keepdims=True)).astype(BF)
        e = jnp.exp(logits - jnp.max(logits, axis=0, keepdims=True))
        comb = (e / jnp.sum(e, axis=0, keepdims=True)).astype(BF)
        disp_ref[b] = disp
        comb_ref[b] = comb
        slot_rows[0].append(mm(disp, tok).astype(BF))
        slot_rows[1].append(mm(comb, grad_ref[b]).astype(BF))
    perm = perm_ref[...]
    step = gb * k
    rows = perm.shape[0]
    for i in range(slots // step):
        block = jnp.concatenate(
            [r[i * step : (i + 1) * step] for kind in slot_rows for r in kind], axis=0
        )
        send_ref[i * rows : (i + 1) * rows] = mm(perm, block).astype(BF)


def expert_kernel(
    images, n_expert, k, gb, got_ref, win_hbm, bin_ref, wout_hbm, q_ref, t_ref, back_ref,
    win, wout, sems,
):
    copies = []
    for e in range(k):
        pair = []
        for i, (src, dst) in enumerate(((win_hbm, win), (wout_hbm, wout))):
            copy = pltpu.make_async_copy(src.at[e], dst.at[e], sems.at[e, i])
            copy.start()
            pair.append(copy)
        copies.append(pair)
    rows = gb * images
    q = q_ref[...]
    per_block = q.shape[0]
    blocks = n_expert // gb
    sorted_rows = [
        mm(q, got_ref[i * per_block : (i + 1) * per_block]).astype(BF) for i in range(blocks)
    ]

    def pick(kind, e):
        start = (kind * k + e) * rows
        return jnp.concatenate([s[start : start + rows] for s in sorted_rows], axis=0)

    width = got_ref.shape[1]
    half = width // 2
    results = [[None] * k, [None] * k]
    for e in range(k):
        copies[e][0].wait()
        pre = mm(pick(0, e), win[e]) + bin_ref[e : e + 1]
        cdf = 0.5 * (1.0 + lax.erf(pre * 0.7071067811865476))
        hidden = (pre * cdf).astype(BF)
        slope = cdf + pre * jnp.exp(-0.5 * pre * pre) * 0.3989422804014327
        copies[e][1].wait()
        act_grad = mm(pick(1, e), wout[e], NT)
        results[0][e] = mm(hidden, wout[e]).astype(BF)
        pre_grad = (act_grad * slope).astype(BF)
        results[1][e] = mm(pre_grad, win[e], NT).astype(BF)
    t = t_ref[...]
    out_rows = t.shape[0]
    for i in range(blocks):
        stack = jnp.concatenate(
            [
                r[i * rows : (i + 1) * rows, h * half : (h + 1) * half]
                for kind in results
                for r in kind
                for h in range(2)
            ],
            axis=0,
        )
        back_ref[i * out_rows : (i + 1) * out_rows] = mm(t, stack).astype(BF)


def final_kernel(
    quarter, k, gb, home_ref, bias_ref, tok_ref, grad_ref, disp_ref, comb_ref, keys_ref, sel_ref, out_ref,
):
    slots = keys_ref.shape[0]
    step = gb * k
    blocks = slots // step
    per_block = home_ref.shape[0] // blocks
    sel = sel_ref[...]
    sums = [mm(sel, home_ref[i * per_block : (i + 1) * per_block]) for i in range(blocks)]

    def assemble(kind, m):
        halves = []
        for h in range(2):
            start = ((m * 2 + kind) * 2 + h) * step
            halves.append(jnp.concatenate([s[start : start + step] for s in sums], axis=0))
        return jnp.concatenate(halves, axis=1)

    keys = keys_ref[...]
    for m in range(quarter):
        slot_out = (assemble(0, m) + bias_ref[...]).astype(BF)
        slot_in_grad = assemble(1, m).astype(BF)
        comb_grad = mm(slot_out, grad_ref[m], NT)
        disp_grad = mm(slot_in_grad, tok_ref[m], NT)
        disp = disp_ref[m]
        comb = comb_ref[m].astype(F32)
        wide = disp.astype(F32)
        logit_grad = comb * (comb_grad - jnp.sum(comb * comb_grad, axis=0, keepdims=True))
        logit_grad = logit_grad + wide * (
            disp_grad - jnp.sum(wide * disp_grad, axis=1, keepdims=True)
        )
        logit_grad = logit_grad.astype(BF).astype(F32)
        left = jnp.concatenate([wide, logit_grad], axis=0).T.astype(BF)
        right = jnp.concatenate([slot_in_grad, keys], axis=0)
        out_ref[m] = mm(left, right).astype(BF)


def local(n_expert, n_hidden, tokens, slot_keys, w_in, b_in, w_out, b_out, out_grad):
    n_all = n_expert * n_hidden
    images, positions, width = tokens.shape
    quarter = images // n_hidden
    slots = slot_keys.shape[1]
    k, _, units = w_in.shape
    gb = block_of(n_expert)
    half = width // 2
    vmem = pl.BlockSpec(memory_space=pltpu.VMEM)
    anywhere = pl.BlockSpec(memory_space=pl.ANY)
    keys = slot_keys.T

    order = np.arange(2 * images * gb * k).reshape(2, images, gb, k).transpose(2, 0, 3, 1)
    perm = one_hot_rows(order, order.size)
    send_rows = 2 * k * images
    send, disp, comb = pl.pallas_call(
        functools.partial(dispatch_kernel, images, k, gb),
        out_shape=(
            jax.ShapeDtypeStruct((n_expert * send_rows, width), BF),
            jax.ShapeDtypeStruct((images, slots, positions), BF),
            jax.ShapeDtypeStruct((images, slots, positions), BF),
        ),
        in_specs=[vmem] * 4,
        out_specs=(vmem,) * 3,
        compiler_params=pltpu.CompilerParams(vmem_limit_bytes=24 << 20),
        name="dispatch",
    )(tokens, out_grad, keys, perm)

    got = lax.all_to_all(
        send.reshape(n_expert, send_rows, width), "expert", split_axis=0, concat_axis=0, tiled=True
    )

    order = np.arange(gb * send_rows).reshape(gb, 2, k, images).transpose(1, 2, 0, 3)
    sort = one_hot_rows(order, order.size)
    order = np.arange(2 * k * 2 * gb * images).reshape(2, k, 2, gb, n_hidden, quarter)
    order = order.transpose(3, 4, 0, 1, 5, 2)
    spread = one_hot_rows(order, order.size)
    back_rows = 2 * k * quarter * 2
    back = pl.pallas_call(
        functools.partial(expert_kernel, images, n_expert, k, gb),
        out_shape=jax.ShapeDtypeStruct((n_all * back_rows, half), BF),
        in_specs=[vmem, anywhere, vmem, anywhere, vmem, vmem],
        out_specs=vmem,
        scratch_shapes=[
            pltpu.VMEM(w_in.shape, BF),
            pltpu.VMEM(w_out.shape, BF),
            pltpu.SemaphoreType.DMA((k, 2)),
        ],
        compiler_params=pltpu.CompilerParams(vmem_limit_bytes=40 << 20),
        name="experts",
    )(got.reshape(n_expert * send_rows, width), w_in, b_in, w_out, sort, spread)

    home = lax.all_to_all(
        back.reshape(n_all, back_rows, half),
        ("expert", "hidden"),
        split_axis=0,
        concat_axis=0,
        tiled=True,
    )

    offset = lax.axis_index("hidden") * quarter
    mine = functools.partial(lax.dynamic_slice_in_dim, start_index=offset, slice_size=quarter, axis=0)
    label = np.arange(quarter * 2 * 2 * gb * k).reshape(quarter, 2, 2, gb, k).transpose(3, 1, 4, 0, 2)
    label = np.broadcast_to(label[:, None], (gb, n_hidden) + label.shape[1:])
    select = np.ascontiguousarray(one_hot_rows(label, quarter * 4 * gb * k).T)
    return pl.pallas_call(
        functools.partial(final_kernel, quarter, k, gb),
        out_shape=jax.ShapeDtypeStruct((quarter, positions, width), BF),
        in_specs=[vmem] * 8,
        out_specs=vmem,
        compiler_params=pltpu.CompilerParams(vmem_limit_bytes=24 << 20),
        name="tokens_back",
    )(home.reshape(n_all * back_rows, half), b_out, mine(tokens), mine(out_grad), mine(disp), mine(comb), keys, select)


def solution(mesh):
    return jax.shard_map(
        functools.partial(local, mesh.shape["expert"], mesh.shape["hidden"]),
        mesh=mesh,
        in_specs=(
            P("expert", None, None),
            P(),
            P("expert", None, "hidden"),
            P("expert", "hidden"),
            P("expert", "hidden", None),
            P(),
            P("expert", None, None),
        ),
        out_specs=P(("expert", "hidden"), None, None),
        check_vma=False,
    )
```

time: 56.9 us -> 44.2 us (0.78)
  matrix products: 23.5 us -> 0 us
  Pallas kernels: 0 us -> 8.63 us
  local copies, waits for them, and re-layouts: 8.2 us -> 10.5 us
  other arithmetic: 1.85 us -> 0 us
  waiting for transfers between devices: 6.86 us -> 8.52 us
    dot_general x9 -> x0, matrix products: 20.7 us -> none  [the longest x1 6.74 us: local(): jnp.einsum('krf,kdf->krd', pre_grad, w_in, preferred_element_type=jnp.flo...]
    pallas_call x0 -> x3, Pallas kernels: none -> 8.63 us  [the longest x1 5.42 us: local(): pl.pallas_call(functools.partial(expert_kernel, images, n_expert, k, gb),...]
    unnamed x17 -> x34, local copies, waits for them, and re-layouts: 4.2 us -> 8.83 us
    sub x2 -> x0, matrix products: 2.78 us -> none  [the longest x1 2.03 us: local(): combine = jax.nn.softmax(logits, axis=2).astype(jnp.bfloat16)]
    dynamic_slice x0 -> x2, local copies, waits for them, and re-layouts: none -> 1.67 us  [the longest x1 0.94 us: local(): mine(out_grad)]
    all_to_all x1, waiting for transfers between devices: 6.86 us -> 8.52 us  [local(): lax.all_to_all(back.reshape(n_all, back_rows, half), ('expert', 'hidden')...]
    reshape x3 -> x0, local copies, waits for them, and re-layouts: 1.41 us -> none  [the longest x1 0.69 us: local(): rows_in = got[:, 0].swapaxes(0, 1).reshape(k, n_expert * images, width)]
    concatenate x2 -> x0, other arithmetic: 0.95 us -> none  [the longest x1 0.92 us: local(): jnp.concatenate([slot_in.reshape(n_expert, k * images, width), slot_grad....]
  transfers between devices with their start and end apart: 1 -> 1, of which waited for: 1 -> 1; matrix products, arithmetic and copies ran while one was open for 6% -> 4% of each run, Pallas kernels for 0% -> 0%
where the time goes in v3:
time: 44.2 us; the launch traced here: 43.7 us
  blocking collectives  11.9 us (27%)
  local copies, waits for them, and re-layouts  10.5 us (24%)
  Pallas kernels  8.63 us (20%)
  waiting for transfers between devices  8.52 us (19%)
  starting transfers between devices  3.97 us (9%)
    all_to_all x1, blocking collectives, local(): lax.all_to_all(send.reshape(n_expert, send_rows, width), 'expert', split_...  11.9 us
    unnamed x34, local copies, waits for them, and re-layouts  8.83 us
    all_to_all x1, waiting for transfers between devices, local(): lax.all_to_all(back.reshape(n_all, back_rows, half), ('expert', 'hidden')...  8.52 us
    pallas_call x1, Pallas kernels, local(): pl.pallas_call(functools.partial(expert_kernel, images, n_expert, k, gb),...  5.42 us
    all_to_all x1, starting transfers between devices, local(): lax.all_to_all(back.reshape(n_all, back_rows, half), ('expert', 'hidden')...  3.97 us
    pallas_call x1, Pallas kernels, local(): pl.pallas_call(functools.partial(dispatch_kernel, images, k, gb), out_sha...  1.63 us
    pallas_call x1, Pallas kernels, local(): pl.pallas_call(functools.partial(final_kernel, quarter, k, gb), out_shape...  1.58 us
    dynamic_slice x1, local copies, waits for them, and re-layouts, local(): mine(out_grad)  0.94 us
  transfers between devices with their start and end apart: 1, of which 1 were waited for; matrix products, arithmetic and copies ran while one was open for 4% of the time, Pallas kernels for 0%

profile of v3, /device:TPU:0, one launch (start us, length us, event | category | flops | bytes accessed | tf_op | source)
XLA Modules:
  0.0 43.7 jit_solution(14859579755865067177)
XLA Ops:
  0.0 0.0 copy-start.15
  0.0 0.0 copy-start.5
  0.0 0.0 copy-start.9
  0.0 0.0 copy-start.1
  0.0 2.0 %copy.12.tok_ref = bf16[4,196,1024]{2,1,0:T(8,128)(2,1)S(1)} copy(bf16[4,196,1024]{2,0,1:T(4,128)(2,1)} %param.11) | data formatting | bytes 3211264 | tf_op args[0]
  2.1 0.0 copy-done.15
  2.1 0.0 copy-start
  2.1 0.5 %copy.13.grad_ref = bf16[4,196,1024]{2,1,0:T(8,128)(2,1)S(1)} copy(bf16[4,196,1024]{2,0,1:T(4,128)(2,1)S(1)} %copy-done.15) | data formatting | bytes 3211264 | tf_op args[6]
  2.6 0.0 copy-done.5
  2.6 0.0 copy-done.9
  2.6 0.0 copy-start.7
  2.6 0.0 copy-start.11
  2.6 0.0 copy-start.12
  2.6 1.6 %dispatch.1 = (bf16[128,1024]{1,0:T(8,128)(2,1)S(1)}, bf16[4,16,196]{2,1,0:T(8,128)(2,1)S(1)}, bf16[4,16,196]{2,1,0:T(8,128)(2,1)S(1)}) custom-call(bf16[4,196,1024]{2,1,0:T(8,128)(2,1)S(1)} %copy.12.tok_ref, bf16[4,196,1024]{2,1,0:T(8,128)(2,1)S(1)} %copy.13.grad_ref, bf16[16,1024]{1,0:T(8,128)(2,1)S(1)} %bitcast.9, bf16[128,128]{1,0:T(8,128)(2,1)S(1)} %copy-done.9), custom_call_target="tpu_custom_call" | custom-call | tf_op jit(solution)/shard_map/dispatch/pallas_call | solution.py:158
  4.3 0.0 copy-start.13
  4.3 0.6 %copy-done.13 = bf16[4,16,196]{2,1,0:T(8,128)(2,1)} copy-done((bf16[4,16,196]{2,1,0:T(8,128)(2,1)}, bf16[4,16,196]{2,1,0:T(8,128)(2,1)S(1)}, u32[]{:S(2)}) %copy-start.13) | copy-done | bytes 25112
  4.9 0.0 copy-start.14
  4.9 0.6 %copy-done.14 = bf16[4,16,196]{2,1,0:T(8,128)(2,1)} copy-done((bf16[4,16,196]{2,1,0:T(8,128)(2,1)}, bf16[4,16,196]{2,1,0:T(8,128)(2,1)S(1)}, u32[]{:S(2)}) %copy-start.14) | copy-done | bytes 25112
  5.5 11.9 %all_to_all.10 = bf16[8,16,1024]{2,1,0:T(8,128)(2,1)S(1)} all-to-all(bf16[8,16,1024]{2,1,0:T(8,128)(2,1)S(1)} %bitcast.8), channel_id=1, replica_groups=mesh['expert'=8,'hidden'=4] {'expert'}, dimensions={0} | all-to-all | bytes 524288 | tf_op jit(solution)/shard_map/all_to_all | solution.py:171
  17.4 0.0 copy-done.1
  17.4 0.0 copy-done
  17.4 0.0 copy-done.7
  17.4 0.0 copy-done.11
  17.4 0.0 copy-done.12
  17.4 5.4 %experts.1 = bf16[256,512]{1,0:T(8,128)(2,1)S(1)} custom-call(bf16[128,1024]{1,0:T(8,128)(2,1)S(1)} %bitcast.7, bf16[2,1024,1024]{2,1,0:T(8,128)(2,1)S(1)} %copy-done, f32[2,1024]{1,0:T(2,128)S(1)} %copy-done.12, bf16[2,1024,1024]{2,1,0:T(8,128)(2,1)S(1)} %copy-done.1, bf16[128,128]{1,0:T(8,128)(2,1)S(1)} %copy-done.11, bf16[256,256]{1,0:T(8,128)(2,1)S(1)} %copy-done.7), custom_call_target="tpu_custom_call" | custom-call | tf_op jit(solution)/shard_map/experts/pallas_call | solution.py:181
  22.8 0.0 copy-start.4
  22.9 0.7 %copy-done.4 = bf16[256,512]{1,0:T(8,128)(2,1)} copy-done((bf16[256,512]{1,0:T(8,128)(2,1)}, bf16[256,512]{1,0:T(8,128)(2,1)S(1)}, u32[]{:S(2)}) %copy-start.4) | copy-done | bytes 262168
  23.5 4.0 %all-to-all-start.1 = ((bf16[32,8,512]{2,1,0:T(8,128)(2,1)}), bf16[32,8,512]{2,1,0:T(8,128)(2,1)S(1)}, u32[]{:S(2)}, u32[]{:S(2)}) async-start(bf16[32,8,512]{2,1,0:T(8,128)(2,1)} %bitcast.6), calls=%async_computation.1 | async-start | bytes 524288 | tf_op jit(solution)/shard_map/all_to_all | solution.py:195
  27.5 0.7 %constant_dynamic-slice_fusion = (bf16[1,16,196]{2,1,0:T(8,128)(2,1)S(1)}, bf16[1,16,196]{2,1,0:T(8,128)(2,1)S(1)}) fusion(bf16[4,16,196]{2,1,0:T(8,128)(2,1)} %copy-done.14, s32[]{:T(128)S(6)} %select_n.2, bf16[4,16,196]{2,1,0:T(8,128)(2,1)} %copy-done.13), kind=kLoop, calls=%fused_computation | loop fusion | bytes 25092 | tf_op jit(solution)/shard_map/dynamic_slice | solution.py:215
  28.3 0.9 %constant_dynamic-slice_fusion.2 = (bf16[1,196,1024]{2,1,0:T(8,128)(2,1)}, bf16[1,196,1024]{2,1,0:T(8,128)(2,1)}) fusion(bf16[4,196,1024]{2,1,0:T(8,128)(2,1)S(1)} %copy.13.grad_ref, s32[]{:T(128)S(6)} %select_n.2, bf16[4,196,1024]{2,1,0:T(8,128)(2,1)S(1)} %copy.12.tok_ref), kind=kLoop, calls=%fused_computation.2 | loop fusion | bytes 1605636 | tf_op jit(solution)/shard_map/dynamic_slice | solution.py:215
  29.2 8.5 %all-to-all-done.1 = bf16[32,8,512]{2,1,0:T(8,128)(2,1)S(1)} async-done(((bf16[32,8,512]{2,1,0:T(8,128)(2,1)}), bf16[32,8,512]{2,1,0:T(8,128)(2,1)S(1)}, u32[]{:S(2)}, u32[]{:S(2)}) %all-to-all-start.1) | async-done | bytes 262176 | tf_op jit(solution)/shard_map/all_to_all | solution.py:195
  37.7 0.0 copy-start.2
  37.7 1.0 %copy-done.2 = bf16[1,196,1024]{2,1,0:T(8,128)(2,1)S(1)} copy-done((bf16[1,196,1024]{2,1,0:T(8,128)(2,1)S(1)}, bf16[1,196,1024]{2,1,0:T(8,128)(2,1)}, u32[]{:S(2)}) %copy-start.2) | copy-done | bytes 401432
  38.7 0.0 copy-start.3
  38.7 1.0 %copy-done.3 = bf16[1,196,1024]{2,1,0:T(8,128)(2,1)S(1)} copy-done((bf16[1,196,1024]{2,1,0:T(8,128)(2,1)S(1)}, bf16[1,196,1024]{2,1,0:T(8,128)(2,1)}, u32[]{:S(2)}) %copy-start.3) | copy-done | bytes 401432
  39.7 0.0 copy-start.6
  39.7 0.8 %copy-done.6 = bf16[1024,16]{0,1:T(8,128)(2,1)S(1)} copy-done((bf16[1024,16]{0,1:T(8,128)(2,1)S(1)}, bf16[1024,16]{0,1:T(8,128)(2,1)}, u32[]{:S(2)}) %copy-start.6) | copy-done | bytes 32792
  40.5 0.0 copy-start.8
  40.5 0.8 %copy-done.8 = f32[16,1024]{1,0:T(8,128)S(1)} copy-done((f32[16,1024]{1,0:T(8,128)S(1)}, f32[16,1024]{1,0:T(8,128)}, u32[]{:S(2)}) %copy-start.8) | copy-done | bytes 65560
  41.3 0.0 copy-start.10
  41.3 0.8 %copy-done.10 = bf16[64,256]{1,0:T(8,128)(2,1)S(1)} copy-done((bf16[64,256]{1,0:T(8,128)(2,1)S(1)}, bf16[64,256]{1,0:T(8,128)(2,1)}, u32[]{:S(2)}) %copy-start.10) | copy-done | bytes 32792
  42.1 1.6 %tokens_back.1 = bf16[1,196,1024]{2,1,0:T(8,128)(2,1)} custom-call(bf16[256,512]{1,0:T(8,128)(2,1)S(1)} %bitcast.5, f32[16,1024]{1,0:T(8,128)S(1)} %copy-done.8, bf16[1,196,1024]{2,1,0:T(8,128)(2,1)S(1)} %copy-done.3, bf16[1,196,1024]{2,1,0:T(8,128)(2,1)S(1)} %copy-done.2, bf16[1,16,196]{2,1,0:T(8,128)(2,1)S(1)} %get-tuple-element.12.disp_ref, ...), custom_call_target="tpu_custom_call" | custom-call | tf_op jit(solution)/shard_map/tokens_back/pallas_call | solution.py:208
Async XLA Ops:
  0.0 2.1 %copy-start.15 = (bf16[4,196,1024]{2,0,1:T(4,128)(2,1)S(1)}, bf16[4,196,1024]{2,0,1:T(4,128)(2,1)}, u32[]{:S(2)}) copy-start(bf16[4,196,1024]{2,0,1:T(4,128)(2,1)} %param.17) | copy-start | bytes 4816900
  0.0 2.6 %copy-start.5 = (bf16[1024,16]{0,1:T(8,128)(2,1)S(1)}, bf16[1024,16]{0,1:T(8,128)(2,1)}, u32[]{:S(2)}) copy-start(bf16[1024,16]{0,1:T(8,128)(2,1)} %param.12) | copy-start | bytes 98308
  0.0 2.6 %copy-start.9 = (bf16[128,128]{1,0:T(8,128)(2,1)S(1)}, bf16[128,128]{1,0:T(8,128)(2,1)}, u32[]{:S(2)}) copy-start(bf16[128,128]{1,0:T(8,128)(2,1)} %constant.16.clone.perm_ref) | copy-start | bytes 98308
  0.0 17.4 %copy-start.1 = (bf16[2,1024,1024]{2,1,0:T(8,128)(2,1)S(1)}, bf16[2,1024,1024]{2,1,0:T(8,128)(2,1)}, u32[]{:S(2)}) copy-start(bf16[2,1024,1024]{2,1,0:T(8,128)(2,1)} %wout_hbm.1) | copy-start | bytes 12582916
  2.1 15.3 %copy-start = (bf16[2,1024,1024]{2,1,0:T(8,128)(2,1)S(1)}, bf16[2,1024,1024]{2,1,0:T(8,128)(2,1)}, u32[]{:S(2)}) copy-start(bf16[2,1024,1024]{2,1,0:T(8,128)(2,1)} %win_hbm.1) | copy-start | bytes 12582916
  2.6 14.8 %copy-start.7 = (bf16[256,256]{1,0:T(8,128)(2,1)S(1)}, bf16[256,256]{1,0:T(8,128)(2,1)}, u32[]{:S(2)}) copy-start(bf16[256,256]{1,0:T(8,128)(2,1)} %constant.18.clone.t_ref) | copy-start | bytes 393220
  2.6 14.8 %copy-start.11 = (bf16[128,128]{1,0:T(8,128)(2,1)S(1)}, bf16[128,128]{1,0:T(8,128)(2,1)}, u32[]{:S(2)}) copy-start(bf16[128,128]{1,0:T(8,128)(2,1)} %constant.17.clone.q_ref) | copy-start | bytes 98308
  2.6 14.8 %copy-start.12 = (f32[2,1024]{1,0:T(2,128)S(1)}, f32[2,1024]{1,0:T(2,128)}, u32[]{:S(2)}) copy-start(f32[2,1024]{1,0:T(2,128)} %bin_ref.1) | copy-start | bytes 24580
  4.3 0.6 %copy-start.13 = (bf16[4,16,196]{2,1,0:T(8,128)(2,1)}, bf16[4,16,196]{2,1,0:T(8,128)(2,1)S(1)}, u32[]{:S(2)}) copy-start(bf16[4,16,196]{2,1,0:T(8,128)(2,1)S(1)} %get-tuple-element.9) | copy-start | bytes 75268
  4.9 0.6 %copy-start.14 = (bf16[4,16,196]{2,1,0:T(8,128)(2,1)}, bf16[4,16,196]{2,1,0:T(8,128)(2,1)S(1)}, u32[]{:S(2)}) copy-start(bf16[4,16,196]{2,1,0:T(8,128)(2,1)S(1)} %get-tuple-element.10) | copy-start | bytes 75268
  22.8 0.7 %copy-start.4 = (bf16[256,512]{1,0:T(8,128)(2,1)}, bf16[256,512]{1,0:T(8,128)(2,1)S(1)}, u32[]{:S(2)}) copy-start(bf16[256,512]{1,0:T(8,128)(2,1)S(1)} %experts.1) | copy-start | bytes 786436
  23.5 14.2 %all-to-all-start.1 = ((bf16[32,8,512]{2,1,0:T(8,128)(2,1)}), bf16[32,8,512]{2,1,0:T(8,128)(2,1)S(1)}, u32[]{:S(2)}, u32[]{:S(2)}) async-start(bf16[32,8,512]{2,1,0:T(8,128)(2,1)} %bitcast.6), calls=%async_computation.1 | async-start | bytes 524288 | tf_op jit(solution)/shard_map/all_to_all | solution.py:195
  37.7 1.0 %copy-start.2 = (bf16[1,196,1024]{2,1,0:T(8,128)(2,1)S(1)}, bf16[1,196,1024]{2,1,0:T(8,128)(2,1)}, u32[]{:S(2)}) copy-start(bf16[1,196,1024]{2,1,0:T(8,128)(2,1)} %get-tuple-element.13.grad_ref) | copy-start | bytes 1204228
  38.7 1.0 %copy-start.3 = (bf16[1,196,1024]{2,1,0:T(8,128)(2,1)S(1)}, bf16[1,196,1024]{2,1,0:T(8,128)(2,1)}, u32[]{:S(2)}) copy-start(bf16[1,196,1024]{2,1,0:T(8,128)(2,1)} %get-tuple-element.14.tok_ref) | copy-start | bytes 1204228
  39.7 0.8 %copy-start.6 = (bf16[1024,16]{0,1:T(8,128)(2,1)S(1)}, bf16[1024,16]{0,1:T(8,128)(2,1)}, u32[]{:S(2)}) copy-start(bf16[1024,16]{0,1:T(8,128)(2,1)} %param.12) | copy-start | bytes 98308
  40.5 0.8 %copy-start.8 = (f32[16,1024]{1,0:T(8,128)S(1)}, f32[16,1024]{1,0:T(8,128)}, u32[]{:S(2)}) copy-start(f32[16,1024]{1,0:T(8,128)} %bias_ref.1) | copy-start | bytes 196612
  41.3 0.8 %copy-start.10 = (bf16[64,256]{1,0:T(8,128)(2,1)S(1)}, bf16[64,256]{1,0:T(8,128)(2,1)}, u32[]{:S(2)}) copy-start(bf16[64,256]{1,0:T(8,128)(2,1)} %constant.19.clone.sel_ref) | copy-start | bytes 98308

commit v4 on v3

--- a/solution.py
+++ b/solution.py
@@ -26,7 +26,10 @@
     return np.asarray(np.asarray(source).reshape(-1)[:, None] == np.arange(count)[None], BF)
 
 
-def dispatch_kernel(images, k, gb, tok_ref, grad_ref, keys_ref, perm_ref, send_ref, disp_ref, comb_ref):
+def dispatch_kernel(
+    images, quarter, k, gb, tok_ref, grad_ref, keys_ref, perm_ref,
+    send_ref, disp_ref, comb_ref, my_tok_ref, my_grad_ref, disp_all, comb_all,
+):
     slots = keys_ref.shape[0]
     keys = keys_ref[...]
     slot_rows = [[], []]
@@ -37,8 +40,8 @@
         disp = (e / jnp.sum(e, axis=1, keepdims=True)).astype(BF)
         e = jnp.exp(logits - jnp.max(logits, axis=0, keepdims=True))
         comb = (e / jnp.sum(e, axis=0, keepdims=True)).astype(BF)
-        disp_ref[b] = disp
-        comb_ref[b] = comb
+        disp_all[b] = disp
+        comb_all[b] = comb
         slot_rows[0].append(mm(disp, tok).astype(BF))
         slot_rows[1].append(mm(comb, grad_ref[b]).astype(BF))
     perm = perm_ref[...]
@@ -49,20 +52,17 @@
             [r[i * step : (i + 1) * step] for kind in slot_rows for r in kind], axis=0
         )
         send_ref[i * rows : (i + 1) * rows] = mm(perm, block).astype(BF)
+    first = lax.axis_index("hidden") * quarter
+    for m in range(quarter):
+        disp_ref[m] = disp_all[first + m]
+        comb_ref[m] = comb_all[first + m]
+        my_tok_ref[m] = tok_ref[first + m]
+        my_grad_ref[m] = grad_ref[first + m]
 
 
 def expert_kernel(
-    images, n_expert, k, gb, got_ref, win_hbm, bin_ref, wout_hbm, q_ref, t_ref, back_ref,
-    win, wout, sems,
+    images, n_expert, k, gb, got_ref, win_ref, bin_ref, wout_ref, q_ref, t_ref, back_ref
 ):
-    copies = []
-    for e in range(k):
-        pair = []
-        for i, (src, dst) in enumerate(((win_hbm, win), (wout_hbm, wout))):
-            copy = pltpu.make_async_copy(src.at[e], dst.at[e], sems.at[e, i])
-            copy.start()
-            pair.append(copy)
-        copies.append(pair)
     rows = gb * images
     q = q_ref[...]
     per_block = q.shape[0]
@@ -79,16 +79,14 @@
     half = width // 2
     results = [[None] * k, [None] * k]
     for e in range(k):
-        copies[e][0].wait()
-        pre = mm(pick(0, e), win[e]) + bin_ref[e : e + 1]
+        pre = mm(pick(0, e), win_ref[e]) + bin_ref[e : e + 1]
         cdf = 0.5 * (1.0 + lax.erf(pre * 0.7071067811865476))
         hidden = (pre * cdf).astype(BF)
         slope = cdf + pre * jnp.exp(-0.5 * pre * pre) * 0.3989422804014327
-        copies[e][1].wait()
-        act_grad = mm(pick(1, e), wout[e], NT)
-        results[0][e] = mm(hidden, wout[e]).astype(BF)
+        act_grad = mm(pick(1, e), wout_ref[e], NT)
+        results[0][e] = mm(hidden, wout_ref[e]).astype(BF)
         pre_grad = (act_grad * slope).astype(BF)
-        results[1][e] = mm(pre_grad, win[e], NT).astype(BF)
+        results[1][e] = mm(pre_grad, win_ref[e], NT).astype(BF)
     t = t_ref[...]
     out_rows = t.shape[0]
     for i in range(blocks):
@@ -149,22 +147,24 @@
     gb = block_of(n_expert)
     half = width // 2
     vmem = pl.BlockSpec(memory_space=pltpu.VMEM)
-    anywhere = pl.BlockSpec(memory_space=pl.ANY)
     keys = slot_keys.T
 
     order = np.arange(2 * images * gb * k).reshape(2, images, gb, k).transpose(2, 0, 3, 1)
     perm = one_hot_rows(order, order.size)
     send_rows = 2 * k * images
-    send, disp, comb = pl.pallas_call(
-        functools.partial(dispatch_kernel, images, k, gb),
+    send, disp, comb, my_tok, my_grad = pl.pallas_call(
+        functools.partial(dispatch_kernel, images, quarter, k, gb),
         out_shape=(
             jax.ShapeDtypeStruct((n_expert * send_rows, width), BF),
-            jax.ShapeDtypeStruct((images, slots, positions), BF),
-            jax.ShapeDtypeStruct((images, slots, positions), BF),
+            jax.ShapeDtypeStruct((quarter, slots, positions), BF),
+            jax.ShapeDtypeStruct((quarter, slots, positions), BF),
+            jax.ShapeDtypeStruct((quarter, positions, width), BF),
+            jax.ShapeDtypeStruct((quarter, positions, width), BF),
         ),
         in_specs=[vmem] * 4,
-        out_specs=(vmem,) * 3,
-        compiler_params=pltpu.CompilerParams(vmem_limit_bytes=24 << 20),
+        out_specs=(vmem,) * 5,
+        scratch_shapes=[pltpu.VMEM((images, slots, positions), BF)] * 2,
+        compiler_params=pltpu.CompilerParams(vmem_limit_bytes=12 << 20),
         name="dispatch",
     )(tokens, out_grad, keys, perm)
 
@@ -181,14 +181,9 @@
     back = pl.pallas_call(
         functools.partial(expert_kernel, images, n_expert, k, gb),
         out_shape=jax.ShapeDtypeStruct((n_all * back_rows, half), BF),
-        in_specs=[vmem, anywhere, vmem, anywhere, vmem, vmem],
+        in_specs=[vmem] * 6,
         out_specs=vmem,
-        scratch_shapes=[
-            pltpu.VMEM(w_in.shape, BF),
-            pltpu.VMEM(w_out.shape, BF),
-            pltpu.SemaphoreType.DMA((k, 2)),
-        ],
-        compiler_params=pltpu.CompilerParams(vmem_limit_bytes=40 << 20),
+        compiler_params=pltpu.CompilerParams(vmem_limit_bytes=20 << 20),
         name="experts",
     )(got.reshape(n_expert * send_rows, width), w_in, b_in, w_out, sort, spread)
 
@@ -200,8 +195,6 @@
         tiled=True,
     )
 
-    offset = lax.axis_index("hidden") * quarter
-    mine = functools.partial(lax.dynamic_slice_in_dim, start_index=offset, slice_size=quarter, axis=0)
     label = np.arange(quarter * 2 * 2 * gb * k).reshape(quarter, 2, 2, gb, k).transpose(3, 1, 4, 0, 2)
     label = np.broadcast_to(label[:, None], (gb, n_hidden) + label.shape[1:])
     select = np.ascontiguousarray(one_hot_rows(label, quarter * 4 * gb * k).T)
@@ -210,9 +203,9 @@
         out_shape=jax.ShapeDtypeStruct((quarter, positions, width), BF),
         in_specs=[vmem] * 8,
         out_specs=vmem,
-        compiler_params=pltpu.CompilerParams(vmem_limit_bytes=24 << 20),
+        compiler_params=pltpu.CompilerParams(vmem_limit_bytes=8 << 20),
         name="tokens_back",
-    )(home.reshape(n_all * back_rows, half), b_out, mine(tokens), mine(out_grad), mine(disp), mine(comb), keys, select)
+    )(home.reshape(n_all * back_rows, half), b_out, my_tok, my_grad, disp, comb, keys, select)
 
 
 def solution(mesh):

time: 44.2 us -> 36.3 us (0.82)
  blocking collectives: 11.9 us -> 25.9 us
  waiting for transfers between devices: 8.52 us -> 0 us
  local copies, waits for them, and re-layouts: 10.5 us -> 2.57 us
  starting transfers between devices: 3.97 us -> 0 us
  Pallas kernels: 8.63 us -> 7.57 us
    all_to_all x0 -> x1, blocking collectives: none -> 14 us  [local(): lax.all_to_all(back.reshape(n_all, back_rows, half), ('expert', 'hidden')...]
    all_to_all x1 -> x0, waiting for transfers between devices: 8.52 us -> none  [local(): lax.all_to_all(back.reshape(n_all, back_rows, half), ('expert', 'hidden')...]
    unnamed x34 -> x22, local copies, waits for them, and re-layouts: 8.83 us -> 2.57 us
    all_to_all x1 -> x0, starting transfers between devices: 3.97 us -> none  [local(): lax.all_to_all(back.reshape(n_all, back_rows, half), ('expert', 'hidden')...]
    dynamic_slice x2 -> x0, local copies, waits for them, and re-layouts: 1.67 us -> none  [the longest x1 0.94 us: local(): mine(out_grad)]
    pallas_call x1, Pallas kernels: 5.42 us -> 4.35 us  [local(): pl.pallas_call(functools.partial(expert_kernel, images, n_expert, k, gb),...]
  transfers between devices with their start and end apart: 1 -> 0, of which waited for: 1 -> 0; matrix products, arithmetic and copies ran while one was open for 4% -> 0% of each run, Pallas kernels for 0% -> 0%
where the time goes in v4:
time: 36.3 us; the launch traced here: 36.2 us
  blocking collectives  25.9 us (71%)
  Pallas kernels  7.57 us (21%)
  local copies, waits for them, and re-layouts  2.57 us (7%)
    all_to_all x1, blocking collectives, local(): lax.all_to_all(back.reshape(n_all, back_rows, half), ('expert', 'hidden')...  14 us
    all_to_all x1, blocking collectives, local(): lax.all_to_all(send.reshape(n_expert, send_rows, width), 'expert', split_...  11.9 us
    pallas_call x1, Pallas kernels, local(): pl.pallas_call(functools.partial(expert_kernel, images, n_expert, k, gb),...  4.35 us
    unnamed x22, local copies, waits for them, and re-layouts  2.57 us
    pallas_call x1, Pallas kernels, local(): pl.pallas_call(functools.partial(dispatch_kernel, images, quarter, k, gb)...  1.64 us
    pallas_call x1, Pallas kernels, local(): pl.pallas_call(functools.partial(final_kernel, quarter, k, gb), out_shape...  1.58 us

profile of v4, /device:TPU:0, one launch (start us, length us, event | category | flops | bytes accessed | tf_op | source)
XLA Modules:
  0.0 36.2 jit_solution(14283585414585151654)
XLA Ops:
  0.0 0.0 copy-start.9
  0.0 0.0 copy-start.2
  0.0 0.0 copy-start.5
  0.0 0.0 copy-start.1
  0.0 2.0 %copy.12.tok_ref = bf16[4,196,1024]{2,1,0:T(8,128)(2,1)S(1)} copy(bf16[4,196,1024]{2,0,1:T(4,128)(2,1)} %param.11) | data formatting | bytes 3211264 | tf_op args[0]
  2.1 0.0 copy-done.9
  2.1 0.0 copy-start
  2.1 0.5 %copy.13.grad_ref = bf16[4,196,1024]{2,1,0:T(8,128)(2,1)S(1)} copy(bf16[4,196,1024]{2,0,1:T(4,128)(2,1)S(1)} %copy-done.9) | data formatting | bytes 3211264 | tf_op args[6]
  2.6 0.0 copy-done.2
  2.6 0.0 copy-done.5
  2.6 0.0 copy-start.3
  2.6 0.0 copy-start.7
  2.6 0.0 copy-start.8
  2.6 1.6 %dispatch.1 = (bf16[128,1024]{1,0:T(8,128)(2,1)S(1)}, bf16[1,16,196]{2,1,0:T(8,128)(2,1)S(1)}, bf16[1,16,196]{2,1,0:T(8,128)(2,1)S(1)}, bf16[1,196,1024]{2,1,0:T(8,128)(2,1)S(1)}, bf16[1,196,1024]{2,1,0:T(8,128)(2,1)S(1)}) custom-call(bf16[4,196,1024]{2,1,0:T(8,128)(2,1)S(1)} %copy.12.tok_ref, bf16[4,196,1024]{2,1,0:T(8,128)(2,1)S(1)} %copy.13.grad_ref, ...), custom_call_target="tpu_custom_call" | custom-call | tf_op jit(solution)/shard_map/dispatch/pallas_call | solution.py:155
  4.3 11.9 %all_to_all.10 = bf16[8,16,1024]{2,1,0:T(8,128)(2,1)S(1)} all-to-all(bf16[8,16,1024]{2,1,0:T(8,128)(2,1)S(1)} %bitcast.8), channel_id=1, replica_groups=mesh['expert'=8,'hidden'=4] {'expert'}, dimensions={0} | all-to-all | bytes 524288 | tf_op jit(solution)/shard_map/all_to_all | solution.py:171
  16.2 0.0 copy-done.1
  16.2 0.0 copy-done
  16.2 0.0 copy-done.3
  16.2 0.0 copy-done.7
  16.2 0.0 copy-done.8
  16.2 0.0 copy-start.4
  16.2 0.0 copy-start.6
  16.2 4.3 %experts.1 = bf16[256,512]{1,0:T(8,128)(2,1)S(1)} custom-call(bf16[128,1024]{1,0:T(8,128)(2,1)S(1)} %bitcast.6, bf16[2,1024,1024]{2,1,0:T(8,128)(2,1)S(1)} %copy-done, f32[2,1024]{1,0:T(2,128)S(1)} %copy-done.8, bf16[2,1024,1024]{2,1,0:T(8,128)(2,1)S(1)} %copy-done.1, bf16[128,128]{1,0:T(8,128)(2,1)S(1)} %copy-done.7, bf16[256,256]{1,0:T(8,128)(2,1)S(1)} %copy-done.3), custom_call_target="tpu_custom_call" | custom-call | tf_op jit(solution)/shard_map/experts/pallas_call | solution.py:181
  20.6 14.0 %all_to_all.11 = bf16[32,8,512]{2,1,0:T(8,128)(2,1)S(1)} all-to-all(bf16[32,8,512]{2,1,0:T(8,128)(2,1)S(1)} %bitcast.7), channel_id=1, replica_groups=mesh['expert'=8,'hidden'=4] {'expert','hidden'}, dimensions={0} | all-to-all | bytes 524288 | tf_op jit(solution)/shard_map/all_to_all | solution.py:190
  34.6 0.0 copy-done.4
  34.6 0.0 copy-done.6
  34.6 1.6 %tokens_back.1 = bf16[1,196,1024]{2,1,0:T(8,128)(2,1)} custom-call(bf16[256,512]{1,0:T(8,128)(2,1)S(1)} %bitcast.5, f32[16,1024]{1,0:T(8,128)S(1)} %copy-done.4, bf16[1,196,1024]{2,1,0:T(8,128)(2,1)S(1)} %get-tuple-element.11.tok_ref, bf16[1,196,1024]{2,1,0:T(8,128)(2,1)S(1)} %get-tuple-element.12.grad_ref, ...), custom_call_target="tpu_custom_call" | custom-call | tf_op jit(solution)/shard_map/tokens_back/pallas_call | solution.py:201
Async XLA Ops:
  0.0 2.1 %copy-start.9 = (bf16[4,196,1024]{2,0,1:T(4,128)(2,1)S(1)}, bf16[4,196,1024]{2,0,1:T(4,128)(2,1)}, u32[]{:S(2)}) copy-start(bf16[4,196,1024]{2,0,1:T(4,128)(2,1)} %param.17) | copy-start | bytes 4816900
  0.0 2.6 %copy-start.2 = (bf16[1024,16]{0,1:T(8,128)(2,1)S(1)}, bf16[1024,16]{0,1:T(8,128)(2,1)}, u32[]{:S(2)}) copy-start(bf16[1024,16]{0,1:T(8,128)(2,1)} %param.12) | copy-start | bytes 98308
  0.0 2.6 %copy-start.5 = (bf16[128,128]{1,0:T(8,128)(2,1)S(1)}, bf16[128,128]{1,0:T(8,128)(2,1)}, u32[]{:S(2)}) copy-start(bf16[128,128]{1,0:T(8,128)(2,1)} %constant.8.clone.perm_ref) | copy-start | bytes 98308
  0.0 16.2 %copy-start.1 = (bf16[2,1024,1024]{2,1,0:T(8,128)(2,1)S(1)}, bf16[2,1024,1024]{2,1,0:T(8,128)(2,1)}, u32[]{:S(2)}) copy-start(bf16[2,1024,1024]{2,1,0:T(8,128)(2,1)} %wout_ref.1) | copy-start | bytes 12582916
  2.1 14.1 %copy-start = (bf16[2,1024,1024]{2,1,0:T(8,128)(2,1)S(1)}, bf16[2,1024,1024]{2,1,0:T(8,128)(2,1)}, u32[]{:S(2)}) copy-start(bf16[2,1024,1024]{2,1,0:T(8,128)(2,1)} %win_ref.1) | copy-start | bytes 12582916
  2.6 13.6 %copy-start.3 = (bf16[256,256]{1,0:T(8,128)(2,1)S(1)}, bf16[256,256]{1,0:T(8,128)(2,1)}, u32[]{:S(2)}) copy-start(bf16[256,256]{1,0:T(8,128)(2,1)} %constant.10.clone.t_ref) | copy-start | bytes 393220
  2.6 13.6 %copy-start.7 = (bf16[128,128]{1,0:T(8,128)(2,1)S(1)}, bf16[128,128]{1,0:T(8,128)(2,1)}, u32[]{:S(2)}) copy-start(bf16[128,128]{1,0:T(8,128)(2,1)} %constant.9.clone.q_ref) | copy-start | bytes 98308
  2.6 13.6 %copy-start.8 = (f32[2,1024]{1,0:T(2,128)S(1)}, f32[2,1024]{1,0:T(2,128)}, u32[]{:S(2)}) copy-start(f32[2,1024]{1,0:T(2,128)} %bin_ref.1) | copy-start | bytes 24580
  16.2 18.4 %copy-start.4 = (f32[16,1024]{1,0:T(8,128)S(1)}, f32[16,1024]{1,0:T(8,128)}, u32[]{:S(2)}) copy-start(f32[16,1024]{1,0:T(8,128)} %bias_ref.1) | copy-start | bytes 196612
  16.2 18.3 %copy-start.6 = (bf16[64,256]{1,0:T(8,128)(2,1)S(1)}, bf16[64,256]{1,0:T(8,128)(2,1)}, u32[]{:S(2)}) copy-start(bf16[64,256]{1,0:T(8,128)(2,1)} %constant.11.clone.sel_ref) | copy-start | bytes 98308

commit v5 on v4

--- a/solution.py
+++ b/solution.py
@@ -26,10 +26,31 @@
     return np.asarray(np.asarray(source).reshape(-1)[:, None] == np.arange(count)[None], BF)
 
 
+def levels(n_expert):
+    inner = 2 if n_expert % 2 == 0 else 1
+    return n_expert // inner, inner
+
+
+def partner(c, j, outer, back=False):
+    if outer & (outer - 1) == 0:
+        return c ^ j
+    return lax.rem(c + (outer - j if back else j), outer) if not isinstance(c, int) else (
+        (c + (outer - j if back else j)) % outer
+    )
+
+
+def position(inner):
+    me = lax.axis_index("expert")
+    return lax.div(me, inner), lax.rem(me, inner)
+
+
 def dispatch_kernel(
-    images, quarter, k, gb, tok_ref, grad_ref, keys_ref, perm_ref,
-    send_ref, disp_ref, comb_ref, my_tok_ref, my_grad_ref, disp_all, comb_all,
+    images, quarter, k, gb, n_expert, tok_ref, grad_ref, keys_ref, perm_ref,
+    disp_ref, comb_ref, my_tok_ref, my_grad_ref, *rest,
 ):
+    outer, inner = levels(n_expert)
+    leave_refs = rest[:outer]
+    send_ref, disp_all, comb_all = rest[outer:]
     slots = keys_ref.shape[0]
     keys = keys_ref[...]
     slot_rows = [[], []]
@@ -52,6 +73,13 @@
             [r[i * step : (i + 1) * step] for kind in slot_rows for r in kind], axis=0
         )
         send_ref[i * rows : (i + 1) * rows] = mm(perm, block).astype(BF)
+    block = send_ref.shape[0] // n_expert
+    c, l = position(inner)
+    for j in range(outer):
+        to = partner(c, j, outer)
+        for i in range(inner):
+            start = pl.multiple_of((to * inner + lax.rem(l + i, inner)) * block, block)
+            leave_refs[j][i * block : (i + 1) * block] = send_ref[pl.ds(start, block)]
     first = lax.axis_index("hidden") * quarter
     for m in range(quarter):
         disp_ref[m] = disp_all[first + m]
@@ -61,8 +89,22 @@
 
 
 def expert_kernel(
-    images, n_expert, k, gb, got_ref, win_ref, bin_ref, wout_ref, q_ref, t_ref, back_ref
+    images, n_expert, k, gb, win_ref, bin_ref, wout_ref, q_ref, t_ref, *rest
 ):
+    outer, inner = levels(n_expert)
+    come_refs = rest[:outer]
+    swap_refs = rest[outer:-2]
+    back_ref, got_ref = rest[-2:]
+    block = got_ref.shape[0] // n_expert
+    c, l = position(inner)
+    for j in range(outer):
+        source = partner(c, j, outer, True)
+        for i in range(inner):
+            start = pl.multiple_of((source * inner + lax.rem(l + i, inner)) * block, block)
+            if i == 0:
+                got_ref[pl.ds(start, block)] = come_refs[j][:block]
+            else:
+                got_ref[pl.ds(start, block)] = swap_refs[0][j * block : (j + 1) * block]
     rows = gb * images
     q = q_ref[...]
     per_block = q.shape[0]
@@ -152,25 +194,33 @@
     order = np.arange(2 * images * gb * k).reshape(2, images, gb, k).transpose(2, 0, 3, 1)
     perm = one_hot_rows(order, order.size)
     send_rows = 2 * k * images
-    send, disp, comb, my_tok, my_grad = pl.pallas_call(
-        functools.partial(dispatch_kernel, images, quarter, k, gb),
+    outer, inner = levels(n_expert)
+    disp, comb, my_tok, my_grad, *leave = pl.pallas_call(
+        functools.partial(dispatch_kernel, images, quarter, k, gb, n_expert),
         out_shape=(
-            jax.ShapeDtypeStruct((n_expert * send_rows, width), BF),
             jax.ShapeDtypeStruct((quarter, slots, positions), BF),
             jax.ShapeDtypeStruct((quarter, slots, positions), BF),
             jax.ShapeDtypeStruct((quarter, positions, width), BF),
             jax.ShapeDtypeStruct((quarter, positions, width), BF),
-        ),
+        )
+        + (jax.ShapeDtypeStruct((inner * send_rows, width), BF),) * outer,
         in_specs=[vmem] * 4,
-        out_specs=(vmem,) * 5,
-        scratch_shapes=[pltpu.VMEM((images, slots, positions), BF)] * 2,
+        out_specs=(vmem,) * (4 + outer),
+        scratch_shapes=[pltpu.VMEM((n_expert * send_rows, width), BF)]
+        + [pltpu.VMEM((images, slots, positions), BF)] * 2,
         compiler_params=pltpu.CompilerParams(vmem_limit_bytes=12 << 20),
         name="dispatch",
     )(tokens, out_grad, keys, perm)
 
-    got = lax.all_to_all(
-        send.reshape(n_expert, send_rows, width), "expert", split_axis=0, concat_axis=0, tiled=True
-    )
+    everyone = [(c, l) for c in range(outer) for l in range(inner)]
+    come = leave[:1] + [None] * (outer - 1)
+    for j in range(outer - 1, 0, -1):
+        pairs = [(c * inner + l, partner(c, j, outer) * inner + l) for c, l in everyone]
+        come[j] = lax.ppermute(leave[j], "expert", pairs)
+    swapped = []
+    if inner == 2:
+        pairs = [(c * inner + l, c * inner + 1 - l) for c, l in everyone]
+        swapped = [lax.ppermute(jnp.concatenate([r[send_rows:] for r in come]), "expert", pairs)]
 
     order = np.arange(gb * send_rows).reshape(gb, 2, k, images).transpose(1, 2, 0, 3)
     sort = one_hot_rows(order, order.size)
@@ -181,11 +231,12 @@
     back = pl.pallas_call(
         functools.partial(expert_kernel, images, n_expert, k, gb),
         out_shape=jax.ShapeDtypeStruct((n_all * back_rows, half), BF),
-        in_specs=[vmem] * 6,
+        in_specs=[vmem] * (5 + outer + len(swapped)),
         out_specs=vmem,
+        scratch_shapes=[pltpu.VMEM((n_expert * send_rows, width), BF)],
         compiler_params=pltpu.CompilerParams(vmem_limit_bytes=20 << 20),
         name="experts",
-    )(got.reshape(n_expert * send_rows, width), w_in, b_in, w_out, sort, spread)
+    )(w_in, b_in, w_out, sort, spread, *come, *swapped)
 
     home = lax.all_to_all(
         back.reshape(n_all, back_rows, half),

time: 36.3 us -> 35.6 us (0.981)
  blocking collectives: 25.9 us -> 14 us
  waiting for transfers between devices: 0 us -> 6.47 us
  starting transfers between devices: 0 us -> 4.63 us
    all_to_all x1 -> x0, blocking collectives: 11.9 us -> none  [local(): lax.all_to_all(send.reshape(n_expert, send_rows, width), 'expert', split_...]
    ppermute x0 -> x4, waiting for transfers between devices: none -> 6.47 us  [the longest x3 5.13 us: local(): come[j] = lax.ppermute(leave[j], 'expert', pairs)]
    ppermute x0 -> x4, starting transfers between devices: none -> 4.63 us  [the longest x3 4.56 us: local(): come[j] = lax.ppermute(leave[j], 'expert', pairs)]
  transfers between devices with their start and end apart: 0 -> 4, of which waited for: 0 -> 4; matrix products, arithmetic and copies ran while one was open for 0% -> 0% of each run, Pallas kernels for 0% -> 0%
where the time goes in v5:
time: 35.6 us; the launch traced here: 35.4 us
  blocking collectives  14 us (39%)
  Pallas kernels  7.63 us (21%)
  waiting for transfers between devices  6.47 us (18%)
  starting transfers between devices  4.63 us (13%)
  local copies, waits for them, and re-layouts  2.59 us (7%)
    all_to_all x1, blocking collectives, local(): lax.all_to_all(back.reshape(n_all, back_rows, half), ('expert', 'hidden')...  14 us
    ppermute x3, waiting for transfers between devices, local(): come[j] = lax.ppermute(leave[j], 'expert', pairs)  5.13 us
    ppermute x3, starting transfers between devices, local(): come[j] = lax.ppermute(leave[j], 'expert', pairs)  4.56 us
    pallas_call x1, Pallas kernels, local(): pl.pallas_call(functools.partial(expert_kernel, images, n_expert, k, gb),...  4.38 us
    unnamed x22, local copies, waits for them, and re-layouts  2.57 us
    pallas_call x1, Pallas kernels, local(): pl.pallas_call(functools.partial(dispatch_kernel, images, quarter, k, gb,...  1.66 us
    pallas_call x1, Pallas kernels, local(): pl.pallas_call(functools.partial(final_kernel, quarter, k, gb), out_shape...  1.59 us
    ppermute x1, waiting for transfers between devices, local(): lax.ppermute(jnp.concatenate([r[send_rows:] for r in come]), 'expert', pa...  1.33 us
  transfers between devices with their start and end apart: 4, of which 4 were waited for; matrix products, arithmetic and copies ran while one was open for 0% of the time, Pallas kernels for 0%

profile of v5, /device:TPU:0, one launch (start us, length us, event | category | flops | bytes accessed | tf_op | source)
XLA Modules:
  0.0 35.4 jit_solution(423220198387937739)
XLA Ops:
  0.0 0.0 copy-start.9
  0.0 0.0 copy-start.3
  0.0 0.0 copy-start.6
  0.0 0.0 copy-start.1
  0.0 2.0 %copy.12.tok_ref = bf16[4,196,1024]{2,1,0:T(8,128)(2,1)S(1)} copy(bf16[4,196,1024]{2,0,1:T(4,128)(2,1)} %param.11) | data formatting | bytes 3211264 | tf_op args[0]
  2.1 0.0 copy-done.9
  2.1 0.0 copy-start
  2.1 0.5 %copy.13.grad_ref = bf16[4,196,1024]{2,1,0:T(8,128)(2,1)S(1)} copy(bf16[4,196,1024]{2,0,1:T(4,128)(2,1)S(1)} %copy-done.9) | data formatting | bytes 3211264 | tf_op args[6]
  2.6 0.0 copy-done.3
  2.6 0.0 copy-done.6
  2.6 0.0 copy-start.2
  2.6 0.0 copy-start.5
  2.6 0.0 copy-start.8
  2.6 1.7 %dispatch.1 = (bf16[1,16,196]{2,1,0:T(8,128)(2,1)S(1)}, bf16[1,16,196]{2,1,0:T(8,128)(2,1)S(1)}, bf16[1,196,1024]{2,1,0:T(8,128)(2,1)S(1)}, bf16[1,196,1024]{2,1...) custom-call(bf16[4,196,1024]{2,1,0:T(8,128)(2,1)S(1)} %copy.12.tok_r, ...), custom_call_target="tpu_custom_call" | custom-call | tf_op jit(solution)/shard_map/dispatch/pallas_call | solution.py:198
  4.3 3.0 %collective-permute-start = (bf16[32,1024]{1,0:T(8,128)(2,1)S(1)}, bf16[32,1024]{1,0:T(8,128)(2,1)S(1)}, u32[]{:S(2)}, u32[]{:S(2)}) collective-permute-start(bf16[32,1024]{1,0:T(8,128)(2,1)S(1)} %get-tuple-element.14), channel_id=1, source_target_pairs={{0,8},{4,12},{8,0},{12,4},{16,24},{20,28},{24,16},{28,20},{1,9},{5... | collective-permute-start | bytes 196616 | tf_op jit(solution)/shard_map/ppermute | solution.py:219
  7.3 1.5 %collective-permute-start.1 = (bf16[32,1024]{1,0:T(8,128)(2,1)S(1)}, bf16[32,1024]{1,0:T(8,128)(2,1)S(1)}, u32[]{:S(2)}, u32[]{:S(2)}) collective-permute-start(bf16[32,1024]{1,0:T(8,128)(2,1)S(1)} %get-tuple-element.15), channel_id=1, source_target_pairs={{0,16},{4,20},{8,24},{12,28},{16,0},{20,4},{24,8},{28,12},{1,17},{... | collective-permute-start | bytes 196616 | tf_op jit(solution)/shard_map/ppermute | solution.py:219
  8.8 0.0 collective-permute-start.2
  8.9 0.8 %collective-permute-done.rest_1_ = bf16[32,1024]{1,0:T(8,128)(2,1)S(1)} collective-permute-done((bf16[32,1024]{1,0:T(8,128)(2,1)S(1)}, bf16[32,1024]{1,0:T(8,128)(2,1)S(1)}, u32[]{:S(2)}, u32[]{:S(2)}) %collective-permute-start) | collective-permute-done | bytes 65568 | tf_op jit(solution)/shard_map/ppermute | solution.py:219
  9.7 1.9 %collective-permute-done.1.rest_2_ = bf16[32,1024]{1,0:T(8,128)(2,1)S(1)} collective-permute-done((bf16[32,1024]{1,0:T(8,128)(2,1)S(1)}, bf16[32,1024]{1,0:T(8,128)(2,1)S(1)}, u32[]{:S(2)}, u32[]{:S(2)}) %collective-permute-start.1) | collective-permute-done | bytes 65568 | tf_op jit(solution)/shard_map/ppermute | solution.py:219
  11.6 2.4 %collective-permute-done.2.rest_3_ = bf16[32,1024]{1,0:T(8,128)(2,1)S(1)} collective-permute-done((bf16[32,1024]{1,0:T(8,128)(2,1)S(1)}, bf16[32,1024]{1,0:T(8,128)(2,1)S(1)}, u32[]{:S(2)}, u32[]{:S(2)}) %collective-permute-start.2) | collective-permute-done | bytes 65568 | tf_op jit(solution)/shard_map/ppermute | solution.py:219
  14.0 0.0 copy-start.4
  14.0 0.0 copy-start.7
  14.0 0.1 collective-permute-start.3
  14.1 1.3 %collective-permute-done.3.rest_4_ = bf16[64,1024]{1,0:T(8,128)(2,1)S(1)} collective-permute-done((bf16[64,1024]{1,0:T(8,128)(2,1)S(1)}, bf16[64,1024]{1,0:T(8,128)(2,1)S(1)}, u32[]{:S(2)}, u32[]{:S(2)}) %collective-permute-start.3) | collective-permute-done | bytes 131104 | tf_op jit(solution)/shard_map/ppermute | solution.py:223
  15.5 0.0 copy-done.1
  15.5 0.0 copy-done
  15.5 0.0 copy-done.2
  15.5 0.0 copy-done.5
  15.5 0.0 copy-done.8
  15.5 4.4 %experts.1 = bf16[256,512]{1,0:T(8,128)(2,1)S(1)} custom-call(bf16[2,1024,1024]{2,1,0:T(8,128)(2,1)S(1)} %copy-done, f32[2,1024]{1,0:T(2,128)S(1)} %copy-done.8, bf16[2,1024,1024]{2,1,0:T(8,128)(2,1)S(1)} %copy-done.1, bf16[128,128]{1,0:T(8,128)(2,1)S(1)} %copy-done.5, bf16[256,256]{1,0:T(8,128)(2,1)S(1)} %copy-done.2, ...), custom_call_target="tpu_custom_call" | custom-call | tf_op jit(solution)/shard_map/experts/pallas_call | solution.py:231
  19.9 14.0 %all_to_all.5 = bf16[32,8,512]{2,1,0:T(8,128)(2,1)S(1)} all-to-all(bf16[32,8,512]{2,1,0:T(8,128)(2,1)S(1)} %bitcast.4), channel_id=1, replica_groups=mesh['expert'=8,'hidden'=4] {'expert','hidden'}, dimensions={0} | all-to-all | bytes 524288 | tf_op jit(solution)/shard_map/all_to_all | solution.py:241
  33.8 0.0 copy-done.4
  33.9 0.0 copy-done.7
  33.9 1.6 %tokens_back.1 = bf16[1,196,1024]{2,1,0:T(8,128)(2,1)} custom-call(bf16[256,512]{1,0:T(8,128)(2,1)S(1)} %bitcast.3, f32[16,1024]{1,0:T(8,128)S(1)} %copy-done.4, bf16[1,196,1024]{2,1,0:T(8,128)(2,1)S(1)} %get-tuple-element.17.tok_ref, bf16[1,196,1024]{2,1,0:T(8,128)(2,1)S(1)} %get-tuple-element.18.grad_ref, ...), custom_call_target="tpu_custom_call" | custom-call | tf_op jit(solution)/shard_map/tokens_back/pallas_call | solution.py:252
  (5 shorter events, 0.0 us)
Async XLA Ops:
  0.0 2.1 %copy-start.9 = (bf16[4,196,1024]{2,0,1:T(4,128)(2,1)S(1)}, bf16[4,196,1024]{2,0,1:T(4,128)(2,1)}, u32[]{:S(2)}) copy-start(bf16[4,196,1024]{2,0,1:T(4,128)(2,1)} %param.17) | copy-start | bytes 4816900
  0.0 2.6 %copy-start.3 = (bf16[1024,16]{0,1:T(8,128)(2,1)S(1)}, bf16[1024,16]{0,1:T(8,128)(2,1)}, u32[]{:S(2)}) copy-start(bf16[1024,16]{0,1:T(8,128)(2,1)} %param.12) | copy-start | bytes 98308
  0.0 2.6 %copy-start.6 = (bf16[128,128]{1,0:T(8,128)(2,1)S(1)}, bf16[128,128]{1,0:T(8,128)(2,1)}, u32[]{:S(2)}) copy-start(bf16[128,128]{1,0:T(8,128)(2,1)} %constant.8.clone.perm_ref) | copy-start | bytes 98308
  0.0 15.4 %copy-start.1 = (bf16[2,1024,1024]{2,1,0:T(8,128)(2,1)S(1)}, bf16[2,1024,1024]{2,1,0:T(8,128)(2,1)}, u32[]{:S(2)}) copy-start(bf16[2,1024,1024]{2,1,0:T(8,128)(2,1)} %wout_ref.1) | copy-start | bytes 12582916
  2.1 13.4 %copy-start = (bf16[2,1024,1024]{2,1,0:T(8,128)(2,1)S(1)}, bf16[2,1024,1024]{2,1,0:T(8,128)(2,1)}, u32[]{:S(2)}) copy-start(bf16[2,1024,1024]{2,1,0:T(8,128)(2,1)} %win_ref.1) | copy-start | bytes 12582916
  2.6 12.9 %copy-start.2 = (bf16[256,256]{1,0:T(8,128)(2,1)S(1)}, bf16[256,256]{1,0:T(8,128)(2,1)}, u32[]{:S(2)}) copy-start(bf16[256,256]{1,0:T(8,128)(2,1)} %constant.10.clone.t_ref) | copy-start | bytes 393220
  2.6 12.9 %copy-start.5 = (bf16[128,128]{1,0:T(8,128)(2,1)S(1)}, bf16[128,128]{1,0:T(8,128)(2,1)}, u32[]{:S(2)}) copy-start(bf16[128,128]{1,0:T(8,128)(2,1)} %constant.9.clone.q_ref) | copy-start | bytes 98308
  2.6 12.9 %copy-start.8 = (f32[2,1024]{1,0:T(2,128)S(1)}, f32[2,1024]{1,0:T(2,128)}, u32[]{:S(2)}) copy-start(f32[2,1024]{1,0:T(2,128)} %bin_ref.1) | copy-start | bytes 24580
  4.3 5.4 %collective-permute-start = (bf16[32,1024]{1,0:T(8,128)(2,1)S(1)}, bf16[32,1024]{1,0:T(8,128)(2,1)S(1)}, u32[]{:S(2)}, u32[]{:S(2)}) collective-permute-start(bf16[32,1024]{1,0:T(8,128)(2,1)S(1)} %get-tuple-element.14), channel_id=1, source_target_pairs={{0,8},{4,12},{8,0},{12,4},{16,24},{20,28},{24,16},{28,20},{1,9},{5... | collective-permute-start | bytes 196616 | tf_op jit(solution)/shard_map/ppermute | solution.py:219
  7.3 4.3 %collective-permute-start.1 = (bf16[32,1024]{1,0:T(8,128)(2,1)S(1)}, bf16[32,1024]{1,0:T(8,128)(2,1)S(1)}, u32[]{:S(2)}, u32[]{:S(2)}) collective-permute-start(bf16[32,1024]{1,0:T(8,128)(2,1)S(1)} %get-tuple-element.15), channel_id=1, source_target_pairs={{0,16},{4,20},{8,24},{12,28},{16,0},{20,4},{24,8},{28,12},{1,17},{... | collective-permute-start | bytes 196616 | tf_op jit(solution)/shard_map/ppermute | solution.py:219
  8.8 5.2 %collective-permute-start.2 = (bf16[32,1024]{1,0:T(8,128)(2,1)S(1)}, bf16[32,1024]{1,0:T(8,128)(2,1)S(1)}, u32[]{:S(2)}, u32[]{:S(2)}) collective-permute-start(bf16[32,1024]{1,0:T(8,128)(2,1)S(1)} %get-tuple-element.16), channel_id=1, source_target_pairs={{0,24},{4,28},{8,16},{12,20},{16,8},{20,12},{24,0},{28,4},{1,25},{... | collective-permute-start | bytes 196616 | tf_op jit(solution)/shard_map/ppermute | solution.py:219
  14.0 19.8 %copy-start.4 = (f32[16,1024]{1,0:T(8,128)S(1)}, f32[16,1024]{1,0:T(8,128)}, u32[]{:S(2)}) copy-start(f32[16,1024]{1,0:T(8,128)} %bias_ref.1) | copy-start | bytes 196612
  14.0 19.8 %copy-start.7 = (bf16[64,256]{1,0:T(8,128)(2,1)S(1)}, bf16[64,256]{1,0:T(8,128)(2,1)}, u32[]{:S(2)}) copy-start(bf16[64,256]{1,0:T(8,128)(2,1)} %constant.11.clone.sel_ref) | copy-start | bytes 98308
  14.0 1.4 %collective-permute-start.3 = (bf16[64,1024]{1,0:T(8,128)(2,1)S(1)}, bf16[64,1024]{1,0:T(8,128)(2,1)S(1)}, u32[]{:S(2)}, u32[]{:S(2)}) collective-permute-start(bf16[64,1024]{1,0:T(8,128)(2,1)S(1)} %pad_maximum_fusion), channel_id=1, source_target_pairs={{0,4},{4,0},{8,12},{12,8},{16,20},{20,16},{24,28},{28,24},{1,5},{5... | collective-permute-start | bytes 393224 | tf_op jit(solution)/shard_map/ppermute | solution.py:223

commit v6 on v4

--- a/solution.py
+++ b/solution.py
@@ -26,10 +26,19 @@
     return np.asarray(np.asarray(source).reshape(-1)[:, None] == np.arange(count)[None], BF)
 
 
+def partner(me, j, n, back=False):
+    if n & (n - 1) == 0:
+        return me ^ j
+    shifted = me + (n - j if back else j)
+    return shifted % n if isinstance(me, int) else lax.rem(shifted, n)
+
+
 def dispatch_kernel(
-    images, quarter, k, gb, tok_ref, grad_ref, keys_ref, perm_ref,
-    send_ref, disp_ref, comb_ref, my_tok_ref, my_grad_ref, disp_all, comb_all,
+    images, quarter, k, gb, n_expert, tok_ref, grad_ref, keys_ref, perm_ref,
+    disp_ref, comb_ref, my_tok_ref, my_grad_ref, *rest,
 ):
+    leave_refs = rest[:n_expert]
+    send_ref, disp_all, comb_all = rest[n_expert:]
     slots = keys_ref.shape[0]
     keys = keys_ref[...]
     slot_rows = [[], []]
@@ -52,6 +61,11 @@
             [r[i * step : (i + 1) * step] for kind in slot_rows for r in kind], axis=0
         )
         send_ref[i * rows : (i + 1) * rows] = mm(perm, block).astype(BF)
+    block = send_ref.shape[0] // n_expert
+    me = lax.axis_index("expert")
+    for j in range(n_expert):
+        start = pl.multiple_of(partner(me, j, n_expert) * block, block)
+        leave_refs[j][...] = send_ref[pl.ds(start, block)]
     first = lax.axis_index("hidden") * quarter
     for m in range(quarter):
         disp_ref[m] = disp_all[first + m]
@@ -60,41 +74,43 @@
         my_grad_ref[m] = grad_ref[first + m]
 
 
-def expert_kernel(
-    images, n_expert, k, gb, got_ref, win_ref, bin_ref, wout_ref, q_ref, t_ref, back_ref
-):
-    rows = gb * images
-    q = q_ref[...]
-    per_block = q.shape[0]
-    blocks = n_expert // gb
-    sorted_rows = [
-        mm(q, got_ref[i * per_block : (i + 1) * per_block]).astype(BF) for i in range(blocks)
-    ]
-
-    def pick(kind, e):
-        start = (kind * k + e) * rows
-        return jnp.concatenate([s[start : start + rows] for s in sorted_rows], axis=0)
-
-    width = got_ref.shape[1]
+def expert_kernel(images, n_expert, k, gb, win_ref, bin_ref, wout_ref, t_ref, *rest):
+    come_refs = rest[:n_expert]
+    back_ref, got_ref = rest[n_expert:]
+    rows = k * images
+    me = lax.axis_index("expert")
+    for j in range(n_expert):
+        got_ref[partner(me, j, n_expert, True)] = come_refs[j][...]
+    width = got_ref.shape[2]
+    total = n_expert * rows
+    got = got_ref[...]
+    rows_in = got[:, :rows].reshape(total, width)
+    rows_grad = got[:, rows:].reshape(total, width)
     half = width // 2
-    results = [[None] * k, [None] * k]
-    for e in range(k):
-        pre = mm(pick(0, e), win_ref[e]) + bin_ref[e : e + 1]
-        cdf = 0.5 * (1.0 + lax.erf(pre * 0.7071067811865476))
-        hidden = (pre * cdf).astype(BF)
-        slope = cdf + pre * jnp.exp(-0.5 * pre * pre) * 0.3989422804014327
-        act_grad = mm(pick(1, e), wout_ref[e], NT)
-        results[0][e] = mm(hidden, wout_ref[e]).astype(BF)
-        pre_grad = (act_grad * slope).astype(BF)
-        results[1][e] = mm(pre_grad, win_ref[e], NT).astype(BF)
+    expert = lax.rem(lax.div(lax.broadcasted_iota(jnp.int32, (total, 1), 0), images), k)
+
+    def own(parts):
+        out = parts[0]
+        for e in range(1, k):
+            out = jnp.where(expert == e, parts[e], out)
+        return out
+
+    pre = own([mm(rows_in, win_ref[e]) + bin_ref[e : e + 1] for e in range(k)])
+    cdf = 0.5 * (1.0 + lax.erf(pre * 0.7071067811865476))
+    hidden = (pre * cdf).astype(BF)
+    slope = cdf + pre * jnp.exp(-0.5 * pre * pre) * 0.3989422804014327
+    out_part = own([mm(hidden, wout_ref[e]) for e in range(k)]).astype(BF)
+    act_grad = own([mm(rows_grad, wout_ref[e], NT) for e in range(k)])
+    pre_grad = (act_grad * slope).astype(BF)
+    in_part = own([mm(pre_grad, win_ref[e], NT) for e in range(k)]).astype(BF)
+    rows = gb * k * images
     t = t_ref[...]
     out_rows = t.shape[0]
-    for i in range(blocks):
+    for i in range(n_expert // gb):
         stack = jnp.concatenate(
             [
-                r[i * rows : (i + 1) * rows, h * half : (h + 1) * half]
-                for kind in results
-                for r in kind
+                part[i * rows : (i + 1) * rows, h * half : (h + 1) * half]
+                for part in (out_part, in_part)
                 for h in range(2)
             ],
             axis=0,
@@ -152,40 +168,41 @@
     order = np.arange(2 * images * gb * k).reshape(2, images, gb, k).transpose(2, 0, 3, 1)
     perm = one_hot_rows(order, order.size)
     send_rows = 2 * k * images
-    send, disp, comb, my_tok, my_grad = pl.pallas_call(
-        functools.partial(dispatch_kernel, images, quarter, k, gb),
+    disp, comb, my_tok, my_grad, *leave = pl.pallas_call(
+        functools.partial(dispatch_kernel, images, quarter, k, gb, n_expert),
         out_shape=(
-            jax.ShapeDtypeStruct((n_expert * send_rows, width), BF),
             jax.ShapeDtypeStruct((quarter, slots, positions), BF),
             jax.ShapeDtypeStruct((quarter, slots, positions), BF),
             jax.ShapeDtypeStruct((quarter, positions, width), BF),
             jax.ShapeDtypeStruct((quarter, positions, width), BF),
-        ),
+        )
+        + (jax.ShapeDtypeStruct((send_rows, width), BF),) * n_expert,
         in_specs=[vmem] * 4,
-        out_specs=(vmem,) * 5,
-        scratch_shapes=[pltpu.VMEM((images, slots, positions), BF)] * 2,
+        out_specs=(vmem,) * (4 + n_expert),
+        scratch_shapes=[pltpu.VMEM((n_expert * send_rows, width), BF)]
+        + [pltpu.VMEM((images, slots, positions), BF)] * 2,
         compiler_params=pltpu.CompilerParams(vmem_limit_bytes=12 << 20),
         name="dispatch",
     )(tokens, out_grad, keys, perm)
 
-    got = lax.all_to_all(
-        send.reshape(n_expert, send_rows, width), "expert", split_axis=0, concat_axis=0, tiled=True
-    )
-
-    order = np.arange(gb * send_rows).reshape(gb, 2, k, images).transpose(1, 2, 0, 3)
-    sort = one_hot_rows(order, order.size)
-    order = np.arange(2 * k * 2 * gb * images).reshape(2, k, 2, gb, n_hidden, quarter)
-    order = order.transpose(3, 4, 0, 1, 5, 2)
+    come = leave[:1] + [None] * (n_expert - 1)
+    for j in range(n_expert - 1, 0, -1):
+        pairs = [(i, partner(i, j, n_expert)) for i in range(n_expert)]
+        come[j] = lax.ppermute(leave[j], "expert", pairs)
+
+    order = np.arange(2 * k * 2 * gb * images).reshape(2, 2, gb, k, n_hidden, quarter)
+    order = order.transpose(2, 4, 0, 3, 5, 1)
     spread = one_hot_rows(order, order.size)
     back_rows = 2 * k * quarter * 2
     back = pl.pallas_call(
         functools.partial(expert_kernel, images, n_expert, k, gb),
         out_shape=jax.ShapeDtypeStruct((n_all * back_rows, half), BF),
-        in_specs=[vmem] * 6,
+        in_specs=[vmem] * (4 + n_expert),
         out_specs=vmem,
+        scratch_shapes=[pltpu.VMEM((n_expert, send_rows, width), BF)],
         compiler_params=pltpu.CompilerParams(vmem_limit_bytes=20 << 20),
         name="experts",
-    )(got.reshape(n_expert * send_rows, width), w_in, b_in, w_out, sort, spread)
+    )(w_in, b_in, w_out, spread, *come)
 
     home = lax.all_to_all(
         back.reshape(n_all, back_rows, half),

time: 36.3 us -> 38.2 us (1.052)
  blocking collectives: 25.9 us -> 14.5 us
  starting transfers between devices: 0 us -> 7.66 us
  waiting for transfers between devices: 0 us -> 4.13 us
  local copies, waits for them, and re-layouts: 2.57 us -> 4.14 us
    all_to_all x1 -> x0, blocking collectives: 11.9 us -> none  [local(): lax.all_to_all(send.reshape(n_expert, send_rows, width), 'expert', split_...]
    ppermute x0 -> x7, starting transfers between devices: none -> 7.66 us  [local(): come[j] = lax.ppermute(leave[j], 'expert', pairs)]
    ppermute x0 -> x7, waiting for transfers between devices: none -> 4.13 us  [local(): come[j] = lax.ppermute(leave[j], 'expert', pairs)]
    unnamed x22 -> x18, local copies, waits for them, and re-layouts: 2.57 us -> 4.14 us
    all_to_all x1, blocking collectives: 14 us -> 14.5 us  [local(): lax.all_to_all(back.reshape(n_all, back_rows, half), ('expert', 'hidden')...]
  transfers between devices with their start and end apart: 0 -> 7, of which waited for: 0 -> 3; matrix products, arithmetic and copies ran while one was open for 0% -> 0% of each run, Pallas kernels for 0% -> 0%
where the time goes in v6:
time: 38.2 us; the launch traced here: 38.1 us
  blocking collectives  14.5 us (38%)
  starting transfers between devices  7.66 us (20%)
  Pallas kernels  7.58 us (20%)
  local copies, waits for them, and re-layouts  4.14 us (11%)
  waiting for transfers between devices  4.13 us (11%)
    all_to_all x1, blocking collectives, local(): lax.all_to_all(back.reshape(n_all, back_rows, half), ('expert', 'hidden')...  14.5 us
    ppermute x7, starting transfers between devices, local(): come[j] = lax.ppermute(leave[j], 'expert', pairs)  7.66 us
    pallas_call x1, Pallas kernels, local(): pl.pallas_call(functools.partial(expert_kernel, images, n_expert, k, gb),...  4.34 us
    unnamed x18, local copies, waits for them, and re-layouts  4.14 us
    ppermute x7, waiting for transfers between devices, local(): come[j] = lax.ppermute(leave[j], 'expert', pairs)  4.13 us
    pallas_call x1, Pallas kernels, local(): pl.pallas_call(functools.partial(dispatch_kernel, images, quarter, k, gb,...  1.66 us
    pallas_call x1, Pallas kernels, local(): pl.pallas_call(functools.partial(final_kernel, quarter, k, gb), out_shape...  1.58 us
  transfers between devices with their start and end apart: 7, of which 3 were waited for; matrix products, arithmetic and copies ran while one was open for 0% of the time, Pallas kernels for 0%

profile of v6, /device:TPU:0, one launch (start us, length us, event | category | flops | bytes accessed | tf_op | source)
XLA Modules:
  0.0 38.1 jit_solution(14175123637085433964)
XLA Ops:
  0.0 0.0 copy-start.3
  0.0 0.0 copy-start.5
  0.0 0.0 copy-start.1
  0.0 2.0 %copy.11.tok_ref = bf16[4,196,1024]{2,1,0:T(8,128)(2,1)S(1)} copy(bf16[4,196,1024]{2,0,1:T(4,128)(2,1)} %param.10) | data formatting | bytes 3211264 | tf_op args[0]
  2.1 0.0 copy-start
  2.1 2.0 %copy.12.grad_ref = bf16[4,196,1024]{2,1,0:T(8,128)(2,1)S(1)} copy(bf16[4,196,1024]{2,0,1:T(4,128)(2,1)} %param.16) | data formatting | bytes 3211264 | tf_op args[6]
  4.1 0.0 copy-done.3
  4.1 0.0 copy-done.5
  4.1 0.0 copy-start.2
  4.2 0.0 copy-start.7
  4.2 1.7 %dispatch.1 = (bf16[1,16,196]{2,1,0:T(8,128)(2,1)S(1)}, bf16[1,16,196]{2,1,0:T(8,128)(2,1)S(1)}, bf16[1,196,1024]{2,1,0:T(8,128)(2,1)S(1)}, bf16[1,196,1024]{2,1...) custom-call(bf16[4,196,1024]{2,1,0:T(8,128)(2,1)S(1)} %copy.11.tok_r, ...), custom_call_target="tpu_custom_call" | custom-call | tf_op jit(solution)/shard_map/dispatch/pallas_call | solution.py:171
  5.8 0.5 %collective-permute-start = (bf16[16,1024]{1,0:T(8,128)(2,1)S(1)}, bf16[16,1024]{1,0:T(8,128)(2,1)S(1)}, u32[]{:S(2)}, u32[]{:S(2)}) collective-permute-start(bf16[16,1024]{1,0:T(8,128)(2,1)S(1)} %get-tuple-element.18), channel_id=1, source_target_pairs={{0,4},{4,0},{8,12},{12,8},{16,20},{20,16},{24,28},{28,24},{1,5},{5... | collective-permute-start | bytes 98312 | tf_op jit(solution)/shard_map/ppermute | solution.py:191
  6.4 2.6 %collective-permute-start.1 = (bf16[16,1024]{1,0:T(8,128)(2,1)S(1)}, bf16[16,1024]{1,0:T(8,128)(2,1)S(1)}, u32[]{:S(2)}, u32[]{:S(2)}) collective-permute-start(bf16[16,1024]{1,0:T(8,128)(2,1)S(1)} %get-tuple-element.19), channel_id=1, source_target_pairs={{0,8},{4,12},{8,0},{12,4},{16,24},{20,28},{24,16},{28,20},{1,9},{5... | collective-permute-start | bytes 98312 | tf_op jit(solution)/shard_map/ppermute | solution.py:191
  8.9 0.1 collective-permute-start.2
  9.0 1.8 %collective-permute-start.3 = (bf16[16,1024]{1,0:T(8,128)(2,1)S(1)}, bf16[16,1024]{1,0:T(8,128)(2,1)S(1)}, u32[]{:S(2)}, u32[]{:S(2)}) collective-permute-start(bf16[16,1024]{1,0:T(8,128)(2,1)S(1)} %get-tuple-element.21), channel_id=1, source_target_pairs={{0,16},{4,20},{8,24},{12,28},{16,0},{20,4},{24,8},{28,12},{1,17},{... | collective-permute-start | bytes 98312 | tf_op jit(solution)/shard_map/ppermute | solution.py:191
  10.8 0.0 collective-permute-start.4
  10.8 0.0 collective-permute-done.rest_1_
  10.8 2.6 %collective-permute-start.5 = (bf16[16,1024]{1,0:T(8,128)(2,1)S(1)}, bf16[16,1024]{1,0:T(8,128)(2,1)S(1)}, u32[]{:S(2)}, u32[]{:S(2)}) collective-permute-start(bf16[16,1024]{1,0:T(8,128)(2,1)S(1)} %get-tuple-element.23), channel_id=1, source_target_pairs={{0,24},{4,28},{8,16},{12,20},{16,8},{20,12},{24,0},{28,4},{1,25},{... | collective-permute-start | bytes 98312 | tf_op jit(solution)/shard_map/ppermute | solution.py:191
  13.4 0.0 collective-permute-done.1.rest_2_
  13.4 0.1 collective-permute-start.6
  13.5 0.0 collective-permute-done.2.rest_3_
  13.5 0.0 collective-permute-done.3.rest_4_
  13.5 0.7 %collective-permute-done.4.rest_5_ = bf16[16,1024]{1,0:T(8,128)(2,1)S(1)} collective-permute-done((bf16[16,1024]{1,0:T(8,128)(2,1)S(1)}, bf16[16,1024]{1,0:T(8,128)(2,1)S(1)}, u32[]{:S(2)}, u32[]{:S(2)}) %collective-permute-start.4) | collective-permute-done | bytes 32800 | tf_op jit(solution)/shard_map/ppermute | solution.py:191
  14.2 1.4 %collective-permute-done.5.rest_6_ = bf16[16,1024]{1,0:T(8,128)(2,1)S(1)} collective-permute-done((bf16[16,1024]{1,0:T(8,128)(2,1)S(1)}, bf16[16,1024]{1,0:T(8,128)(2,1)S(1)}, u32[]{:S(2)}, u32[]{:S(2)}) %collective-permute-start.5) | collective-permute-done | bytes 32800 | tf_op jit(solution)/shard_map/ppermute | solution.py:191
  15.6 2.0 %collective-permute-done.6.rest_7_ = bf16[16,1024]{1,0:T(8,128)(2,1)S(1)} collective-permute-done((bf16[16,1024]{1,0:T(8,128)(2,1)S(1)}, bf16[16,1024]{1,0:T(8,128)(2,1)S(1)}, u32[]{:S(2)}, u32[]{:S(2)}) %collective-permute-start.6) | collective-permute-done | bytes 32800 | tf_op jit(solution)/shard_map/ppermute | solution.py:191
  17.6 0.0 copy-done.1
  17.6 0.0 copy-done
  17.6 0.0 copy-done.2
  17.6 0.0 copy-done.7
  17.7 0.0 copy-start.4
  17.7 0.0 copy-start.6
  17.7 4.3 %experts.1 = bf16[256,512]{1,0:T(8,128)(2,1)S(1)} custom-call(bf16[2,1024,1024]{2,1,0:T(8,128)(2,1)S(1)} %copy-done, f32[2,1024]{1,0:T(2,128)S(1)} %copy-done.7, bf16[2,1024,1024]{2,1,0:T(8,128)(2,1)S(1)} %copy-done.1, bf16[256,256]{1,0:T(8,128)(2,1)S(1)} %copy-done.2, bf16[16,1024]{1,0:T(8,128)(2,1)S(1)} %get-tuple-element.17.rest_0_, ...), custom_call_target="tpu_custom_call" | custom-call | tf_op jit(solution)/shard_map/experts/pallas_call | solution.py:197
  22.0 14.5 %all_to_all.5 = bf16[32,8,512]{2,1,0:T(8,128)(2,1)S(1)} all-to-all(bf16[32,8,512]{2,1,0:T(8,128)(2,1)S(1)} %bitcast.3), channel_id=1, replica_groups=mesh['expert'=8,'hidden'=4] {'expert','hidden'}, dimensions={0} | all-to-all | bytes 524288 | tf_op jit(solution)/shard_map/all_to_all | solution.py:207
  36.5 0.0 copy-done.4
  36.5 0.0 copy-done.6
  36.5 1.6 %tokens_back.1 = bf16[1,196,1024]{2,1,0:T(8,128)(2,1)} custom-call(bf16[256,512]{1,0:T(8,128)(2,1)S(1)} %bitcast.4, f32[16,1024]{1,0:T(8,128)S(1)} %copy-done.4, bf16[1,196,1024]{2,1,0:T(8,128)(2,1)S(1)} %get-tuple-element.25.tok_ref, bf16[1,196,1024]{2,1,0:T(8,128)(2,1)S(1)} %get-tuple-element.26.grad_ref, ...), custom_call_target="tpu_custom_call" | custom-call | tf_op jit(solution)/shard_map/tokens_back/pallas_call | solution.py:218
Async XLA Ops:
  0.0 4.1 %copy-start.3 = (bf16[1024,16]{0,1:T(8,128)(2,1)S(1)}, bf16[1024,16]{0,1:T(8,128)(2,1)}, u32[]{:S(2)}) copy-start(bf16[1024,16]{0,1:T(8,128)(2,1)} %param.11) | copy-start | bytes 98308
  0.0 4.1 %copy-start.5 = (bf16[128,128]{1,0:T(8,128)(2,1)S(1)}, bf16[128,128]{1,0:T(8,128)(2,1)}, u32[]{:S(2)}) copy-start(bf16[128,128]{1,0:T(8,128)(2,1)} %constant.6.clone.perm_ref) | copy-start | bytes 98308
  0.0 17.6 %copy-start.1 = (bf16[2,1024,1024]{2,1,0:T(8,128)(2,1)S(1)}, bf16[2,1024,1024]{2,1,0:T(8,128)(2,1)}, u32[]{:S(2)}) copy-start(bf16[2,1024,1024]{2,1,0:T(8,128)(2,1)} %wout_ref.1) | copy-start | bytes 12582916
  2.1 15.6 %copy-start = (bf16[2,1024,1024]{2,1,0:T(8,128)(2,1)S(1)}, bf16[2,1024,1024]{2,1,0:T(8,128)(2,1)}, u32[]{:S(2)}) copy-start(bf16[2,1024,1024]{2,1,0:T(8,128)(2,1)} %win_ref.1) | copy-start | bytes 12582916
  4.1 13.5 %copy-start.2 = (bf16[256,256]{1,0:T(8,128)(2,1)S(1)}, bf16[256,256]{1,0:T(8,128)(2,1)}, u32[]{:S(2)}) copy-start(bf16[256,256]{1,0:T(8,128)(2,1)} %constant.7.clone.t_ref) | copy-start | bytes 393220
  4.2 13.5 %copy-start.7 = (f32[2,1024]{1,0:T(2,128)S(1)}, f32[2,1024]{1,0:T(2,128)}, u32[]{:S(2)}) copy-start(f32[2,1024]{1,0:T(2,128)} %bin_ref.1) | copy-start | bytes 24580
  5.8 4.9 %collective-permute-start = (bf16[16,1024]{1,0:T(8,128)(2,1)S(1)}, bf16[16,1024]{1,0:T(8,128)(2,1)S(1)}, u32[]{:S(2)}, u32[]{:S(2)}) collective-permute-start(bf16[16,1024]{1,0:T(8,128)(2,1)S(1)} %get-tuple-element.18), channel_id=1, source_target_pairs={{0,4},{4,0},{8,12},{12,8},{16,20},{20,16},{24,28},{28,24},{1,5},{5... | collective-permute-start | bytes 98312 | tf_op jit(solution)/shard_map/ppermute | solution.py:191
  6.4 7.0 %collective-permute-start.1 = (bf16[16,1024]{1,0:T(8,128)(2,1)S(1)}, bf16[16,1024]{1,0:T(8,128)(2,1)S(1)}, u32[]{:S(2)}, u32[]{:S(2)}) collective-permute-start(bf16[16,1024]{1,0:T(8,128)(2,1)S(1)} %get-tuple-element.19), channel_id=1, source_target_pairs={{0,8},{4,12},{8,0},{12,4},{16,24},{20,28},{24,16},{28,20},{1,9},{5... | collective-permute-start | bytes 98312 | tf_op jit(solution)/shard_map/ppermute | solution.py:191
  8.9 4.6 %collective-permute-start.2 = (bf16[16,1024]{1,0:T(8,128)(2,1)S(1)}, bf16[16,1024]{1,0:T(8,128)(2,1)S(1)}, u32[]{:S(2)}, u32[]{:S(2)}) collective-permute-start(bf16[16,1024]{1,0:T(8,128)(2,1)S(1)} %get-tuple-element.20), channel_id=1, source_target_pairs={{0,12},{4,8},{8,4},{12,0},{16,28},{20,24},{24,20},{28,16},{1,13},{... | collective-permute-start | bytes 98312 | tf_op jit(solution)/shard_map/ppermute | solution.py:191
  9.0 4.5 %collective-permute-start.3 = (bf16[16,1024]{1,0:T(8,128)(2,1)S(1)}, bf16[16,1024]{1,0:T(8,128)(2,1)S(1)}, u32[]{:S(2)}, u32[]{:S(2)}) collective-permute-start(bf16[16,1024]{1,0:T(8,128)(2,1)S(1)} %get-tuple-element.21), channel_id=1, source_target_pairs={{0,16},{4,20},{8,24},{12,28},{16,0},{20,4},{24,8},{28,12},{1,17},{... | collective-permute-start | bytes 98312 | tf_op jit(solution)/shard_map/ppermute | solution.py:191
  10.8 3.5 %collective-permute-start.4 = (bf16[16,1024]{1,0:T(8,128)(2,1)S(1)}, bf16[16,1024]{1,0:T(8,128)(2,1)S(1)}, u32[]{:S(2)}, u32[]{:S(2)}) collective-permute-start(bf16[16,1024]{1,0:T(8,128)(2,1)S(1)} %get-tuple-element.22), channel_id=1, source_target_pairs={{0,20},{4,16},{8,28},{12,24},{16,4},{20,0},{24,12},{28,8},{1,21},{... | collective-permute-start | bytes 98312 | tf_op jit(solution)/shard_map/ppermute | solution.py:191
  10.8 4.8 %collective-permute-start.5 = (bf16[16,1024]{1,0:T(8,128)(2,1)S(1)}, bf16[16,1024]{1,0:T(8,128)(2,1)S(1)}, u32[]{:S(2)}, u32[]{:S(2)}) collective-permute-start(bf16[16,1024]{1,0:T(8,128)(2,1)S(1)} %get-tuple-element.23), channel_id=1, source_target_pairs={{0,24},{4,28},{8,16},{12,20},{16,8},{20,12},{24,0},{28,4},{1,25},{... | collective-permute-start | bytes 98312 | tf_op jit(solution)/shard_map/ppermute | solution.py:191
  13.4 4.2 %collective-permute-start.6 = (bf16[16,1024]{1,0:T(8,128)(2,1)S(1)}, bf16[16,1024]{1,0:T(8,128)(2,1)S(1)}, u32[]{:S(2)}, u32[]{:S(2)}) collective-permute-start(bf16[16,1024]{1,0:T(8,128)(2,1)S(1)} %get-tuple-element.24), channel_id=1, source_target_pairs={{0,28},{4,24},{8,20},{12,16},{16,12},{20,8},{24,4},{28,0},{1,29},{... | collective-permute-start | bytes 98312 | tf_op jit(solution)/shard_map/ppermute | solution.py:191
  17.7 18.8 %copy-start.4 = (f32[16,1024]{1,0:T(8,128)S(1)}, f32[16,1024]{1,0:T(8,128)}, u32[]{:S(2)}) copy-start(f32[16,1024]{1,0:T(8,128)} %bias_ref.1) | copy-start | bytes 196612
  17.7 18.8 %copy-start.6 = (bf16[64,256]{1,0:T(8,128)(2,1)S(1)}, bf16[64,256]{1,0:T(8,128)(2,1)}, u32[]{:S(2)}) copy-start(bf16[64,256]{1,0:T(8,128)(2,1)} %constant.8.clone.sel_ref) | copy-start | bytes 98308

commit v7 on v6

--- a/solution.py
+++ b/solution.py
@@ -33,12 +33,23 @@
     return shifted % n if isinstance(me, int) else lax.rem(shifted, n)
 
 
+def levels(n_expert):
+    inner = 2 if n_expert % 2 == 0 else 1
+    return n_expert // inner, inner
+
+
+def position(inner):
+    me = lax.axis_index("expert")
+    return lax.div(me, inner), lax.rem(me, inner)
+
+
 def dispatch_kernel(
     images, quarter, k, gb, n_expert, tok_ref, grad_ref, keys_ref, perm_ref,
     disp_ref, comb_ref, my_tok_ref, my_grad_ref, *rest,
 ):
-    leave_refs = rest[:n_expert]
-    send_ref, disp_all, comb_all = rest[n_expert:]
+    outer, inner = levels(n_expert)
+    leave_refs = rest[:inner]
+    send_ref, disp_all, comb_all = rest[inner:]
     slots = keys_ref.shape[0]
     keys = keys_ref[...]
     slot_rows = [[], []]
@@ -62,10 +73,13 @@
         )
         send_ref[i * rows : (i + 1) * rows] = mm(perm, block).astype(BF)
     block = send_ref.shape[0] // n_expert
-    me = lax.axis_index("expert")
-    for j in range(n_expert):
-        start = pl.multiple_of(partner(me, j, n_expert) * block, block)
-        leave_refs[j][...] = send_ref[pl.ds(start, block)]
+    c, l = position(inner)
+    for i in range(inner):
+        for j in range(outer):
+            to = partner(c, j, outer) * inner + lax.rem(l + i, inner)
+            leave_refs[i][j * block : (j + 1) * block] = send_ref[
+                pl.ds(pl.multiple_of(to * block, block), block)
+            ]
     first = lax.axis_index("hidden") * quarter
     for m in range(quarter):
         disp_ref[m] = disp_all[first + m]
@@ -75,12 +89,16 @@
 
 
 def expert_kernel(images, n_expert, k, gb, win_ref, bin_ref, wout_ref, t_ref, *rest):
-    come_refs = rest[:n_expert]
-    back_ref, got_ref = rest[n_expert:]
+    outer, inner = levels(n_expert)
+    come_refs = rest[:outer]
+    back_ref, got_ref = rest[outer:]
     rows = k * images
-    me = lax.axis_index("expert")
-    for j in range(n_expert):
-        got_ref[partner(me, j, n_expert, True)] = come_refs[j][...]
+    c, l = position(inner)
+    block = got_ref.shape[1]
+    for j in range(outer):
+        source = partner(c, j, outer, True) * inner
+        for i in range(inner):
+            got_ref[source + lax.rem(l + i, inner)] = come_refs[j][i * block : (i + 1) * block]
     width = got_ref.shape[2]
     total = n_expert * rows
     got = got_ref[...]
@@ -168,6 +186,7 @@
     order = np.arange(2 * images * gb * k).reshape(2, images, gb, k).transpose(2, 0, 3, 1)
     perm = one_hot_rows(order, order.size)
     send_rows = 2 * k * images
+    outer, inner = levels(n_expert)
     disp, comb, my_tok, my_grad, *leave = pl.pallas_call(
         functools.partial(dispatch_kernel, images, quarter, k, gb, n_expert),
         out_shape=(
@@ -176,19 +195,25 @@
             jax.ShapeDtypeStruct((quarter, positions, width), BF),
             jax.ShapeDtypeStruct((quarter, positions, width), BF),
         )
-        + (jax.ShapeDtypeStruct((send_rows, width), BF),) * n_expert,
+        + (jax.ShapeDtypeStruct((outer * send_rows, width), BF),) * inner,
         in_specs=[vmem] * 4,
-        out_specs=(vmem,) * (4 + n_expert),
+        out_specs=(vmem,) * (4 + inner),
         scratch_shapes=[pltpu.VMEM((n_expert * send_rows, width), BF)]
         + [pltpu.VMEM((images, slots, positions), BF)] * 2,
         compiler_params=pltpu.CompilerParams(vmem_limit_bytes=12 << 20),
         name="dispatch",
     )(tokens, out_grad, keys, perm)
 
-    come = leave[:1] + [None] * (n_expert - 1)
-    for j in range(n_expert - 1, 0, -1):
-        pairs = [(i, partner(i, j, n_expert)) for i in range(n_expert)]
-        come[j] = lax.ppermute(leave[j], "expert", pairs)
+    everyone = [(c, l) for c in range(outer) for l in range(inner)]
+    held = leave[:1]
+    if inner == 2:
+        pairs = [(c * inner + l, c * inner + 1 - l) for c, l in everyone]
+        held.append(lax.ppermute(leave[1], "expert", pairs))
+    come = []
+    for j in range(outer):
+        both = jnp.concatenate([r[j * send_rows : (j + 1) * send_rows] for r in held])
+        pairs = [(c * inner + l, partner(c, j, outer) * inner + l) for c, l in everyone]
+        come.append(lax.ppermute(both, "expert", pairs) if j else both)
 
     order = np.arange(2 * k * 2 * gb * images).reshape(2, 2, gb, k, n_hidden, quarter)
     order = order.transpose(2, 4, 0, 3, 5, 1)
@@ -197,7 +222,7 @@
     back = pl.pallas_call(
         functools.partial(expert_kernel, images, n_expert, k, gb),
         out_shape=jax.ShapeDtypeStruct((n_all * back_rows, half), BF),
-        in_specs=[vmem] * (4 + n_expert),
+        in_specs=[vmem] * (4 + outer),
         out_specs=vmem,
         scratch_shapes=[pltpu.VMEM((n_expert, send_rows, width), BF)],
         compiler_params=pltpu.CompilerParams(vmem_limit_bytes=20 << 20),

time: 38.2 us -> 35.9 us (0.940)
  starting transfers between devices: 7.66 us -> 5 us
  waiting for transfers between devices: 4.13 us -> 6.07 us
  local copies, waits for them, and re-layouts: 4.14 us -> 2.96 us
  blocking collectives: 14.5 us -> 14 us
    ppermute x7 -> x4, starting transfers between devices: 7.66 us -> 5 us  [the longest x3 4.48 us: local(): come.append(lax.ppermute(both, 'expert', pairs) if j else both)]
    ppermute x7 -> x4, waiting for transfers between devices: 4.13 us -> 6.07 us  [the longest x3 5.1 us: local(): come.append(lax.ppermute(both, 'expert', pairs) if j else both)]
    unnamed x18 -> x20, local copies, waits for them, and re-layouts: 4.14 us -> 2.94 us
    all_to_all x1, blocking collectives: 14.5 us -> 14 us  [local(): lax.all_to_all(back.reshape(n_all, back_rows, half), ('expert', 'hidden')...]
  transfers between devices with their start and end apart: 7 -> 4, of which waited for: 3 -> 4; matrix products, arithmetic and copies ran while one was open for 0% -> 0% of each run, Pallas kernels for 0% -> 0%
where the time goes in v7:
time: 35.9 us; the launch traced here: 35.7 us
  blocking collectives  14 us (39%)
  Pallas kernels  7.57 us (21%)
  waiting for transfers between devices  6.07 us (17%)
  starting transfers between devices  5 us (14%)
  local copies, waits for them, and re-layouts  2.96 us (8%)
    all_to_all x1, blocking collectives, local(): lax.all_to_all(back.reshape(n_all, back_rows, half), ('expert', 'hidden')...  14 us
    ppermute x3, waiting for transfers between devices, local(): come.append(lax.ppermute(both, 'expert', pairs) if j else both)  5.1 us
    ppermute x3, starting transfers between devices, local(): come.append(lax.ppermute(both, 'expert', pairs) if j else both)  4.48 us
    pallas_call x1, Pallas kernels, local(): pl.pallas_call(functools.partial(expert_kernel, images, n_expert, k, gb),...  4.33 us
    unnamed x20, local copies, waits for them, and re-layouts  2.94 us
    pallas_call x1, Pallas kernels, local(): pl.pallas_call(functools.partial(dispatch_kernel, images, quarter, k, gb,...  1.66 us
    pallas_call x1, Pallas kernels, local(): pl.pallas_call(functools.partial(final_kernel, quarter, k, gb), out_shape...  1.58 us
    ppermute x1, waiting for transfers between devices, local(): held.append(lax.ppermute(leave[1], 'expert', pairs))  0.97 us
  transfers between devices with their start and end apart: 4, of which 4 were waited for; matrix products, arithmetic and copies ran while one was open for 0% of the time, Pallas kernels for 0%

profile of v7, /device:TPU:0, one launch (start us, length us, event | category | flops | bytes accessed | tf_op | source)
XLA Modules:
  0.0 35.7 jit_solution(6995516531275472007)
XLA Ops:
  0.0 0.0 copy-start.8
  0.0 0.0 copy-start.1
  0.0 2.0 %copy.11.tok_ref = bf16[4,196,1024]{2,1,0:T(8,128)(2,1)S(1)} copy(bf16[4,196,1024]{2,0,1:T(4,128)(2,1)} %param.10) | data formatting | bytes 3211264 | tf_op args[0]
  2.1 0.0 copy-done.8
  2.1 0.0 copy-start.3
  2.1 0.0 copy-start.5
  2.1 0.5 %copy.12.grad_ref = bf16[4,196,1024]{2,1,0:T(8,128)(2,1)S(1)} copy(bf16[4,196,1024]{2,0,1:T(4,128)(2,1)S(1)} %copy-done.8) | data formatting | bytes 3211264 | tf_op args[6]
  2.6 0.4 %copy-done.3 = bf16[1024,16]{0,1:T(8,128)(2,1)S(1)} copy-done((bf16[1024,16]{0,1:T(8,128)(2,1)S(1)}, bf16[1024,16]{0,1:T(8,128)(2,1)}, u32[]{:S(2)}) %copy-start.3) | copy-done | bytes 32792
  2.9 0.0 copy-done.5
  3.0 0.0 copy-start
  3.0 0.0 copy-start.2
  3.0 0.0 copy-start.7
  3.0 1.7 %dispatch.1 = (bf16[1,16,196]{2,1,0:T(8,128)(2,1)S(1)}, bf16[1,16,196]{2,1,0:T(8,128)(2,1)S(1)}, bf16[1,196,1024]{2,1,0:T(8,128)(2,1)S(1)}, bf16[1,196,1024]{2,1...) custom-call(bf16[4,196,1024]{2,1,0:T(8,128)(2,1)S(1)} %copy.11.tok_ref, ...), custom_call_target="tpu_custom_call" | custom-call | tf_op jit(solution)/shard_map/dispatch/pallas_call | solution.py:190
  4.6 0.5 %collective-permute-start = (bf16[64,1024]{1,0:T(8,128)(2,1)S(1)}, bf16[64,1024]{1,0:T(8,128)(2,1)S(1)}, u32[]{:S(2)}, u32[]{:S(2)}) collective-permute-start(bf16[64,1024]{1,0:T(8,128)(2,1)S(1)} %get-tuple-element.12), channel_id=1, source_target_pairs={{0,4},{4,0},{8,12},{12,8},{16,20},{20,16},{24,28},{28,24},{1,5},{5... | collective-permute-start | bytes 393224 | tf_op jit(solution)/shard_map/ppermute | solution.py:211
  5.2 1.0 %collective-permute-done = bf16[64,1024]{1,0:T(8,128)(2,1)S(1)} collective-permute-done((bf16[64,1024]{1,0:T(8,128)(2,1)S(1)}, bf16[64,1024]{1,0:T(8,128)(2,1)S(1)}, u32[]{:S(2)}, u32[]{:S(2)}) %collective-permute-start) | collective-permute-done | bytes 131104 | tf_op jit(solution)/shard_map/ppermute | solution.py:211
  6.2 2.9 %collective-permute-start.1 = (bf16[32,1024]{1,0:T(8,128)(2,1)S(1)}, bf16[32,1024]{1,0:T(8,128)(2,1)S(1)}, u32[]{:S(2)}, u32[]{:S(2)}) collective-permute-start(bf16[32,1024]{1,0:T(8,128)(2,1)S(1)} %pad_maximum_fusion.1), channel_id=1, source_target_pairs={{0,8},{4,12},{8,0},{12,4},{16,24},{20,28},{24,16},{28,20},{1,9},{5... | collective-permute-start | bytes 196616 | tf_op jit(solution)/shard_map/ppermute | solution.py:216
  9.1 1.5 %collective-permute-start.2 = (bf16[32,1024]{1,0:T(8,128)(2,1)S(1)}, bf16[32,1024]{1,0:T(8,128)(2,1)S(1)}, u32[]{:S(2)}, u32[]{:S(2)}) collective-permute-start(bf16[32,1024]{1,0:T(8,128)(2,1)S(1)} %pad_maximum_fusion.2), channel_id=1, source_target_pairs={{0,16},{4,20},{8,24},{12,28},{16,0},{20,4},{24,8},{28,12},{1,17},{... | collective-permute-start | bytes 196616 | tf_op jit(solution)/shard_map/ppermute | solution.py:216
  10.6 0.1 collective-permute-start.3
  10.7 0.0 copy-start.4
  10.7 0.0 copy-start.6
  10.7 0.8 %collective-permute-done.1.rest_1_ = bf16[32,1024]{1,0:T(8,128)(2,1)S(1)} collective-permute-done((bf16[32,1024]{1,0:T(8,128)(2,1)S(1)}, bf16[32,1024]{1,0:T(8,128)(2,1)S(1)}, u32[]{:S(2)}, u32[]{:S(2)}) %collective-permute-start.1) | collective-permute-done | bytes 65568 | tf_op jit(solution)/shard_map/ppermute | solution.py:216
  11.5 1.9 %collective-permute-done.2.rest_2_ = bf16[32,1024]{1,0:T(8,128)(2,1)S(1)} collective-permute-done((bf16[32,1024]{1,0:T(8,128)(2,1)S(1)}, bf16[32,1024]{1,0:T(8,128)(2,1)S(1)}, u32[]{:S(2)}, u32[]{:S(2)}) %collective-permute-start.2) | collective-permute-done | bytes 65568 | tf_op jit(solution)/shard_map/ppermute | solution.py:216
  13.4 2.4 %collective-permute-done.3.rest_3_ = bf16[32,1024]{1,0:T(8,128)(2,1)S(1)} collective-permute-done((bf16[32,1024]{1,0:T(8,128)(2,1)S(1)}, bf16[32,1024]{1,0:T(8,128)(2,1)S(1)}, u32[]{:S(2)}, u32[]{:S(2)}) %collective-permute-start.3) | collective-permute-done | bytes 65568 | tf_op jit(solution)/shard_map/ppermute | solution.py:216
  15.8 0.0 copy-done.1
  15.8 0.0 copy-done
  15.8 0.0 copy-done.2
  15.8 0.0 copy-done.7
  15.8 4.3 %experts.1 = bf16[256,512]{1,0:T(8,128)(2,1)S(1)} custom-call(bf16[2,1024,1024]{2,1,0:T(8,128)(2,1)S(1)} %copy-done, f32[2,1024]{1,0:T(2,128)S(1)} %copy-done.7, bf16[2,1024,1024]{2,1,0:T(8,128)(2,1)S(1)} %copy-done.1, bf16[256,256]{1,0:T(8,128)(2,1)S(1)} %copy-done.2, bf16[32,1024]{1,0:T(8,128)(2,1)S(1)} %pad_maximum_fusion.rest_0_, ...), custom_call_target="tpu_custom_call" | custom-call | tf_op jit(solution)/shard_map/experts/pallas_call | solution.py:222
  20.1 14.0 %all_to_all.5 = bf16[32,8,512]{2,1,0:T(8,128)(2,1)S(1)} all-to-all(bf16[32,8,512]{2,1,0:T(8,128)(2,1)S(1)} %bitcast.4), channel_id=1, replica_groups=mesh['expert'=8,'hidden'=4] {'expert','hidden'}, dimensions={0} | all-to-all | bytes 524288 | tf_op jit(solution)/shard_map/all_to_all | solution.py:232
  34.1 0.0 copy-done.4
  34.1 0.0 copy-done.6
  34.1 1.6 %tokens_back.1 = bf16[1,196,1024]{2,1,0:T(8,128)(2,1)} custom-call(bf16[256,512]{1,0:T(8,128)(2,1)S(1)} %bitcast.3, f32[16,1024]{1,0:T(8,128)S(1)} %copy-done.4, bf16[1,196,1024]{2,1,0:T(8,128)(2,1)S(1)} %get-tuple-element.13.tok_ref, bf16[1,196,1024]{2,1,0:T(8,128)(2,1)S(1)} %get-tuple-element.14.grad_ref, ...), custom_call_target="tpu_custom_call" | custom-call | tf_op jit(solution)/shard_map/tokens_back/pallas_call | solution.py:243
  (6 shorter events, 0.0 us)
Async XLA Ops:
  0.0 2.1 %copy-start.8 = (bf16[4,196,1024]{2,0,1:T(4,128)(2,1)S(1)}, bf16[4,196,1024]{2,0,1:T(4,128)(2,1)}, u32[]{:S(2)}) copy-start(bf16[4,196,1024]{2,0,1:T(4,128)(2,1)} %param.16) | copy-start | bytes 4816900
  0.0 15.8 %copy-start.1 = (bf16[2,1024,1024]{2,1,0:T(8,128)(2,1)S(1)}, bf16[2,1024,1024]{2,1,0:T(8,128)(2,1)}, u32[]{:S(2)}) copy-start(bf16[2,1024,1024]{2,1,0:T(8,128)(2,1)} %wout_ref.1) | copy-start | bytes 12582916
  2.1 0.9 %copy-start.3 = (bf16[1024,16]{0,1:T(8,128)(2,1)S(1)}, bf16[1024,16]{0,1:T(8,128)(2,1)}, u32[]{:S(2)}) copy-start(bf16[1024,16]{0,1:T(8,128)(2,1)} %param.11) | copy-start | bytes 98308
  2.1 0.9 %copy-start.5 = (bf16[128,128]{1,0:T(8,128)(2,1)S(1)}, bf16[128,128]{1,0:T(8,128)(2,1)}, u32[]{:S(2)}) copy-start(bf16[128,128]{1,0:T(8,128)(2,1)} %constant.6.clone.perm_ref) | copy-start | bytes 98308
  3.0 12.8 %copy-start = (bf16[2,1024,1024]{2,1,0:T(8,128)(2,1)S(1)}, bf16[2,1024,1024]{2,1,0:T(8,128)(2,1)}, u32[]{:S(2)}) copy-start(bf16[2,1024,1024]{2,1,0:T(8,128)(2,1)} %win_ref.1) | copy-start | bytes 12582916
  3.0 12.8 %copy-start.2 = (bf16[256,256]{1,0:T(8,128)(2,1)S(1)}, bf16[256,256]{1,0:T(8,128)(2,1)}, u32[]{:S(2)}) copy-start(bf16[256,256]{1,0:T(8,128)(2,1)} %constant.7.clone.t_ref) | copy-start | bytes 393220
  3.0 12.8 %copy-start.7 = (f32[2,1024]{1,0:T(2,128)S(1)}, f32[2,1024]{1,0:T(2,128)}, u32[]{:S(2)}) copy-start(f32[2,1024]{1,0:T(2,128)} %bin_ref.1) | copy-start | bytes 24580
  4.6 1.5 %collective-permute-start = (bf16[64,1024]{1,0:T(8,128)(2,1)S(1)}, bf16[64,1024]{1,0:T(8,128)(2,1)S(1)}, u32[]{:S(2)}, u32[]{:S(2)}) collective-permute-start(bf16[64,1024]{1,0:T(8,128)(2,1)S(1)} %get-tuple-element.12), channel_id=1, source_target_pairs={{0,4},{4,0},{8,12},{12,8},{16,20},{20,16},{24,28},{28,24},{1,5},{5... | collective-permute-start | bytes 393224 | tf_op jit(solution)/shard_map/ppermute | solution.py:211
  6.2 5.3 %collective-permute-start.1 = (bf16[32,1024]{1,0:T(8,128)(2,1)S(1)}, bf16[32,1024]{1,0:T(8,128)(2,1)S(1)}, u32[]{:S(2)}, u32[]{:S(2)}) collective-permute-start(bf16[32,1024]{1,0:T(8,128)(2,1)S(1)} %pad_maximum_fusion.1), channel_id=1, source_target_pairs={{0,8},{4,12},{8,0},{12,4},{16,24},{20,28},{24,16},{28,20},{1,9},{5... | collective-permute-start | bytes 196616 | tf_op jit(solution)/shard_map/ppermute | solution.py:216
  9.1 4.3 %collective-permute-start.2 = (bf16[32,1024]{1,0:T(8,128)(2,1)S(1)}, bf16[32,1024]{1,0:T(8,128)(2,1)S(1)}, u32[]{:S(2)}, u32[]{:S(2)}) collective-permute-start(bf16[32,1024]{1,0:T(8,128)(2,1)S(1)} %pad_maximum_fusion.2), channel_id=1, source_target_pairs={{0,16},{4,20},{8,24},{12,28},{16,0},{20,4},{24,8},{28,12},{1,17},{... | collective-permute-start | bytes 196616 | tf_op jit(solution)/shard_map/ppermute | solution.py:216
  10.6 5.2 %collective-permute-start.3 = (bf16[32,1024]{1,0:T(8,128)(2,1)S(1)}, bf16[32,1024]{1,0:T(8,128)(2,1)S(1)}, u32[]{:S(2)}, u32[]{:S(2)}) collective-permute-start(bf16[32,1024]{1,0:T(8,128)(2,1)S(1)} %pad_maximum_fusion.3), channel_id=1, source_target_pairs={{0,24},{4,28},{8,16},{12,20},{16,8},{20,12},{24,0},{28,4},{1,25},{... | collective-permute-start | bytes 196616 | tf_op jit(solution)/shard_map/ppermute | solution.py:216
  10.7 23.4 %copy-start.4 = (f32[16,1024]{1,0:T(8,128)S(1)}, f32[16,1024]{1,0:T(8,128)}, u32[]{:S(2)}) copy-start(f32[16,1024]{1,0:T(8,128)} %bias_ref.1) | copy-start | bytes 196612
  10.7 23.4 %copy-start.6 = (bf16[64,256]{1,0:T(8,128)(2,1)S(1)}, bf16[64,256]{1,0:T(8,128)(2,1)}, u32[]{:S(2)}) copy-start(bf16[64,256]{1,0:T(8,128)(2,1)} %constant.8.clone.sel_ref) | copy-start | bytes 98308

commit v8 on v7

--- a/solution.py
+++ b/solution.py
@@ -12,6 +12,7 @@
 F32 = jnp.float32
 NN = (((1,), (0,)), ((), ()))
 NT = (((1,), (1,)), ((), ()))
+DISPATCH_VMEM = 16
 
 
 def mm(a, b, dims=NN):
@@ -43,35 +44,120 @@
     return lax.div(me, inner), lax.rem(me, inner)
 
 
+def softmax_rows(logits):
+    e = jnp.exp(logits - jnp.max(logits, axis=0, keepdims=True))
+    return e / jnp.sum(e, axis=0, keepdims=True)
+
+
+def across_class(x, combine, group):
+    shift = group
+    while shift < 128:
+        x = combine(x, pltpu.roll(x, shift, 1))
+        shift *= 2
+    return x
+
+
 def dispatch_kernel(
-    images, quarter, k, gb, n_expert, tok_ref, grad_ref, keys_ref, perm_ref,
-    disp_ref, comb_ref, my_tok_ref, my_grad_ref, *rest,
+    images, quarter, k, gb, n_expert, tok_hbm, grad_hbm, keys_hbm, perm_hbm, first_ref, *rest
 ):
     outer, inner = levels(n_expert)
     leave_refs = rest[:inner]
-    send_ref, disp_all, comb_all = rest[inner:]
+    tok_ref, grad_ref, keys_ref, perm_ref, send_ref, sems = rest[inner:]
+    positions, _, lanes = tok_hbm.shape
+    padded, group, part = tok_ref.shape
+    first_ref[0] = lax.axis_index("hidden") * quarter
+    if padded > positions:
+        for ref in (tok_ref, grad_ref):
+            ref[positions:] = jnp.zeros((padded - positions, group, part), BF)
+    copies = [pltpu.make_async_copy(keys_hbm, keys_ref, sems.at[0])]
+    for i, (hbm, ref) in enumerate(((tok_hbm, tok_ref), (grad_hbm, grad_ref))):
+        for j in range(part // lanes):
+            copies.append(
+                pltpu.make_async_copy(
+                    hbm.at[:, j * group : (j + 1) * group],
+                    ref.at[:positions, :, j * lanes : (j + 1) * lanes],
+                    sems.at[1 + i],
+                )
+            )
+    copies.append(pltpu.make_async_copy(perm_hbm, perm_ref, sems.at[3]))
+    for copy in copies:
+        copy.start()
+    blocks = part // lanes
+    rows = padded * group
     slots = keys_ref.shape[0]
+    halves = group // images
+    lane = lax.broadcasted_iota(jnp.int32, (1, rows), 1)
+    which = lax.rem(lane, group)
+    for copy in copies[: 1 + blocks]:
+        copy.wait()
     keys = keys_ref[...]
-    slot_rows = [[], []]
-    for b in range(images):
-        tok = tok_ref[b]
-        logits = mm(keys, tok, NT)
-        e = jnp.exp(logits - jnp.max(logits, axis=1, keepdims=True))
-        disp = (e / jnp.sum(e, axis=1, keepdims=True)).astype(BF)
-        e = jnp.exp(logits - jnp.max(logits, axis=0, keepdims=True))
-        comb = (e / jnp.sum(e, axis=0, keepdims=True)).astype(BF)
-        disp_all[b] = disp
-        comb_all[b] = comb
-        slot_rows[0].append(mm(disp, tok).astype(BF))
-        slot_rows[1].append(mm(comb, grad_ref[b]).astype(BF))
+    tok = tok_ref[...].reshape(rows, part)
+    split = jnp.concatenate(
+        [
+            jnp.concatenate(
+                [
+                    keys[:, (j * halves + h) * lanes : (j * halves + h + 1) * lanes]
+                    for j in range(blocks)
+                ],
+                axis=1,
+            )
+            for h in range(halves)
+        ],
+        axis=0,
+    )
+    each = mm(split, tok, NT)
+    partial = each[:slots]
+    for h in range(1, halves):
+        partial = jnp.where(which < h * images, partial, each[h * slots : (h + 1) * slots])
+    logits = partial
+    for h in range(1, halves):
+        ahead = pltpu.roll(partial, rows - h * images, 1)
+        behind = pltpu.roll(partial, group - h * images, 1)
+        logits = logits + jnp.where(which < (halves - h) * images, ahead, behind)
+    tiles = rows // 128
+    valid = lane < positions * group
+    top = jnp.where(valid, logits, -jnp.inf)
+    best = functools.reduce(jnp.maximum, [top[:, i * 128 : (i + 1) * 128] for i in range(tiles)])
+    best = across_class(best, jnp.maximum, group)
+    e = jnp.exp(top - jnp.concatenate([best] * tiles, axis=1))
+    total = functools.reduce(jnp.add, [e[:, i * 128 : (i + 1) * 128] for i in range(tiles)])
+    total = across_class(total, jnp.add, group)
+    disp = e / jnp.concatenate([total] * tiles, axis=1)
+    comb = jnp.where(valid, softmax_rows(logits), 0.0)
+
+    def slot_sums(weights, x):
+        wide = jnp.concatenate(
+            [jnp.where(which == i, weights, 0.0) for i in range(group)], axis=0
+        ).astype(BF)
+        out = mm(wide, x).astype(BF)
+        per = images * slots
+        return jnp.concatenate(
+            [
+                out[h * per : (h + 1) * per, j * lanes : (j + 1) * lanes]
+                for j in range(blocks)
+                for h in range(halves)
+            ],
+            axis=1,
+        )
+
+    sums = [slot_sums(disp, tok)]
+    for copy in copies[1 + blocks : 1 + 2 * blocks]:
+        copy.wait()
+    sums.append(slot_sums(comb, grad_ref[...].reshape(rows, part)))
+    copies[-1].wait()
     perm = perm_ref[...]
     step = gb * k
-    rows = perm.shape[0]
+    count = perm.shape[0]
     for i in range(slots // step):
         block = jnp.concatenate(
-            [r[i * step : (i + 1) * step] for kind in slot_rows for r in kind], axis=0
+            [
+                r[b * slots + i * step : b * slots + (i + 1) * step]
+                for r in sums
+                for b in range(images)
+            ],
+            axis=0,
         )
-        send_ref[i * rows : (i + 1) * rows] = mm(perm, block).astype(BF)
+        send_ref[i * count : (i + 1) * count] = mm(perm, block).astype(BF)
     block = send_ref.shape[0] // n_expert
     c, l = position(inner)
     for i in range(inner):
@@ -80,12 +166,15 @@
             leave_refs[i][j * block : (j + 1) * block] = send_ref[
                 pl.ds(pl.multiple_of(to * block, block), block)
             ]
-    first = lax.axis_index("hidden") * quarter
-    for m in range(quarter):
-        disp_ref[m] = disp_all[first + m]
-        comb_ref[m] = comb_all[first + m]
-        my_tok_ref[m] = tok_ref[first + m]
-        my_grad_ref[m] = grad_ref[first + m]
+
+
+def own_kernel(tok_ref, keys_ref, disp_ref, comb_ref):
+    keys = keys_ref[...]
+    for m in range(tok_ref.shape[0]):
+        logits = mm(keys, tok_ref[m], NT)
+        e = jnp.exp(logits - jnp.max(logits, axis=1, keepdims=True))
+        disp_ref[m] = (e / jnp.sum(e, axis=1, keepdims=True)).astype(BF)
+        comb_ref[m] = softmax_rows(logits).astype(BF)
 
 
 def expert_kernel(images, n_expert, k, gb, win_ref, bin_ref, wout_ref, t_ref, *rest):
@@ -187,33 +276,65 @@
     perm = one_hot_rows(order, order.size)
     send_rows = 2 * k * images
     outer, inner = levels(n_expert)
-    disp, comb, my_tok, my_grad, *leave = pl.pallas_call(
+    hbm = pl.BlockSpec(memory_space=pltpu.HBM)
+    smem = pl.BlockSpec(memory_space=pltpu.SMEM)
+    group = 8
+    lanes = 128
+    part = width * images // group
+    padded = -(-positions * group // 128) * 128 // group
+
+    def in_hbm(x):
+        return pltpu.with_memory_space_constraint(x, pltpu.HBM)
+
+    def as_it_lies(x):
+        x = x.transpose(1, 0, 2).reshape(positions, images, width // lanes, lanes)
+        x = x.transpose(0, 2, 1, 3).reshape(positions, width // lanes * images, lanes)
+        return in_hbm(x)
+
+    first, *leave = pl.pallas_call(
         functools.partial(dispatch_kernel, images, quarter, k, gb, n_expert),
-        out_shape=(
-            jax.ShapeDtypeStruct((quarter, slots, positions), BF),
-            jax.ShapeDtypeStruct((quarter, slots, positions), BF),
-            jax.ShapeDtypeStruct((quarter, positions, width), BF),
-            jax.ShapeDtypeStruct((quarter, positions, width), BF),
-        )
+        out_shape=(jax.ShapeDtypeStruct((1,), jnp.int32),)
         + (jax.ShapeDtypeStruct((outer * send_rows, width), BF),) * inner,
-        in_specs=[vmem] * 4,
-        out_specs=(vmem,) * (4 + inner),
-        scratch_shapes=[pltpu.VMEM((n_expert * send_rows, width), BF)]
-        + [pltpu.VMEM((images, slots, positions), BF)] * 2,
-        compiler_params=pltpu.CompilerParams(vmem_limit_bytes=12 << 20),
+        in_specs=[hbm] * 4,
+        out_specs=(smem,) + (vmem,) * inner,
+        scratch_shapes=[pltpu.VMEM((padded, group, part), BF)] * 2
+        + [
+            pltpu.VMEM(keys.shape, BF),
+            pltpu.VMEM(perm.shape, BF),
+            pltpu.VMEM((n_expert * send_rows, width), BF),
+            pltpu.SemaphoreType.DMA((4,)),
+        ],
+        compiler_params=pltpu.CompilerParams(vmem_limit_bytes=DISPATCH_VMEM << 20),
         name="dispatch",
-    )(tokens, out_grad, keys, perm)
+    )(as_it_lies(tokens), as_it_lies(out_grad), in_hbm(keys), in_hbm(jnp.asarray(perm)))
 
     everyone = [(c, l) for c in range(outer) for l in range(inner)]
     held = leave[:1]
     if inner == 2:
         pairs = [(c * inner + l, c * inner + 1 - l) for c, l in everyone]
         held.append(lax.ppermute(leave[1], "expert", pairs))
-    come = []
-    for j in range(outer):
-        both = jnp.concatenate([r[j * send_rows : (j + 1) * send_rows] for r in held])
+    both = [
+        jnp.concatenate([r[j * send_rows : (j + 1) * send_rows] for r in held])
+        for j in range(outer)
+    ]
+    *both, first = lax.optimization_barrier((*both, first))
+    come = both[:1]
+    for j in range(1, outer):
         pairs = [(c * inner + l, partner(c, j, outer) * inner + l) for c, l in everyone]
-        come.append(lax.ppermute(both, "expert", pairs) if j else both)
+        come.append(lax.ppermute(both[j], "expert", pairs))
+
+    mine = functools.partial(
+        lax.dynamic_slice_in_dim, start_index=first[0], slice_size=quarter, axis=0
+    )
+    my_tok, my_grad = mine(tokens), mine(out_grad)
+    disp, comb = pl.pallas_call(
+        own_kernel,
+        out_shape=(jax.ShapeDtypeStruct((quarter, slots, positions), BF),) * 2,
+        in_specs=[vmem] * 2,
+        out_specs=(vmem,) * 2,
+        compiler_params=pltpu.CompilerParams(vmem_limit_bytes=8 << 20),
+        name="own_softmax",
+    )(my_tok, keys)
 
     order = np.arange(2 * k * 2 * gb * images).reshape(2, 2, gb, k, n_hidden, quarter)
     order = order.transpose(2, 4, 0, 3, 5, 1)

time: 35.9 us -> 38.6 us (1.075)
  blocking collectives: 14 us -> 0 us
  waiting for transfers between devices: 6.07 us -> 12.2 us
  starting transfers between devices: 5 us -> 8.95 us
  Pallas kernels: 7.57 us -> 11.2 us
  between operations: 0.1 us -> 1.82 us
  local copies, waits for them, and re-layouts: 2.96 us -> 4.16 us
    all_to_all x1 -> x0, blocking collectives: 14 us -> none  [local(): lax.all_to_all(back.reshape(n_all, back_rows, half), ('expert', 'hidden')...]
    all_to_all x0 -> x1, waiting for transfers between devices: none -> 6.11 us  [local(): lax.all_to_all(back.reshape(n_all, back_rows, half), ('expert', 'hidden')...]
    all_to_all x0 -> x1, starting transfers between devices: none -> 3.97 us  [local(): lax.all_to_all(back.reshape(n_all, back_rows, half), ('expert', 'hidden')...]
    pallas_call x1, Pallas kernels: 1.66 us -> 4.22 us  [local(): pl.pallas_call(functools.partial(dispatch_kernel, images, quarter, k, gb,...]
    dynamic_slice x0 -> x2, local copies, waits for them, and re-layouts: none -> 1.67 us  [local(): my_tok, my_grad = (mine(tokens), mine(out_grad))]
    pallas_call x1, Pallas kernels: 4.33 us -> 5.04 us  [local(): pl.pallas_call(functools.partial(expert_kernel, images, n_expert, k, gb),...]
    unnamed x20, local copies, waits for them, and re-layouts: 2.94 us -> 2.48 us
    pallas_call x0 -> x1, Pallas kernels: none -> 0.39 us  [local(): pl.pallas_call(own_kernel, out_shape=(jax.ShapeDtypeStruct((quarter, slot...]
  transfers between devices with their start and end apart: 4 -> 5, of which waited for: 4 -> 5; matrix products, arithmetic and copies ran while one was open for 0% -> 5% of each run, Pallas kernels for 0% -> 1%
where the time goes in v8:
time: 38.6 us; the launch traced here: 38.4 us
  waiting for transfers between devices  12.2 us (32%)
  Pallas kernels  11.2 us (29%)
  starting transfers between devices  8.95 us (23%)
  local copies, waits for them, and re-layouts  4.16 us (11%)
  between operations  1.82 us (5%)
    all_to_all x1, waiting for transfers between devices, local(): lax.all_to_all(back.reshape(n_all, back_rows, half), ('expert', 'hidden')...  6.11 us
    ppermute x3, waiting for transfers between devices, local(): come.append(lax.ppermute(both[j], 'expert', pairs))  5.14 us
    pallas_call x1, Pallas kernels, local(): pl.pallas_call(functools.partial(expert_kernel, images, n_expert, k, gb),...  5.04 us
    ppermute x3, starting transfers between devices, local(): come.append(lax.ppermute(both[j], 'expert', pairs))  4.45 us
    pallas_call x1, Pallas kernels, local(): pl.pallas_call(functools.partial(dispatch_kernel, images, quarter, k, gb,...  4.22 us
    all_to_all x1, starting transfers between devices, local(): lax.all_to_all(back.reshape(n_all, back_rows, half), ('expert', 'hidden')...  3.97 us
    unnamed x20, local copies, waits for them, and re-layouts  2.48 us
    dynamic_slice x2, local copies, waits for them, and re-layouts, local(): my_tok, my_grad = (mine(tokens), mine(out_grad))  1.67 us
  transfers between devices with their start and end apart: 5, of which 5 were waited for; matrix products, arithmetic and copies ran while one was open for 5% of the time, Pallas kernels for 1%

profile of v8, /device:TPU:0, one launch (start us, length us, event | category | flops | bytes accessed | tf_op | source)
XLA Modules:
  0.0 38.4 jit_solution(6871469527670074795)
XLA Ops:
  0.0 0.0 copy-start
  0.0 0.0 copy-start.3
  0.0 0.0 copy-start.6
  0.0 4.2 %dispatch.1 = (s32[1]{0:T(128)}, bf16[64,1024]{1,0:T(8,128)(2,1)S(1)}, bf16[64,1024]{1,0:T(8,128)(2,1)S(1)}) custom-call(bf16[196,32,128]{2,1,0:T(8,128)(2,1)} %bitcast.23, bf16[196,32,128]{2,1,0:T(8,128)(2,1)} %bitcast.22, bf16[16,1024]{1,0:T(8,128)(2,1)} %bitcast.19, bf16[128,128]{1,0:T(8,128)(2,1)} %constant.10.clone.perm_hbm), custom_call_target="tpu_custom_call" | custom-call | tf_op jit(solution)/shard_map/dispatch/pallas_call | solution.py:294
  4.2 0.5 %collective-permute-start = (bf16[64,1024]{1,0:T(8,128)(2,1)S(1)}, bf16[64,1024]{1,0:T(8,128)(2,1)S(1)}, u32[]{:S(2)}, u32[]{:S(2)}) collective-permute-start(bf16[64,1024]{1,0:T(8,128)(2,1)S(1)} %get-tuple-element.16), channel_id=1, source_target_pairs={{0,4},{4,0},{8,12},{12,8},{16,20},{20,16},{24,28},{28,24},{1,5},{5... | collective-permute-start | bytes 393224 | tf_op jit(solution)/shard_map/ppermute | solution.py:315
  4.8 1.0 %collective-permute-done = bf16[64,1024]{1,0:T(8,128)(2,1)S(1)} collective-permute-done((bf16[64,1024]{1,0:T(8,128)(2,1)S(1)}, bf16[64,1024]{1,0:T(8,128)(2,1)S(1)}, u32[]{:S(2)}, u32[]{:S(2)}) %collective-permute-start) | collective-permute-done | bytes 131104 | tf_op jit(solution)/shard_map/ppermute | solution.py:315
  5.8 2.9 %collective-permute-start.1 = (bf16[32,1024]{1,0:T(8,128)(2,1)S(1)}, bf16[32,1024]{1,0:T(8,128)(2,1)S(1)}, u32[]{:S(2)}, u32[]{:S(2)}) collective-permute-start(bf16[32,1024]{1,0:T(8,128)(2,1)S(1)} %get-tuple-element.19), channel_id=1, source_target_pairs={{0,8},{4,12},{8,0},{12,4},{16,24},{20,28},{24,16},{28,20},{1,9},{5... | collective-permute-start | bytes 196616 | tf_op jit(solution)/shard_map/ppermute | solution.py:324
  8.7 1.5 %collective-permute-start.2 = (bf16[32,1024]{1,0:T(8,128)(2,1)S(1)}, bf16[32,1024]{1,0:T(8,128)(2,1)S(1)}, u32[]{:S(2)}, u32[]{:S(2)}) collective-permute-start(bf16[32,1024]{1,0:T(8,128)(2,1)S(1)} %get-tuple-element.20), channel_id=1, source_target_pairs={{0,16},{4,20},{8,24},{12,28},{16,0},{20,4},{24,8},{28,12},{1,17},{... | collective-permute-start | bytes 196616 | tf_op jit(solution)/shard_map/ppermute | solution.py:324
  10.2 0.0 collective-permute-start.3
  10.3 0.9 %collective-permute-done.1.rest_1_ = bf16[32,1024]{1,0:T(8,128)(2,1)S(1)} collective-permute-done((bf16[32,1024]{1,0:T(8,128)(2,1)S(1)}, bf16[32,1024]{1,0:T(8,128)(2,1)S(1)}, u32[]{:S(2)}, u32[]{:S(2)}) %collective-permute-start.1) | collective-permute-done | bytes 65568 | tf_op jit(solution)/shard_map/ppermute | solution.py:324
  11.1 1.9 %collective-permute-done.2.rest_2_ = bf16[32,1024]{1,0:T(8,128)(2,1)S(1)} collective-permute-done((bf16[32,1024]{1,0:T(8,128)(2,1)S(1)}, bf16[32,1024]{1,0:T(8,128)(2,1)S(1)}, u32[]{:S(2)}, u32[]{:S(2)}) %collective-permute-start.2) | collective-permute-done | bytes 65568 | tf_op jit(solution)/shard_map/ppermute | solution.py:324
  13.0 2.4 %collective-permute-done.3.rest_3_ = bf16[32,1024]{1,0:T(8,128)(2,1)S(1)} collective-permute-done((bf16[32,1024]{1,0:T(8,128)(2,1)S(1)}, bf16[32,1024]{1,0:T(8,128)(2,1)S(1)}, u32[]{:S(2)}, u32[]{:S(2)}) %collective-permute-start.3) | collective-permute-done | bytes 65568 | tf_op jit(solution)/shard_map/ppermute | solution.py:324
  15.4 0.0 copy-done
  15.4 0.0 copy-done.3
  15.4 0.0 copy-done.6
  15.4 0.0 copy-start.1
  15.4 2.2 %copy-done.1 = bf16[2,1024,1024]{2,1,0:T(8,128)(2,1)S(1)} copy-done((bf16[2,1024,1024]{2,1,0:T(8,128)(2,1)S(1)}, bf16[2,1024,1024]{2,1,0:T(8,128)(2,1)}, u32[]{:S(2)}) %copy-start.1) | copy-done | bytes 4194328
  17.6 0.0 copy-start.7
  17.6 5.0 %experts.1 = bf16[256,512]{1,0:T(8,128)(2,1)} custom-call(bf16[2,1024,1024]{2,1,0:T(8,128)(2,1)S(1)} %copy-done, f32[2,1024]{1,0:T(2,128)S(1)} %copy-done.6, bf16[2,1024,1024]{2,1,0:T(8,128)(2,1)S(1)} %copy-done.1, bf16[256,256]{1,0:T(8,128)(2,1)S(1)} %copy-done.3, bf16[32,1024]{1,0:T(8,128)(2,1)S(1)} %get-tuple-element.18.rest_0_, ...), custom_call_target="tpu_custom_call" | custom-call | tf_op jit(solution)/shard_map/experts/pallas_call | solution.py:343
  22.6 0.0 copy-start.8
  22.6 4.0 %all-to-all-start = ((bf16[32,8,512]{2,1,0:T(8,128)(2,1)}), bf16[32,8,512]{2,1,0:T(8,128)(2,1)S(1)}, u32[]{:S(2)}, u32[]{:S(2)}) async-start(bf16[32,8,512]{2,1,0:T(8,128)(2,1)} %bitcast.9), calls=%async_computation | async-start | bytes 524288 | tf_op jit(solution)/shard_map/all_to_all | solution.py:353
  28.3 0.0 copy-done.7
  28.3 0.8 %constant_dynamic-slice_fusion = bf16[1,196,1024]{2,0,1:T(2,128)(2,1)S(1)} fusion(bf16[4,196,1024]{2,0,1:T(4,128)(2,1)S(1)} %copy-done.7, s32[]{:T(128)S(6)} %select_n.4), kind=kLoop, calls=%fused_computation.4 | loop fusion | bytes 802820 | tf_op jit(solution)/shard_map/dynamic_slice | solution.py:329
  29.1 0.1 copy.16.grad_ref
  29.3 0.0 copy-done.8
  29.3 0.0 copy-start.2
  29.3 0.0 copy-start.4
  29.3 0.0 copy-start.5
  29.3 0.8 %constant_dynamic-slice_fusion.1 = bf16[1,196,1024]{2,0,1:T(2,128)(2,1)S(1)} fusion(bf16[4,196,1024]{2,0,1:T(4,128)(2,1)S(1)} %copy-done.8, s32[]{:T(128)S(6)} %select_n.4), kind=kLoop, calls=%fused_computation.5 | loop fusion | bytes 802820 | tf_op jit(solution)/shard_map/dynamic_slice | solution.py:329
  30.2 0.1 copy.15.tok_ref
  30.3 0.0 copy-done.2
  30.3 0.4 %own_softmax.1 = (bf16[1,16,196]{2,1,0:T(8,128)(2,1)S(1)}, bf16[1,16,196]{2,1,0:T(8,128)(2,1)S(1)}) custom-call(bf16[1,196,1024]{2,1,0:T(8,128)(2,1)S(1)} %copy.15.tok_ref, bf16[16,1024]{1,0:T(8,128)(2,1)S(1)} %bitcast.20), custom_call_target="tpu_custom_call" | custom-call | tf_op jit(solution)/shard_map/own_softmax/pallas_call | solution.py:330
  30.7 6.1 %all-to-all-done = bf16[32,8,512]{2,1,0:T(8,128)(2,1)S(1)} async-done(((bf16[32,8,512]{2,1,0:T(8,128)(2,1)}), bf16[32,8,512]{2,1,0:T(8,128)(2,1)S(1)}, u32[]{:S(2)}, u32[]{:S(2)}) %all-to-all-start) | async-done | bytes 262176 | tf_op jit(solution)/shard_map/all_to_all | solution.py:353
  36.8 0.0 copy-done.4
  36.8 0.0 copy-done.5
  36.8 1.6 %tokens_back.1 = bf16[1,196,1024]{2,1,0:T(8,128)(2,1)} custom-call(bf16[256,512]{1,0:T(8,128)(2,1)S(1)} %bitcast.18, f32[16,1024]{1,0:T(8,128)S(1)} %copy-done.4, bf16[1,196,1024]{2,1,0:T(8,128)(2,1)S(1)} %copy.15.tok_ref, bf16[1,196,1024]{2,1,0:T(8,128)(2,1)S(1)} %copy.16.grad_ref, bf16[1,16,196]{2,1,0:T(8,128)(2,1)S(1)} %get-tuple-element.23.disp_ref, ...), custom_call_target="tpu_custom_call" | custom-call | tf_op jit(solution)/shard_map/tokens_back/pallas_call | solution.py:364
  (4 shorter events, 0.0 us)
Async XLA Ops:
  0.0 15.4 %copy-start = (bf16[2,1024,1024]{2,1,0:T(8,128)(2,1)S(1)}, bf16[2,1024,1024]{2,1,0:T(8,128)(2,1)}, u32[]{:S(2)}) copy-start(bf16[2,1024,1024]{2,1,0:T(8,128)(2,1)} %win_ref.1) | copy-start | bytes 12582916
  0.0 15.4 %copy-start.3 = (bf16[256,256]{1,0:T(8,128)(2,1)S(1)}, bf16[256,256]{1,0:T(8,128)(2,1)}, u32[]{:S(2)}) copy-start(bf16[256,256]{1,0:T(8,128)(2,1)} %constant.11.clone.t_ref) | copy-start | bytes 393220
  0.0 15.4 %copy-start.6 = (f32[2,1024]{1,0:T(2,128)S(1)}, f32[2,1024]{1,0:T(2,128)}, u32[]{:S(2)}) copy-start(f32[2,1024]{1,0:T(2,128)} %bin_ref.1) | copy-start | bytes 24580
  4.2 1.5 %collective-permute-start = (bf16[64,1024]{1,0:T(8,128)(2,1)S(1)}, bf16[64,1024]{1,0:T(8,128)(2,1)S(1)}, u32[]{:S(2)}, u32[]{:S(2)}) collective-permute-start(bf16[64,1024]{1,0:T(8,128)(2,1)S(1)} %get-tuple-element.16), channel_id=1, source_target_pairs={{0,4},{4,0},{8,12},{12,8},{16,20},{20,16},{24,28},{28,24},{1,5},{5... | collective-permute-start | bytes 393224 | tf_op jit(solution)/shard_map/ppermute | solution.py:315
  5.8 5.3 %collective-permute-start.1 = (bf16[32,1024]{1,0:T(8,128)(2,1)S(1)}, bf16[32,1024]{1,0:T(8,128)(2,1)S(1)}, u32[]{:S(2)}, u32[]{:S(2)}) collective-permute-start(bf16[32,1024]{1,0:T(8,128)(2,1)S(1)} %get-tuple-element.19), channel_id=1, source_target_pairs={{0,8},{4,12},{8,0},{12,4},{16,24},{20,28},{24,16},{28,20},{1,9},{5... | collective-permute-start | bytes 196616 | tf_op jit(solution)/shard_map/ppermute | solution.py:324
  8.7 4.3 %collective-permute-start.2 = (bf16[32,1024]{1,0:T(8,128)(2,1)S(1)}, bf16[32,1024]{1,0:T(8,128)(2,1)S(1)}, u32[]{:S(2)}, u32[]{:S(2)}) collective-permute-start(bf16[32,1024]{1,0:T(8,128)(2,1)S(1)} %get-tuple-element.20), channel_id=1, source_target_pairs={{0,16},{4,20},{8,24},{12,28},{16,0},{20,4},{24,8},{28,12},{1,17},{... | collective-permute-start | bytes 196616 | tf_op jit(solution)/shard_map/ppermute | solution.py:324
  10.2 5.2 %collective-permute-start.3 = (bf16[32,1024]{1,0:T(8,128)(2,1)S(1)}, bf16[32,1024]{1,0:T(8,128)(2,1)S(1)}, u32[]{:S(2)}, u32[]{:S(2)}) collective-permute-start(bf16[32,1024]{1,0:T(8,128)(2,1)S(1)} %get-tuple-element.21), channel_id=1, source_target_pairs={{0,24},{4,28},{8,16},{12,20},{16,8},{20,12},{24,0},{28,4},{1,25},{... | collective-permute-start | bytes 196616 | tf_op jit(solution)/shard_map/ppermute | solution.py:324
  15.4 2.2 %copy-start.1 = (bf16[2,1024,1024]{2,1,0:T(8,128)(2,1)S(1)}, bf16[2,1024,1024]{2,1,0:T(8,128)(2,1)}, u32[]{:S(2)}) copy-start(bf16[2,1024,1024]{2,1,0:T(8,128)(2,1)} %wout_ref.1) | copy-start | bytes 12582916
  17.6 10.7 %copy-start.7 = (bf16[4,196,1024]{2,0,1:T(4,128)(2,1)S(1)}, bf16[4,196,1024]{2,0,1:T(4,128)(2,1)}, u32[]{:S(2)}) copy-start(bf16[4,196,1024]{2,0,1:T(4,128)(2,1)} %param.16) | copy-start | bytes 4816900
  22.6 6.6 %copy-start.8 = (bf16[4,196,1024]{2,0,1:T(4,128)(2,1)S(1)}, bf16[4,196,1024]{2,0,1:T(4,128)(2,1)}, u32[]{:S(2)}) copy-start(bf16[4,196,1024]{2,0,1:T(4,128)(2,1)} %param.10) | copy-start | bytes 4816900
  22.6 14.2 %all-to-all-start = ((bf16[32,8,512]{2,1,0:T(8,128)(2,1)}), bf16[32,8,512]{2,1,0:T(8,128)(2,1)S(1)}, u32[]{:S(2)}, u32[]{:S(2)}) async-start(bf16[32,8,512]{2,1,0:T(8,128)(2,1)} %bitcast.9), calls=%async_computation | async-start | bytes 524288 | tf_op jit(solution)/shard_map/all_to_all | solution.py:353
  29.3 1.0 %copy-start.2 = (bf16[1024,16]{0,1:T(8,128)(2,1)S(1)}, bf16[1024,16]{0,1:T(8,128)(2,1)}, u32[]{:S(2)}) copy-start(bf16[1024,16]{0,1:T(8,128)(2,1)} %param.11) | copy-start | bytes 98308
  29.3 7.5 %copy-start.4 = (f32[16,1024]{1,0:T(8,128)S(1)}, f32[16,1024]{1,0:T(8,128)}, u32[]{:S(2)}) copy-start(f32[16,1024]{1,0:T(8,128)} %bias_ref.1) | copy-start | bytes 196612
  29.3 7.5 %copy-start.5 = (bf16[64,256]{1,0:T(8,128)(2,1)S(1)}, bf16[64,256]{1,0:T(8,128)(2,1)}, u32[]{:S(2)}) copy-start(bf16[64,256]{1,0:T(8,128)(2,1)} %constant.12.clone.sel_ref) | copy-start | bytes 98308

commit v9 on v7

--- a/solution.py
+++ b/solution.py
@@ -88,7 +88,7 @@
         my_grad_ref[m] = grad_ref[first + m]
 
 
-def expert_kernel(images, n_expert, k, gb, win_ref, bin_ref, wout_ref, t_ref, *rest):
+def expert_kernel(images, n_expert, n_hidden, k, gb, win_ref, bin_ref, wout_ref, t_ref, *rest):
     outer, inner = levels(n_expert)
     come_refs = rest[:outer]
     back_ref, got_ref = rest[outer:]
@@ -114,11 +114,11 @@
         return out
 
     pre = own([mm(rows_in, win_ref[e]) + bin_ref[e : e + 1] for e in range(k)])
+    act_grad = own([mm(rows_grad, wout_ref[e], NT) for e in range(k)])
     cdf = 0.5 * (1.0 + lax.erf(pre * 0.7071067811865476))
     hidden = (pre * cdf).astype(BF)
     slope = cdf + pre * jnp.exp(-0.5 * pre * pre) * 0.3989422804014327
     out_part = own([mm(hidden, wout_ref[e]) for e in range(k)]).astype(BF)
-    act_grad = own([mm(rows_grad, wout_ref[e], NT) for e in range(k)])
     pre_grad = (act_grad * slope).astype(BF)
     in_part = own([mm(pre_grad, win_ref[e], NT) for e in range(k)]).astype(BF)
     rows = gb * k * images
@@ -133,18 +133,26 @@
             ],
             axis=0,
         )
-        back_ref[i * out_rows : (i + 1) * out_rows] = mm(t, stack).astype(BF)
+        spread = mm(t, stack).astype(BF)
+        per = out_rows // n_hidden
+        for h in range(n_hidden):
+            start = (h * n_expert // gb + i) * per
+            back_ref[start : start + per] = spread[h * per : (h + 1) * per]
 
 
 def final_kernel(
-    quarter, k, gb, home_ref, bias_ref, tok_ref, grad_ref, disp_ref, comb_ref, keys_ref, sel_ref, out_ref,
+    quarter, n_hidden, k, gb, home_ref, bias_ref, tok_ref, grad_ref, disp_ref, comb_ref, keys_ref, sel_ref, out_hbm,
+    out_ref, sems,
 ):
     slots = keys_ref.shape[0]
     step = gb * k
     blocks = slots // step
-    per_block = home_ref.shape[0] // blocks
+    per = home_ref.shape[0] // (blocks * n_hidden)
     sel = sel_ref[...]
-    sums = [mm(sel, home_ref[i * per_block : (i + 1) * per_block]) for i in range(blocks)]
+    sums = []
+    for i in range(blocks):
+        starts = [(q * blocks + i) * per for q in range(n_hidden)]
+        sums.append(mm(sel, jnp.concatenate([home_ref[a : a + per] for a in starts], axis=0)))
 
     def assemble(kind, m):
         halves = []
@@ -154,6 +162,7 @@
         return jnp.concatenate(halves, axis=1)
 
     keys = keys_ref[...]
+    copies = []
     for m in range(quarter):
         slot_out = (assemble(0, m) + bias_ref[...]).astype(BF)
         slot_in_grad = assemble(1, m).astype(BF)
@@ -169,7 +178,18 @@
         logit_grad = logit_grad.astype(BF).astype(F32)
         left = jnp.concatenate([wide, logit_grad], axis=0).T.astype(BF)
         right = jnp.concatenate([slot_in_grad, keys], axis=0)
-        out_ref[m] = mm(left, right).astype(BF)
+        chunk = right.shape[1] // sems.shape[1]
+        for i in range(sems.shape[1]):
+            columns = slice(i * chunk, (i + 1) * chunk)
+            out_ref[m, :, columns] = mm(left, right[:, columns]).astype(BF)
+            copies.append(
+                pltpu.make_async_copy(
+                    out_ref.at[m, :, columns], out_hbm.at[m, :, columns], sems.at[m, i]
+                )
+            )
+            copies[-1].start()
+    for copy in copies:
+        copy.wait()
 
 
 def local(n_expert, n_hidden, tokens, slot_keys, w_in, b_in, w_out, b_out, out_grad):
@@ -216,11 +236,11 @@
         come.append(lax.ppermute(both, "expert", pairs) if j else both)
 
     order = np.arange(2 * k * 2 * gb * images).reshape(2, 2, gb, k, n_hidden, quarter)
-    order = order.transpose(2, 4, 0, 3, 5, 1)
+    order = order.transpose(4, 2, 0, 3, 5, 1)
     spread = one_hot_rows(order, order.size)
     back_rows = 2 * k * quarter * 2
     back = pl.pallas_call(
-        functools.partial(expert_kernel, images, n_expert, k, gb),
+        functools.partial(expert_kernel, images, n_expert, n_hidden, k, gb),
         out_shape=jax.ShapeDtypeStruct((n_all * back_rows, half), BF),
         in_specs=[vmem] * (4 + outer),
         out_specs=vmem,
@@ -231,20 +251,24 @@
 
     home = lax.all_to_all(
         back.reshape(n_all, back_rows, half),
-        ("expert", "hidden"),
+        ("hidden", "expert"),
         split_axis=0,
         concat_axis=0,
         tiled=True,
     )
 
     label = np.arange(quarter * 2 * 2 * gb * k).reshape(quarter, 2, 2, gb, k).transpose(3, 1, 4, 0, 2)
-    label = np.broadcast_to(label[:, None], (gb, n_hidden) + label.shape[1:])
+    label = np.broadcast_to(label[None], (n_hidden,) + label.shape)
     select = np.ascontiguousarray(one_hot_rows(label, quarter * 4 * gb * k).T)
     return pl.pallas_call(
-        functools.partial(final_kernel, quarter, k, gb),
+        functools.partial(final_kernel, quarter, n_hidden, k, gb),
         out_shape=jax.ShapeDtypeStruct((quarter, positions, width), BF),
         in_specs=[vmem] * 8,
-        out_specs=vmem,
+        out_specs=pl.BlockSpec(memory_space=pltpu.HBM),
+        scratch_shapes=[
+            pltpu.VMEM((quarter, positions, width), BF),
+            pltpu.SemaphoreType.DMA((quarter, 4)),
+        ],
         compiler_params=pltpu.CompilerParams(vmem_limit_bytes=8 << 20),
         name="tokens_back",
     )(home.reshape(n_all * back_rows, half), b_out, my_tok, my_grad, disp, comb, keys, select)

time: 35.9 us -> 36.2 us (level)
  blocking collectives: 14 us -> 14.4 us
    all_to_all x1, blocking collectives: 14 us -> 14.4 us  [local(): lax.all_to_all(back.reshape(n_all, back_rows, half), ('hidden', 'expert')...]
where the time goes in v9:
time: 36.2 us; the launch traced here: 36.1 us
  blocking collectives  14.4 us (40%)
  Pallas kernels  7.55 us (21%)
  waiting for transfers between devices  6.07 us (17%)
  starting transfers between devices  5 us (14%)
  local copies, waits for them, and re-layouts  2.96 us (8%)
    all_to_all x1, blocking collectives, local(): lax.all_to_all(back.reshape(n_all, back_rows, half), ('hidden', 'expert')...  14.4 us
    ppermute x3, waiting for transfers between devices, local(): come.append(lax.ppermute(both, 'expert', pairs) if j else both)  5.1 us
    ppermute x3, starting transfers between devices, local(): come.append(lax.ppermute(both, 'expert', pairs) if j else both)  4.48 us
    pallas_call x1, Pallas kernels, local(): pl.pallas_call(functools.partial(expert_kernel, images, n_expert, n_hidde...  4.34 us
    unnamed x20, local copies, waits for them, and re-layouts  2.94 us
    pallas_call x1, Pallas kernels, local(): pl.pallas_call(functools.partial(dispatch_kernel, images, quarter, k, gb,...  1.66 us
    pallas_call x1, Pallas kernels, local(): pl.pallas_call(functools.partial(final_kernel, quarter, n_hidden, k, gb),...  1.55 us
    ppermute x1, waiting for transfers between devices, local(): held.append(lax.ppermute(leave[1], 'expert', pairs))  0.97 us
  transfers between devices with their start and end apart: 4, of which 4 were waited for; matrix products, arithmetic and copies ran while one was open for 0% of the time, Pallas kernels for 0%

profile of v9, /device:TPU:0, one launch (start us, length us, event | category | flops | bytes accessed | tf_op | source)
XLA Modules:
  0.0 36.1 jit_solution(17075728144907470529)
XLA Ops:
  0.0 0.0 copy-start.8
  0.0 0.0 copy-start.1
  0.0 2.0 %copy.11.tok_ref = bf16[4,196,1024]{2,1,0:T(8,128)(2,1)S(1)} copy(bf16[4,196,1024]{2,0,1:T(4,128)(2,1)} %param.10) | data formatting | bytes 3211264 | tf_op args[0]
  2.1 0.0 copy-done.8
  2.1 0.0 copy-start.3
  2.1 0.0 copy-start.5
  2.1 0.5 %copy.12.grad_ref = bf16[4,196,1024]{2,1,0:T(8,128)(2,1)S(1)} copy(bf16[4,196,1024]{2,0,1:T(4,128)(2,1)S(1)} %copy-done.8) | data formatting | bytes 3211264 | tf_op args[6]
  2.6 0.4 %copy-done.3 = bf16[1024,16]{0,1:T(8,128)(2,1)S(1)} copy-done((bf16[1024,16]{0,1:T(8,128)(2,1)S(1)}, bf16[1024,16]{0,1:T(8,128)(2,1)}, u32[]{:S(2)}) %copy-start.3) | copy-done | bytes 32792
  2.9 0.0 copy-done.5
  3.0 0.0 copy-start
  3.0 0.0 copy-start.2
  3.0 0.0 copy-start.7
  3.0 1.7 %dispatch.1 = (bf16[1,16,196]{2,1,0:T(8,128)(2,1)S(1)}, bf16[1,16,196]{2,1,0:T(8,128)(2,1)S(1)}, bf16[1,196,1024]{2,1,0:T(8,128)(2,1)S(1)}, bf16[1,196,1024]{2,1...) custom-call(bf16[4,196,1024]{2,1,0:T(8,128)(2,1)S(1)} %copy.11.tok_ref, ...), custom_call_target="tpu_custom_call" | custom-call | tf_op jit(solution)/shard_map/dispatch/pallas_call | solution.py:210
  4.6 0.5 %collective-permute-start = (bf16[64,1024]{1,0:T(8,128)(2,1)S(1)}, bf16[64,1024]{1,0:T(8,128)(2,1)S(1)}, u32[]{:S(2)}, u32[]{:S(2)}) collective-permute-start(bf16[64,1024]{1,0:T(8,128)(2,1)S(1)} %get-tuple-element.12), channel_id=1, source_target_pairs={{0,4},{4,0},{8,12},{12,8},{16,20},{20,16},{24,28},{28,24},{1,5},{5... | collective-permute-start | bytes 393224 | tf_op jit(solution)/shard_map/ppermute | solution.py:231
  5.2 1.0 %collective-permute-done = bf16[64,1024]{1,0:T(8,128)(2,1)S(1)} collective-permute-done((bf16[64,1024]{1,0:T(8,128)(2,1)S(1)}, bf16[64,1024]{1,0:T(8,128)(2,1)S(1)}, u32[]{:S(2)}, u32[]{:S(2)}) %collective-permute-start) | collective-permute-done | bytes 131104 | tf_op jit(solution)/shard_map/ppermute | solution.py:231
  6.2 2.9 %collective-permute-start.1 = (bf16[32,1024]{1,0:T(8,128)(2,1)S(1)}, bf16[32,1024]{1,0:T(8,128)(2,1)S(1)}, u32[]{:S(2)}, u32[]{:S(2)}) collective-permute-start(bf16[32,1024]{1,0:T(8,128)(2,1)S(1)} %pad_maximum_fusion.1), channel_id=1, source_target_pairs={{0,8},{4,12},{8,0},{12,4},{16,24},{20,28},{24,16},{28,20},{1,9},{5... | collective-permute-start | bytes 196616 | tf_op jit(solution)/shard_map/ppermute | solution.py:236
  9.1 1.5 %collective-permute-start.2 = (bf16[32,1024]{1,0:T(8,128)(2,1)S(1)}, bf16[32,1024]{1,0:T(8,128)(2,1)S(1)}, u32[]{:S(2)}, u32[]{:S(2)}) collective-permute-start(bf16[32,1024]{1,0:T(8,128)(2,1)S(1)} %pad_maximum_fusion.2), channel_id=1, source_target_pairs={{0,16},{4,20},{8,24},{12,28},{16,0},{20,4},{24,8},{28,12},{1,17},{... | collective-permute-start | bytes 196616 | tf_op jit(solution)/shard_map/ppermute | solution.py:236
  10.6 0.1 collective-permute-start.3
  10.7 0.0 copy-start.4
  10.7 0.0 copy-start.6
  10.7 0.8 %collective-permute-done.1.rest_1_ = bf16[32,1024]{1,0:T(8,128)(2,1)S(1)} collective-permute-done((bf16[32,1024]{1,0:T(8,128)(2,1)S(1)}, bf16[32,1024]{1,0:T(8,128)(2,1)S(1)}, u32[]{:S(2)}, u32[]{:S(2)}) %collective-permute-start.1) | collective-permute-done | bytes 65568 | tf_op jit(solution)/shard_map/ppermute | solution.py:236
  11.5 1.9 %collective-permute-done.2.rest_2_ = bf16[32,1024]{1,0:T(8,128)(2,1)S(1)} collective-permute-done((bf16[32,1024]{1,0:T(8,128)(2,1)S(1)}, bf16[32,1024]{1,0:T(8,128)(2,1)S(1)}, u32[]{:S(2)}, u32[]{:S(2)}) %collective-permute-start.2) | collective-permute-done | bytes 65568 | tf_op jit(solution)/shard_map/ppermute | solution.py:236
  13.4 2.4 %collective-permute-done.3.rest_3_ = bf16[32,1024]{1,0:T(8,128)(2,1)S(1)} collective-permute-done((bf16[32,1024]{1,0:T(8,128)(2,1)S(1)}, bf16[32,1024]{1,0:T(8,128)(2,1)S(1)}, u32[]{:S(2)}, u32[]{:S(2)}) %collective-permute-start.3) | collective-permute-done | bytes 65568 | tf_op jit(solution)/shard_map/ppermute | solution.py:236
  15.8 0.0 copy-done.1
  15.8 0.0 copy-done
  15.8 0.0 copy-done.2
  15.8 0.0 copy-done.7
  15.8 4.3 %experts.1 = bf16[256,512]{1,0:T(8,128)(2,1)S(1)} custom-call(bf16[2,1024,1024]{2,1,0:T(8,128)(2,1)S(1)} %copy-done, f32[2,1024]{1,0:T(2,128)S(1)} %copy-done.7, bf16[2,1024,1024]{2,1,0:T(8,128)(2,1)S(1)} %copy-done.1, bf16[256,256]{1,0:T(8,128)(2,1)S(1)} %copy-done.2, bf16[32,1024]{1,0:T(8,128)(2,1)S(1)} %pad_maximum_fusion.rest_0_, ...), custom_call_target="tpu_custom_call" | custom-call | tf_op jit(solution)/shard_map/experts/pallas_call | solution.py:242
  20.1 14.4 %all_to_all.5 = bf16[32,8,512]{2,1,0:T(8,128)(2,1)S(1)} all-to-all(bf16[32,8,512]{2,1,0:T(8,128)(2,1)S(1)} %bitcast.4), channel_id=1, replica_groups=mesh['expert'=8,'hidden'=4] {'hidden','expert'}, dimensions={0} | all-to-all | bytes 524288 | tf_op jit(solution)/shard_map/all_to_all | solution.py:252
  34.5 0.0 copy-done.4
  34.5 0.0 copy-done.6
  34.5 1.6 %tokens_back.1 = bf16[1,196,1024]{2,1,0:T(8,128)(2,1)} custom-call(bf16[256,512]{1,0:T(8,128)(2,1)S(1)} %bitcast.3, f32[16,1024]{1,0:T(8,128)S(1)} %copy-done.4, bf16[1,196,1024]{2,1,0:T(8,128)(2,1)S(1)} %get-tuple-element.13.tok_ref, bf16[1,196,1024]{2,1,0:T(8,128)(2,1)S(1)} %get-tuple-element.14.grad_ref, ...), custom_call_target="tpu_custom_call" | custom-call | tf_op jit(solution)/shard_map/tokens_back/pallas_call | solution.py:263
  (6 shorter events, 0.0 us)
Async XLA Ops:
  0.0 2.1 %copy-start.8 = (bf16[4,196,1024]{2,0,1:T(4,128)(2,1)S(1)}, bf16[4,196,1024]{2,0,1:T(4,128)(2,1)}, u32[]{:S(2)}) copy-start(bf16[4,196,1024]{2,0,1:T(4,128)(2,1)} %param.16) | copy-start | bytes 4816900
  0.0 15.8 %copy-start.1 = (bf16[2,1024,1024]{2,1,0:T(8,128)(2,1)S(1)}, bf16[2,1024,1024]{2,1,0:T(8,128)(2,1)}, u32[]{:S(2)}) copy-start(bf16[2,1024,1024]{2,1,0:T(8,128)(2,1)} %wout_ref.1) | copy-start | bytes 12582916
  2.1 0.9 %copy-start.3 = (bf16[1024,16]{0,1:T(8,128)(2,1)S(1)}, bf16[1024,16]{0,1:T(8,128)(2,1)}, u32[]{:S(2)}) copy-start(bf16[1024,16]{0,1:T(8,128)(2,1)} %param.11) | copy-start | bytes 98308
  2.1 0.9 %copy-start.5 = (bf16[128,128]{1,0:T(8,128)(2,1)S(1)}, bf16[128,128]{1,0:T(8,128)(2,1)}, u32[]{:S(2)}) copy-start(bf16[128,128]{1,0:T(8,128)(2,1)} %constant.6.clone.perm_ref) | copy-start | bytes 98308
  3.0 12.8 %copy-start = (bf16[2,1024,1024]{2,1,0:T(8,128)(2,1)S(1)}, bf16[2,1024,1024]{2,1,0:T(8,128)(2,1)}, u32[]{:S(2)}) copy-start(bf16[2,1024,1024]{2,1,0:T(8,128)(2,1)} %win_ref.1) | copy-start | bytes 12582916
  3.0 12.8 %copy-start.2 = (bf16[256,256]{1,0:T(8,128)(2,1)S(1)}, bf16[256,256]{1,0:T(8,128)(2,1)}, u32[]{:S(2)}) copy-start(bf16[256,256]{1,0:T(8,128)(2,1)} %constant.7.clone.t_ref) | copy-start | bytes 393220
  3.0 12.8 %copy-start.7 = (f32[2,1024]{1,0:T(2,128)S(1)}, f32[2,1024]{1,0:T(2,128)}, u32[]{:S(2)}) copy-start(f32[2,1024]{1,0:T(2,128)} %bin_ref.1) | copy-start | bytes 24580
  4.6 1.5 %collective-permute-start = (bf16[64,1024]{1,0:T(8,128)(2,1)S(1)}, bf16[64,1024]{1,0:T(8,128)(2,1)S(1)}, u32[]{:S(2)}, u32[]{:S(2)}) collective-permute-start(bf16[64,1024]{1,0:T(8,128)(2,1)S(1)} %get-tuple-element.12), channel_id=1, source_target_pairs={{0,4},{4,0},{8,12},{12,8},{16,20},{20,16},{24,28},{28,24},{1,5},{5... | collective-permute-start | bytes 393224 | tf_op jit(solution)/shard_map/ppermute | solution.py:231
  6.2 5.3 %collective-permute-start.1 = (bf16[32,1024]{1,0:T(8,128)(2,1)S(1)}, bf16[32,1024]{1,0:T(8,128)(2,1)S(1)}, u32[]{:S(2)}, u32[]{:S(2)}) collective-permute-start(bf16[32,1024]{1,0:T(8,128)(2,1)S(1)} %pad_maximum_fusion.1), channel_id=1, source_target_pairs={{0,8},{4,12},{8,0},{12,4},{16,24},{20,28},{24,16},{28,20},{1,9},{5... | collective-permute-start | bytes 196616 | tf_op jit(solution)/shard_map/ppermute | solution.py:236
  9.1 4.3 %collective-permute-start.2 = (bf16[32,1024]{1,0:T(8,128)(2,1)S(1)}, bf16[32,1024]{1,0:T(8,128)(2,1)S(1)}, u32[]{:S(2)}, u32[]{:S(2)}) collective-permute-start(bf16[32,1024]{1,0:T(8,128)(2,1)S(1)} %pad_maximum_fusion.2), channel_id=1, source_target_pairs={{0,16},{4,20},{8,24},{12,28},{16,0},{20,4},{24,8},{28,12},{1,17},{... | collective-permute-start | bytes 196616 | tf_op jit(solution)/shard_map/ppermute | solution.py:236
  10.6 5.2 %collective-permute-start.3 = (bf16[32,1024]{1,0:T(8,128)(2,1)S(1)}, bf16[32,1024]{1,0:T(8,128)(2,1)S(1)}, u32[]{:S(2)}, u32[]{:S(2)}) collective-permute-start(bf16[32,1024]{1,0:T(8,128)(2,1)S(1)} %pad_maximum_fusion.3), channel_id=1, source_target_pairs={{0,24},{4,28},{8,16},{12,20},{16,8},{20,12},{24,0},{28,4},{1,25},{... | collective-permute-start | bytes 196616 | tf_op jit(solution)/shard_map/ppermute | solution.py:236
  10.7 23.9 %copy-start.4 = (f32[16,1024]{1,0:T(8,128)S(1)}, f32[16,1024]{1,0:T(8,128)}, u32[]{:S(2)}) copy-start(f32[16,1024]{1,0:T(8,128)} %bias_ref.1) | copy-start | bytes 196612
  10.7 23.9 %copy-start.6 = (bf16[64,256]{1,0:T(8,128)(2,1)S(1)}, bf16[64,256]{1,0:T(8,128)(2,1)}, u32[]{:S(2)}) copy-start(bf16[64,256]{1,0:T(8,128)(2,1)} %constant.8.clone.sel_ref) | copy-start | bytes 98308

commit v10 on v7

--- a/solution.py
+++ b/solution.py
@@ -201,6 +201,7 @@
         scratch_shapes=[pltpu.VMEM((n_expert * send_rows, width), BF)]
         + [pltpu.VMEM((images, slots, positions), BF)] * 2,
         compiler_params=pltpu.CompilerParams(vmem_limit_bytes=12 << 20),
+        cost_estimate=pl.CostEstimate(flops=8000000000, bytes_accessed=0, transcendentals=0),
         name="dispatch",
     )(tokens, out_grad, keys, perm)
 

time: 35.9 us -> 35.8 us (level)
  no operation moved by 1% of the time
where the time goes in v10:
time: 35.8 us; the launch traced here: 35.6 us
  blocking collectives  14 us (39%)
  Pallas kernels  7.58 us (21%)
  waiting for transfers between devices  6.07 us (17%)
  starting transfers between devices  5 us (14%)
  local copies, waits for them, and re-layouts  2.81 us (8%)
    all_to_all x1, blocking collectives, local(): lax.all_to_all(back.reshape(n_all, back_rows, half), ('expert', 'hidden')...  14 us
    ppermute x3, waiting for transfers between devices, local(): come.append(lax.ppermute(both, 'expert', pairs) if j else both)  5.1 us
    ppermute x3, starting transfers between devices, local(): come.append(lax.ppermute(both, 'expert', pairs) if j else both)  4.48 us
    pallas_call x1, Pallas kernels, local(): pl.pallas_call(functools.partial(expert_kernel, images, n_expert, k, gb),...  4.34 us
    unnamed x20, local copies, waits for them, and re-layouts  2.8 us
    pallas_call x1, Pallas kernels, local(): pl.pallas_call(functools.partial(dispatch_kernel, images, quarter, k, gb,...  1.66 us
    pallas_call x1, Pallas kernels, local(): pl.pallas_call(functools.partial(final_kernel, quarter, k, gb), out_shape...  1.59 us
    ppermute x1, waiting for transfers between devices, local(): held.append(lax.ppermute(leave[1], 'expert', pairs))  0.97 us
  transfers between devices with their start and end apart: 4, of which 4 were waited for; matrix products, arithmetic and copies ran while one was open for 0% of the time, Pallas kernels for 0%

profile of v10, /device:TPU:0, one launch (start us, length us, event | category | flops | bytes accessed | tf_op | source)
XLA Modules:
  0.0 35.6 jit_solution(9732260235956728294)
XLA Ops:
  0.0 0.0 copy-start.8
  0.0 2.0 %copy.11.tok_ref = bf16[4,196,1024]{2,1,0:T(8,128)(2,1)S(1)} copy(bf16[4,196,1024]{2,0,1:T(4,128)(2,1)} %param.10) | data formatting | bytes 3211264 | tf_op args[0]
  2.0 0.0 copy-done.8
  2.0 0.0 copy-start.4
  2.0 0.0 copy-start.7
  2.1 0.5 %copy.12.grad_ref = bf16[4,196,1024]{2,1,0:T(8,128)(2,1)S(1)} copy(bf16[4,196,1024]{2,0,1:T(4,128)(2,1)S(1)} %copy-done.8) | data formatting | bytes 3211264 | tf_op args[6]
  2.5 0.3 copy-done.4
  2.8 0.0 copy-done.7
  2.8 0.0 copy-start
  2.8 0.0 copy-start.1
  2.8 0.0 copy-start.2
  2.8 0.0 copy-start.6
  2.8 1.7 %dispatch.1 = (bf16[1,16,196]{2,1,0:T(8,128)(2,1)S(1)}, bf16[1,16,196]{2,1,0:T(8,128)(2,1)S(1)}, bf16[1,196,1024]{2,1,0:T(8,128)(2,1)S(1)}, bf16[1,196,1024]{2,1...) custom-call(bf16[4,196,1024]{2,1,0:T(8,128)(2,1)S(1)} %copy.11.tok_ref, ...), custom_call_target="tpu_custom_call" | custom-call | flops 8000000000 | tf_op jit(solution)/shard_map/dispatch/pallas_call | solution.py:190
  4.5 0.5 %collective-permute-start = (bf16[64,1024]{1,0:T(8,128)(2,1)S(1)}, bf16[64,1024]{1,0:T(8,128)(2,1)S(1)}, u32[]{:S(2)}, u32[]{:S(2)}) collective-permute-start(bf16[64,1024]{1,0:T(8,128)(2,1)S(1)} %get-tuple-element.12), channel_id=1, source_target_pairs={{0,4},{4,0},{8,12},{12,8},{16,20},{20,16},{24,28},{28,24},{1,5},{5... | collective-permute-start | bytes 393224 | tf_op jit(solution)/shard_map/ppermute | solution.py:212
  5.0 1.0 %collective-permute-done = bf16[64,1024]{1,0:T(8,128)(2,1)S(1)} collective-permute-done((bf16[64,1024]{1,0:T(8,128)(2,1)S(1)}, bf16[64,1024]{1,0:T(8,128)(2,1)S(1)}, u32[]{:S(2)}, u32[]{:S(2)}) %collective-permute-start) | collective-permute-done | bytes 131104 | tf_op jit(solution)/shard_map/ppermute | solution.py:212
  6.0 2.9 %collective-permute-start.1 = (bf16[32,1024]{1,0:T(8,128)(2,1)S(1)}, bf16[32,1024]{1,0:T(8,128)(2,1)S(1)}, u32[]{:S(2)}, u32[]{:S(2)}) collective-permute-start(bf16[32,1024]{1,0:T(8,128)(2,1)S(1)} %pad_maximum_fusion.1), channel_id=1, source_target_pairs={{0,8},{4,12},{8,0},{12,4},{16,24},{20,28},{24,16},{28,20},{1,9},{5... | collective-permute-start | bytes 196616 | tf_op jit(solution)/shard_map/ppermute | solution.py:217
  8.9 1.5 %collective-permute-start.2 = (bf16[32,1024]{1,0:T(8,128)(2,1)S(1)}, bf16[32,1024]{1,0:T(8,128)(2,1)S(1)}, u32[]{:S(2)}, u32[]{:S(2)}) collective-permute-start(bf16[32,1024]{1,0:T(8,128)(2,1)S(1)} %pad_maximum_fusion.2), channel_id=1, source_target_pairs={{0,16},{4,20},{8,24},{12,28},{16,0},{20,4},{24,8},{28,12},{1,17},{... | collective-permute-start | bytes 196616 | tf_op jit(solution)/shard_map/ppermute | solution.py:217
  10.5 0.0 collective-permute-start.3
  10.5 0.0 copy-start.3
  10.5 0.0 copy-start.5
  10.5 0.8 %collective-permute-done.1.rest_1_ = bf16[32,1024]{1,0:T(8,128)(2,1)S(1)} collective-permute-done((bf16[32,1024]{1,0:T(8,128)(2,1)S(1)}, bf16[32,1024]{1,0:T(8,128)(2,1)S(1)}, u32[]{:S(2)}, u32[]{:S(2)}) %collective-permute-start.1) | collective-permute-done | bytes 65568 | tf_op jit(solution)/shard_map/ppermute | solution.py:217
  11.3 1.9 %collective-permute-done.2.rest_2_ = bf16[32,1024]{1,0:T(8,128)(2,1)S(1)} collective-permute-done((bf16[32,1024]{1,0:T(8,128)(2,1)S(1)}, bf16[32,1024]{1,0:T(8,128)(2,1)S(1)}, u32[]{:S(2)}, u32[]{:S(2)}) %collective-permute-start.2) | collective-permute-done | bytes 65568 | tf_op jit(solution)/shard_map/ppermute | solution.py:217
  13.2 2.4 %collective-permute-done.3.rest_3_ = bf16[32,1024]{1,0:T(8,128)(2,1)S(1)} collective-permute-done((bf16[32,1024]{1,0:T(8,128)(2,1)S(1)}, bf16[32,1024]{1,0:T(8,128)(2,1)S(1)}, u32[]{:S(2)}, u32[]{:S(2)}) %collective-permute-start.3) | collective-permute-done | bytes 65568 | tf_op jit(solution)/shard_map/ppermute | solution.py:217
  15.6 0.0 copy-done
  15.6 0.0 copy-done.1
  15.6 0.0 copy-done.2
  15.6 0.0 copy-done.6
  15.7 4.3 %experts.1 = bf16[256,512]{1,0:T(8,128)(2,1)S(1)} custom-call(bf16[2,1024,1024]{2,1,0:T(8,128)(2,1)S(1)} %copy-done, f32[2,1024]{1,0:T(2,128)S(1)} %copy-done.6, bf16[2,1024,1024]{2,1,0:T(8,128)(2,1)S(1)} %copy-done.1, bf16[256,256]{1,0:T(8,128)(2,1)S(1)} %copy-done.2, bf16[32,1024]{1,0:T(8,128)(2,1)S(1)} %pad_maximum_fusion.rest_0_, ...), custom_call_target="tpu_custom_call" | custom-call | tf_op jit(solution)/shard_map/experts/pallas_call | solution.py:223
  20.0 14.0 %all_to_all.5 = bf16[32,8,512]{2,1,0:T(8,128)(2,1)S(1)} all-to-all(bf16[32,8,512]{2,1,0:T(8,128)(2,1)S(1)} %bitcast.4), channel_id=1, replica_groups=mesh['expert'=8,'hidden'=4] {'expert','hidden'}, dimensions={0} | all-to-all | bytes 524288 | tf_op jit(solution)/shard_map/all_to_all | solution.py:233
  34.0 0.0 copy-done.3
  34.0 0.0 copy-done.5
  34.0 1.6 %tokens_back.1 = bf16[1,196,1024]{2,1,0:T(8,128)(2,1)} custom-call(bf16[256,512]{1,0:T(8,128)(2,1)S(1)} %bitcast.3, f32[16,1024]{1,0:T(8,128)S(1)} %copy-done.3, bf16[1,196,1024]{2,1,0:T(8,128)(2,1)S(1)} %get-tuple-element.13.tok_ref, bf16[1,196,1024]{2,1,0:T(8,128)(2,1)S(1)} %get-tuple-element.14.grad_ref, ...), custom_call_target="tpu_custom_call" | custom-call | tf_op jit(solution)/shard_map/tokens_back/pallas_call | solution.py:244
  (6 shorter events, 0.0 us)
Async XLA Ops:
  0.0 2.0 %copy-start.8 = (bf16[4,196,1024]{2,0,1:T(4,128)(2,1)S(1)}, bf16[4,196,1024]{2,0,1:T(4,128)(2,1)}, u32[]{:S(2)}) copy-start(bf16[4,196,1024]{2,0,1:T(4,128)(2,1)} %param.16) | copy-start | bytes 4816900
  2.0 0.8 %copy-start.4 = (bf16[1024,16]{0,1:T(8,128)(2,1)S(1)}, bf16[1024,16]{0,1:T(8,128)(2,1)}, u32[]{:S(2)}) copy-start(bf16[1024,16]{0,1:T(8,128)(2,1)} %param.11) | copy-start | bytes 98308
  2.0 0.8 %copy-start.7 = (bf16[128,128]{1,0:T(8,128)(2,1)S(1)}, bf16[128,128]{1,0:T(8,128)(2,1)}, u32[]{:S(2)}) copy-start(bf16[128,128]{1,0:T(8,128)(2,1)} %constant.6.clone.perm_ref) | copy-start | bytes 98308
  2.8 12.8 %copy-start = (bf16[2,1024,1024]{2,1,0:T(8,128)(2,1)S(1)}, bf16[2,1024,1024]{2,1,0:T(8,128)(2,1)}, u32[]{:S(2)}) copy-start(bf16[2,1024,1024]{2,1,0:T(8,128)(2,1)} %win_ref.1) | copy-start | bytes 12582916
  2.8 12.8 %copy-start.1 = (bf16[2,1024,1024]{2,1,0:T(8,128)(2,1)S(1)}, bf16[2,1024,1024]{2,1,0:T(8,128)(2,1)}, u32[]{:S(2)}) copy-start(bf16[2,1024,1024]{2,1,0:T(8,128)(2,1)} %wout_ref.1) | copy-start | bytes 12582916
  2.8 12.8 %copy-start.2 = (bf16[256,256]{1,0:T(8,128)(2,1)S(1)}, bf16[256,256]{1,0:T(8,128)(2,1)}, u32[]{:S(2)}) copy-start(bf16[256,256]{1,0:T(8,128)(2,1)} %constant.7.clone.t_ref) | copy-start | bytes 393220
  2.8 12.8 %copy-start.6 = (f32[2,1024]{1,0:T(2,128)S(1)}, f32[2,1024]{1,0:T(2,128)}, u32[]{:S(2)}) copy-start(f32[2,1024]{1,0:T(2,128)} %bin_ref.1) | copy-start | bytes 24580
  4.5 1.5 %collective-permute-start = (bf16[64,1024]{1,0:T(8,128)(2,1)S(1)}, bf16[64,1024]{1,0:T(8,128)(2,1)S(1)}, u32[]{:S(2)}, u32[]{:S(2)}) collective-permute-start(bf16[64,1024]{1,0:T(8,128)(2,1)S(1)} %get-tuple-element.12), channel_id=1, source_target_pairs={{0,4},{4,0},{8,12},{12,8},{16,20},{20,16},{24,28},{28,24},{1,5},{5... | collective-permute-start | bytes 393224 | tf_op jit(solution)/shard_map/ppermute | solution.py:212
  6.0 5.3 %collective-permute-start.1 = (bf16[32,1024]{1,0:T(8,128)(2,1)S(1)}, bf16[32,1024]{1,0:T(8,128)(2,1)S(1)}, u32[]{:S(2)}, u32[]{:S(2)}) collective-permute-start(bf16[32,1024]{1,0:T(8,128)(2,1)S(1)} %pad_maximum_fusion.1), channel_id=1, source_target_pairs={{0,8},{4,12},{8,0},{12,4},{16,24},{20,28},{24,16},{28,20},{1,9},{5... | collective-permute-start | bytes 196616 | tf_op jit(solution)/shard_map/ppermute | solution.py:217
  8.9 4.3 %collective-permute-start.2 = (bf16[32,1024]{1,0:T(8,128)(2,1)S(1)}, bf16[32,1024]{1,0:T(8,128)(2,1)S(1)}, u32[]{:S(2)}, u32[]{:S(2)}) collective-permute-start(bf16[32,1024]{1,0:T(8,128)(2,1)S(1)} %pad_maximum_fusion.2), channel_id=1, source_target_pairs={{0,16},{4,20},{8,24},{12,28},{16,0},{20,4},{24,8},{28,12},{1,17},{... | collective-permute-start | bytes 196616 | tf_op jit(solution)/shard_map/ppermute | solution.py:217
  10.5 5.2 %collective-permute-start.3 = (bf16[32,1024]{1,0:T(8,128)(2,1)S(1)}, bf16[32,1024]{1,0:T(8,128)(2,1)S(1)}, u32[]{:S(2)}, u32[]{:S(2)}) collective-permute-start(bf16[32,1024]{1,0:T(8,128)(2,1)S(1)} %pad_maximum_fusion.3), channel_id=1, source_target_pairs={{0,24},{4,28},{8,16},{12,20},{16,8},{20,12},{24,0},{28,4},{1,25},{... | collective-permute-start | bytes 196616 | tf_op jit(solution)/shard_map/ppermute | solution.py:217
  10.5 23.4 %copy-start.3 = (f32[16,1024]{1,0:T(8,128)S(1)}, f32[16,1024]{1,0:T(8,128)}, u32[]{:S(2)}) copy-start(f32[16,1024]{1,0:T(8,128)} %bias_ref.1) | copy-start | bytes 196612
  10.5 23.5 %copy-start.5 = (bf16[64,256]{1,0:T(8,128)(2,1)S(1)}, bf16[64,256]{1,0:T(8,128)(2,1)}, u32[]{:S(2)}) copy-start(bf16[64,256]{1,0:T(8,128)(2,1)} %constant.8.clone.sel_ref) | copy-start | bytes 98308

commit v11 on v8

--- a/solution.py
+++ b/solution.py
@@ -177,7 +177,10 @@
         comb_ref[m] = softmax_rows(logits).astype(BF)
 
 
-def expert_kernel(images, n_expert, k, gb, win_ref, bin_ref, wout_ref, t_ref, *rest):
+def expert_kernel(
+    images, n_expert, k, gb, ahead, win_ref, bin_ref, wout_ref, t_ref, *rest
+):
+    rest = rest[ahead:]
     outer, inner = levels(n_expert)
     come_refs = rest[:outer]
     back_ref, got_ref = rest[outer:]
@@ -333,6 +336,7 @@
         in_specs=[vmem] * 2,
         out_specs=(vmem,) * 2,
         compiler_params=pltpu.CompilerParams(vmem_limit_bytes=8 << 20),
+        cost_estimate=pl.CostEstimate(flops=1000000000, bytes_accessed=0, transcendentals=0),
         name="own_softmax",
     )(my_tok, keys)
 
@@ -340,15 +344,16 @@
     order = order.transpose(2, 4, 0, 3, 5, 1)
     spread = one_hot_rows(order, order.size)
     back_rows = 2 * k * quarter * 2
+    ahead = (my_tok, my_grad, disp, comb)
     back = pl.pallas_call(
-        functools.partial(expert_kernel, images, n_expert, k, gb),
+        functools.partial(expert_kernel, images, n_expert, k, gb, len(ahead)),
         out_shape=jax.ShapeDtypeStruct((n_all * back_rows, half), BF),
-        in_specs=[vmem] * (4 + outer),
+        in_specs=[vmem] * 4 + [pl.BlockSpec(memory_space=pl.ANY)] * len(ahead) + [vmem] * outer,
         out_specs=vmem,
         scratch_shapes=[pltpu.VMEM((n_expert, send_rows, width), BF)],
         compiler_params=pltpu.CompilerParams(vmem_limit_bytes=20 << 20),
         name="experts",
-    )(w_in, b_in, w_out, spread, *come)
+    )(w_in, b_in, w_out, spread, *ahead, *come)
 
     home = lax.all_to_all(
         back.reshape(n_all, back_rows, half),

time: 38.6 us -> 39.2 us (1.016)
  blocking collectives: 0 us -> 14 us
  waiting for transfers between devices: 12.2 us -> 5.42 us
  starting transfers between devices: 8.95 us -> 4.97 us
  local copies, waits for them, and re-layouts: 4.16 us -> 2 us
  Pallas kernels: 11.2 us -> 10.5 us
    all_to_all x0 -> x1, blocking collectives: none -> 14 us  [local(): lax.all_to_all(back.reshape(n_all, back_rows, half), ('expert', 'hidden')...]
    all_to_all x1 -> x0, waiting for transfers between devices: 6.11 us -> none  [local(): lax.all_to_all(back.reshape(n_all, back_rows, half), ('expert', 'hidden')...]
    all_to_all x1 -> x0, starting transfers between devices: 3.97 us -> none  [local(): lax.all_to_all(back.reshape(n_all, back_rows, half), ('expert', 'hidden')...]
    unnamed x20, local copies, waits for them, and re-layouts: 2.48 us -> 0.31 us
    pallas_call x1, Pallas kernels: 5.04 us -> 4.34 us  [local(): pl.pallas_call(functools.partial(expert_kernel, images, n_expert, k, gb,...]
    ppermute x3, waiting for transfers between devices: 5.14 us -> 4.45 us  [local(): come.append(lax.ppermute(both[j], 'expert', pairs))]
  transfers between devices with their start and end apart: 5 -> 4, of which waited for: 5 -> 4; matrix products, arithmetic and copies ran while one was open for 5% -> 1% of each run, Pallas kernels for 1% -> 1%
where the time goes in v11:
time: 39.2 us; the launch traced here: 39 us
  blocking collectives  14 us (36%)
  Pallas kernels  10.5 us (27%)
  waiting for transfers between devices  5.42 us (14%)
  starting transfers between devices  4.97 us (13%)
  between operations  2.11 us (5%)
  local copies, waits for them, and re-layouts  2 us (5%)
    all_to_all x1, blocking collectives, local(): lax.all_to_all(back.reshape(n_all, back_rows, half), ('expert', 'hidden')...  14 us
    ppermute x3, starting transfers between devices, local(): come.append(lax.ppermute(both[j], 'expert', pairs))  4.45 us
    ppermute x3, waiting for transfers between devices, local(): come.append(lax.ppermute(both[j], 'expert', pairs))  4.45 us
    pallas_call x1, Pallas kernels, local(): pl.pallas_call(functools.partial(expert_kernel, images, n_expert, k, gb,...  4.34 us
    pallas_call x1, Pallas kernels, local(): pl.pallas_call(functools.partial(dispatch_kernel, images, quarter, k, gb,...  4.19 us
    dynamic_slice x2, local copies, waits for them, and re-layouts, local(): my_tok, my_grad = (mine(tokens), mine(out_grad))  1.67 us
    pallas_call x1, Pallas kernels, local(): pl.pallas_call(functools.partial(final_kernel, quarter, k, gb), out_shape...  1.59 us
    ppermute x1, waiting for transfers between devices, local(): held.append(lax.ppermute(leave[1], 'expert', pairs))  0.97 us
  transfers between devices with their start and end apart: 4, of which 4 were waited for; matrix products, arithmetic and copies ran while one was open for 1% of the time, Pallas kernels for 1%

profile of v11, /device:TPU:0, one launch (start us, length us, event | category | flops | bytes accessed | tf_op | source)
XLA Modules:
  0.0 39.0 jit_solution(11012182728235181554)
XLA Ops:
  0.0 0.0 copy-start.7
  0.0 4.2 %dispatch.1 = (s32[1]{0:T(128)}, bf16[64,1024]{1,0:T(8,128)(2,1)S(1)}, bf16[64,1024]{1,0:T(8,128)(2,1)S(1)}) custom-call(bf16[196,32,128]{2,1,0:T(8,128)(2,1)} %bitcast.24, bf16[196,32,128]{2,1,0:T(8,128)(2,1)} %bitcast.23, bf16[16,1024]{1,0:T(8,128)(2,1)} %bitcast.20, bf16[128,128]{1,0:T(8,128)(2,1)} %constant.10.clone.perm_hbm), custom_call_target="tpu_custom_call" | custom-call | tf_op jit(solution)/shard_map/dispatch/pallas_call | solution.py:297
  4.2 0.0 copy-start.8
  4.2 0.5 %collective-permute-start = (bf16[64,1024]{1,0:T(8,128)(2,1)S(1)}, bf16[64,1024]{1,0:T(8,128)(2,1)S(1)}, u32[]{:S(2)}, u32[]{:S(2)}) collective-permute-start(bf16[64,1024]{1,0:T(8,128)(2,1)S(1)} %get-tuple-element.16), channel_id=1, source_target_pairs={{0,4},{4,0},{8,12},{12,8},{16,20},{20,16},{24,28},{28,24},{1,5},{5... | collective-permute-start | bytes 393224 | tf_op jit(solution)/shard_map/ppermute | solution.py:318
  4.7 1.0 %collective-permute-done = bf16[64,1024]{1,0:T(8,128)(2,1)S(1)} collective-permute-done((bf16[64,1024]{1,0:T(8,128)(2,1)S(1)}, bf16[64,1024]{1,0:T(8,128)(2,1)S(1)}, u32[]{:S(2)}, u32[]{:S(2)}) %collective-permute-start) | collective-permute-done | bytes 131104 | tf_op jit(solution)/shard_map/ppermute | solution.py:318
  7.7 0.0 copy-done.7
  7.7 0.0 copy-start.1
  7.7 0.8 %constant_dynamic-slice_fusion = bf16[1,196,1024]{2,0,1:T(2,128)(2,1)S(1)} fusion(bf16[4,196,1024]{2,0,1:T(4,128)(2,1)S(1)} %copy-done.7, s32[]{:T(128)S(6)} %select_n.4), kind=kLoop, calls=%fused_computation.4 | loop fusion | bytes 802820 | tf_op jit(solution)/shard_map/dynamic_slice | solution.py:332
  8.6 0.0 copy-done.8
  8.6 0.8 %constant_dynamic-slice_fusion.1 = bf16[1,196,1024]{2,0,1:T(2,128)(2,1)S(1)} fusion(bf16[4,196,1024]{2,0,1:T(4,128)(2,1)S(1)} %copy-done.8, s32[]{:T(128)S(6)} %select_n.4), kind=kLoop, calls=%fused_computation.5 | loop fusion | bytes 802820 | tf_op jit(solution)/shard_map/dynamic_slice | solution.py:332
  9.4 0.0 copy-start.3
  9.4 2.9 %collective-permute-start.1 = (bf16[32,1024]{1,0:T(8,128)(2,1)S(1)}, bf16[32,1024]{1,0:T(8,128)(2,1)S(1)}, u32[]{:S(2)}, u32[]{:S(2)}) collective-permute-start(bf16[32,1024]{1,0:T(8,128)(2,1)S(1)} %get-tuple-element.22), channel_id=1, source_target_pairs={{0,8},{4,12},{8,0},{12,4},{16,24},{20,28},{24,16},{28,20},{1,9},{5... | collective-permute-start | bytes 196616 | tf_op jit(solution)/shard_map/ppermute | solution.py:327
  12.4 1.5 %collective-permute-start.2 = (bf16[32,1024]{1,0:T(8,128)(2,1)S(1)}, bf16[32,1024]{1,0:T(8,128)(2,1)S(1)}, u32[]{:S(2)}, u32[]{:S(2)}) collective-permute-start(bf16[32,1024]{1,0:T(8,128)(2,1)S(1)} %get-tuple-element.23), channel_id=1, source_target_pairs={{0,16},{4,20},{8,24},{12,28},{16,0},{20,4},{24,8},{28,12},{1,17},{... | collective-permute-start | bytes 196616 | tf_op jit(solution)/shard_map/ppermute | solution.py:327
  13.9 0.0 collective-permute-start.3
  13.9 0.1 copy.16.rest_1_.grad_ref
  14.0 0.0 copy-start
  14.0 0.1 copy.15.tok_ref.rest_0_
  14.2 0.0 copy-done.3
  14.2 0.0 copy-start.2
  14.2 0.0 copy-start.6
  14.2 0.4 own_softmax.1
  14.6 0.2 collective-permute-done.1.rest_5_
  14.8 1.9 %collective-permute-done.2.rest_6_ = bf16[32,1024]{1,0:T(8,128)(2,1)S(1)} collective-permute-done((bf16[32,1024]{1,0:T(8,128)(2,1)S(1)}, bf16[32,1024]{1,0:T(8,128)(2,1)S(1)}, u32[]{:S(2)}, u32[]{:S(2)}) %collective-permute-start.2) | collective-permute-done | bytes 65568 | tf_op jit(solution)/shard_map/ppermute | solution.py:327
  16.6 2.4 %collective-permute-done.3.rest_7_ = bf16[32,1024]{1,0:T(8,128)(2,1)S(1)} collective-permute-done((bf16[32,1024]{1,0:T(8,128)(2,1)S(1)}, bf16[32,1024]{1,0:T(8,128)(2,1)S(1)}, u32[]{:S(2)}, u32[]{:S(2)}) %collective-permute-start.3) | collective-permute-done | bytes 65568 | tf_op jit(solution)/shard_map/ppermute | solution.py:327
  19.0 0.0 copy-done.1
  19.0 0.0 copy-done
  19.1 0.0 copy-done.2
  19.1 0.0 copy-done.6
  19.1 0.0 copy-start.4
  19.1 0.0 copy-start.5
  19.1 4.3 %experts.1 = bf16[256,512]{1,0:T(8,128)(2,1)S(1)} custom-call(bf16[2,1024,1024]{2,1,0:T(8,128)(2,1)S(1)} %copy-done, f32[2,1024]{1,0:T(2,128)S(1)} %copy-done.6, bf16[2,1024,1024]{2,1,0:T(8,128)(2,1)S(1)} %copy-done.1, bf16[256,256]{1,0:T(8,128)(2,1)S(1)} %copy-done.2, bf16[1,196,1024]{2,1,0:T(8,128)(2,1)S(1)} %copy.15.tok_ref.rest_0_, ...), custom_call_target="tpu_custom_call" | custom-call | tf_op jit(solution)/shard_map/experts/pallas_call | solution.py:348
  23.4 14.0 %all_to_all.5 = bf16[32,8,512]{2,1,0:T(8,128)(2,1)S(1)} all-to-all(bf16[32,8,512]{2,1,0:T(8,128)(2,1)S(1)} %bitcast.19), channel_id=1, replica_groups=mesh['expert'=8,'hidden'=4] {'expert','hidden'}, dimensions={0} | all-to-all | bytes 524288 | tf_op jit(solution)/shard_map/all_to_all | solution.py:358
  37.4 0.0 copy-done.4
  37.4 0.0 copy-done.5
  37.4 1.6 %tokens_back.1 = bf16[1,196,1024]{2,1,0:T(8,128)(2,1)} custom-call(bf16[256,512]{1,0:T(8,128)(2,1)S(1)} %bitcast.18, f32[16,1024]{1,0:T(8,128)S(1)} %copy-done.4, bf16[1,196,1024]{2,1,0:T(8,128)(2,1)S(1)} %copy.15.tok_ref.rest_0_, bf16[1,196,1024]{2,1,0:T(8,128)(2,1)S(1)} %copy.16.rest_1_.grad_ref, ...), custom_call_target="tpu_custom_call" | custom-call | tf_op jit(solution)/shard_map/tokens_back/pallas_call | solution.py:369
  (4 shorter events, 0.0 us)
Async XLA Ops:
  0.0 7.7 %copy-start.7 = (bf16[4,196,1024]{2,0,1:T(4,128)(2,1)S(1)}, bf16[4,196,1024]{2,0,1:T(4,128)(2,1)}, u32[]{:S(2)}) copy-start(bf16[4,196,1024]{2,0,1:T(4,128)(2,1)} %param.16) | copy-start | bytes 4816900
  4.2 4.4 %copy-start.8 = (bf16[4,196,1024]{2,0,1:T(4,128)(2,1)S(1)}, bf16[4,196,1024]{2,0,1:T(4,128)(2,1)}, u32[]{:S(2)}) copy-start(bf16[4,196,1024]{2,0,1:T(4,128)(2,1)} %param.10) | copy-start | bytes 4816900
  4.2 1.5 %collective-permute-start = (bf16[64,1024]{1,0:T(8,128)(2,1)S(1)}, bf16[64,1024]{1,0:T(8,128)(2,1)S(1)}, u32[]{:S(2)}, u32[]{:S(2)}) collective-permute-start(bf16[64,1024]{1,0:T(8,128)(2,1)S(1)} %get-tuple-element.16), channel_id=1, source_target_pairs={{0,4},{4,0},{8,12},{12,8},{16,20},{20,16},{24,28},{28,24},{1,5},{5... | collective-permute-start | bytes 393224 | tf_op jit(solution)/shard_map/ppermute | solution.py:318
  7.7 11.3 %copy-start.1 = (bf16[2,1024,1024]{2,1,0:T(8,128)(2,1)S(1)}, bf16[2,1024,1024]{2,1,0:T(8,128)(2,1)}, u32[]{:S(2)}) copy-start(bf16[2,1024,1024]{2,1,0:T(8,128)(2,1)} %wout_ref.1) | copy-start | bytes 12582916
  9.4 4.8 %copy-start.3 = (bf16[1024,16]{0,1:T(8,128)(2,1)S(1)}, bf16[1024,16]{0,1:T(8,128)(2,1)}, u32[]{:S(2)}) copy-start(bf16[1024,16]{0,1:T(8,128)(2,1)} %param.11) | copy-start | bytes 98308
  9.4 5.3 %collective-permute-start.1 = (bf16[32,1024]{1,0:T(8,128)(2,1)S(1)}, bf16[32,1024]{1,0:T(8,128)(2,1)S(1)}, u32[]{:S(2)}, u32[]{:S(2)}) collective-permute-start(bf16[32,1024]{1,0:T(8,128)(2,1)S(1)} %get-tuple-element.22), channel_id=1, source_target_pairs={{0,8},{4,12},{8,0},{12,4},{16,24},{20,28},{24,16},{28,20},{1,9},{5... | collective-permute-start | bytes 196616 | tf_op jit(solution)/shard_map/ppermute | solution.py:327
  12.4 4.3 %collective-permute-start.2 = (bf16[32,1024]{1,0:T(8,128)(2,1)S(1)}, bf16[32,1024]{1,0:T(8,128)(2,1)S(1)}, u32[]{:S(2)}, u32[]{:S(2)}) collective-permute-start(bf16[32,1024]{1,0:T(8,128)(2,1)S(1)} %get-tuple-element.23), channel_id=1, source_target_pairs={{0,16},{4,20},{8,24},{12,28},{16,0},{20,4},{24,8},{28,12},{1,17},{... | collective-permute-start | bytes 196616 | tf_op jit(solution)/shard_map/ppermute | solution.py:327
  13.9 5.2 %collective-permute-start.3 = (bf16[32,1024]{1,0:T(8,128)(2,1)S(1)}, bf16[32,1024]{1,0:T(8,128)(2,1)S(1)}, u32[]{:S(2)}, u32[]{:S(2)}) collective-permute-start(bf16[32,1024]{1,0:T(8,128)(2,1)S(1)} %get-tuple-element.24), channel_id=1, source_target_pairs={{0,24},{4,28},{8,16},{12,20},{16,8},{20,12},{24,0},{28,4},{1,25},{... | collective-permute-start | bytes 196616 | tf_op jit(solution)/shard_map/ppermute | solution.py:327
  14.0 5.0 %copy-start = (bf16[2,1024,1024]{2,1,0:T(8,128)(2,1)S(1)}, bf16[2,1024,1024]{2,1,0:T(8,128)(2,1)}, u32[]{:S(2)}) copy-start(bf16[2,1024,1024]{2,1,0:T(8,128)(2,1)} %win_ref.1) | copy-start | bytes 12582916
  14.2 4.9 %copy-start.2 = (bf16[256,256]{1,0:T(8,128)(2,1)S(1)}, bf16[256,256]{1,0:T(8,128)(2,1)}, u32[]{:S(2)}) copy-start(bf16[256,256]{1,0:T(8,128)(2,1)} %constant.11.clone.t_ref) | copy-start | bytes 393220
  14.2 4.9 %copy-start.6 = (f32[2,1024]{1,0:T(2,128)S(1)}, f32[2,1024]{1,0:T(2,128)}, u32[]{:S(2)}) copy-start(f32[2,1024]{1,0:T(2,128)} %bin_ref.1) | copy-start | bytes 24580
  19.1 18.3 %copy-start.4 = (f32[16,1024]{1,0:T(8,128)S(1)}, f32[16,1024]{1,0:T(8,128)}, u32[]{:S(2)}) copy-start(f32[16,1024]{1,0:T(8,128)} %bias_ref.1) | copy-start | bytes 196612
  19.1 18.3 %copy-start.5 = (bf16[64,256]{1,0:T(8,128)(2,1)S(1)}, bf16[64,256]{1,0:T(8,128)(2,1)}, u32[]{:S(2)}) copy-start(bf16[64,256]{1,0:T(8,128)(2,1)} %constant.12.clone.sel_ref) | copy-start | bytes 98308

commit v12 on v10

--- a/solution.py
+++ b/solution.py
@@ -41,6 +41,34 @@
 def position(inner):
     me = lax.axis_index("expert")
     return lax.div(me, inner), lax.rem(me, inner)
+
+
+def load_kernel(count, *refs):
+    sources, targets, sems = refs[:count], refs[count:-1], refs[-1]
+    copies = [
+        pltpu.make_async_copy(source, target, sems.at[i])
+        for i, (source, target) in enumerate(zip(sources, targets))
+    ]
+    for copy in copies:
+        copy.start()
+    for copy in copies:
+        copy.wait()
+
+
+def load(*arrays):
+    hbm = pl.BlockSpec(memory_space=pltpu.HBM)
+    return pl.pallas_call(
+        functools.partial(load_kernel, len(arrays)),
+        out_shape=[jax.ShapeDtypeStruct(x.shape, x.dtype) for x in arrays],
+        in_specs=[hbm] * len(arrays),
+        out_specs=[pl.BlockSpec(memory_space=pltpu.VMEM)] * len(arrays),
+        scratch_shapes=[pltpu.SemaphoreType.DMA((len(arrays),))],
+        compiler_params=pltpu.CompilerParams(vmem_limit_bytes=8 << 20),
+        cost_estimate=pl.CostEstimate(
+            flops=0, bytes_accessed=4 * sum(x.size for x in arrays), transcendentals=0
+        ),
+        name="load",
+    )(*(pltpu.with_memory_space_constraint(x, pltpu.HBM) for x in arrays))
 
 
 def dispatch_kernel(
@@ -186,6 +214,10 @@
     order = np.arange(2 * images * gb * k).reshape(2, images, gb, k).transpose(2, 0, 3, 1)
     perm = one_hot_rows(order, order.size)
     send_rows = 2 * k * images
+    keys, perm, *across = load(
+        keys, jnp.asarray(perm), *(x.transpose(1, 0, 2) for x in (tokens, out_grad))
+    )
+    tokens, out_grad = (x.transpose(1, 0, 2) for x in across)
     outer, inner = levels(n_expert)
     disp, comb, my_tok, my_grad, *leave = pl.pallas_call(
         functools.partial(dispatch_kernel, images, quarter, k, gb, n_expert),

time: 35.8 us -> 36 us (level)
  Pallas kernels: 7.58 us -> 9.56 us
  local copies, waits for them, and re-layouts: 2.81 us -> 1.08 us
    unnamed x20 -> x12, local copies, waits for them, and re-layouts: 2.8 us -> 0.03 us
    pallas_call x0 -> x1, Pallas kernels: none -> 1.97 us  [load(): pl.pallas_call(functools.partial(load_kernel, len(arrays)), out_shape=[ja...]
    transpose x0 -> x1, local copies, waits for them, and re-layouts: none -> 1.03 us  [local(): tokens, out_grad = (x.transpose(1, 0, 2) for x in across)]
where the time goes in v12:
time: 36 us; the launch traced here: 35.8 us
  blocking collectives  14 us (39%)
  Pallas kernels  9.56 us (27%)
  waiting for transfers between devices  6.07 us (17%)
  starting transfers between devices  5 us (14%)
  local copies, waits for them, and re-layouts  1.08 us (3%)
    all_to_all x1, blocking collectives, local(): lax.all_to_all(back.reshape(n_all, back_rows, half), ('expert', 'hidden')...  14 us
    ppermute x3, waiting for transfers between devices, local(): come.append(lax.ppermute(both, 'expert', pairs) if j else both)  5.1 us
    ppermute x3, starting transfers between devices, local(): come.append(lax.ppermute(both, 'expert', pairs) if j else both)  4.48 us
    pallas_call x1, Pallas kernels, local(): pl.pallas_call(functools.partial(expert_kernel, images, n_expert, k, gb),...  4.34 us
    pallas_call x1, Pallas kernels, load(): pl.pallas_call(functools.partial(load_kernel, len(arrays)), out_shape=[ja...  1.97 us
    pallas_call x1, Pallas kernels, local(): pl.pallas_call(functools.partial(dispatch_kernel, images, quarter, k, gb,...  1.66 us
    pallas_call x1, Pallas kernels, local(): pl.pallas_call(functools.partial(final_kernel, quarter, k, gb), out_shape...  1.59 us
    transpose x1, local copies, waits for them, and re-layouts, local(): tokens, out_grad = (x.transpose(1, 0, 2) for x in across)  1.03 us
  transfers between devices with their start and end apart: 4, of which 4 were waited for; matrix products, arithmetic and copies ran while one was open for 0% of the time, Pallas kernels for 0%

profile of v12, /device:TPU:0, one launch (start us, length us, event | category | flops | bytes accessed | tf_op | source)
XLA Modules:
  0.0 35.8 jit_solution(9440764007445639819)
XLA Ops:
  0.0 2.0 %load.1 = (bf16[16,1024]{1,0:T(8,128)(2,1)S(1)}, bf16[128,128]{1,0:T(8,128)(2,1)S(1)}, bf16[196,4,1024]{2,1,0:T(4,128)(2,1)S(1)}, bf16[196,4,1024]{2,1,0:T(4,128)(2,1)S(1)}) custom-call(bf16[16,1024]{1,0:T(8,128)(2,1)} %bitcast.13, bf16[128,128]{1,0:T(8,128)(2,1)} %constant.6.clone.refs_1_, bf16[196,4,1024]{2,1,0:T(4,128)(2,1)} %bitcast.11, ...), custom_call_target="tpu_custom_call" | custom-call | bytes 6553600 | tf_op jit(solution)/shard_map/load/pallas_call | solution.py:60
  2.0 1.0 %copy_bitcast_fusion = (bf16[4,196,1024]{2,1,0:T(8,128)(2,1)S(1)}, bf16[4,196,1024]{2,1,0:T(8,128)(2,1)S(1)}) fusion(bf16[196,4,1024]{2,1,0:T(4,128)(2,1)S(1)} %get-tuple-element.16, bf16[196,4,1024]{2,1,0:T(4,128)(2,1)S(1)} %get-tuple-element.15), kind=kLoop, calls=%fused_computation | loop fusion | bytes 6422528 | tf_op jit(solution)/shard_map/transpose | solution.py:220
  3.0 0.0 copy-start
  3.0 0.0 copy-start.1
  3.0 0.0 copy-start.2
  3.1 0.0 copy-start.5
  3.1 1.7 %dispatch.1 = (bf16[1,16,196]{2,1,0:T(8,128)(2,1)S(1)}, bf16[1,16,196]{2,1,0:T(8,128)(2,1)S(1)}, bf16[1,196,1024]{2,1,0:T(8,128)(2,1)S(1)}, bf16[1,196,1024]{2,1...) custom-call(bf16[4,196,1024]{2,1,0:T(8,128)(2,1)S(1)} %get-tuple-element.34.tok_ref, ...), custom_call_target="tpu_custom_call" | custom-call | flops 8000000000 | tf_op jit(solution)/shard_map/dispatch/pallas_call | solution.py:222
  4.7 0.5 %collective-permute-start = (bf16[64,1024]{1,0:T(8,128)(2,1)S(1)}, bf16[64,1024]{1,0:T(8,128)(2,1)S(1)}, u32[]{:S(2)}, u32[]{:S(2)}) collective-permute-start(bf16[64,1024]{1,0:T(8,128)(2,1)S(1)} %get-tuple-element.20), channel_id=1, source_target_pairs={{0,4},{4,0},{8,12},{12,8},{16,20},{20,16},{24,28},{28,24},{1,5},{5... | collective-permute-start | bytes 393224 | tf_op jit(solution)/shard_map/ppermute | solution.py:244
  5.3 1.0 %collective-permute-done = bf16[64,1024]{1,0:T(8,128)(2,1)S(1)} collective-permute-done((bf16[64,1024]{1,0:T(8,128)(2,1)S(1)}, bf16[64,1024]{1,0:T(8,128)(2,1)S(1)}, u32[]{:S(2)}, u32[]{:S(2)}) %collective-permute-start) | collective-permute-done | bytes 131104 | tf_op jit(solution)/shard_map/ppermute | solution.py:244
  6.3 2.9 %collective-permute-start.1 = (bf16[32,1024]{1,0:T(8,128)(2,1)S(1)}, bf16[32,1024]{1,0:T(8,128)(2,1)S(1)}, u32[]{:S(2)}, u32[]{:S(2)}) collective-permute-start(bf16[32,1024]{1,0:T(8,128)(2,1)S(1)} %pad_maximum_fusion.1), channel_id=1, source_target_pairs={{0,8},{4,12},{8,0},{12,4},{16,24},{20,28},{24,16},{28,20},{1,9},{5... | collective-permute-start | bytes 196616 | tf_op jit(solution)/shard_map/ppermute | solution.py:249
  9.2 1.5 %collective-permute-start.2 = (bf16[32,1024]{1,0:T(8,128)(2,1)S(1)}, bf16[32,1024]{1,0:T(8,128)(2,1)S(1)}, u32[]{:S(2)}, u32[]{:S(2)}) collective-permute-start(bf16[32,1024]{1,0:T(8,128)(2,1)S(1)} %pad_maximum_fusion.2), channel_id=1, source_target_pairs={{0,16},{4,20},{8,24},{12,28},{16,0},{20,4},{24,8},{28,12},{1,17},{... | collective-permute-start | bytes 196616 | tf_op jit(solution)/shard_map/ppermute | solution.py:249
  10.7 0.1 collective-permute-start.3
  10.8 0.0 copy-start.3
  10.8 0.0 copy-start.4
  10.8 0.8 %collective-permute-done.1.rest_1_ = bf16[32,1024]{1,0:T(8,128)(2,1)S(1)} collective-permute-done((bf16[32,1024]{1,0:T(8,128)(2,1)S(1)}, bf16[32,1024]{1,0:T(8,128)(2,1)S(1)}, u32[]{:S(2)}, u32[]{:S(2)}) %collective-permute-start.1) | collective-permute-done | bytes 65568 | tf_op jit(solution)/shard_map/ppermute | solution.py:249
  11.6 1.9 %collective-permute-done.2.rest_2_ = bf16[32,1024]{1,0:T(8,128)(2,1)S(1)} collective-permute-done((bf16[32,1024]{1,0:T(8,128)(2,1)S(1)}, bf16[32,1024]{1,0:T(8,128)(2,1)S(1)}, u32[]{:S(2)}, u32[]{:S(2)}) %collective-permute-start.2) | collective-permute-done | bytes 65568 | tf_op jit(solution)/shard_map/ppermute | solution.py:249
  13.5 2.4 %collective-permute-done.3.rest_3_ = bf16[32,1024]{1,0:T(8,128)(2,1)S(1)} collective-permute-done((bf16[32,1024]{1,0:T(8,128)(2,1)S(1)}, bf16[32,1024]{1,0:T(8,128)(2,1)S(1)}, u32[]{:S(2)}, u32[]{:S(2)}) %collective-permute-start.3) | collective-permute-done | bytes 65568 | tf_op jit(solution)/shard_map/ppermute | solution.py:249
  15.9 0.0 copy-done
  15.9 0.0 copy-done.1
  15.9 0.0 copy-done.2
  15.9 0.0 copy-done.5
  15.9 4.3 %experts.1 = bf16[256,512]{1,0:T(8,128)(2,1)S(1)} custom-call(bf16[2,1024,1024]{2,1,0:T(8,128)(2,1)S(1)} %copy-done, f32[2,1024]{1,0:T(2,128)S(1)} %copy-done.5, bf16[2,1024,1024]{2,1,0:T(8,128)(2,1)S(1)} %copy-done.1, bf16[256,256]{1,0:T(8,128)(2,1)S(1)} %copy-done.2, bf16[32,1024]{1,0:T(8,128)(2,1)S(1)} %pad_maximum_fusion.rest_0_, ...), custom_call_target="tpu_custom_call" | custom-call | tf_op jit(solution)/shard_map/experts/pallas_call | solution.py:255
  20.2 14.0 %all_to_all.5 = bf16[32,8,512]{2,1,0:T(8,128)(2,1)S(1)} all-to-all(bf16[32,8,512]{2,1,0:T(8,128)(2,1)S(1)} %bitcast.10), channel_id=1, replica_groups=mesh['expert'=8,'hidden'=4] {'expert','hidden'}, dimensions={0} | all-to-all | bytes 524288 | tf_op jit(solution)/shard_map/all_to_all | solution.py:265
  34.2 0.0 copy-done.3
  34.2 0.0 copy-done.4
  34.2 1.6 %tokens_back.1 = bf16[1,196,1024]{2,1,0:T(8,128)(2,1)} custom-call(bf16[256,512]{1,0:T(8,128)(2,1)S(1)} %bitcast.9, f32[16,1024]{1,0:T(8,128)S(1)} %copy-done.3, bf16[1,196,1024]{2,1,0:T(8,128)(2,1)S(1)} %get-tuple-element.21.tok_ref, bf16[1,196,1024]{2,1,0:T(8,128)(2,1)S(1)} %get-tuple-element.22.grad_ref, ...), custom_call_target="tpu_custom_call" | custom-call | tf_op jit(solution)/shard_map/tokens_back/pallas_call | solution.py:276
  (6 shorter events, 0.0 us)
Async XLA Ops:
  3.0 12.9 %copy-start = (bf16[2,1024,1024]{2,1,0:T(8,128)(2,1)S(1)}, bf16[2,1024,1024]{2,1,0:T(8,128)(2,1)}, u32[]{:S(2)}) copy-start(bf16[2,1024,1024]{2,1,0:T(8,128)(2,1)} %win_ref.1) | copy-start | bytes 12582916
  3.0 12.9 %copy-start.1 = (bf16[2,1024,1024]{2,1,0:T(8,128)(2,1)S(1)}, bf16[2,1024,1024]{2,1,0:T(8,128)(2,1)}, u32[]{:S(2)}) copy-start(bf16[2,1024,1024]{2,1,0:T(8,128)(2,1)} %wout_ref.1) | copy-start | bytes 12582916
  3.0 12.8 %copy-start.2 = (bf16[256,256]{1,0:T(8,128)(2,1)S(1)}, bf16[256,256]{1,0:T(8,128)(2,1)}, u32[]{:S(2)}) copy-start(bf16[256,256]{1,0:T(8,128)(2,1)} %constant.7.clone.t_ref) | copy-start | bytes 393220
  3.1 12.8 %copy-start.5 = (f32[2,1024]{1,0:T(2,128)S(1)}, f32[2,1024]{1,0:T(2,128)}, u32[]{:S(2)}) copy-start(f32[2,1024]{1,0:T(2,128)} %bin_ref.1) | copy-start | bytes 24580
  4.7 1.5 %collective-permute-start = (bf16[64,1024]{1,0:T(8,128)(2,1)S(1)}, bf16[64,1024]{1,0:T(8,128)(2,1)S(1)}, u32[]{:S(2)}, u32[]{:S(2)}) collective-permute-start(bf16[64,1024]{1,0:T(8,128)(2,1)S(1)} %get-tuple-element.20), channel_id=1, source_target_pairs={{0,4},{4,0},{8,12},{12,8},{16,20},{20,16},{24,28},{28,24},{1,5},{5... | collective-permute-start | bytes 393224 | tf_op jit(solution)/shard_map/ppermute | solution.py:244
  6.3 5.3 %collective-permute-start.1 = (bf16[32,1024]{1,0:T(8,128)(2,1)S(1)}, bf16[32,1024]{1,0:T(8,128)(2,1)S(1)}, u32[]{:S(2)}, u32[]{:S(2)}) collective-permute-start(bf16[32,1024]{1,0:T(8,128)(2,1)S(1)} %pad_maximum_fusion.1), channel_id=1, source_target_pairs={{0,8},{4,12},{8,0},{12,4},{16,24},{20,28},{24,16},{28,20},{1,9},{5... | collective-permute-start | bytes 196616 | tf_op jit(solution)/shard_map/ppermute | solution.py:249
  9.2 4.3 %collective-permute-start.2 = (bf16[32,1024]{1,0:T(8,128)(2,1)S(1)}, bf16[32,1024]{1,0:T(8,128)(2,1)S(1)}, u32[]{:S(2)}, u32[]{:S(2)}) collective-permute-start(bf16[32,1024]{1,0:T(8,128)(2,1)S(1)} %pad_maximum_fusion.2), channel_id=1, source_target_pairs={{0,16},{4,20},{8,24},{12,28},{16,0},{20,4},{24,8},{28,12},{1,17},{... | collective-permute-start | bytes 196616 | tf_op jit(solution)/shard_map/ppermute | solution.py:249
  10.7 5.2 %collective-permute-start.3 = (bf16[32,1024]{1,0:T(8,128)(2,1)S(1)}, bf16[32,1024]{1,0:T(8,128)(2,1)S(1)}, u32[]{:S(2)}, u32[]{:S(2)}) collective-permute-start(bf16[32,1024]{1,0:T(8,128)(2,1)S(1)} %pad_maximum_fusion.3), channel_id=1, source_target_pairs={{0,24},{4,28},{8,16},{12,20},{16,8},{20,12},{24,0},{28,4},{1,25},{... | collective-permute-start | bytes 196616 | tf_op jit(solution)/shard_map/ppermute | solution.py:249
  10.8 23.5 %copy-start.3 = (f32[16,1024]{1,0:T(8,128)S(1)}, f32[16,1024]{1,0:T(8,128)}, u32[]{:S(2)}) copy-start(f32[16,1024]{1,0:T(8,128)} %bias_ref.1) | copy-start | bytes 196612
  10.8 23.5 %copy-start.4 = (bf16[64,256]{1,0:T(8,128)(2,1)S(1)}, bf16[64,256]{1,0:T(8,128)(2,1)}, u32[]{:S(2)}) copy-start(bf16[64,256]{1,0:T(8,128)(2,1)} %constant.8.clone.sel_ref) | copy-start | bytes 98308

commit v13 on v12

--- a/solution.py
+++ b/solution.py
@@ -71,16 +71,11 @@
     )(*(pltpu.with_memory_space_constraint(x, pltpu.HBM) for x in arrays))
 
 
-def dispatch_kernel(
-    images, quarter, k, gb, n_expert, tok_ref, grad_ref, keys_ref, perm_ref,
-    disp_ref, comb_ref, my_tok_ref, my_grad_ref, *rest,
+def slots_in_kernel(
+    images, quarter, tok_ref, keys_ref, sums_ref, all_ref, disp_ref, comb_ref, my_tok_ref, disp_all
 ):
-    outer, inner = levels(n_expert)
-    leave_refs = rest[:inner]
-    send_ref, disp_all, comb_all = rest[inner:]
     slots = keys_ref.shape[0]
     keys = keys_ref[...]
-    slot_rows = [[], []]
     for b in range(images):
         tok = tok_ref[b]
         logits = mm(keys, tok, NT)
@@ -89,16 +84,30 @@
         e = jnp.exp(logits - jnp.max(logits, axis=0, keepdims=True))
         comb = (e / jnp.sum(e, axis=0, keepdims=True)).astype(BF)
         disp_all[b] = disp
-        comb_all[b] = comb
-        slot_rows[0].append(mm(disp, tok).astype(BF))
-        slot_rows[1].append(mm(comb, grad_ref[b]).astype(BF))
+        all_ref[b] = comb
+        sums_ref[b * slots : (b + 1) * slots] = mm(disp, tok).astype(BF)
+    first = lax.axis_index("hidden") * quarter
+    for m in range(quarter):
+        disp_ref[m] = disp_all[first + m]
+        comb_ref[m] = all_ref[first + m]
+        my_tok_ref[m] = tok_ref[first + m]
+
+
+def slots_grad_kernel(
+    images, quarter, k, gb, n_expert, grad_ref, comb_ref, sums_ref, perm_ref, my_grad_ref, *rest
+):
+    outer, inner = levels(n_expert)
+    leave_refs = rest[:inner]
+    send_ref = rest[inner]
+    slots = comb_ref.shape[1]
+    sums = sums_ref[...]
+    slot_rows = [sums[b * slots : (b + 1) * slots] for b in range(images)]
+    slot_rows += [mm(comb_ref[b], grad_ref[b]).astype(BF) for b in range(images)]
     perm = perm_ref[...]
     step = gb * k
     rows = perm.shape[0]
     for i in range(slots // step):
-        block = jnp.concatenate(
-            [r[i * step : (i + 1) * step] for kind in slot_rows for r in kind], axis=0
-        )
+        block = jnp.concatenate([r[i * step : (i + 1) * step] for r in slot_rows], axis=0)
         send_ref[i * rows : (i + 1) * rows] = mm(perm, block).astype(BF)
     block = send_ref.shape[0] // n_expert
     c, l = position(inner)
@@ -110,9 +119,6 @@
             ]
     first = lax.axis_index("hidden") * quarter
     for m in range(quarter):
-        disp_ref[m] = disp_all[first + m]
-        comb_ref[m] = comb_all[first + m]
-        my_tok_ref[m] = tok_ref[first + m]
         my_grad_ref[m] = grad_ref[first + m]
 
 
@@ -214,28 +220,36 @@
     order = np.arange(2 * images * gb * k).reshape(2, images, gb, k).transpose(2, 0, 3, 1)
     perm = one_hot_rows(order, order.size)
     send_rows = 2 * k * images
-    keys, perm, *across = load(
-        keys, jnp.asarray(perm), *(x.transpose(1, 0, 2) for x in (tokens, out_grad))
-    )
-    tokens, out_grad = (x.transpose(1, 0, 2) for x in across)
+    keys, perm, across = load(keys, jnp.asarray(perm), tokens.transpose(1, 0, 2))
     outer, inner = levels(n_expert)
-    disp, comb, my_tok, my_grad, *leave = pl.pallas_call(
-        functools.partial(dispatch_kernel, images, quarter, k, gb, n_expert),
+    shape = jax.ShapeDtypeStruct
+    sums, comb_all, disp, comb, my_tok = pl.pallas_call(
+        functools.partial(slots_in_kernel, images, quarter),
         out_shape=(
-            jax.ShapeDtypeStruct((quarter, slots, positions), BF),
-            jax.ShapeDtypeStruct((quarter, slots, positions), BF),
-            jax.ShapeDtypeStruct((quarter, positions, width), BF),
-            jax.ShapeDtypeStruct((quarter, positions, width), BF),
-        )
-        + (jax.ShapeDtypeStruct((outer * send_rows, width), BF),) * inner,
+            shape((images * slots, width), BF),
+            shape((images, slots, positions), BF),
+            shape((quarter, slots, positions), BF),
+            shape((quarter, slots, positions), BF),
+            shape((quarter, positions, width), BF),
+        ),
+        in_specs=[vmem] * 2,
+        out_specs=(vmem,) * 5,
+        scratch_shapes=[pltpu.VMEM((images, slots, positions), BF)],
+        compiler_params=pltpu.CompilerParams(vmem_limit_bytes=10 << 20),
+        name="slots_in",
+    )(across.transpose(1, 0, 2), keys)
+    out_grad, comb_all = lax.optimization_barrier((out_grad, comb_all))
+    my_grad, *leave = pl.pallas_call(
+        functools.partial(slots_grad_kernel, images, quarter, k, gb, n_expert),
+        out_shape=(shape((quarter, positions, width), BF),)
+        + (shape((outer * send_rows, width), BF),) * inner,
         in_specs=[vmem] * 4,
-        out_specs=(vmem,) * (4 + inner),
-        scratch_shapes=[pltpu.VMEM((n_expert * send_rows, width), BF)]
-        + [pltpu.VMEM((images, slots, positions), BF)] * 2,
-        compiler_params=pltpu.CompilerParams(vmem_limit_bytes=12 << 20),
+        out_specs=(vmem,) * (1 + inner),
+        scratch_shapes=[pltpu.VMEM((n_expert * send_rows, width), BF)],
+        compiler_params=pltpu.CompilerParams(vmem_limit_bytes=10 << 20),
         cost_estimate=pl.CostEstimate(flops=8000000000, bytes_accessed=0, transcendentals=0),
-        name="dispatch",
-    )(tokens, out_grad, keys, perm)
+        name="slots_grad",
+    )(out_grad, comb_all, sums, perm)
 
     everyone = [(c, l) for c in range(outer) for l in range(inner)]
     held = leave[:1]

time: 36 us -> 36.8 us (1.022)
  Pallas kernels: 9.56 us -> 10.4 us
    pallas_call x1 -> x2, Pallas kernels: 1.66 us -> 2.98 us  [the longest x1 2.46 us: local(): pl.pallas_call(functools.partial(slots_in_kernel, images, quarter), out_s...]
    transpose x1 -> x0, local copies, waits for them, and re-layouts: 1.03 us -> none  [local(): tokens, out_grad = (x.transpose(1, 0, 2) for x in across)]
    optimization_barrier x0 -> x1, local copies, waits for them, and re-layouts: none -> 0.5 us  [local(): out_grad, comb_all = lax.optimization_barrier((out_grad, comb_all))]
    pallas_call x1, Pallas kernels: 1.97 us -> 1.48 us  [load(): pl.pallas_call(functools.partial(load_kernel, len(arrays)), out_shape=[ja...]
    pallas_call x0 -> x1, local copies, waits for them, and re-layouts: none -> 0.48 us  [load(): pl.pallas_call(functools.partial(load_kernel, len(arrays)), out_shape=[ja...]
where the time goes in v13:
time: 36.8 us; the launch traced here: 36.6 us
  blocking collectives  14 us (38%)
  Pallas kernels  10.4 us (28%)
  waiting for transfers between devices  6.07 us (16%)
  starting transfers between devices  5 us (14%)
  local copies, waits for them, and re-layouts  1.03 us (3%)
    all_to_all x1, blocking collectives, local(): lax.all_to_all(back.reshape(n_all, back_rows, half), ('expert', 'hidden')...  14 us
    ppermute x3, waiting for transfers between devices, local(): come.append(lax.ppermute(both, 'expert', pairs) if j else both)  5.1 us
    ppermute x3, starting transfers between devices, local(): come.append(lax.ppermute(both, 'expert', pairs) if j else both)  4.48 us
    pallas_call x1, Pallas kernels, local(): pl.pallas_call(functools.partial(expert_kernel, images, n_expert, k, gb),...  4.34 us
    pallas_call x1, Pallas kernels, local(): pl.pallas_call(functools.partial(slots_in_kernel, images, quarter), out_s...  2.46 us
    pallas_call x1, Pallas kernels, local(): pl.pallas_call(functools.partial(final_kernel, quarter, k, gb), out_shape...  1.59 us
    pallas_call x1, Pallas kernels, load(): pl.pallas_call(functools.partial(load_kernel, len(arrays)), out_shape=[ja...  1.48 us
    ppermute x1, waiting for transfers between devices, local(): held.append(lax.ppermute(leave[1], 'expert', pairs))  0.97 us
  transfers between devices with their start and end apart: 4, of which 4 were waited for; matrix products, arithmetic and copies ran while one was open for 0% of the time, Pallas kernels for 0%

profile of v13, /device:TPU:0, one launch (start us, length us, event | category | flops | bytes accessed | tf_op | source)
XLA Modules:
  0.0 36.6 jit_solution(17092465210954611436)
XLA Ops:
  0.0 1.5 %load.1 = (bf16[16,1024]{1,0:T(8,128)(2,1)S(1)}, bf16[128,128]{1,0:T(8,128)(2,1)S(1)}, bf16[196,4,1024]{2,1,0:T(4,128)(2,1)S(1)}) custom-call(bf16[16,1024]{1,0:T(8,128)(2,1)} %bitcast.11, bf16[128,128]{1,0:T(8,128)(2,1)} %constant.6.clone.refs_1_, bf16[196,4,1024]{2,1,0:T(4,128)(2,1)} %bitcast.10), custom_call_target="tpu_custom_call" | custom-call | bytes 3342336 | tf_op jit(solution)/shard_map/load/pallas_call | solution.py:60
  1.5 0.5 %copy.14 = bf16[196,4,1024]{2,0,1:T(8,128)(2,1)S(1)} copy(bf16[196,4,1024]{2,1,0:T(4,128)(2,1)S(1)} %get-tuple-element.18) | data formatting | bytes 3211264 | tf_op jit(solution)/shard_map/load/pallas_call | solution.py:60
  2.0 0.0 copy-start.6
  2.0 2.5 %slots_in.1 = (bf16[64,1024]{1,0:T(8,128)(2,1)S(1)}, bf16[4,16,196]{2,1,0:T(8,128)(2,1)S(1)}, bf16[1,16,196]{2,1,0:T(8,128)(2,1)S(1)}, bf16[1,16,196]{2,1,0:T(8,128)(2,1)S(1)}, bf16[1,196,1024]{2,1,0:T(8,128)(2,1)S(1)}) custom-call(bf16[4,196,1024]{2,1,0:T(8,128)(2,1)S(1)} %bitcast.7, bf16[16,1024]{1,0:T(8,128)(2,1)S(1)} %get-tuple-element.19.keys_ref), custom_call_target="tpu_custom_call" | custom-call | tf_op jit(solution)/shard_map/slots_in/pallas_call | solution.py:226
  4.4 0.0 copy-done.6
  4.4 0.5 %copy.12.grad_ref = bf16[4,196,1024]{2,1,0:T(8,128)(2,1)S(1)} copy(bf16[4,196,1024]{2,0,1:T(4,128)(2,1)S(1)} %copy-done.6) | data formatting | bytes 3211264 | tf_op jit(solution)/shard_map/optimization_barrier | solution.py:241
  5.0 0.0 copy-start
  5.0 0.0 copy-start.1
  5.0 0.0 copy-start.2
  5.0 0.0 copy-start.5
  5.0 0.5 %slots_grad.1 = (bf16[1,196,1024]{2,1,0:T(8,128)(2,1)S(1)}, bf16[64,1024]{1,0:T(8,128)(2,1)S(1)}, bf16[64,1024]{1,0:T(8,128)(2,1)S(1)}) custom-call(bf16[4,196,1024]{2,1,0:T(8,128)(2,1)S(1)} %copy.12.grad_ref, bf16[4,16,196]{2,1,0:T(8,128)(2,1)S(1)} %get-tuple-element.22.comb_ref, bf16[64,1024]{1,0:T(8,128)(2,1)S(1)} %get-tuple-element.23.sums_ref, ...), custom_call_target="tpu_custom_call" | custom-call | flops 8000000000 | tf_op jit(solution)/shard_map/slots_grad/pallas_call | solution.py:242
  5.5 0.5 %collective-permute-start = (bf16[64,1024]{1,0:T(8,128)(2,1)S(1)}, bf16[64,1024]{1,0:T(8,128)(2,1)S(1)}, u32[]{:S(2)}, u32[]{:S(2)}) collective-permute-start(bf16[64,1024]{1,0:T(8,128)(2,1)S(1)} %get-tuple-element.26), channel_id=1, source_target_pairs={{0,4},{4,0},{8,12},{12,8},{16,20},{20,16},{24,28},{28,24},{1,5},{5... | collective-permute-start | bytes 393224 | tf_op jit(solution)/shard_map/ppermute | solution.py:258
  6.1 1.0 %collective-permute-done = bf16[64,1024]{1,0:T(8,128)(2,1)S(1)} collective-permute-done((bf16[64,1024]{1,0:T(8,128)(2,1)S(1)}, bf16[64,1024]{1,0:T(8,128)(2,1)S(1)}, u32[]{:S(2)}, u32[]{:S(2)}) %collective-permute-start) | collective-permute-done | bytes 131104 | tf_op jit(solution)/shard_map/ppermute | solution.py:258
  7.1 2.9 %collective-permute-start.1 = (bf16[32,1024]{1,0:T(8,128)(2,1)S(1)}, bf16[32,1024]{1,0:T(8,128)(2,1)S(1)}, u32[]{:S(2)}, u32[]{:S(2)}) collective-permute-start(bf16[32,1024]{1,0:T(8,128)(2,1)S(1)} %pad_maximum_fusion.1), channel_id=1, source_target_pairs={{0,8},{4,12},{8,0},{12,4},{16,24},{20,28},{24,16},{28,20},{1,9},{5... | collective-permute-start | bytes 196616 | tf_op jit(solution)/shard_map/ppermute | solution.py:263
  10.0 1.5 %collective-permute-start.2 = (bf16[32,1024]{1,0:T(8,128)(2,1)S(1)}, bf16[32,1024]{1,0:T(8,128)(2,1)S(1)}, u32[]{:S(2)}, u32[]{:S(2)}) collective-permute-start(bf16[32,1024]{1,0:T(8,128)(2,1)S(1)} %pad_maximum_fusion.2), channel_id=1, source_target_pairs={{0,16},{4,20},{8,24},{12,28},{16,0},{20,4},{24,8},{28,12},{1,17},{... | collective-permute-start | bytes 196616 | tf_op jit(solution)/shard_map/ppermute | solution.py:263
  11.5 0.1 collective-permute-start.3
  11.6 0.0 copy-start.3
  11.6 0.0 copy-start.4
  11.6 0.8 %collective-permute-done.1.rest_1_ = bf16[32,1024]{1,0:T(8,128)(2,1)S(1)} collective-permute-done((bf16[32,1024]{1,0:T(8,128)(2,1)S(1)}, bf16[32,1024]{1,0:T(8,128)(2,1)S(1)}, u32[]{:S(2)}, u32[]{:S(2)}) %collective-permute-start.1) | collective-permute-done | bytes 65568 | tf_op jit(solution)/shard_map/ppermute | solution.py:263
  12.4 1.9 %collective-permute-done.2.rest_2_ = bf16[32,1024]{1,0:T(8,128)(2,1)S(1)} collective-permute-done((bf16[32,1024]{1,0:T(8,128)(2,1)S(1)}, bf16[32,1024]{1,0:T(8,128)(2,1)S(1)}, u32[]{:S(2)}, u32[]{:S(2)}) %collective-permute-start.2) | collective-permute-done | bytes 65568 | tf_op jit(solution)/shard_map/ppermute | solution.py:263
  14.3 2.4 %collective-permute-done.3.rest_3_ = bf16[32,1024]{1,0:T(8,128)(2,1)S(1)} collective-permute-done((bf16[32,1024]{1,0:T(8,128)(2,1)S(1)}, bf16[32,1024]{1,0:T(8,128)(2,1)S(1)}, u32[]{:S(2)}, u32[]{:S(2)}) %collective-permute-start.3) | collective-permute-done | bytes 65568 | tf_op jit(solution)/shard_map/ppermute | solution.py:263
  16.7 0.0 copy-done
  16.7 0.0 copy-done.1
  16.7 0.0 copy-done.2
  16.7 0.0 copy-done.5
  16.7 4.3 %experts.1 = bf16[256,512]{1,0:T(8,128)(2,1)S(1)} custom-call(bf16[2,1024,1024]{2,1,0:T(8,128)(2,1)S(1)} %copy-done, f32[2,1024]{1,0:T(2,128)S(1)} %copy-done.5, bf16[2,1024,1024]{2,1,0:T(8,128)(2,1)S(1)} %copy-done.1, bf16[256,256]{1,0:T(8,128)(2,1)S(1)} %copy-done.2, bf16[32,1024]{1,0:T(8,128)(2,1)S(1)} %pad_maximum_fusion.rest_0_, ...), custom_call_target="tpu_custom_call" | custom-call | tf_op jit(solution)/shard_map/experts/pallas_call | solution.py:269
  21.0 14.0 %all_to_all.5 = bf16[32,8,512]{2,1,0:T(8,128)(2,1)S(1)} all-to-all(bf16[32,8,512]{2,1,0:T(8,128)(2,1)S(1)} %bitcast.9), channel_id=1, replica_groups=mesh['expert'=8,'hidden'=4] {'expert','hidden'}, dimensions={0} | all-to-all | bytes 524288 | tf_op jit(solution)/shard_map/all_to_all | solution.py:279
  35.0 0.0 copy-done.3
  35.0 0.0 copy-done.4
  35.0 1.6 %tokens_back.1 = bf16[1,196,1024]{2,1,0:T(8,128)(2,1)} custom-call(bf16[256,512]{1,0:T(8,128)(2,1)S(1)} %bitcast.8, f32[16,1024]{1,0:T(8,128)S(1)} %copy-done.3, bf16[1,196,1024]{2,1,0:T(8,128)(2,1)S(1)} %get-tuple-element.27.tok_ref, bf16[1,196,1024]{2,1,0:T(8,128)(2,1)S(1)} %get-tuple-element.28.grad_ref, ...), custom_call_target="tpu_custom_call" | custom-call | tf_op jit(solution)/shard_map/tokens_back/pallas_call | solution.py:290
  (6 shorter events, 0.0 us)
Async XLA Ops:
  2.0 2.5 %copy-start.6 = (bf16[4,196,1024]{2,0,1:T(4,128)(2,1)S(1)}, bf16[4,196,1024]{2,0,1:T(4,128)(2,1)}, u32[]{:S(2)}) copy-start(bf16[4,196,1024]{2,0,1:T(4,128)(2,1)} %param.16) | copy-start | bytes 4816900
  5.0 11.7 %copy-start = (bf16[2,1024,1024]{2,1,0:T(8,128)(2,1)S(1)}, bf16[2,1024,1024]{2,1,0:T(8,128)(2,1)}, u32[]{:S(2)}) copy-start(bf16[2,1024,1024]{2,1,0:T(8,128)(2,1)} %win_ref.1) | copy-start | bytes 12582916
  5.0 11.7 %copy-start.1 = (bf16[2,1024,1024]{2,1,0:T(8,128)(2,1)S(1)}, bf16[2,1024,1024]{2,1,0:T(8,128)(2,1)}, u32[]{:S(2)}) copy-start(bf16[2,1024,1024]{2,1,0:T(8,128)(2,1)} %wout_ref.1) | copy-start | bytes 12582916
  5.0 11.7 %copy-start.2 = (bf16[256,256]{1,0:T(8,128)(2,1)S(1)}, bf16[256,256]{1,0:T(8,128)(2,1)}, u32[]{:S(2)}) copy-start(bf16[256,256]{1,0:T(8,128)(2,1)} %constant.7.clone.t_ref) | copy-start | bytes 393220
  5.0 11.7 %copy-start.5 = (f32[2,1024]{1,0:T(2,128)S(1)}, f32[2,1024]{1,0:T(2,128)}, u32[]{:S(2)}) copy-start(f32[2,1024]{1,0:T(2,128)} %bin_ref.1) | copy-start | bytes 24580
  5.5 1.5 %collective-permute-start = (bf16[64,1024]{1,0:T(8,128)(2,1)S(1)}, bf16[64,1024]{1,0:T(8,128)(2,1)S(1)}, u32[]{:S(2)}, u32[]{:S(2)}) collective-permute-start(bf16[64,1024]{1,0:T(8,128)(2,1)S(1)} %get-tuple-element.26), channel_id=1, source_target_pairs={{0,4},{4,0},{8,12},{12,8},{16,20},{20,16},{24,28},{28,24},{1,5},{5... | collective-permute-start | bytes 393224 | tf_op jit(solution)/shard_map/ppermute | solution.py:258
  7.1 5.3 %collective-permute-start.1 = (bf16[32,1024]{1,0:T(8,128)(2,1)S(1)}, bf16[32,1024]{1,0:T(8,128)(2,1)S(1)}, u32[]{:S(2)}, u32[]{:S(2)}) collective-permute-start(bf16[32,1024]{1,0:T(8,128)(2,1)S(1)} %pad_maximum_fusion.1), channel_id=1, source_target_pairs={{0,8},{4,12},{8,0},{12,4},{16,24},{20,28},{24,16},{28,20},{1,9},{5... | collective-permute-start | bytes 196616 | tf_op jit(solution)/shard_map/ppermute | solution.py:263
  10.0 4.3 %collective-permute-start.2 = (bf16[32,1024]{1,0:T(8,128)(2,1)S(1)}, bf16[32,1024]{1,0:T(8,128)(2,1)S(1)}, u32[]{:S(2)}, u32[]{:S(2)}) collective-permute-start(bf16[32,1024]{1,0:T(8,128)(2,1)S(1)} %pad_maximum_fusion.2), channel_id=1, source_target_pairs={{0,16},{4,20},{8,24},{12,28},{16,0},{20,4},{24,8},{28,12},{1,17},{... | collective-permute-start | bytes 196616 | tf_op jit(solution)/shard_map/ppermute | solution.py:263
  11.5 5.2 %collective-permute-start.3 = (bf16[32,1024]{1,0:T(8,128)(2,1)S(1)}, bf16[32,1024]{1,0:T(8,128)(2,1)S(1)}, u32[]{:S(2)}, u32[]{:S(2)}) collective-permute-start(bf16[32,1024]{1,0:T(8,128)(2,1)S(1)} %pad_maximum_fusion.3), channel_id=1, source_target_pairs={{0,24},{4,28},{8,16},{12,20},{16,8},{20,12},{24,0},{28,4},{1,25},{... | collective-permute-start | bytes 196616 | tf_op jit(solution)/shard_map/ppermute | solution.py:263
  11.6 23.5 %copy-start.3 = (f32[16,1024]{1,0:T(8,128)S(1)}, f32[16,1024]{1,0:T(8,128)}, u32[]{:S(2)}) copy-start(f32[16,1024]{1,0:T(8,128)} %bias_ref.1) | copy-start | bytes 196612
  11.6 23.5 %copy-start.4 = (bf16[64,256]{1,0:T(8,128)(2,1)S(1)}, bf16[64,256]{1,0:T(8,128)(2,1)}, u32[]{:S(2)}) copy-start(bf16[64,256]{1,0:T(8,128)(2,1)} %constant.8.clone.sel_ref) | copy-start | bytes 98308

commit v14 on v10

--- a/solution.py
+++ b/solution.py
@@ -36,6 +36,16 @@
 def levels(n_expert):
     inner = 2 if n_expert % 2 == 0 else 1
     return n_expert // inner, inner
+
+
+def turn(l, j, outer):
+    if j == 0:
+        return 0
+    steps = [outer - 1, *range(1, outer - 1)]
+    mine, other = steps[j - 1], steps[j - 2]
+    if isinstance(l, int):
+        return other if l else mine
+    return jnp.where(l == 1, other, mine)
 
 
 def position(inner):
@@ -76,7 +86,8 @@
     c, l = position(inner)
     for i in range(inner):
         for j in range(outer):
-            to = partner(c, j, outer) * inner + lax.rem(l + i, inner)
+            core = lax.rem(l + i, inner)
+            to = partner(c, turn(core, j, outer), outer) * inner + core
             leave_refs[i][j * block : (j + 1) * block] = send_ref[
                 pl.ds(pl.multiple_of(to * block, block), block)
             ]
@@ -96,7 +107,7 @@
     c, l = position(inner)
     block = got_ref.shape[1]
     for j in range(outer):
-        source = partner(c, j, outer, True) * inner
+        source = partner(c, turn(l, j, outer), outer, True) * inner
         for i in range(inner):
             got_ref[source + lax.rem(l + i, inner)] = come_refs[j][i * block : (i + 1) * block]
     width = got_ref.shape[2]
@@ -213,7 +224,9 @@
     come = []
     for j in range(outer):
         both = jnp.concatenate([r[j * send_rows : (j + 1) * send_rows] for r in held])
-        pairs = [(c * inner + l, partner(c, j, outer) * inner + l) for c, l in everyone]
+        pairs = [
+            (c * inner + l, partner(c, turn(l, j, outer), outer) * inner + l) for c, l in everyone
+        ]
         come.append(lax.ppermute(both, "expert", pairs) if j else both)
 
     order = np.arange(2 * k * 2 * gb * images).reshape(2, 2, gb, k, n_hidden, quarter)

time: 35.8 us -> 35.8 us (level)
  blocking collectives: 14 us -> 15 us
  waiting for transfers between devices: 6.07 us -> 5.11 us
    all_to_all x1, blocking collectives: 14 us -> 15 us  [local(): lax.all_to_all(back.reshape(n_all, back_rows, half), ('expert', 'hidden')...]
    ppermute x3, waiting for transfers between devices: 5.1 us -> 4.13 us  [local(): come.append(lax.ppermute(both, 'expert', pairs) if j else both)]
where the time goes in v14:
time: 35.8 us; the launch traced here: 35.7 us
  blocking collectives  15 us (42%)
  Pallas kernels  7.58 us (21%)
  waiting for transfers between devices  5.11 us (14%)
  starting transfers between devices  5.04 us (14%)
  local copies, waits for them, and re-layouts  2.81 us (8%)
    all_to_all x1, blocking collectives, local(): lax.all_to_all(back.reshape(n_all, back_rows, half), ('expert', 'hidden')...  15 us
    ppermute x3, starting transfers between devices, local(): come.append(lax.ppermute(both, 'expert', pairs) if j else both)  4.52 us
    pallas_call x1, Pallas kernels, local(): pl.pallas_call(functools.partial(expert_kernel, images, n_expert, k, gb),...  4.34 us
    ppermute x3, waiting for transfers between devices, local(): come.append(lax.ppermute(both, 'expert', pairs) if j else both)  4.13 us
    unnamed x20, local copies, waits for them, and re-layouts  2.8 us
    pallas_call x1, Pallas kernels, local(): pl.pallas_call(functools.partial(dispatch_kernel, images, quarter, k, gb,...  1.66 us
    pallas_call x1, Pallas kernels, local(): pl.pallas_call(functools.partial(final_kernel, quarter, k, gb), out_shape...  1.58 us
    ppermute x1, waiting for transfers between devices, local(): held.append(lax.ppermute(leave[1], 'expert', pairs))  0.97 us
  transfers between devices with their start and end apart: 4, of which 4 were waited for; matrix products, arithmetic and copies ran while one was open for 0% of the time, Pallas kernels for 0%

profile of v14, /device:TPU:0, one launch (start us, length us, event | category | flops | bytes accessed | tf_op | source)
XLA Modules:
  0.0 35.7 jit_solution(4239174418574438776)
XLA Ops:
  0.0 0.0 copy-start.8
  0.0 2.0 %copy.11.tok_ref = bf16[4,196,1024]{2,1,0:T(8,128)(2,1)S(1)} copy(bf16[4,196,1024]{2,0,1:T(4,128)(2,1)} %param.10) | data formatting | bytes 3211264 | tf_op args[0]
  2.0 0.0 copy-done.8
  2.0 0.0 copy-start.4
  2.0 0.0 copy-start.7
  2.1 0.5 %copy.12.grad_ref = bf16[4,196,1024]{2,1,0:T(8,128)(2,1)S(1)} copy(bf16[4,196,1024]{2,0,1:T(4,128)(2,1)S(1)} %copy-done.8) | data formatting | bytes 3211264 | tf_op args[6]
  2.5 0.3 copy-done.4
  2.8 0.0 copy-done.7
  2.8 0.0 copy-start
  2.8 0.0 copy-start.1
  2.8 0.0 copy-start.2
  2.8 0.0 copy-start.6
  2.8 1.7 %dispatch.1 = (bf16[1,16,196]{2,1,0:T(8,128)(2,1)S(1)}, bf16[1,16,196]{2,1,0:T(8,128)(2,1)S(1)}, bf16[1,196,1024]{2,1,0:T(8,128)(2,1)S(1)}, bf16[1,196,1024]{2,1...) custom-call(bf16[4,196,1024]{2,1,0:T(8,128)(2,1)S(1)} %copy.11.tok_ref, ...), custom_call_target="tpu_custom_call" | custom-call | flops 8000000000 | tf_op jit(solution)/shard_map/dispatch/pallas_call | solution.py:201
  4.5 0.5 %collective-permute-start = (bf16[64,1024]{1,0:T(8,128)(2,1)S(1)}, bf16[64,1024]{1,0:T(8,128)(2,1)S(1)}, u32[]{:S(2)}, u32[]{:S(2)}) collective-permute-start(bf16[64,1024]{1,0:T(8,128)(2,1)S(1)} %get-tuple-element.12), channel_id=1, source_target_pairs={{0,4},{4,0},{8,12},{12,8},{16,20},{20,16},{24,28},{28,24},{1,5},{5... | collective-permute-start | bytes 393224 | tf_op jit(solution)/shard_map/ppermute | solution.py:223
  5.0 1.0 %collective-permute-done = bf16[64,1024]{1,0:T(8,128)(2,1)S(1)} collective-permute-done((bf16[64,1024]{1,0:T(8,128)(2,1)S(1)}, bf16[64,1024]{1,0:T(8,128)(2,1)S(1)}, u32[]{:S(2)}, u32[]{:S(2)}) %collective-permute-start) | collective-permute-done | bytes 131104 | tf_op jit(solution)/shard_map/ppermute | solution.py:223
  6.0 3.9 %collective-permute-start.1 = (bf16[32,1024]{1,0:T(8,128)(2,1)S(1)}, bf16[32,1024]{1,0:T(8,128)(2,1)S(1)}, u32[]{:S(2)}, u32[]{:S(2)}) collective-permute-start(bf16[32,1024]{1,0:T(8,128)(2,1)S(1)} %pad_maximum_fusion.1), channel_id=1, source_target_pairs={{0,24},{4,20},{8,16},{12,28},{16,8},{20,4},{24,0},{28,12},{1,25},{... | collective-permute-start | bytes 196616 | tf_op jit(solution)/shard_map/ppermute | solution.py:230
  9.9 0.5 %collective-permute-start.2 = (bf16[32,1024]{1,0:T(8,128)(2,1)S(1)}, bf16[32,1024]{1,0:T(8,128)(2,1)S(1)}, u32[]{:S(2)}, u32[]{:S(2)}) collective-permute-start(bf16[32,1024]{1,0:T(8,128)(2,1)S(1)} %pad_maximum_fusion.2), channel_id=1, source_target_pairs={{0,8},{4,28},{8,0},{12,20},{16,24},{20,12},{24,16},{28,4},{1,9},{5... | collective-permute-start | bytes 196616 | tf_op jit(solution)/shard_map/ppermute | solution.py:230
  10.4 0.1 collective-permute-start.3
  10.6 0.0 copy-start.3
  10.6 0.0 copy-start.5
  10.6 1.8 %collective-permute-done.1.rest_1_ = bf16[32,1024]{1,0:T(8,128)(2,1)S(1)} collective-permute-done((bf16[32,1024]{1,0:T(8,128)(2,1)S(1)}, bf16[32,1024]{1,0:T(8,128)(2,1)S(1)}, u32[]{:S(2)}, u32[]{:S(2)}) %collective-permute-start.1) | collective-permute-done | bytes 65568 | tf_op jit(solution)/shard_map/ppermute | solution.py:230
  12.3 1.8 %collective-permute-done.2.rest_2_ = bf16[32,1024]{1,0:T(8,128)(2,1)S(1)} collective-permute-done((bf16[32,1024]{1,0:T(8,128)(2,1)S(1)}, bf16[32,1024]{1,0:T(8,128)(2,1)S(1)}, u32[]{:S(2)}, u32[]{:S(2)}) %collective-permute-start.2) | collective-permute-done | bytes 65568 | tf_op jit(solution)/shard_map/ppermute | solution.py:230
  14.2 0.5 %collective-permute-done.3.rest_3_ = bf16[32,1024]{1,0:T(8,128)(2,1)S(1)} collective-permute-done((bf16[32,1024]{1,0:T(8,128)(2,1)S(1)}, bf16[32,1024]{1,0:T(8,128)(2,1)S(1)}, u32[]{:S(2)}, u32[]{:S(2)}) %collective-permute-start.3) | collective-permute-done | bytes 65568 | tf_op jit(solution)/shard_map/ppermute | solution.py:230
  14.7 0.0 copy-done
  14.7 0.0 copy-done.1
  14.7 0.0 copy-done.2
  14.7 0.0 copy-done.6
  14.7 4.3 %experts.1 = bf16[256,512]{1,0:T(8,128)(2,1)S(1)} custom-call(bf16[2,1024,1024]{2,1,0:T(8,128)(2,1)S(1)} %copy-done, f32[2,1024]{1,0:T(2,128)S(1)} %copy-done.6, bf16[2,1024,1024]{2,1,0:T(8,128)(2,1)S(1)} %copy-done.1, bf16[256,256]{1,0:T(8,128)(2,1)S(1)} %copy-done.2, bf16[32,1024]{1,0:T(8,128)(2,1)S(1)} %pad_maximum_fusion.rest_0_, ...), custom_call_target="tpu_custom_call" | custom-call | tf_op jit(solution)/shard_map/experts/pallas_call | solution.py:236
  19.1 15.0 %all_to_all.5 = bf16[32,8,512]{2,1,0:T(8,128)(2,1)S(1)} all-to-all(bf16[32,8,512]{2,1,0:T(8,128)(2,1)S(1)} %bitcast.4), channel_id=1, replica_groups=mesh['expert'=8,'hidden'=4] {'expert','hidden'}, dimensions={0} | all-to-all | bytes 524288 | tf_op jit(solution)/shard_map/all_to_all | solution.py:246
  34.1 0.0 copy-done.3
  34.1 0.0 copy-done.5
  34.1 1.6 %tokens_back.1 = bf16[1,196,1024]{2,1,0:T(8,128)(2,1)} custom-call(bf16[256,512]{1,0:T(8,128)(2,1)S(1)} %bitcast.3, f32[16,1024]{1,0:T(8,128)S(1)} %copy-done.3, bf16[1,196,1024]{2,1,0:T(8,128)(2,1)S(1)} %get-tuple-element.13.tok_ref, bf16[1,196,1024]{2,1,0:T(8,128)(2,1)S(1)} %get-tuple-element.14.grad_ref, ...), custom_call_target="tpu_custom_call" | custom-call | tf_op jit(solution)/shard_map/tokens_back/pallas_call | solution.py:257
  (6 shorter events, 0.0 us)
Async XLA Ops:
  0.0 2.0 %copy-start.8 = (bf16[4,196,1024]{2,0,1:T(4,128)(2,1)S(1)}, bf16[4,196,1024]{2,0,1:T(4,128)(2,1)}, u32[]{:S(2)}) copy-start(bf16[4,196,1024]{2,0,1:T(4,128)(2,1)} %param.16) | copy-start | bytes 4816900
  2.0 0.8 %copy-start.4 = (bf16[1024,16]{0,1:T(8,128)(2,1)S(1)}, bf16[1024,16]{0,1:T(8,128)(2,1)}, u32[]{:S(2)}) copy-start(bf16[1024,16]{0,1:T(8,128)(2,1)} %param.11) | copy-start | bytes 98308
  2.0 0.8 %copy-start.7 = (bf16[128,128]{1,0:T(8,128)(2,1)S(1)}, bf16[128,128]{1,0:T(8,128)(2,1)}, u32[]{:S(2)}) copy-start(bf16[128,128]{1,0:T(8,128)(2,1)} %constant.6.clone.perm_ref) | copy-start | bytes 98308
  2.8 11.9 %copy-start = (bf16[2,1024,1024]{2,1,0:T(8,128)(2,1)S(1)}, bf16[2,1024,1024]{2,1,0:T(8,128)(2,1)}, u32[]{:S(2)}) copy-start(bf16[2,1024,1024]{2,1,0:T(8,128)(2,1)} %win_ref.1) | copy-start | bytes 12582916
  2.8 11.9 %copy-start.1 = (bf16[2,1024,1024]{2,1,0:T(8,128)(2,1)S(1)}, bf16[2,1024,1024]{2,1,0:T(8,128)(2,1)}, u32[]{:S(2)}) copy-start(bf16[2,1024,1024]{2,1,0:T(8,128)(2,1)} %wout_ref.1) | copy-start | bytes 12582916
  2.8 11.9 %copy-start.2 = (bf16[256,256]{1,0:T(8,128)(2,1)S(1)}, bf16[256,256]{1,0:T(8,128)(2,1)}, u32[]{:S(2)}) copy-start(bf16[256,256]{1,0:T(8,128)(2,1)} %constant.7.clone.t_ref) | copy-start | bytes 393220
  2.8 11.9 %copy-start.6 = (f32[2,1024]{1,0:T(2,128)S(1)}, f32[2,1024]{1,0:T(2,128)}, u32[]{:S(2)}) copy-start(f32[2,1024]{1,0:T(2,128)} %bin_ref.1) | copy-start | bytes 24580
  4.5 1.5 %collective-permute-start = (bf16[64,1024]{1,0:T(8,128)(2,1)S(1)}, bf16[64,1024]{1,0:T(8,128)(2,1)S(1)}, u32[]{:S(2)}, u32[]{:S(2)}) collective-permute-start(bf16[64,1024]{1,0:T(8,128)(2,1)S(1)} %get-tuple-element.12), channel_id=1, source_target_pairs={{0,4},{4,0},{8,12},{12,8},{16,20},{20,16},{24,28},{28,24},{1,5},{5... | collective-permute-start | bytes 393224 | tf_op jit(solution)/shard_map/ppermute | solution.py:223
  6.0 6.3 %collective-permute-start.1 = (bf16[32,1024]{1,0:T(8,128)(2,1)S(1)}, bf16[32,1024]{1,0:T(8,128)(2,1)S(1)}, u32[]{:S(2)}, u32[]{:S(2)}) collective-permute-start(bf16[32,1024]{1,0:T(8,128)(2,1)S(1)} %pad_maximum_fusion.1), channel_id=1, source_target_pairs={{0,24},{4,20},{8,16},{12,28},{16,8},{20,4},{24,0},{28,12},{1,25},{... | collective-permute-start | bytes 196616 | tf_op jit(solution)/shard_map/ppermute | solution.py:230
  9.9 4.3 %collective-permute-start.2 = (bf16[32,1024]{1,0:T(8,128)(2,1)S(1)}, bf16[32,1024]{1,0:T(8,128)(2,1)S(1)}, u32[]{:S(2)}, u32[]{:S(2)}) collective-permute-start(bf16[32,1024]{1,0:T(8,128)(2,1)S(1)} %pad_maximum_fusion.2), channel_id=1, source_target_pairs={{0,8},{4,28},{8,0},{12,20},{16,24},{20,12},{24,16},{28,4},{1,9},{5... | collective-permute-start | bytes 196616 | tf_op jit(solution)/shard_map/ppermute | solution.py:230
  10.4 4.3 %collective-permute-start.3 = (bf16[32,1024]{1,0:T(8,128)(2,1)S(1)}, bf16[32,1024]{1,0:T(8,128)(2,1)S(1)}, u32[]{:S(2)}, u32[]{:S(2)}) collective-permute-start(bf16[32,1024]{1,0:T(8,128)(2,1)S(1)} %pad_maximum_fusion.3), channel_id=1, source_target_pairs={{0,16},{4,12},{8,24},{12,4},{16,0},{20,28},{24,8},{28,20},{1,17},{... | collective-permute-start | bytes 196616 | tf_op jit(solution)/shard_map/ppermute | solution.py:230
  10.6 23.5 %copy-start.3 = (f32[16,1024]{1,0:T(8,128)S(1)}, f32[16,1024]{1,0:T(8,128)}, u32[]{:S(2)}) copy-start(f32[16,1024]{1,0:T(8,128)} %bias_ref.1) | copy-start | bytes 196612
  10.6 23.5 %copy-start.5 = (bf16[64,256]{1,0:T(8,128)(2,1)S(1)}, bf16[64,256]{1,0:T(8,128)(2,1)}, u32[]{:S(2)}) copy-start(bf16[64,256]{1,0:T(8,128)(2,1)} %constant.8.clone.sel_ref) | copy-start | bytes 98308

commit v15 on v10

--- a/solution.py
+++ b/solution.py
@@ -48,8 +48,8 @@
     disp_ref, comb_ref, my_tok_ref, my_grad_ref, *rest,
 ):
     outer, inner = levels(n_expert)
-    leave_refs = rest[:inner]
-    send_ref, disp_all, comb_all = rest[inner:]
+    keep_ref, *give_refs = rest[: 2 * inner - 1]
+    send_ref, disp_all, comb_all = rest[2 * inner - 1 :]
     slots = keys_ref.shape[0]
     keys = keys_ref[...]
     slot_rows = [[], []]
@@ -77,9 +77,13 @@
     for i in range(inner):
         for j in range(outer):
             to = partner(c, j, outer) * inner + lax.rem(l + i, inner)
-            leave_refs[i][j * block : (j + 1) * block] = send_ref[
-                pl.ds(pl.multiple_of(to * block, block), block)
-            ]
+            rows = send_ref[pl.ds(pl.multiple_of(to * block, block), block)]
+            if i == 0:
+                keep_ref[j * block : (j + 1) * block] = rows
+            elif j == 0:
+                give_refs[1][...] = rows
+            else:
+                give_refs[0][(j - 1) * block : j * block] = rows
     first = lax.axis_index("hidden") * quarter
     for m in range(quarter):
         disp_ref[m] = disp_all[first + m]
@@ -90,15 +94,19 @@
 
 def expert_kernel(images, n_expert, k, gb, win_ref, bin_ref, wout_ref, t_ref, *rest):
     outer, inner = levels(n_expert)
-    come_refs = rest[:outer]
-    back_ref, got_ref = rest[outer:]
+    come_refs = rest[: outer + inner - 1]
+    back_ref, got_ref = rest[outer + inner - 1 :]
     rows = k * images
     c, l = position(inner)
     block = got_ref.shape[1]
     for j in range(outer):
         source = partner(c, j, outer, True) * inner
         for i in range(inner):
-            got_ref[source + lax.rem(l + i, inner)] = come_refs[j][i * block : (i + 1) * block]
+            if j == 0:
+                rows_here = come_refs[i * outer][:block]
+            else:
+                rows_here = come_refs[j][i * block : (i + 1) * block]
+            got_ref[source + lax.rem(l + i, inner)] = rows_here
     width = got_ref.shape[2]
     total = n_expert * rows
     got = got_ref[...]
@@ -187,7 +195,8 @@
     perm = one_hot_rows(order, order.size)
     send_rows = 2 * k * images
     outer, inner = levels(n_expert)
-    disp, comb, my_tok, my_grad, *leave = pl.pallas_call(
+    counts = [outer] + [outer - 1, 1] * (inner - 1)
+    disp, comb, my_tok, my_grad, keep, *give = pl.pallas_call(
         functools.partial(dispatch_kernel, images, quarter, k, gb, n_expert),
         out_shape=(
             jax.ShapeDtypeStruct((quarter, slots, positions), BF),
@@ -195,9 +204,9 @@
             jax.ShapeDtypeStruct((quarter, positions, width), BF),
             jax.ShapeDtypeStruct((quarter, positions, width), BF),
         )
-        + (jax.ShapeDtypeStruct((outer * send_rows, width), BF),) * inner,
+        + tuple(jax.ShapeDtypeStruct((n * send_rows, width), BF) for n in counts),
         in_specs=[vmem] * 4,
-        out_specs=(vmem,) * (4 + inner),
+        out_specs=(vmem,) * (4 + len(counts)),
         scratch_shapes=[pltpu.VMEM((n_expert * send_rows, width), BF)]
         + [pltpu.VMEM((images, slots, positions), BF)] * 2,
         compiler_params=pltpu.CompilerParams(vmem_limit_bytes=12 << 20),
@@ -206,15 +215,19 @@
     )(tokens, out_grad, keys, perm)
 
     everyone = [(c, l) for c in range(outer) for l in range(inner)]
-    held = leave[:1]
+    swap = [(c * inner + l, c * inner + inner - 1 - l) for c, l in everyone]
+    block = lambda x, j: x[j * send_rows : (j + 1) * send_rows]
+    both = [block(keep, j) for j in range(1, outer)]
     if inner == 2:
-        pairs = [(c * inner + l, c * inner + 1 - l) for c, l in everyone]
-        held.append(lax.ppermute(leave[1], "expert", pairs))
-    come = []
-    for j in range(outer):
-        both = jnp.concatenate([r[j * send_rows : (j + 1) * send_rows] for r in held])
+        other = lax.ppermute(give[0], "expert", swap)
+        both = [jnp.concatenate([x, block(other, j)]) for j, x in enumerate(both)]
+        *both, own = lax.optimization_barrier((*both, give[1]))
+    come = [keep]
+    for j in range(1, outer):
         pairs = [(c * inner + l, partner(c, j, outer) * inner + l) for c, l in everyone]
-        come.append(lax.ppermute(both, "expert", pairs) if j else both)
+        come.append(lax.ppermute(both[j - 1], "expert", pairs))
+    if inner == 2:
+        come.append(lax.ppermute(own, "expert", swap))
 
     order = np.arange(2 * k * 2 * gb * images).reshape(2, 2, gb, k, n_hidden, quarter)
     order = order.transpose(2, 4, 0, 3, 5, 1)
@@ -223,7 +236,7 @@
     back = pl.pallas_call(
         functools.partial(expert_kernel, images, n_expert, k, gb),
         out_shape=jax.ShapeDtypeStruct((n_all * back_rows, half), BF),
-        in_specs=[vmem] * (4 + outer),
+        in_specs=[vmem] * (4 + len(come)),
         out_specs=vmem,
         scratch_shapes=[pltpu.VMEM((n_expert, send_rows, width), BF)],
         compiler_params=pltpu.CompilerParams(vmem_limit_bytes=20 << 20),

time: 35.8 us -> 35.7 us (level)
    ppermute x4 -> x5, starting transfers between devices: 5 us -> 4.98 us  [the longest x3 4.46 us: local(): come.append(lax.ppermute(both[j - 1], 'expert', pairs))]
    ppermute x4 -> x5, waiting for transfers between devices: 6.07 us -> 6.07 us  [the longest x3 3.93 us: local(): come.append(lax.ppermute(both[j - 1], 'expert', pairs))]
  transfers between devices with their start and end apart: 4 -> 5, of which waited for: 4 -> 4; matrix products, arithmetic and copies ran while one was open for 0% -> 0% of each run, Pallas kernels for 0% -> 0%
where the time goes in v15:
time: 35.7 us; the launch traced here: 35.6 us
  blocking collectives  14 us (39%)
  Pallas kernels  7.58 us (21%)
  waiting for transfers between devices  6.07 us (17%)
  starting transfers between devices  4.98 us (14%)
  local copies, waits for them, and re-layouts  2.82 us (8%)
    all_to_all x1, blocking collectives, local(): lax.all_to_all(back.reshape(n_all, back_rows, half), ('expert', 'hidden')...  14 us
    ppermute x3, starting transfers between devices, local(): come.append(lax.ppermute(both[j - 1], 'expert', pairs))  4.46 us
    pallas_call x1, Pallas kernels, local(): pl.pallas_call(functools.partial(expert_kernel, images, n_expert, k, gb),...  4.33 us
    ppermute x3, waiting for transfers between devices, local(): come.append(lax.ppermute(both[j - 1], 'expert', pairs))  3.93 us
    unnamed x20, local copies, waits for them, and re-layouts  2.8 us
    pallas_call x1, Pallas kernels, local(): pl.pallas_call(functools.partial(dispatch_kernel, images, quarter, k, gb,...  1.66 us
    pallas_call x1, Pallas kernels, local(): pl.pallas_call(functools.partial(final_kernel, quarter, k, gb), out_shape...  1.59 us
    ppermute x1, waiting for transfers between devices, local(): come.append(lax.ppermute(own, 'expert', swap))  1.2 us
  transfers between devices with their start and end apart: 5, of which 4 were waited for; matrix products, arithmetic and copies ran while one was open for 0% of the time, Pallas kernels for 0%

profile of v15, /device:TPU:0, one launch (start us, length us, event | category | flops | bytes accessed | tf_op | source)
XLA Modules:
  0.0 35.6 jit_solution(12309634128511003450)
XLA Ops:
  0.0 0.0 copy-start.8
  0.0 2.0 %copy.11.tok_ref = bf16[4,196,1024]{2,1,0:T(8,128)(2,1)S(1)} copy(bf16[4,196,1024]{2,0,1:T(4,128)(2,1)} %param.10) | data formatting | bytes 3211264 | tf_op args[0]
  2.0 0.0 copy-done.8
  2.0 0.0 copy-start.4
  2.0 0.0 copy-start.7
  2.1 0.5 %copy.12.grad_ref = bf16[4,196,1024]{2,1,0:T(8,128)(2,1)S(1)} copy(bf16[4,196,1024]{2,0,1:T(4,128)(2,1)S(1)} %copy-done.8) | data formatting | bytes 3211264 | tf_op args[6]
  2.5 0.3 copy-done.4
  2.8 0.0 copy-done.7
  2.8 0.0 copy-start
  2.8 0.0 copy-start.1
  2.8 0.0 copy-start.2
  2.8 0.0 copy-start.6
  2.8 1.7 %dispatch.1 = (bf16[1,16,196]{2,1,0:T(8,128)(2,1)S(1)}, bf16[1,16,196]{2,1,0:T(8,128)(2,1)S(1)}, bf16[1,196,1024]{2,1,0:T(8,128)(2,1)S(1)}, bf16[1,196,1024]{2,1...) custom-call(bf16[4,196,1024]{2,1,0:T(8,128)(2,1)S(1)} %copy.11.tok_re, ...), custom_call_target="tpu_custom_call" | custom-call | flops 8000000000 | tf_op jit(solution)/shard_map/dispatch/pallas_call | solution.py:199
  4.5 0.5 %collective-permute-start = (bf16[48,1024]{1,0:T(8,128)(2,1)S(1)}, bf16[48,1024]{1,0:T(8,128)(2,1)S(1)}, u32[]{:S(2)}, u32[]{:S(2)}) collective-permute-start(bf16[48,1024]{1,0:T(8,128)(2,1)S(1)} %get-tuple-element.17), channel_id=1, source_target_pairs={{0,4},{4,0},{8,12},{12,8},{16,20},{20,16},{24,28},{28,24},{1,5},{5... | collective-permute-start | bytes 294920 | tf_op jit(solution)/shard_map/ppermute | solution.py:222
  5.0 0.9 %collective-permute-done = bf16[48,1024]{1,0:T(8,128)(2,1)S(1)} collective-permute-done((bf16[48,1024]{1,0:T(8,128)(2,1)S(1)}, bf16[48,1024]{1,0:T(8,128)(2,1)S(1)}, u32[]{:S(2)}, u32[]{:S(2)}) %collective-permute-start) | collective-permute-done | bytes 98336 | tf_op jit(solution)/shard_map/ppermute | solution.py:222
  6.0 0.0 copy-start.3
  6.0 0.0 copy-start.5
  6.0 2.9 %collective-permute-start.1 = (bf16[32,1024]{1,0:T(8,128)(2,1)S(1)}, bf16[32,1024]{1,0:T(8,128)(2,1)S(1)}, u32[]{:S(2)}, u32[]{:S(2)}) collective-permute-start(bf16[32,1024]{1,0:T(8,128)(2,1)S(1)} %get-tuple-element.19), channel_id=1, source_target_pairs={{0,8},{4,12},{8,0},{12,4},{16,24},{20,28},{24,16},{28,20},{1,9},{5... | collective-permute-start | bytes 196616 | tf_op jit(solution)/shard_map/ppermute | solution.py:228
  8.9 1.5 %collective-permute-start.2 = (bf16[32,1024]{1,0:T(8,128)(2,1)S(1)}, bf16[32,1024]{1,0:T(8,128)(2,1)S(1)}, u32[]{:S(2)}, u32[]{:S(2)}) collective-permute-start(bf16[32,1024]{1,0:T(8,128)(2,1)S(1)} %get-tuple-element.20), channel_id=1, source_target_pairs={{0,16},{4,20},{8,24},{12,28},{16,0},{20,4},{24,8},{28,12},{1,17},{... | collective-permute-start | bytes 196616 | tf_op jit(solution)/shard_map/ppermute | solution.py:228
  10.5 0.0 collective-permute-start.3
  10.5 0.0 collective-permute-start.4
  10.5 1.2 %collective-permute-done.4.rest_4_ = bf16[16,1024]{1,0:T(8,128)(2,1)S(1)} collective-permute-done((bf16[16,1024]{1,0:T(8,128)(2,1)S(1)}, bf16[16,1024]{1,0:T(8,128)(2,1)S(1)}, u32[]{:S(2)}, u32[]{:S(2)}) %collective-permute-start.4) | collective-permute-done | bytes 32800 | tf_op jit(solution)/shard_map/ppermute | solution.py:230
  11.7 0.0 collective-permute-done.1.rest_1_
  11.7 1.5 %collective-permute-done.2.rest_2_ = bf16[32,1024]{1,0:T(8,128)(2,1)S(1)} collective-permute-done((bf16[32,1024]{1,0:T(8,128)(2,1)S(1)}, bf16[32,1024]{1,0:T(8,128)(2,1)S(1)}, u32[]{:S(2)}, u32[]{:S(2)}) %collective-permute-start.2) | collective-permute-done | bytes 65568 | tf_op jit(solution)/shard_map/ppermute | solution.py:228
  13.2 2.4 %collective-permute-done.3.rest_3_ = bf16[32,1024]{1,0:T(8,128)(2,1)S(1)} collective-permute-done((bf16[32,1024]{1,0:T(8,128)(2,1)S(1)}, bf16[32,1024]{1,0:T(8,128)(2,1)S(1)}, u32[]{:S(2)}, u32[]{:S(2)}) %collective-permute-start.3) | collective-permute-done | bytes 65568 | tf_op jit(solution)/shard_map/ppermute | solution.py:228
  15.6 0.0 copy-done
  15.6 0.0 copy-done.1
  15.6 0.0 copy-done.2
  15.6 0.0 copy-done.6
  15.6 4.3 %experts.1 = bf16[256,512]{1,0:T(8,128)(2,1)S(1)} custom-call(bf16[2,1024,1024]{2,1,0:T(8,128)(2,1)S(1)} %copy-done, f32[2,1024]{1,0:T(2,128)S(1)} %copy-done.6, bf16[2,1024,1024]{2,1,0:T(8,128)(2,1)S(1)} %copy-done.1, bf16[256,256]{1,0:T(8,128)(2,1)S(1)} %copy-done.2, bf16[64,1024]{1,0:T(8,128)(2,1)S(1)} %get-tuple-element.16.rest_0_, ...), custom_call_target="tpu_custom_call" | custom-call | tf_op jit(solution)/shard_map/experts/pallas_call | solution.py:236
  20.0 14.0 %all_to_all.5 = bf16[32,8,512]{2,1,0:T(8,128)(2,1)S(1)} all-to-all(bf16[32,8,512]{2,1,0:T(8,128)(2,1)S(1)} %bitcast.4), channel_id=1, replica_groups=mesh['expert'=8,'hidden'=4] {'expert','hidden'}, dimensions={0} | all-to-all | bytes 524288 | tf_op jit(solution)/shard_map/all_to_all | solution.py:246
  34.0 0.0 copy-done.3
  34.0 0.0 copy-done.5
  34.0 1.6 %tokens_back.1 = bf16[1,196,1024]{2,1,0:T(8,128)(2,1)} custom-call(bf16[256,512]{1,0:T(8,128)(2,1)S(1)} %bitcast.3, f32[16,1024]{1,0:T(8,128)S(1)} %copy-done.3, bf16[1,196,1024]{2,1,0:T(8,128)(2,1)S(1)} %get-tuple-element.23.tok_ref, bf16[1,196,1024]{2,1,0:T(8,128)(2,1)S(1)} %get-tuple-element.24.grad_ref, ...), custom_call_target="tpu_custom_call" | custom-call | tf_op jit(solution)/shard_map/tokens_back/pallas_call | solution.py:257
  (4 shorter events, 0.0 us)
Async XLA Ops:
  0.0 2.0 %copy-start.8 = (bf16[4,196,1024]{2,0,1:T(4,128)(2,1)S(1)}, bf16[4,196,1024]{2,0,1:T(4,128)(2,1)}, u32[]{:S(2)}) copy-start(bf16[4,196,1024]{2,0,1:T(4,128)(2,1)} %param.16) | copy-start | bytes 4816900
  2.0 0.8 %copy-start.4 = (bf16[1024,16]{0,1:T(8,128)(2,1)S(1)}, bf16[1024,16]{0,1:T(8,128)(2,1)}, u32[]{:S(2)}) copy-start(bf16[1024,16]{0,1:T(8,128)(2,1)} %param.11) | copy-start | bytes 98308
  2.0 0.8 %copy-start.7 = (bf16[128,128]{1,0:T(8,128)(2,1)S(1)}, bf16[128,128]{1,0:T(8,128)(2,1)}, u32[]{:S(2)}) copy-start(bf16[128,128]{1,0:T(8,128)(2,1)} %constant.6.clone.perm_ref) | copy-start | bytes 98308
  2.8 12.8 %copy-start = (bf16[2,1024,1024]{2,1,0:T(8,128)(2,1)S(1)}, bf16[2,1024,1024]{2,1,0:T(8,128)(2,1)}, u32[]{:S(2)}) copy-start(bf16[2,1024,1024]{2,1,0:T(8,128)(2,1)} %win_ref.1) | copy-start | bytes 12582916
  2.8 12.8 %copy-start.1 = (bf16[2,1024,1024]{2,1,0:T(8,128)(2,1)S(1)}, bf16[2,1024,1024]{2,1,0:T(8,128)(2,1)}, u32[]{:S(2)}) copy-start(bf16[2,1024,1024]{2,1,0:T(8,128)(2,1)} %wout_ref.1) | copy-start | bytes 12582916
  2.8 12.8 %copy-start.2 = (bf16[256,256]{1,0:T(8,128)(2,1)S(1)}, bf16[256,256]{1,0:T(8,128)(2,1)}, u32[]{:S(2)}) copy-start(bf16[256,256]{1,0:T(8,128)(2,1)} %constant.7.clone.t_ref) | copy-start | bytes 393220
  2.8 12.8 %copy-start.6 = (f32[2,1024]{1,0:T(2,128)S(1)}, f32[2,1024]{1,0:T(2,128)}, u32[]{:S(2)}) copy-start(f32[2,1024]{1,0:T(2,128)} %bin_ref.1) | copy-start | bytes 24580
  4.5 1.5 %collective-permute-start = (bf16[48,1024]{1,0:T(8,128)(2,1)S(1)}, bf16[48,1024]{1,0:T(8,128)(2,1)S(1)}, u32[]{:S(2)}, u32[]{:S(2)}) collective-permute-start(bf16[48,1024]{1,0:T(8,128)(2,1)S(1)} %get-tuple-element.17), channel_id=1, source_target_pairs={{0,4},{4,0},{8,12},{12,8},{16,20},{20,16},{24,28},{28,24},{1,5},{5... | collective-permute-start | bytes 294920 | tf_op jit(solution)/shard_map/ppermute | solution.py:222
  6.0 28.0 %copy-start.3 = (f32[16,1024]{1,0:T(8,128)S(1)}, f32[16,1024]{1,0:T(8,128)}, u32[]{:S(2)}) copy-start(f32[16,1024]{1,0:T(8,128)} %bias_ref.1) | copy-start | bytes 196612
  6.0 28.0 %copy-start.5 = (bf16[64,256]{1,0:T(8,128)(2,1)S(1)}, bf16[64,256]{1,0:T(8,128)(2,1)}, u32[]{:S(2)}) copy-start(bf16[64,256]{1,0:T(8,128)(2,1)} %constant.8.clone.sel_ref) | copy-start | bytes 98308
  6.0 5.7 %collective-permute-start.1 = (bf16[32,1024]{1,0:T(8,128)(2,1)S(1)}, bf16[32,1024]{1,0:T(8,128)(2,1)S(1)}, u32[]{:S(2)}, u32[]{:S(2)}) collective-permute-start(bf16[32,1024]{1,0:T(8,128)(2,1)S(1)} %get-tuple-element.19), channel_id=1, source_target_pairs={{0,8},{4,12},{8,0},{12,4},{16,24},{20,28},{24,16},{28,20},{1,9},{5... | collective-permute-start | bytes 196616 | tf_op jit(solution)/shard_map/ppermute | solution.py:228
  8.9 4.3 %collective-permute-start.2 = (bf16[32,1024]{1,0:T(8,128)(2,1)S(1)}, bf16[32,1024]{1,0:T(8,128)(2,1)S(1)}, u32[]{:S(2)}, u32[]{:S(2)}) collective-permute-start(bf16[32,1024]{1,0:T(8,128)(2,1)S(1)} %get-tuple-element.20), channel_id=1, source_target_pairs={{0,16},{4,20},{8,24},{12,28},{16,0},{20,4},{24,8},{28,12},{1,17},{... | collective-permute-start | bytes 196616 | tf_op jit(solution)/shard_map/ppermute | solution.py:228
  10.5 5.2 %collective-permute-start.3 = (bf16[32,1024]{1,0:T(8,128)(2,1)S(1)}, bf16[32,1024]{1,0:T(8,128)(2,1)S(1)}, u32[]{:S(2)}, u32[]{:S(2)}) collective-permute-start(bf16[32,1024]{1,0:T(8,128)(2,1)S(1)} %pad_maximum_fusion.2), channel_id=1, source_target_pairs={{0,24},{4,28},{8,16},{12,20},{16,8},{20,12},{24,0},{28,4},{1,25},{... | collective-permute-start | bytes 196616 | tf_op jit(solution)/shard_map/ppermute | solution.py:228
  10.5 1.2 %collective-permute-start.4 = (bf16[16,1024]{1,0:T(8,128)(2,1)S(1)}, bf16[16,1024]{1,0:T(8,128)(2,1)S(1)}, u32[]{:S(2)}, u32[]{:S(2)}) collective-permute-start(bf16[16,1024]{1,0:T(8,128)(2,1)S(1)} %get-tuple-element.22), channel_id=1, source_target_pairs={{0,4},{4,0},{8,12},{12,8},{16,20},{20,16},{24,28},{28,24},{1,5},{5... | collective-permute-start | bytes 98312 | tf_op jit(solution)/shard_map/ppermute | solution.py:230

commit v16 on v10

--- a/solution.py
+++ b/solution.py
@@ -48,8 +48,8 @@
     disp_ref, comb_ref, my_tok_ref, my_grad_ref, *rest,
 ):
     outer, inner = levels(n_expert)
-    leave_refs = rest[:inner]
-    send_ref, disp_all, comb_all = rest[inner:]
+    leave_refs = rest[:outer]
+    send_ref, disp_all, comb_all = rest[outer:]
     slots = keys_ref.shape[0]
     keys = keys_ref[...]
     slot_rows = [[], []]
@@ -77,7 +77,7 @@
     for i in range(inner):
         for j in range(outer):
             to = partner(c, j, outer) * inner + lax.rem(l + i, inner)
-            leave_refs[i][j * block : (j + 1) * block] = send_ref[
+            leave_refs[j][i * block : (i + 1) * block] = send_ref[
                 pl.ds(pl.multiple_of(to * block, block), block)
             ]
     first = lax.axis_index("hidden") * quarter
@@ -90,15 +90,15 @@
 
 def expert_kernel(images, n_expert, k, gb, win_ref, bin_ref, wout_ref, t_ref, *rest):
     outer, inner = levels(n_expert)
-    come_refs = rest[:outer]
-    back_ref, got_ref = rest[outer:]
+    come_refs = rest[: outer * inner]
+    back_ref, got_ref = rest[outer * inner :]
     rows = k * images
     c, l = position(inner)
     block = got_ref.shape[1]
     for j in range(outer):
         source = partner(c, j, outer, True) * inner
         for i in range(inner):
-            got_ref[source + lax.rem(l + i, inner)] = come_refs[j][i * block : (i + 1) * block]
+            got_ref[source + lax.rem(l + i, inner)] = come_refs[i * outer + j][:block]
     width = got_ref.shape[2]
     total = n_expert * rows
     got = got_ref[...]
@@ -195,9 +195,9 @@
             jax.ShapeDtypeStruct((quarter, positions, width), BF),
             jax.ShapeDtypeStruct((quarter, positions, width), BF),
         )
-        + (jax.ShapeDtypeStruct((outer * send_rows, width), BF),) * inner,
+        + (jax.ShapeDtypeStruct((inner * send_rows, width), BF),) * outer,
         in_specs=[vmem] * 4,
-        out_specs=(vmem,) * (4 + inner),
+        out_specs=(vmem,) * (4 + outer),
         scratch_shapes=[pltpu.VMEM((n_expert * send_rows, width), BF)]
         + [pltpu.VMEM((images, slots, positions), BF)] * 2,
         compiler_params=pltpu.CompilerParams(vmem_limit_bytes=12 << 20),
@@ -206,15 +206,13 @@
     )(tokens, out_grad, keys, perm)
 
     everyone = [(c, l) for c in range(outer) for l in range(inner)]
-    held = leave[:1]
+    come = leave[:1]
+    for j in range(1, outer):
+        pairs = [(c * inner + l, partner(c, j, outer) * inner + l) for c, l in everyone]
+        come.append(lax.ppermute(leave[j], "expert", pairs))
     if inner == 2:
-        pairs = [(c * inner + l, c * inner + 1 - l) for c, l in everyone]
-        held.append(lax.ppermute(leave[1], "expert", pairs))
-    come = []
-    for j in range(outer):
-        both = jnp.concatenate([r[j * send_rows : (j + 1) * send_rows] for r in held])
-        pairs = [(c * inner + l, partner(c, j, outer) * inner + l) for c, l in everyone]
-        come.append(lax.ppermute(both, "expert", pairs) if j else both)
+        swap = [(c * inner + l, c * inner + 1 - l) for c, l in everyone]
+        come += [lax.ppermute(x[send_rows:], "expert", swap) for x in come]
 
     order = np.arange(2 * k * 2 * gb * images).reshape(2, 2, gb, k, n_hidden, quarter)
     order = order.transpose(2, 4, 0, 3, 5, 1)
@@ -223,7 +221,7 @@
     back = pl.pallas_call(
         functools.partial(expert_kernel, images, n_expert, k, gb),
         out_shape=jax.ShapeDtypeStruct((n_all * back_rows, half), BF),
-        in_specs=[vmem] * (4 + outer),
+        in_specs=[vmem] * (4 + len(come)),
         out_specs=vmem,
         scratch_shapes=[pltpu.VMEM((n_expert, send_rows, width), BF)],
         compiler_params=pltpu.CompilerParams(vmem_limit_bytes=20 << 20),

time: 35.8 us -> 35.6 us (level)
  starting transfers between devices: 5 us -> 4.62 us
    ppermute x4 -> x7, starting transfers between devices: 5 us -> 4.62 us  [the longest x3 4.54 us: local(): come.append(lax.ppermute(leave[j], 'expert', pairs))]
    ppermute x4 -> x7, waiting for transfers between devices: 6.07 us -> 6.29 us  [the longest x3 5.12 us: local(): come.append(lax.ppermute(leave[j], 'expert', pairs))]
  transfers between devices with their start and end apart: 4 -> 7, of which waited for: 4 -> 4; matrix products, arithmetic and copies ran while one was open for 0% -> 0% of each run, Pallas kernels for 0% -> 0%
where the time goes in v16:
time: 35.6 us; the launch traced here: 35.4 us
  blocking collectives  14 us (39%)
  Pallas kernels  7.59 us (21%)
  waiting for transfers between devices  6.29 us (18%)
  starting transfers between devices  4.62 us (13%)
  local copies, waits for them, and re-layouts  2.81 us (8%)
    all_to_all x1, blocking collectives, local(): lax.all_to_all(back.reshape(n_all, back_rows, half), ('expert', 'hidden')...  14 us
    ppermute x3, waiting for transfers between devices, local(): come.append(lax.ppermute(leave[j], 'expert', pairs))  5.12 us
    ppermute x3, starting transfers between devices, local(): come.append(lax.ppermute(leave[j], 'expert', pairs))  4.54 us
    pallas_call x1, Pallas kernels, local(): pl.pallas_call(functools.partial(expert_kernel, images, n_expert, k, gb),...  4.34 us
    unnamed x20, local copies, waits for them, and re-layouts  2.8 us
    pallas_call x1, Pallas kernels, local(): pl.pallas_call(functools.partial(dispatch_kernel, images, quarter, k, gb,...  1.66 us
    pallas_call x1, Pallas kernels, local(): pl.pallas_call(functools.partial(final_kernel, quarter, k, gb), out_shape...  1.58 us
    ppermute x4, waiting for transfers between devices, local(): come += [lax.ppermute(x[send_rows:], 'expert', swap) for x in come]  1.17 us
  transfers between devices with their start and end apart: 7, of which 4 were waited for; matrix products, arithmetic and copies ran while one was open for 0% of the time, Pallas kernels for 0%

profile of v16, /device:TPU:0, one launch (start us, length us, event | category | flops | bytes accessed | tf_op | source)
XLA Modules:
  0.0 35.4 jit_solution(1451417938501484712)
XLA Ops:
  0.0 0.0 copy-start.8
  0.0 2.0 %copy.11.tok_ref = bf16[4,196,1024]{2,1,0:T(8,128)(2,1)S(1)} copy(bf16[4,196,1024]{2,0,1:T(4,128)(2,1)} %param.10) | data formatting | bytes 3211264 | tf_op args[0]
  2.0 0.0 copy-done.8
  2.0 0.0 copy-start.4
  2.0 0.0 copy-start.7
  2.1 0.5 %copy.12.grad_ref = bf16[4,196,1024]{2,1,0:T(8,128)(2,1)S(1)} copy(bf16[4,196,1024]{2,0,1:T(4,128)(2,1)S(1)} %copy-done.8) | data formatting | bytes 3211264 | tf_op args[6]
  2.5 0.3 copy-done.4
  2.8 0.0 copy-done.7
  2.8 0.0 copy-start
  2.8 0.0 copy-start.1
  2.8 0.0 copy-start.2
  2.8 0.0 copy-start.6
  2.8 1.7 %dispatch.1 = (bf16[1,16,196]{2,1,0:T(8,128)(2,1)S(1)}, bf16[1,16,196]{2,1,0:T(8,128)(2,1)S(1)}, bf16[1,196,1024]{2,1,0:T(8,128)(2,1)S(1)}, bf16[1,196,1024]{2,1...) custom-call(bf16[4,196,1024]{2,1,0:T(8,128)(2,1)S(1)} %copy.11.tok_r, ...), custom_call_target="tpu_custom_call" | custom-call | flops 8000000000 | tf_op jit(solution)/shard_map/dispatch/pallas_call | solution.py:190
  4.5 3.0 %collective-permute-start = (bf16[32,1024]{1,0:T(8,128)(2,1)S(1)}, bf16[32,1024]{1,0:T(8,128)(2,1)S(1)}, u32[]{:S(2)}, u32[]{:S(2)}) collective-permute-start(bf16[32,1024]{1,0:T(8,128)(2,1)S(1)} %get-tuple-element.14), channel_id=1, source_target_pairs={{0,8},{4,12},{8,0},{12,4},{16,24},{20,28},{24,16},{28,20},{1,9},{5... | collective-permute-start | bytes 196616 | tf_op jit(solution)/shard_map/ppermute | solution.py:212
  7.5 1.5 %collective-permute-start.1 = (bf16[32,1024]{1,0:T(8,128)(2,1)S(1)}, bf16[32,1024]{1,0:T(8,128)(2,1)S(1)}, u32[]{:S(2)}, u32[]{:S(2)}) collective-permute-start(bf16[32,1024]{1,0:T(8,128)(2,1)S(1)} %get-tuple-element.15), channel_id=1, source_target_pairs={{0,16},{4,20},{8,24},{12,28},{16,0},{20,4},{24,8},{28,12},{1,17},{... | collective-permute-start | bytes 196616 | tf_op jit(solution)/shard_map/ppermute | solution.py:212
  9.0 0.0 collective-permute-start.2
  9.0 0.0 collective-permute-start.3
  9.0 0.8 %collective-permute-done.rest_1_ = bf16[32,1024]{1,0:T(8,128)(2,1)S(1)} collective-permute-done((bf16[32,1024]{1,0:T(8,128)(2,1)S(1)}, bf16[32,1024]{1,0:T(8,128)(2,1)S(1)}, u32[]{:S(2)}, u32[]{:S(2)}) %collective-permute-start) | collective-permute-done | bytes 65568 | tf_op jit(solution)/shard_map/ppermute | solution.py:212
  9.9 0.0 collective-permute-start.4
  9.9 1.9 %collective-permute-done.1.rest_2_ = bf16[32,1024]{1,0:T(8,128)(2,1)S(1)} collective-permute-done((bf16[32,1024]{1,0:T(8,128)(2,1)S(1)}, bf16[32,1024]{1,0:T(8,128)(2,1)S(1)}, u32[]{:S(2)}, u32[]{:S(2)}) %collective-permute-start.1) | collective-permute-done | bytes 65568 | tf_op jit(solution)/shard_map/ppermute | solution.py:212
  11.8 0.0 collective-permute-start.5
  11.8 2.4 %collective-permute-done.2.rest_3_ = bf16[32,1024]{1,0:T(8,128)(2,1)S(1)} collective-permute-done((bf16[32,1024]{1,0:T(8,128)(2,1)S(1)}, bf16[32,1024]{1,0:T(8,128)(2,1)S(1)}, u32[]{:S(2)}, u32[]{:S(2)}) %collective-permute-start.2) | collective-permute-done | bytes 65568 | tf_op jit(solution)/shard_map/ppermute | solution.py:212
  14.2 0.0 copy-start.3
  14.2 0.0 copy-start.5
  14.2 0.1 collective-permute-start.6
  14.3 0.0 collective-permute-done.3.rest_4_
  14.3 0.0 collective-permute-done.4.rest_5_
  14.3 0.0 collective-permute-done.5.rest_6_
  14.3 1.2 %collective-permute-done.6.rest_7_ = bf16[16,1024]{1,0:T(8,128)(2,1)S(1)} collective-permute-done((bf16[16,1024]{1,0:T(8,128)(2,1)S(1)}, bf16[16,1024]{1,0:T(8,128)(2,1)S(1)}, u32[]{:S(2)}, u32[]{:S(2)}) %collective-permute-start.6) | collective-permute-done | bytes 32800 | tf_op jit(solution)/shard_map/ppermute | solution.py:215
  15.5 0.0 copy-done
  15.5 0.0 copy-done.1
  15.5 0.0 copy-done.2
  15.5 0.0 copy-done.6
  15.5 4.3 %experts.1 = bf16[256,512]{1,0:T(8,128)(2,1)S(1)} custom-call(bf16[2,1024,1024]{2,1,0:T(8,128)(2,1)S(1)} %copy-done, f32[2,1024]{1,0:T(2,128)S(1)} %copy-done.6, bf16[2,1024,1024]{2,1,0:T(8,128)(2,1)S(1)} %copy-done.1, bf16[256,256]{1,0:T(8,128)(2,1)S(1)} %copy-done.2, bf16[32,1024]{1,0:T(8,128)(2,1)S(1)} %get-tuple-element.13.rest_0_, ...), custom_call_target="tpu_custom_call" | custom-call | tf_op jit(solution)/shard_map/experts/pallas_call | solution.py:221
  19.8 14.0 %all_to_all.5 = bf16[32,8,512]{2,1,0:T(8,128)(2,1)S(1)} all-to-all(bf16[32,8,512]{2,1,0:T(8,128)(2,1)S(1)} %bitcast.4), channel_id=1, replica_groups=mesh['expert'=8,'hidden'=4] {'expert','hidden'}, dimensions={0} | all-to-all | bytes 524288 | tf_op jit(solution)/shard_map/all_to_all | solution.py:231
  33.8 0.0 copy-done.3
  33.8 0.0 copy-done.5
  33.8 1.6 %tokens_back.1 = bf16[1,196,1024]{2,1,0:T(8,128)(2,1)} custom-call(bf16[256,512]{1,0:T(8,128)(2,1)S(1)} %bitcast.3, f32[16,1024]{1,0:T(8,128)S(1)} %copy-done.3, bf16[1,196,1024]{2,1,0:T(8,128)(2,1)S(1)} %get-tuple-element.17.tok_ref, bf16[1,196,1024]{2,1,0:T(8,128)(2,1)S(1)} %get-tuple-element.18.grad_ref, ...), custom_call_target="tpu_custom_call" | custom-call | tf_op jit(solution)/shard_map/tokens_back/pallas_call | solution.py:242
  (4 shorter events, 0.0 us)
Async XLA Ops:
  0.0 2.0 %copy-start.8 = (bf16[4,196,1024]{2,0,1:T(4,128)(2,1)S(1)}, bf16[4,196,1024]{2,0,1:T(4,128)(2,1)}, u32[]{:S(2)}) copy-start(bf16[4,196,1024]{2,0,1:T(4,128)(2,1)} %param.16) | copy-start | bytes 4816900
  2.0 0.8 %copy-start.4 = (bf16[1024,16]{0,1:T(8,128)(2,1)S(1)}, bf16[1024,16]{0,1:T(8,128)(2,1)}, u32[]{:S(2)}) copy-start(bf16[1024,16]{0,1:T(8,128)(2,1)} %param.11) | copy-start | bytes 98308
  2.0 0.8 %copy-start.7 = (bf16[128,128]{1,0:T(8,128)(2,1)S(1)}, bf16[128,128]{1,0:T(8,128)(2,1)}, u32[]{:S(2)}) copy-start(bf16[128,128]{1,0:T(8,128)(2,1)} %constant.6.clone.perm_ref) | copy-start | bytes 98308
  2.8 12.7 %copy-start = (bf16[2,1024,1024]{2,1,0:T(8,128)(2,1)S(1)}, bf16[2,1024,1024]{2,1,0:T(8,128)(2,1)}, u32[]{:S(2)}) copy-start(bf16[2,1024,1024]{2,1,0:T(8,128)(2,1)} %win_ref.1) | copy-start | bytes 12582916
  2.8 12.7 %copy-start.1 = (bf16[2,1024,1024]{2,1,0:T(8,128)(2,1)S(1)}, bf16[2,1024,1024]{2,1,0:T(8,128)(2,1)}, u32[]{:S(2)}) copy-start(bf16[2,1024,1024]{2,1,0:T(8,128)(2,1)} %wout_ref.1) | copy-start | bytes 12582916
  2.8 12.7 %copy-start.2 = (bf16[256,256]{1,0:T(8,128)(2,1)S(1)}, bf16[256,256]{1,0:T(8,128)(2,1)}, u32[]{:S(2)}) copy-start(bf16[256,256]{1,0:T(8,128)(2,1)} %constant.7.clone.t_ref) | copy-start | bytes 393220
  2.8 12.7 %copy-start.6 = (f32[2,1024]{1,0:T(2,128)S(1)}, f32[2,1024]{1,0:T(2,128)}, u32[]{:S(2)}) copy-start(f32[2,1024]{1,0:T(2,128)} %bin_ref.1) | copy-start | bytes 24580
  4.5 5.4 %collective-permute-start = (bf16[32,1024]{1,0:T(8,128)(2,1)S(1)}, bf16[32,1024]{1,0:T(8,128)(2,1)S(1)}, u32[]{:S(2)}, u32[]{:S(2)}) collective-permute-start(bf16[32,1024]{1,0:T(8,128)(2,1)S(1)} %get-tuple-element.14), channel_id=1, source_target_pairs={{0,8},{4,12},{8,0},{12,4},{16,24},{20,28},{24,16},{28,20},{1,9},{5... | collective-permute-start | bytes 196616 | tf_op jit(solution)/shard_map/ppermute | solution.py:212
  7.5 4.3 %collective-permute-start.1 = (bf16[32,1024]{1,0:T(8,128)(2,1)S(1)}, bf16[32,1024]{1,0:T(8,128)(2,1)S(1)}, u32[]{:S(2)}, u32[]{:S(2)}) collective-permute-start(bf16[32,1024]{1,0:T(8,128)(2,1)S(1)} %get-tuple-element.15), channel_id=1, source_target_pairs={{0,16},{4,20},{8,24},{12,28},{16,0},{20,4},{24,8},{28,12},{1,17},{... | collective-permute-start | bytes 196616 | tf_op jit(solution)/shard_map/ppermute | solution.py:212
  9.0 5.2 %collective-permute-start.2 = (bf16[32,1024]{1,0:T(8,128)(2,1)S(1)}, bf16[32,1024]{1,0:T(8,128)(2,1)S(1)}, u32[]{:S(2)}, u32[]{:S(2)}) collective-permute-start(bf16[32,1024]{1,0:T(8,128)(2,1)S(1)} %get-tuple-element.16), channel_id=1, source_target_pairs={{0,24},{4,28},{8,16},{12,20},{16,8},{20,12},{24,0},{28,4},{1,25},{... | collective-permute-start | bytes 196616 | tf_op jit(solution)/shard_map/ppermute | solution.py:212
  9.0 5.2 %collective-permute-start.3 = (bf16[16,1024]{1,0:T(8,128)(2,1)S(1)}, bf16[16,1024]{1,0:T(8,128)(2,1)S(1)}, u32[]{:S(2)}, u32[]{:S(2)}) collective-permute-start(bf16[16,1024]{1,0:T(8,128)(2,1)S(1)} %slice.12), channel_id=1, source_target_pairs={{0,4},{4,0},{8,12},{12,8},{16,20},{20,16},{24,28},{28,24},{1,5},{5... | collective-permute-start | bytes 98312 | tf_op jit(solution)/shard_map/ppermute | solution.py:215
  9.9 4.4 %collective-permute-start.4 = (bf16[16,1024]{1,0:T(8,128)(2,1)S(1)}, bf16[16,1024]{1,0:T(8,128)(2,1)S(1)}, u32[]{:S(2)}, u32[]{:S(2)}) collective-permute-start(bf16[16,1024]{1,0:T(8,128)(2,1)S(1)} %slice.16), channel_id=1, source_target_pairs={{0,4},{4,0},{8,12},{12,8},{16,20},{20,16},{24,28},{28,24},{1,5},{5... | collective-permute-start | bytes 98312 | tf_op jit(solution)/shard_map/ppermute | solution.py:215
  11.8 2.5 %collective-permute-start.5 = (bf16[16,1024]{1,0:T(8,128)(2,1)S(1)}, bf16[16,1024]{1,0:T(8,128)(2,1)S(1)}, u32[]{:S(2)}, u32[]{:S(2)}) collective-permute-start(bf16[16,1024]{1,0:T(8,128)(2,1)S(1)} %slice.17), channel_id=1, source_target_pairs={{0,4},{4,0},{8,12},{12,8},{16,20},{20,16},{24,28},{28,24},{1,5},{5... | collective-permute-start | bytes 98312 | tf_op jit(solution)/shard_map/ppermute | solution.py:215
  14.2 19.6 %copy-start.3 = (f32[16,1024]{1,0:T(8,128)S(1)}, f32[16,1024]{1,0:T(8,128)}, u32[]{:S(2)}) copy-start(f32[16,1024]{1,0:T(8,128)} %bias_ref.1) | copy-start | bytes 196612
  14.2 19.6 %copy-start.5 = (bf16[64,256]{1,0:T(8,128)(2,1)S(1)}, bf16[64,256]{1,0:T(8,128)(2,1)}, u32[]{:S(2)}) copy-start(bf16[64,256]{1,0:T(8,128)(2,1)} %constant.8.clone.sel_ref) | copy-start | bytes 98308
  14.2 1.3 %collective-permute-start.6 = (bf16[16,1024]{1,0:T(8,128)(2,1)S(1)}, bf16[16,1024]{1,0:T(8,128)(2,1)S(1)}, u32[]{:S(2)}, u32[]{:S(2)}) collective-permute-start(bf16[16,1024]{1,0:T(8,128)(2,1)S(1)} %slice.18), channel_id=1, source_target_pairs={{0,4},{4,0},{8,12},{12,8},{16,20},{20,16},{24,28},{28,24},{1,5},{5... | collective-permute-start | bytes 98312 | tf_op jit(solution)/shard_map/ppermute | solution.py:215

commit v17 on v16

--- a/solution.py
+++ b/solution.py
@@ -36,6 +36,16 @@
 def levels(n_expert):
     inner = 2 if n_expert % 2 == 0 else 1
     return n_expert // inner, inner
+
+
+def turn(l, j, outer):
+    if j == 0:
+        return 0
+    steps = [outer - 1, *range(1, outer - 1)]
+    mine, other = steps[j - 1], steps[j - 2]
+    if isinstance(l, int):
+        return other if l else mine
+    return jnp.where(l == 1, other, mine)
 
 
 def position(inner):
@@ -76,7 +86,7 @@
     c, l = position(inner)
     for i in range(inner):
         for j in range(outer):
-            to = partner(c, j, outer) * inner + lax.rem(l + i, inner)
+            to = partner(c, turn(l, j, outer), outer) * inner + lax.rem(l + i, inner)
             leave_refs[j][i * block : (i + 1) * block] = send_ref[
                 pl.ds(pl.multiple_of(to * block, block), block)
             ]
@@ -96,9 +106,10 @@
     c, l = position(inner)
     block = got_ref.shape[1]
     for j in range(outer):
-        source = partner(c, j, outer, True) * inner
         for i in range(inner):
-            got_ref[source + lax.rem(l + i, inner)] = come_refs[i * outer + j][:block]
+            core = lax.rem(l + i, inner)
+            source = partner(c, turn(core, j, outer), outer, True) * inner + core
+            got_ref[source] = come_refs[i * outer + j][:block]
     width = got_ref.shape[2]
     total = n_expert * rows
     got = got_ref[...]
@@ -201,14 +212,15 @@
         scratch_shapes=[pltpu.VMEM((n_expert * send_rows, width), BF)]
         + [pltpu.VMEM((images, slots, positions), BF)] * 2,
         compiler_params=pltpu.CompilerParams(vmem_limit_bytes=12 << 20),
-        cost_estimate=pl.CostEstimate(flops=8000000000, bytes_accessed=0, transcendentals=0),
         name="dispatch",
     )(tokens, out_grad, keys, perm)
 
     everyone = [(c, l) for c in range(outer) for l in range(inner)]
     come = leave[:1]
     for j in range(1, outer):
-        pairs = [(c * inner + l, partner(c, j, outer) * inner + l) for c, l in everyone]
+        pairs = [
+            (c * inner + l, partner(c, turn(l, j, outer), outer) * inner + l) for c, l in everyone
+        ]
         come.append(lax.ppermute(leave[j], "expert", pairs))
     if inner == 2:
         swap = [(c * inner + l, c * inner + 1 - l) for c, l in everyone]

time: 35.6 us -> 37 us (1.039)
  local copies, waits for them, and re-layouts: 2.81 us -> 4.14 us
  blocking collectives: 14 us -> 15 us
  waiting for transfers between devices: 6.29 us -> 5.31 us
    unnamed x20 -> x18, local copies, waits for them, and re-layouts: 2.8 us -> 4.13 us
    all_to_all x1, blocking collectives: 14 us -> 15 us  [local(): lax.all_to_all(back.reshape(n_all, back_rows, half), ('expert', 'hidden')...]
    ppermute x3, waiting for transfers between devices: 5.12 us -> 4.14 us  [local(): come.append(lax.ppermute(leave[j], 'expert', pairs))]
  transfers between devices with their start and end apart: 7 -> 7, of which waited for: 4 -> 5; matrix products, arithmetic and copies ran while one was open for 0% -> 0% of each run, Pallas kernels for 0% -> 0%
where the time goes in v17:
time: 37 us; the launch traced here: 36.8 us
  blocking collectives  15 us (41%)
  Pallas kernels  7.59 us (21%)
  waiting for transfers between devices  5.31 us (14%)
  starting transfers between devices  4.68 us (13%)
  local copies, waits for them, and re-layouts  4.14 us (11%)
    all_to_all x1, blocking collectives, local(): lax.all_to_all(back.reshape(n_all, back_rows, half), ('expert', 'hidden')...  15 us
    ppermute x3, starting transfers between devices, local(): come.append(lax.ppermute(leave[j], 'expert', pairs))  4.61 us
    pallas_call x1, Pallas kernels, local(): pl.pallas_call(functools.partial(expert_kernel, images, n_expert, k, gb),...  4.34 us
    ppermute x3, waiting for transfers between devices, local(): come.append(lax.ppermute(leave[j], 'expert', pairs))  4.14 us
    unnamed x18, local copies, waits for them, and re-layouts  4.13 us
    pallas_call x1, Pallas kernels, local(): pl.pallas_call(functools.partial(dispatch_kernel, images, quarter, k, gb,...  1.66 us
    pallas_call x1, Pallas kernels, local(): pl.pallas_call(functools.partial(final_kernel, quarter, k, gb), out_shape...  1.59 us
    ppermute x4, waiting for transfers between devices, local(): come += [lax.ppermute(x[send_rows:], 'expert', swap) for x in come]  1.18 us
  transfers between devices with their start and end apart: 7, of which 5 were waited for; matrix products, arithmetic and copies ran while one was open for 0% of the time, Pallas kernels for 0%

profile of v17, /device:TPU:0, one launch (start us, length us, event | category | flops | bytes accessed | tf_op | source)
XLA Modules:
  0.0 36.8 jit_solution(111633826613269182)
XLA Ops:
  0.0 0.0 copy-start.2
  0.0 0.0 copy-start.5
  0.0 0.0 copy-start.1
  0.0 2.0 %copy.11.tok_ref = bf16[4,196,1024]{2,1,0:T(8,128)(2,1)S(1)} copy(bf16[4,196,1024]{2,0,1:T(4,128)(2,1)} %param.10) | data formatting | bytes 3211264 | tf_op args[0]
  2.1 0.0 copy-start
  2.1 2.0 %copy.12.grad_ref = bf16[4,196,1024]{2,1,0:T(8,128)(2,1)S(1)} copy(bf16[4,196,1024]{2,0,1:T(4,128)(2,1)} %param.16) | data formatting | bytes 3211264 | tf_op args[6]
  4.1 0.0 copy-done.2
  4.1 0.0 copy-done.5
  4.1 0.0 copy-start.3
  4.2 0.0 copy-start.7
  4.2 1.7 %dispatch.1 = (bf16[1,16,196]{2,1,0:T(8,128)(2,1)S(1)}, bf16[1,16,196]{2,1,0:T(8,128)(2,1)S(1)}, bf16[1,196,1024]{2,1,0:T(8,128)(2,1)S(1)}, bf16[1,196,1024]{2,1...) custom-call(bf16[4,196,1024]{2,1,0:T(8,128)(2,1)S(1)} %copy.11.tok_r, ...), custom_call_target="tpu_custom_call" | custom-call | tf_op jit(solution)/shard_map/dispatch/pallas_call | solution.py:201
  5.8 4.0 %collective-permute-start = (bf16[32,1024]{1,0:T(8,128)(2,1)S(1)}, bf16[32,1024]{1,0:T(8,128)(2,1)S(1)}, u32[]{:S(2)}, u32[]{:S(2)}) collective-permute-start(bf16[32,1024]{1,0:T(8,128)(2,1)S(1)} %get-tuple-element.14), channel_id=1, source_target_pairs={{0,24},{4,20},{8,16},{12,28},{16,8},{20,4},{24,0},{28,12},{1,25},{... | collective-permute-start | bytes 196616 | tf_op jit(solution)/shard_map/ppermute | solution.py:224
  9.8 0.5 %collective-permute-start.1 = (bf16[32,1024]{1,0:T(8,128)(2,1)S(1)}, bf16[32,1024]{1,0:T(8,128)(2,1)S(1)}, u32[]{:S(2)}, u32[]{:S(2)}) collective-permute-start(bf16[32,1024]{1,0:T(8,128)(2,1)S(1)} %get-tuple-element.15), channel_id=1, source_target_pairs={{0,8},{4,28},{8,0},{12,20},{16,24},{20,12},{24,16},{28,4},{1,9},{5... | collective-permute-start | bytes 196616 | tf_op jit(solution)/shard_map/ppermute | solution.py:224
  10.3 0.1 collective-permute-start.2
  10.5 0.0 collective-permute-start.3
  10.5 1.8 %collective-permute-done.rest_1_ = bf16[32,1024]{1,0:T(8,128)(2,1)S(1)} collective-permute-done((bf16[32,1024]{1,0:T(8,128)(2,1)S(1)}, bf16[32,1024]{1,0:T(8,128)(2,1)S(1)}, u32[]{:S(2)}, u32[]{:S(2)}) %collective-permute-start) | collective-permute-done | bytes 65568 | tf_op jit(solution)/shard_map/ppermute | solution.py:224
  12.2 0.0 collective-permute-start.4
  12.2 1.8 %collective-permute-done.1.rest_2_ = bf16[32,1024]{1,0:T(8,128)(2,1)S(1)} collective-permute-done((bf16[32,1024]{1,0:T(8,128)(2,1)S(1)}, bf16[32,1024]{1,0:T(8,128)(2,1)S(1)}, u32[]{:S(2)}, u32[]{:S(2)}) %collective-permute-start.1) | collective-permute-done | bytes 65568 | tf_op jit(solution)/shard_map/ppermute | solution.py:224
  14.1 0.0 collective-permute-start.5
  14.1 0.5 %collective-permute-done.2.rest_3_ = bf16[32,1024]{1,0:T(8,128)(2,1)S(1)} collective-permute-done((bf16[32,1024]{1,0:T(8,128)(2,1)S(1)}, bf16[32,1024]{1,0:T(8,128)(2,1)S(1)}, u32[]{:S(2)}, u32[]{:S(2)}) %collective-permute-start.2) | collective-permute-done | bytes 65568 | tf_op jit(solution)/shard_map/ppermute | solution.py:224
  14.6 0.0 copy-start.4
  14.6 0.0 copy-start.6
  14.6 0.1 collective-permute-start.6
  14.7 0.0 collective-permute-done.3.rest_4_
  14.7 0.0 collective-permute-done.4.rest_5_
  14.7 0.6 %collective-permute-done.5.rest_6_ = bf16[16,1024]{1,0:T(8,128)(2,1)S(1)} collective-permute-done((bf16[16,1024]{1,0:T(8,128)(2,1)S(1)}, bf16[16,1024]{1,0:T(8,128)(2,1)S(1)}, u32[]{:S(2)}, u32[]{:S(2)}) %collective-permute-start.5) | collective-permute-done | bytes 32800 | tf_op jit(solution)/shard_map/ppermute | solution.py:227
  15.3 0.6 %collective-permute-done.6.rest_7_ = bf16[16,1024]{1,0:T(8,128)(2,1)S(1)} collective-permute-done((bf16[16,1024]{1,0:T(8,128)(2,1)S(1)}, bf16[16,1024]{1,0:T(8,128)(2,1)S(1)}, u32[]{:S(2)}, u32[]{:S(2)}) %collective-permute-start.6) | collective-permute-done | bytes 32800 | tf_op jit(solution)/shard_map/ppermute | solution.py:227
  15.9 0.0 copy-done.1
  15.9 0.0 copy-done
  15.9 0.0 copy-done.3
  15.9 0.0 copy-done.7
  15.9 4.3 %experts.1 = bf16[256,512]{1,0:T(8,128)(2,1)S(1)} custom-call(bf16[2,1024,1024]{2,1,0:T(8,128)(2,1)S(1)} %copy-done, f32[2,1024]{1,0:T(2,128)S(1)} %copy-done.7, bf16[2,1024,1024]{2,1,0:T(8,128)(2,1)S(1)} %copy-done.1, bf16[256,256]{1,0:T(8,128)(2,1)S(1)} %copy-done.3, bf16[32,1024]{1,0:T(8,128)(2,1)S(1)} %get-tuple-element.13.rest_0_, ...), custom_call_target="tpu_custom_call" | custom-call | tf_op jit(solution)/shard_map/experts/pallas_call | solution.py:233
  20.3 15.0 %all_to_all.5 = bf16[32,8,512]{2,1,0:T(8,128)(2,1)S(1)} all-to-all(bf16[32,8,512]{2,1,0:T(8,128)(2,1)S(1)} %bitcast.4), channel_id=1, replica_groups=mesh['expert'=8,'hidden'=4] {'expert','hidden'}, dimensions={0} | all-to-all | bytes 524288 | tf_op jit(solution)/shard_map/all_to_all | solution.py:243
  35.2 0.0 copy-done.4
  35.3 0.0 copy-done.6
  35.3 1.6 %tokens_back.1 = bf16[1,196,1024]{2,1,0:T(8,128)(2,1)} custom-call(bf16[256,512]{1,0:T(8,128)(2,1)S(1)} %bitcast.3, f32[16,1024]{1,0:T(8,128)S(1)} %copy-done.4, bf16[1,196,1024]{2,1,0:T(8,128)(2,1)S(1)} %get-tuple-element.17.tok_ref, bf16[1,196,1024]{2,1,0:T(8,128)(2,1)S(1)} %get-tuple-element.18.grad_ref, ...), custom_call_target="tpu_custom_call" | custom-call | tf_op jit(solution)/shard_map/tokens_back/pallas_call | solution.py:254
  (4 shorter events, 0.0 us)
Async XLA Ops:
  0.0 4.1 %copy-start.2 = (bf16[1024,16]{0,1:T(8,128)(2,1)S(1)}, bf16[1024,16]{0,1:T(8,128)(2,1)}, u32[]{:S(2)}) copy-start(bf16[1024,16]{0,1:T(8,128)(2,1)} %param.11) | copy-start | bytes 98308
  0.0 4.1 %copy-start.5 = (bf16[128,128]{1,0:T(8,128)(2,1)S(1)}, bf16[128,128]{1,0:T(8,128)(2,1)}, u32[]{:S(2)}) copy-start(bf16[128,128]{1,0:T(8,128)(2,1)} %constant.6.clone.perm_ref) | copy-start | bytes 98308
  0.0 15.9 %copy-start.1 = (bf16[2,1024,1024]{2,1,0:T(8,128)(2,1)S(1)}, bf16[2,1024,1024]{2,1,0:T(8,128)(2,1)}, u32[]{:S(2)}) copy-start(bf16[2,1024,1024]{2,1,0:T(8,128)(2,1)} %wout_ref.1) | copy-start | bytes 12582916
  2.1 13.8 %copy-start = (bf16[2,1024,1024]{2,1,0:T(8,128)(2,1)S(1)}, bf16[2,1024,1024]{2,1,0:T(8,128)(2,1)}, u32[]{:S(2)}) copy-start(bf16[2,1024,1024]{2,1,0:T(8,128)(2,1)} %win_ref.1) | copy-start | bytes 12582916
  4.1 11.8 %copy-start.3 = (bf16[256,256]{1,0:T(8,128)(2,1)S(1)}, bf16[256,256]{1,0:T(8,128)(2,1)}, u32[]{:S(2)}) copy-start(bf16[256,256]{1,0:T(8,128)(2,1)} %constant.7.clone.t_ref) | copy-start | bytes 393220
  4.2 11.7 %copy-start.7 = (f32[2,1024]{1,0:T(2,128)S(1)}, f32[2,1024]{1,0:T(2,128)}, u32[]{:S(2)}) copy-start(f32[2,1024]{1,0:T(2,128)} %bin_ref.1) | copy-start | bytes 24580
  5.8 6.4 %collective-permute-start = (bf16[32,1024]{1,0:T(8,128)(2,1)S(1)}, bf16[32,1024]{1,0:T(8,128)(2,1)S(1)}, u32[]{:S(2)}, u32[]{:S(2)}) collective-permute-start(bf16[32,1024]{1,0:T(8,128)(2,1)S(1)} %get-tuple-element.14), channel_id=1, source_target_pairs={{0,24},{4,20},{8,16},{12,28},{16,8},{20,4},{24,0},{28,12},{1,25},{... | collective-permute-start | bytes 196616 | tf_op jit(solution)/shard_map/ppermute | solution.py:224
  9.8 4.3 %collective-permute-start.1 = (bf16[32,1024]{1,0:T(8,128)(2,1)S(1)}, bf16[32,1024]{1,0:T(8,128)(2,1)S(1)}, u32[]{:S(2)}, u32[]{:S(2)}) collective-permute-start(bf16[32,1024]{1,0:T(8,128)(2,1)S(1)} %get-tuple-element.15), channel_id=1, source_target_pairs={{0,8},{4,28},{8,0},{12,20},{16,24},{20,12},{24,16},{28,4},{1,9},{5... | collective-permute-start | bytes 196616 | tf_op jit(solution)/shard_map/ppermute | solution.py:224
  10.3 4.3 %collective-permute-start.2 = (bf16[32,1024]{1,0:T(8,128)(2,1)S(1)}, bf16[32,1024]{1,0:T(8,128)(2,1)S(1)}, u32[]{:S(2)}, u32[]{:S(2)}) collective-permute-start(bf16[32,1024]{1,0:T(8,128)(2,1)S(1)} %get-tuple-element.16), channel_id=1, source_target_pairs={{0,16},{4,12},{8,24},{12,4},{16,0},{20,28},{24,8},{28,20},{1,17},{... | collective-permute-start | bytes 196616 | tf_op jit(solution)/shard_map/ppermute | solution.py:224
  10.5 4.2 %collective-permute-start.3 = (bf16[16,1024]{1,0:T(8,128)(2,1)S(1)}, bf16[16,1024]{1,0:T(8,128)(2,1)S(1)}, u32[]{:S(2)}, u32[]{:S(2)}) collective-permute-start(bf16[16,1024]{1,0:T(8,128)(2,1)S(1)} %slice.12), channel_id=1, source_target_pairs={{0,4},{4,0},{8,12},{12,8},{16,20},{20,16},{24,28},{28,24},{1,5},{5... | collective-permute-start | bytes 98312 | tf_op jit(solution)/shard_map/ppermute | solution.py:227
  12.2 2.5 %collective-permute-start.4 = (bf16[16,1024]{1,0:T(8,128)(2,1)S(1)}, bf16[16,1024]{1,0:T(8,128)(2,1)S(1)}, u32[]{:S(2)}, u32[]{:S(2)}) collective-permute-start(bf16[16,1024]{1,0:T(8,128)(2,1)S(1)} %slice.16), channel_id=1, source_target_pairs={{0,4},{4,0},{8,12},{12,8},{16,20},{20,16},{24,28},{28,24},{1,5},{5... | collective-permute-start | bytes 98312 | tf_op jit(solution)/shard_map/ppermute | solution.py:227
  14.1 1.2 %collective-permute-start.5 = (bf16[16,1024]{1,0:T(8,128)(2,1)S(1)}, bf16[16,1024]{1,0:T(8,128)(2,1)S(1)}, u32[]{:S(2)}, u32[]{:S(2)}) collective-permute-start(bf16[16,1024]{1,0:T(8,128)(2,1)S(1)} %slice.17), channel_id=1, source_target_pairs={{0,4},{4,0},{8,12},{12,8},{16,20},{20,16},{24,28},{28,24},{1,5},{5... | collective-permute-start | bytes 98312 | tf_op jit(solution)/shard_map/ppermute | solution.py:227
  14.6 20.6 %copy-start.4 = (f32[16,1024]{1,0:T(8,128)S(1)}, f32[16,1024]{1,0:T(8,128)}, u32[]{:S(2)}) copy-start(f32[16,1024]{1,0:T(8,128)} %bias_ref.1) | copy-start | bytes 196612
  14.6 20.6 %copy-start.6 = (bf16[64,256]{1,0:T(8,128)(2,1)S(1)}, bf16[64,256]{1,0:T(8,128)(2,1)}, u32[]{:S(2)}) copy-start(bf16[64,256]{1,0:T(8,128)(2,1)} %constant.8.clone.sel_ref) | copy-start | bytes 98308
  14.6 1.3 %collective-permute-start.6 = (bf16[16,1024]{1,0:T(8,128)(2,1)S(1)}, bf16[16,1024]{1,0:T(8,128)(2,1)S(1)}, u32[]{:S(2)}, u32[]{:S(2)}) collective-permute-start(bf16[16,1024]{1,0:T(8,128)(2,1)S(1)} %slice.18), channel_id=1, source_target_pairs={{0,4},{4,0},{8,12},{12,8},{16,20},{20,16},{24,28},{28,24},{1,5},{5... | collective-permute-start | bytes 98312 | tf_op jit(solution)/shard_map/ppermute | solution.py:227

commit v18 on v16

--- a/solution.py
+++ b/solution.py
@@ -157,19 +157,16 @@
     for m in range(quarter):
         slot_out = (assemble(0, m) + bias_ref[...]).astype(BF)
         slot_in_grad = assemble(1, m).astype(BF)
-        comb_grad = mm(slot_out, grad_ref[m], NT)
-        disp_grad = mm(slot_in_grad, tok_ref[m], NT)
-        disp = disp_ref[m]
-        comb = comb_ref[m].astype(F32)
-        wide = disp.astype(F32)
-        logit_grad = comb * (comb_grad - jnp.sum(comb * comb_grad, axis=0, keepdims=True))
+        wide = disp_ref[m].astype(F32).T
+        comb = comb_ref[m].astype(F32).T
+        from_slots = mm(wide.astype(BF), slot_in_grad)
+        comb_grad = mm(grad_ref[m], slot_out, NT)
+        disp_grad = mm(tok_ref[m], slot_in_grad, NT)
+        logit_grad = comb * (comb_grad - jnp.sum(comb * comb_grad, axis=1, keepdims=True))
         logit_grad = logit_grad + wide * (
-            disp_grad - jnp.sum(wide * disp_grad, axis=1, keepdims=True)
-        )
-        logit_grad = logit_grad.astype(BF).astype(F32)
-        left = jnp.concatenate([wide, logit_grad], axis=0).T.astype(BF)
-        right = jnp.concatenate([slot_in_grad, keys], axis=0)
-        out_ref[m] = mm(left, right).astype(BF)
+            disp_grad - jnp.sum(wide * disp_grad, axis=0, keepdims=True)
+        )
+        out_ref[m] = (from_slots + mm(logit_grad.astype(BF), keys)).astype(BF)
 
 
 def local(n_expert, n_hidden, tokens, slot_keys, w_in, b_in, w_out, b_out, out_grad):

time: 35.6 us -> 35.6 us (level)
  no operation moved by 1% of the time
where the time goes in v18:
time: 35.6 us; the launch traced here: 35.5 us
  blocking collectives  14 us (39%)
  Pallas kernels  7.64 us (21%)
  waiting for transfers between devices  6.29 us (18%)
  starting transfers between devices  4.62 us (13%)
  local copies, waits for them, and re-layouts  2.81 us (8%)
    all_to_all x1, blocking collectives, local(): lax.all_to_all(back.reshape(n_all, back_rows, half), ('expert', 'hidden')...  14 us
    ppermute x3, waiting for transfers between devices, local(): come.append(lax.ppermute(leave[j], 'expert', pairs))  5.12 us
    ppermute x3, starting transfers between devices, local(): come.append(lax.ppermute(leave[j], 'expert', pairs))  4.54 us
    pallas_call x1, Pallas kernels, local(): pl.pallas_call(functools.partial(expert_kernel, images, n_expert, k, gb),...  4.34 us
    unnamed x20, local copies, waits for them, and re-layouts  2.8 us
    pallas_call x1, Pallas kernels, local(): pl.pallas_call(functools.partial(dispatch_kernel, images, quarter, k, gb,...  1.66 us
    pallas_call x1, Pallas kernels, local(): pl.pallas_call(functools.partial(final_kernel, quarter, k, gb), out_shape...  1.64 us
    ppermute x4, waiting for transfers between devices, local(): come += [lax.ppermute(x[send_rows:], 'expert', swap) for x in come]  1.17 us
  transfers between devices with their start and end apart: 7, of which 4 were waited for; matrix products, arithmetic and copies ran while one was open for 0% of the time, Pallas kernels for 0%

profile of v18, /device:TPU:0, one launch (start us, length us, event | category | flops | bytes accessed | tf_op | source)
XLA Modules:
  0.0 35.5 jit_solution(12005678414177658124)
XLA Ops:
  0.0 0.0 copy-start.8
  0.0 2.0 %copy.11.tok_ref = bf16[4,196,1024]{2,1,0:T(8,128)(2,1)S(1)} copy(bf16[4,196,1024]{2,0,1:T(4,128)(2,1)} %param.10) | data formatting | bytes 3211264 | tf_op args[0]
  2.0 0.0 copy-done.8
  2.0 0.0 copy-start.4
  2.0 0.0 copy-start.7
  2.1 0.5 %copy.12.grad_ref = bf16[4,196,1024]{2,1,0:T(8,128)(2,1)S(1)} copy(bf16[4,196,1024]{2,0,1:T(4,128)(2,1)S(1)} %copy-done.8) | data formatting | bytes 3211264 | tf_op args[6]
  2.5 0.3 copy-done.4
  2.8 0.0 copy-done.7
  2.8 0.0 copy-start
  2.8 0.0 copy-start.1
  2.8 0.0 copy-start.2
  2.8 0.0 copy-start.6
  2.8 1.7 %dispatch.1 = (bf16[1,16,196]{2,1,0:T(8,128)(2,1)S(1)}, bf16[1,16,196]{2,1,0:T(8,128)(2,1)S(1)}, bf16[1,196,1024]{2,1,0:T(8,128)(2,1)S(1)}, bf16[1,196,1024]{2,1...) custom-call(bf16[4,196,1024]{2,1,0:T(8,128)(2,1)S(1)} %copy.11.tok_r, ...), custom_call_target="tpu_custom_call" | custom-call | flops 8000000000 | tf_op jit(solution)/shard_map/dispatch/pallas_call | solution.py:187
  4.5 3.0 %collective-permute-start = (bf16[32,1024]{1,0:T(8,128)(2,1)S(1)}, bf16[32,1024]{1,0:T(8,128)(2,1)S(1)}, u32[]{:S(2)}, u32[]{:S(2)}) collective-permute-start(bf16[32,1024]{1,0:T(8,128)(2,1)S(1)} %get-tuple-element.14), channel_id=1, source_target_pairs={{0,8},{4,12},{8,0},{12,4},{16,24},{20,28},{24,16},{28,20},{1,9},{5... | collective-permute-start | bytes 196616 | tf_op jit(solution)/shard_map/ppermute | solution.py:209
  7.5 1.5 %collective-permute-start.1 = (bf16[32,1024]{1,0:T(8,128)(2,1)S(1)}, bf16[32,1024]{1,0:T(8,128)(2,1)S(1)}, u32[]{:S(2)}, u32[]{:S(2)}) collective-permute-start(bf16[32,1024]{1,0:T(8,128)(2,1)S(1)} %get-tuple-element.15), channel_id=1, source_target_pairs={{0,16},{4,20},{8,24},{12,28},{16,0},{20,4},{24,8},{28,12},{1,17},{... | collective-permute-start | bytes 196616 | tf_op jit(solution)/shard_map/ppermute | solution.py:209
  9.0 0.0 collective-permute-start.2
  9.0 0.0 collective-permute-start.3
  9.0 0.8 %collective-permute-done.rest_1_ = bf16[32,1024]{1,0:T(8,128)(2,1)S(1)} collective-permute-done((bf16[32,1024]{1,0:T(8,128)(2,1)S(1)}, bf16[32,1024]{1,0:T(8,128)(2,1)S(1)}, u32[]{:S(2)}, u32[]{:S(2)}) %collective-permute-start) | collective-permute-done | bytes 65568 | tf_op jit(solution)/shard_map/ppermute | solution.py:209
  9.9 0.0 collective-permute-start.4
  9.9 1.9 %collective-permute-done.1.rest_2_ = bf16[32,1024]{1,0:T(8,128)(2,1)S(1)} collective-permute-done((bf16[32,1024]{1,0:T(8,128)(2,1)S(1)}, bf16[32,1024]{1,0:T(8,128)(2,1)S(1)}, u32[]{:S(2)}, u32[]{:S(2)}) %collective-permute-start.1) | collective-permute-done | bytes 65568 | tf_op jit(solution)/shard_map/ppermute | solution.py:209
  11.8 0.0 collective-permute-start.5
  11.8 2.4 %collective-permute-done.2.rest_3_ = bf16[32,1024]{1,0:T(8,128)(2,1)S(1)} collective-permute-done((bf16[32,1024]{1,0:T(8,128)(2,1)S(1)}, bf16[32,1024]{1,0:T(8,128)(2,1)S(1)}, u32[]{:S(2)}, u32[]{:S(2)}) %collective-permute-start.2) | collective-permute-done | bytes 65568 | tf_op jit(solution)/shard_map/ppermute | solution.py:209
  14.2 0.0 copy-start.3
  14.2 0.0 copy-start.5
  14.2 0.1 collective-permute-start.6
  14.3 0.0 collective-permute-done.3.rest_4_
  14.3 0.0 collective-permute-done.4.rest_5_
  14.3 0.0 collective-permute-done.5.rest_6_
  14.3 1.2 %collective-permute-done.6.rest_7_ = bf16[16,1024]{1,0:T(8,128)(2,1)S(1)} collective-permute-done((bf16[16,1024]{1,0:T(8,128)(2,1)S(1)}, bf16[16,1024]{1,0:T(8,128)(2,1)S(1)}, u32[]{:S(2)}, u32[]{:S(2)}) %collective-permute-start.6) | collective-permute-done | bytes 32800 | tf_op jit(solution)/shard_map/ppermute | solution.py:212
  15.5 0.0 copy-done
  15.5 0.0 copy-done.1
  15.5 0.0 copy-done.2
  15.5 0.0 copy-done.6
  15.5 4.3 %experts.1 = bf16[256,512]{1,0:T(8,128)(2,1)S(1)} custom-call(bf16[2,1024,1024]{2,1,0:T(8,128)(2,1)S(1)} %copy-done, f32[2,1024]{1,0:T(2,128)S(1)} %copy-done.6, bf16[2,1024,1024]{2,1,0:T(8,128)(2,1)S(1)} %copy-done.1, bf16[256,256]{1,0:T(8,128)(2,1)S(1)} %copy-done.2, bf16[32,1024]{1,0:T(8,128)(2,1)S(1)} %get-tuple-element.13.rest_0_, ...), custom_call_target="tpu_custom_call" | custom-call | tf_op jit(solution)/shard_map/experts/pallas_call | solution.py:218
  19.8 14.0 %all_to_all.5 = bf16[32,8,512]{2,1,0:T(8,128)(2,1)S(1)} all-to-all(bf16[32,8,512]{2,1,0:T(8,128)(2,1)S(1)} %bitcast.4), channel_id=1, replica_groups=mesh['expert'=8,'hidden'=4] {'expert','hidden'}, dimensions={0} | all-to-all | bytes 524288 | tf_op jit(solution)/shard_map/all_to_all | solution.py:228
  33.8 0.0 copy-done.3
  33.8 0.0 copy-done.5
  33.8 1.6 %tokens_back.1 = bf16[1,196,1024]{2,1,0:T(8,128)(2,1)} custom-call(bf16[256,512]{1,0:T(8,128)(2,1)S(1)} %bitcast.3, f32[16,1024]{1,0:T(8,128)S(1)} %copy-done.3, bf16[1,196,1024]{2,1,0:T(8,128)(2,1)S(1)} %get-tuple-element.17.tok_ref, bf16[1,196,1024]{2,1,0:T(8,128)(2,1)S(1)} %get-tuple-element.18.grad_ref, ...), custom_call_target="tpu_custom_call" | custom-call | tf_op jit(solution)/shard_map/tokens_back/pallas_call | solution.py:239
  (4 shorter events, 0.0 us)
Async XLA Ops:
  0.0 2.0 %copy-start.8 = (bf16[4,196,1024]{2,0,1:T(4,128)(2,1)S(1)}, bf16[4,196,1024]{2,0,1:T(4,128)(2,1)}, u32[]{:S(2)}) copy-start(bf16[4,196,1024]{2,0,1:T(4,128)(2,1)} %param.16) | copy-start | bytes 4816900
  2.0 0.8 %copy-start.4 = (bf16[1024,16]{0,1:T(8,128)(2,1)S(1)}, bf16[1024,16]{0,1:T(8,128)(2,1)}, u32[]{:S(2)}) copy-start(bf16[1024,16]{0,1:T(8,128)(2,1)} %param.11) | copy-start | bytes 98308
  2.0 0.8 %copy-start.7 = (bf16[128,128]{1,0:T(8,128)(2,1)S(1)}, bf16[128,128]{1,0:T(8,128)(2,1)}, u32[]{:S(2)}) copy-start(bf16[128,128]{1,0:T(8,128)(2,1)} %constant.6.clone.perm_ref) | copy-start | bytes 98308
  2.8 12.7 %copy-start = (bf16[2,1024,1024]{2,1,0:T(8,128)(2,1)S(1)}, bf16[2,1024,1024]{2,1,0:T(8,128)(2,1)}, u32[]{:S(2)}) copy-start(bf16[2,1024,1024]{2,1,0:T(8,128)(2,1)} %win_ref.1) | copy-start | bytes 12582916
  2.8 12.7 %copy-start.1 = (bf16[2,1024,1024]{2,1,0:T(8,128)(2,1)S(1)}, bf16[2,1024,1024]{2,1,0:T(8,128)(2,1)}, u32[]{:S(2)}) copy-start(bf16[2,1024,1024]{2,1,0:T(8,128)(2,1)} %wout_ref.1) | copy-start | bytes 12582916
  2.8 12.7 %copy-start.2 = (bf16[256,256]{1,0:T(8,128)(2,1)S(1)}, bf16[256,256]{1,0:T(8,128)(2,1)}, u32[]{:S(2)}) copy-start(bf16[256,256]{1,0:T(8,128)(2,1)} %constant.7.clone.t_ref) | copy-start | bytes 393220
  2.8 12.7 %copy-start.6 = (f32[2,1024]{1,0:T(2,128)S(1)}, f32[2,1024]{1,0:T(2,128)}, u32[]{:S(2)}) copy-start(f32[2,1024]{1,0:T(2,128)} %bin_ref.1) | copy-start | bytes 24580
  4.5 5.4 %collective-permute-start = (bf16[32,1024]{1,0:T(8,128)(2,1)S(1)}, bf16[32,1024]{1,0:T(8,128)(2,1)S(1)}, u32[]{:S(2)}, u32[]{:S(2)}) collective-permute-start(bf16[32,1024]{1,0:T(8,128)(2,1)S(1)} %get-tuple-element.14), channel_id=1, source_target_pairs={{0,8},{4,12},{8,0},{12,4},{16,24},{20,28},{24,16},{28,20},{1,9},{5... | collective-permute-start | bytes 196616 | tf_op jit(solution)/shard_map/ppermute | solution.py:209
  7.5 4.3 %collective-permute-start.1 = (bf16[32,1024]{1,0:T(8,128)(2,1)S(1)}, bf16[32,1024]{1,0:T(8,128)(2,1)S(1)}, u32[]{:S(2)}, u32[]{:S(2)}) collective-permute-start(bf16[32,1024]{1,0:T(8,128)(2,1)S(1)} %get-tuple-element.15), channel_id=1, source_target_pairs={{0,16},{4,20},{8,24},{12,28},{16,0},{20,4},{24,8},{28,12},{1,17},{... | collective-permute-start | bytes 196616 | tf_op jit(solution)/shard_map/ppermute | solution.py:209
  9.0 5.2 %collective-permute-start.2 = (bf16[32,1024]{1,0:T(8,128)(2,1)S(1)}, bf16[32,1024]{1,0:T(8,128)(2,1)S(1)}, u32[]{:S(2)}, u32[]{:S(2)}) collective-permute-start(bf16[32,1024]{1,0:T(8,128)(2,1)S(1)} %get-tuple-element.16), channel_id=1, source_target_pairs={{0,24},{4,28},{8,16},{12,20},{16,8},{20,12},{24,0},{28,4},{1,25},{... | collective-permute-start | bytes 196616 | tf_op jit(solution)/shard_map/ppermute | solution.py:209
  9.0 5.2 %collective-permute-start.3 = (bf16[16,1024]{1,0:T(8,128)(2,1)S(1)}, bf16[16,1024]{1,0:T(8,128)(2,1)S(1)}, u32[]{:S(2)}, u32[]{:S(2)}) collective-permute-start(bf16[16,1024]{1,0:T(8,128)(2,1)S(1)} %slice.12), channel_id=1, source_target_pairs={{0,4},{4,0},{8,12},{12,8},{16,20},{20,16},{24,28},{28,24},{1,5},{5... | collective-permute-start | bytes 98312 | tf_op jit(solution)/shard_map/ppermute | solution.py:212
  9.9 4.4 %collective-permute-start.4 = (bf16[16,1024]{1,0:T(8,128)(2,1)S(1)}, bf16[16,1024]{1,0:T(8,128)(2,1)S(1)}, u32[]{:S(2)}, u32[]{:S(2)}) collective-permute-start(bf16[16,1024]{1,0:T(8,128)(2,1)S(1)} %slice.16), channel_id=1, source_target_pairs={{0,4},{4,0},{8,12},{12,8},{16,20},{20,16},{24,28},{28,24},{1,5},{5... | collective-permute-start | bytes 98312 | tf_op jit(solution)/shard_map/ppermute | solution.py:212
  11.8 2.5 %collective-permute-start.5 = (bf16[16,1024]{1,0:T(8,128)(2,1)S(1)}, bf16[16,1024]{1,0:T(8,128)(2,1)S(1)}, u32[]{:S(2)}, u32[]{:S(2)}) collective-permute-start(bf16[16,1024]{1,0:T(8,128)(2,1)S(1)} %slice.17), channel_id=1, source_target_pairs={{0,4},{4,0},{8,12},{12,8},{16,20},{20,16},{24,28},{28,24},{1,5},{5... | collective-permute-start | bytes 98312 | tf_op jit(solution)/shard_map/ppermute | solution.py:212
  14.2 19.6 %copy-start.3 = (f32[16,1024]{1,0:T(8,128)S(1)}, f32[16,1024]{1,0:T(8,128)}, u32[]{:S(2)}) copy-start(f32[16,1024]{1,0:T(8,128)} %bias_ref.1) | copy-start | bytes 196612
  14.2 19.6 %copy-start.5 = (bf16[64,256]{1,0:T(8,128)(2,1)S(1)}, bf16[64,256]{1,0:T(8,128)(2,1)}, u32[]{:S(2)}) copy-start(bf16[64,256]{1,0:T(8,128)(2,1)} %constant.8.clone.sel_ref) | copy-start | bytes 98308
  14.2 1.3 %collective-permute-start.6 = (bf16[16,1024]{1,0:T(8,128)(2,1)S(1)}, bf16[16,1024]{1,0:T(8,128)(2,1)S(1)}, u32[]{:S(2)}, u32[]{:S(2)}) collective-permute-start(bf16[16,1024]{1,0:T(8,128)(2,1)S(1)} %slice.18), channel_id=1, source_target_pairs={{0,4},{4,0},{8,12},{12,8},{16,20},{20,16},{24,28},{28,24},{1,5},{5... | collective-permute-start | bytes 98312 | tf_op jit(solution)/shard_map/ppermute | solution.py:212

commit v19 on v16

--- a/solution.py
+++ b/solution.py
@@ -48,8 +48,7 @@
     disp_ref, comb_ref, my_tok_ref, my_grad_ref, *rest,
 ):
     outer, inner = levels(n_expert)
-    leave_refs = rest[:outer]
-    send_ref, disp_all, comb_all = rest[outer:]
+    leave_ref, send_ref, disp_all, comb_all = rest
     slots = keys_ref.shape[0]
     keys = keys_ref[...]
     slot_rows = [[], []]
@@ -76,8 +75,8 @@
     c, l = position(inner)
     for i in range(inner):
         for j in range(outer):
-            to = partner(c, j, outer) * inner + lax.rem(l + i, inner)
-            leave_refs[j][i * block : (i + 1) * block] = send_ref[
+            to = j * inner + lax.rem(l + i, inner)
+            leave_ref[j, i * block : (i + 1) * block] = send_ref[
                 pl.ds(pl.multiple_of(to * block, block), block)
             ]
     first = lax.axis_index("hidden") * quarter
@@ -90,15 +89,15 @@
 
 def expert_kernel(images, n_expert, k, gb, win_ref, bin_ref, wout_ref, t_ref, *rest):
     outer, inner = levels(n_expert)
-    come_refs = rest[: outer * inner]
-    back_ref, got_ref = rest[outer * inner :]
+    come_refs = rest[:inner]
+    back_ref, got_ref = rest[inner:]
     rows = k * images
     c, l = position(inner)
     block = got_ref.shape[1]
     for j in range(outer):
-        source = partner(c, j, outer, True) * inner
+        source = j * inner
         for i in range(inner):
-            got_ref[source + lax.rem(l + i, inner)] = come_refs[i * outer + j][:block]
+            got_ref[source + lax.rem(l + i, inner)] = come_refs[i][j, :block]
     width = got_ref.shape[2]
     total = n_expert * rows
     got = got_ref[...]
@@ -187,7 +186,7 @@
     perm = one_hot_rows(order, order.size)
     send_rows = 2 * k * images
     outer, inner = levels(n_expert)
-    disp, comb, my_tok, my_grad, *leave = pl.pallas_call(
+    disp, comb, my_tok, my_grad, leave = pl.pallas_call(
         functools.partial(dispatch_kernel, images, quarter, k, gb, n_expert),
         out_shape=(
             jax.ShapeDtypeStruct((quarter, slots, positions), BF),
@@ -195,9 +194,9 @@
             jax.ShapeDtypeStruct((quarter, positions, width), BF),
             jax.ShapeDtypeStruct((quarter, positions, width), BF),
         )
-        + (jax.ShapeDtypeStruct((inner * send_rows, width), BF),) * outer,
+        + (jax.ShapeDtypeStruct((outer, inner * send_rows, width), BF),),
         in_specs=[vmem] * 4,
-        out_specs=(vmem,) * (4 + outer),
+        out_specs=(vmem,) * 5,
         scratch_shapes=[pltpu.VMEM((n_expert * send_rows, width), BF)]
         + [pltpu.VMEM((images, slots, positions), BF)] * 2,
         compiler_params=pltpu.CompilerParams(vmem_limit_bytes=12 << 20),
@@ -206,13 +205,15 @@
     )(tokens, out_grad, keys, perm)
 
     everyone = [(c, l) for c in range(outer) for l in range(inner)]
-    come = leave[:1]
-    for j in range(1, outer):
-        pairs = [(c * inner + l, partner(c, j, outer) * inner + l) for c, l in everyone]
-        come.append(lax.ppermute(leave[j], "expert", pairs))
+    groups = [[c * inner + l for c in range(outer)] for l in range(inner)]
+    come = [
+        lax.all_to_all(
+            leave, "expert", split_axis=0, concat_axis=0, axis_index_groups=groups, tiled=True
+        )
+    ]
     if inner == 2:
         swap = [(c * inner + l, c * inner + 1 - l) for c, l in everyone]
-        come += [lax.ppermute(x[send_rows:], "expert", swap) for x in come]
+        come.append(lax.ppermute(come[0][:, send_rows:], "expert", swap))
 
     order = np.arange(2 * k * 2 * gb * images).reshape(2, 2, gb, k, n_hidden, quarter)
     order = order.transpose(2, 4, 0, 3, 5, 1)

time: 35.6 us -> 37.4 us (1.051)
  blocking collectives: 14 us -> 25.3 us
  waiting for transfers between devices: 6.29 us -> 1.33 us
  starting transfers between devices: 4.62 us -> 0.07 us
    all_to_all x0 -> x1, blocking collectives: none -> 11 us  [local(): lax.all_to_all(leave, 'expert', split_axis=0, concat_axis=0, axis_index_g...]
    ppermute x7 -> x1, waiting for transfers between devices: 6.29 us -> 1.33 us  [local(): come.append(lax.ppermute(come[0][:, send_rows:], 'expert', swap))]
    ppermute x7 -> x1, starting transfers between devices: 4.62 us -> 0.07 us  [local(): come.append(lax.ppermute(come[0][:, send_rows:], 'expert', swap))]
  transfers between devices with their start and end apart: 7 -> 1, of which waited for: 4 -> 1; matrix products, arithmetic and copies ran while one was open for 0% -> 0% of each run, Pallas kernels for 0% -> 0%
where the time goes in v19:
time: 37.4 us; the launch traced here: 37.2 us
  blocking collectives  25.3 us (68%)
  Pallas kernels  7.58 us (20%)
  local copies, waits for them, and re-layouts  2.81 us (8%)
  waiting for transfers between devices  1.33 us (4%)
    all_to_all x1, blocking collectives, local(): lax.all_to_all(back.reshape(n_all, back_rows, half), ('expert', 'hidden')...  14.3 us
    all_to_all x1, blocking collectives, local(): lax.all_to_all(leave, 'expert', split_axis=0, concat_axis=0, axis_index_g...  11 us
    pallas_call x1, Pallas kernels, local(): pl.pallas_call(functools.partial(expert_kernel, images, n_expert, k, gb),...  4.34 us
    unnamed x20, local copies, waits for them, and re-layouts  2.8 us
    pallas_call x1, Pallas kernels, local(): pl.pallas_call(functools.partial(dispatch_kernel, images, quarter, k, gb,...  1.66 us
    pallas_call x1, Pallas kernels, local(): pl.pallas_call(functools.partial(final_kernel, quarter, k, gb), out_shape...  1.58 us
    ppermute x1, waiting for transfers between devices, local(): come.append(lax.ppermute(come[0][:, send_rows:], 'expert', swap))  1.33 us
  transfers between devices with their start and end apart: 1, of which 1 were waited for; matrix products, arithmetic and copies ran while one was open for 0% of the time, Pallas kernels for 0%

profile of v19, /device:TPU:0, one launch (start us, length us, event | category | flops | bytes accessed | tf_op | source)
XLA Modules:
  0.0 37.2 jit_solution(16430867998914355231)
XLA Ops:
  0.0 0.0 copy-start.8
  0.0 2.0 %copy.11.tok_ref = bf16[4,196,1024]{2,1,0:T(8,128)(2,1)S(1)} copy(bf16[4,196,1024]{2,0,1:T(4,128)(2,1)} %param.10) | data formatting | bytes 3211264 | tf_op args[0]
  2.0 0.0 copy-done.8
  2.0 0.0 copy-start.4
  2.0 0.0 copy-start.7
  2.1 0.5 %copy.12.grad_ref = bf16[4,196,1024]{2,1,0:T(8,128)(2,1)S(1)} copy(bf16[4,196,1024]{2,0,1:T(4,128)(2,1)S(1)} %copy-done.8) | data formatting | bytes 3211264 | tf_op args[6]
  2.5 0.3 copy-done.4
  2.8 0.0 copy-done.7
  2.8 0.0 copy-start
  2.8 0.0 copy-start.1
  2.8 0.0 copy-start.2
  2.8 0.0 copy-start.6
  2.8 1.7 %dispatch.1 = (bf16[1,16,196]{2,1,0:T(8,128)(2,1)S(1)}, bf16[1,16,196]{2,1,0:T(8,128)(2,1)S(1)}, bf16[1,196,1024]{2,1,0:T(8,128)(2,1)S(1)}, bf16[1,196,1024]{2,1,0:T(8,128)(2,1)S(1)}, bf16[4,32,1024]{2,1,0:T(8,128)(2,1)S(1)}) custom-call(bf16[4,196,1024]{2,1,0:T(8,128)(2,1)S(1)} %copy.11.tok_ref, bf16[4,196,1024]{2,1,0:T(8,128)(2,1)S(1)} %copy.12.grad_ref, ...), custom_call_target="tpu_custom_call" | custom-call | flops 8000000000 | tf_op jit(solution)/shard_map/dispatch/pallas_call | solution.py:189
  4.5 11.0 %all_to_all.10.rest_0_ = bf16[4,32,1024]{2,1,0:T(8,128)(2,1)S(1)} all-to-all(bf16[4,32,1024]{2,1,0:T(8,128)(2,1)S(1)} %get-tuple-element.10), channel_id=1, replica_groups={{0,8,16,24},{4,12,20,28},{1,9,17,25},{5,13,21,29},{2,10,18,26},{6,14,22..., dimensions={0} | all-to-all | bytes 524288 | tf_op jit(solution)/shard_map/all_to_all | solution.py:210
  15.5 0.0 copy-start.3
  15.5 0.0 copy-start.5
  15.5 0.1 collective-permute-start
  15.6 1.3 %collective-permute-done.rest_1_ = bf16[4,16,1024]{2,1,0:T(8,128)(2,1)S(1)} collective-permute-done((bf16[4,16,1024]{2,1,0:T(8,128)(2,1)S(1)}, bf16[4,16,1024]{2,1,0:T(8,128)(2,1)S(1)}, u32[]{:S(2)}, u32[]{:S(2)}) %collective-permute-start) | collective-permute-done | bytes 131104 | tf_op jit(solution)/shard_map/ppermute | solution.py:216
  16.9 0.0 copy-done
  16.9 0.0 copy-done.1
  16.9 0.0 copy-done.2
  16.9 0.0 copy-done.6
  16.9 4.3 %experts.1 = bf16[256,512]{1,0:T(8,128)(2,1)S(1)} custom-call(bf16[2,1024,1024]{2,1,0:T(8,128)(2,1)S(1)} %copy-done, f32[2,1024]{1,0:T(2,128)S(1)} %copy-done.6, bf16[2,1024,1024]{2,1,0:T(8,128)(2,1)S(1)} %copy-done.1, bf16[256,256]{1,0:T(8,128)(2,1)S(1)} %copy-done.2, bf16[4,32,1024]{2,1,0:T(8,128)(2,1)S(1)} %all_to_all.10.rest_0_, ...), custom_call_target="tpu_custom_call" | custom-call | tf_op jit(solution)/shard_map/experts/pallas_call | solution.py:222
  21.3 14.3 %all_to_all.11 = bf16[32,8,512]{2,1,0:T(8,128)(2,1)S(1)} all-to-all(bf16[32,8,512]{2,1,0:T(8,128)(2,1)S(1)} %bitcast.4), channel_id=1, replica_groups=mesh['expert'=8,'hidden'=4] {'expert','hidden'}, dimensions={0} | all-to-all | bytes 524288 | tf_op jit(solution)/shard_map/all_to_all | solution.py:232
  35.6 0.0 copy-done.3
  35.6 0.0 copy-done.5
  35.6 1.6 %tokens_back.1 = bf16[1,196,1024]{2,1,0:T(8,128)(2,1)} custom-call(bf16[256,512]{1,0:T(8,128)(2,1)S(1)} %bitcast.3, f32[16,1024]{1,0:T(8,128)S(1)} %copy-done.3, bf16[1,196,1024]{2,1,0:T(8,128)(2,1)S(1)} %get-tuple-element.11.tok_ref, bf16[1,196,1024]{2,1,0:T(8,128)(2,1)S(1)} %get-tuple-element.12.grad_ref, ...), custom_call_target="tpu_custom_call" | custom-call | tf_op jit(solution)/shard_map/tokens_back/pallas_call | solution.py:243
  (1 shorter events, 0.0 us)
Async XLA Ops:
  0.0 2.0 %copy-start.8 = (bf16[4,196,1024]{2,0,1:T(4,128)(2,1)S(1)}, bf16[4,196,1024]{2,0,1:T(4,128)(2,1)}, u32[]{:S(2)}) copy-start(bf16[4,196,1024]{2,0,1:T(4,128)(2,1)} %param.16) | copy-start | bytes 4816900
  2.0 0.8 %copy-start.4 = (bf16[1024,16]{0,1:T(8,128)(2,1)S(1)}, bf16[1024,16]{0,1:T(8,128)(2,1)}, u32[]{:S(2)}) copy-start(bf16[1024,16]{0,1:T(8,128)(2,1)} %param.11) | copy-start | bytes 98308
  2.0 0.8 %copy-start.7 = (bf16[128,128]{1,0:T(8,128)(2,1)S(1)}, bf16[128,128]{1,0:T(8,128)(2,1)}, u32[]{:S(2)}) copy-start(bf16[128,128]{1,0:T(8,128)(2,1)} %constant.6.clone.perm_ref) | copy-start | bytes 98308
  2.8 14.1 %copy-start = (bf16[2,1024,1024]{2,1,0:T(8,128)(2,1)S(1)}, bf16[2,1024,1024]{2,1,0:T(8,128)(2,1)}, u32[]{:S(2)}) copy-start(bf16[2,1024,1024]{2,1,0:T(8,128)(2,1)} %win_ref.1) | copy-start | bytes 12582916
  2.8 14.1 %copy-start.1 = (bf16[2,1024,1024]{2,1,0:T(8,128)(2,1)S(1)}, bf16[2,1024,1024]{2,1,0:T(8,128)(2,1)}, u32[]{:S(2)}) copy-start(bf16[2,1024,1024]{2,1,0:T(8,128)(2,1)} %wout_ref.1) | copy-start | bytes 12582916
  2.8 14.1 %copy-start.2 = (bf16[256,256]{1,0:T(8,128)(2,1)S(1)}, bf16[256,256]{1,0:T(8,128)(2,1)}, u32[]{:S(2)}) copy-start(bf16[256,256]{1,0:T(8,128)(2,1)} %constant.7.clone.t_ref) | copy-start | bytes 393220
  2.8 14.1 %copy-start.6 = (f32[2,1024]{1,0:T(2,128)S(1)}, f32[2,1024]{1,0:T(2,128)}, u32[]{:S(2)}) copy-start(f32[2,1024]{1,0:T(2,128)} %bin_ref.1) | copy-start | bytes 24580
  15.5 20.1 %copy-start.3 = (f32[16,1024]{1,0:T(8,128)S(1)}, f32[16,1024]{1,0:T(8,128)}, u32[]{:S(2)}) copy-start(f32[16,1024]{1,0:T(8,128)} %bias_ref.1) | copy-start | bytes 196612
  15.5 20.1 %copy-start.5 = (bf16[64,256]{1,0:T(8,128)(2,1)S(1)}, bf16[64,256]{1,0:T(8,128)(2,1)}, u32[]{:S(2)}) copy-start(bf16[64,256]{1,0:T(8,128)(2,1)} %constant.8.clone.sel_ref) | copy-start | bytes 98308
  15.5 1.4 %collective-permute-start = (bf16[4,16,1024]{2,1,0:T(8,128)(2,1)S(1)}, bf16[4,16,1024]{2,1,0:T(8,128)(2,1)S(1)}, u32[]{:S(2)}, u32[]{:S(2)}) collective-permute-start(bf16[4,16,1024]{2,1,0:T(8,128)(2,1)S(1)} %slice.4), channel_id=1, source_target_pairs={{0,4},{4,0},{8,12},{12,8},{16,20},{20,16},{24,28},{28,24},{1,5},{5... | collective-permute-start | bytes 393224 | tf_op jit(solution)/shard_map/ppermute | solution.py:216

commit v20 on v16

--- a/solution.py
+++ b/solution.py
@@ -206,10 +206,10 @@
     )(tokens, out_grad, keys, perm)
 
     everyone = [(c, l) for c in range(outer) for l in range(inner)]
-    come = leave[:1]
-    for j in range(1, outer):
+    come = leave[:1] + [None] * (outer - 1)
+    for j in range(outer - 1, 0, -1):
         pairs = [(c * inner + l, partner(c, j, outer) * inner + l) for c, l in everyone]
-        come.append(lax.ppermute(leave[j], "expert", pairs))
+        come[j] = lax.ppermute(leave[j], "expert", pairs)
     if inner == 2:
         swap = [(c * inner + l, c * inner + 1 - l) for c, l in everyone]
         come += [lax.ppermute(x[send_rows:], "expert", swap) for x in come]

time: 35.6 us -> 35.6 us (level)
  no operation moved by 1% of the time
where the time goes in v20:
time: 35.6 us; the launch traced here: 35.4 us
  blocking collectives  14 us (39%)
  Pallas kernels  7.59 us (21%)
  waiting for transfers between devices  6.29 us (18%)
  starting transfers between devices  4.62 us (13%)
  local copies, waits for them, and re-layouts  2.81 us (8%)
    all_to_all x1, blocking collectives, local(): lax.all_to_all(back.reshape(n_all, back_rows, half), ('expert', 'hidden')...  14 us
    ppermute x3, waiting for transfers between devices, local(): come[j] = lax.ppermute(leave[j], 'expert', pairs)  5.12 us
    ppermute x3, starting transfers between devices, local(): come[j] = lax.ppermute(leave[j], 'expert', pairs)  4.54 us
    pallas_call x1, Pallas kernels, local(): pl.pallas_call(functools.partial(expert_kernel, images, n_expert, k, gb),...  4.34 us
    unnamed x20, local copies, waits for them, and re-layouts  2.8 us
    pallas_call x1, Pallas kernels, local(): pl.pallas_call(functools.partial(dispatch_kernel, images, quarter, k, gb,...  1.66 us
    pallas_call x1, Pallas kernels, local(): pl.pallas_call(functools.partial(final_kernel, quarter, k, gb), out_shape...  1.58 us
    ppermute x4, waiting for transfers between devices, local(): come += [lax.ppermute(x[send_rows:], 'expert', swap) for x in come]  1.17 us
  transfers between devices with their start and end apart: 7, of which 4 were waited for; matrix products, arithmetic and copies ran while one was open for 0% of the time, Pallas kernels for 0%

profile of v20, /device:TPU:0, one launch (start us, length us, event | category | flops | bytes accessed | tf_op | source)
XLA Modules:
  0.0 35.4 jit_solution(1451417938501484712)
XLA Ops:
  0.0 0.0 copy-start.8
  0.0 2.0 %copy.11.tok_ref = bf16[4,196,1024]{2,1,0:T(8,128)(2,1)S(1)} copy(bf16[4,196,1024]{2,0,1:T(4,128)(2,1)} %param.10) | data formatting | bytes 3211264 | tf_op args[0]
  2.0 0.0 copy-done.8
  2.0 0.0 copy-start.4
  2.0 0.0 copy-start.7
  2.1 0.5 %copy.12.grad_ref = bf16[4,196,1024]{2,1,0:T(8,128)(2,1)S(1)} copy(bf16[4,196,1024]{2,0,1:T(4,128)(2,1)S(1)} %copy-done.8) | data formatting | bytes 3211264 | tf_op args[6]
  2.5 0.3 copy-done.4
  2.8 0.0 copy-done.7
  2.8 0.0 copy-start
  2.8 0.0 copy-start.1
  2.8 0.0 copy-start.2
  2.8 0.0 copy-start.6
  2.8 1.7 %dispatch.1 = (bf16[1,16,196]{2,1,0:T(8,128)(2,1)S(1)}, bf16[1,16,196]{2,1,0:T(8,128)(2,1)S(1)}, bf16[1,196,1024]{2,1,0:T(8,128)(2,1)S(1)}, bf16[1,196,1024]{2,1...) custom-call(bf16[4,196,1024]{2,1,0:T(8,128)(2,1)S(1)} %copy.11.tok_r, ...), custom_call_target="tpu_custom_call" | custom-call | flops 8000000000 | tf_op jit(solution)/shard_map/dispatch/pallas_call | solution.py:190
  4.5 3.0 %collective-permute-start = (bf16[32,1024]{1,0:T(8,128)(2,1)S(1)}, bf16[32,1024]{1,0:T(8,128)(2,1)S(1)}, u32[]{:S(2)}, u32[]{:S(2)}) collective-permute-start(bf16[32,1024]{1,0:T(8,128)(2,1)S(1)} %get-tuple-element.14), channel_id=1, source_target_pairs={{0,8},{4,12},{8,0},{12,4},{16,24},{20,28},{24,16},{28,20},{1,9},{5... | collective-permute-start | bytes 196616 | tf_op jit(solution)/shard_map/ppermute | solution.py:212
  7.5 1.5 %collective-permute-start.1 = (bf16[32,1024]{1,0:T(8,128)(2,1)S(1)}, bf16[32,1024]{1,0:T(8,128)(2,1)S(1)}, u32[]{:S(2)}, u32[]{:S(2)}) collective-permute-start(bf16[32,1024]{1,0:T(8,128)(2,1)S(1)} %get-tuple-element.15), channel_id=1, source_target_pairs={{0,16},{4,20},{8,24},{12,28},{16,0},{20,4},{24,8},{28,12},{1,17},{... | collective-permute-start | bytes 196616 | tf_op jit(solution)/shard_map/ppermute | solution.py:212
  9.0 0.0 collective-permute-start.2
  9.0 0.0 collective-permute-start.3
  9.0 0.8 %collective-permute-done.rest_1_ = bf16[32,1024]{1,0:T(8,128)(2,1)S(1)} collective-permute-done((bf16[32,1024]{1,0:T(8,128)(2,1)S(1)}, bf16[32,1024]{1,0:T(8,128)(2,1)S(1)}, u32[]{:S(2)}, u32[]{:S(2)}) %collective-permute-start) | collective-permute-done | bytes 65568 | tf_op jit(solution)/shard_map/ppermute | solution.py:212
  9.9 0.0 collective-permute-start.4
  9.9 1.9 %collective-permute-done.1.rest_2_ = bf16[32,1024]{1,0:T(8,128)(2,1)S(1)} collective-permute-done((bf16[32,1024]{1,0:T(8,128)(2,1)S(1)}, bf16[32,1024]{1,0:T(8,128)(2,1)S(1)}, u32[]{:S(2)}, u32[]{:S(2)}) %collective-permute-start.1) | collective-permute-done | bytes 65568 | tf_op jit(solution)/shard_map/ppermute | solution.py:212
  11.8 0.0 collective-permute-start.5
  11.8 2.4 %collective-permute-done.2.rest_3_ = bf16[32,1024]{1,0:T(8,128)(2,1)S(1)} collective-permute-done((bf16[32,1024]{1,0:T(8,128)(2,1)S(1)}, bf16[32,1024]{1,0:T(8,128)(2,1)S(1)}, u32[]{:S(2)}, u32[]{:S(2)}) %collective-permute-start.2) | collective-permute-done | bytes 65568 | tf_op jit(solution)/shard_map/ppermute | solution.py:212
  14.2 0.0 copy-start.3
  14.2 0.0 copy-start.5
  14.2 0.1 collective-permute-start.6
  14.3 0.0 collective-permute-done.3.rest_4_
  14.3 0.0 collective-permute-done.4.rest_5_
  14.3 0.0 collective-permute-done.5.rest_6_
  14.3 1.2 %collective-permute-done.6.rest_7_ = bf16[16,1024]{1,0:T(8,128)(2,1)S(1)} collective-permute-done((bf16[16,1024]{1,0:T(8,128)(2,1)S(1)}, bf16[16,1024]{1,0:T(8,128)(2,1)S(1)}, u32[]{:S(2)}, u32[]{:S(2)}) %collective-permute-start.6) | collective-permute-done | bytes 32800 | tf_op jit(solution)/shard_map/ppermute | solution.py:215
  15.5 0.0 copy-done
  15.5 0.0 copy-done.1
  15.5 0.0 copy-done.2
  15.5 0.0 copy-done.6
  15.5 4.3 %experts.1 = bf16[256,512]{1,0:T(8,128)(2,1)S(1)} custom-call(bf16[2,1024,1024]{2,1,0:T(8,128)(2,1)S(1)} %copy-done, f32[2,1024]{1,0:T(2,128)S(1)} %copy-done.6, bf16[2,1024,1024]{2,1,0:T(8,128)(2,1)S(1)} %copy-done.1, bf16[256,256]{1,0:T(8,128)(2,1)S(1)} %copy-done.2, bf16[32,1024]{1,0:T(8,128)(2,1)S(1)} %get-tuple-element.13.rest_0_, ...), custom_call_target="tpu_custom_call" | custom-call | tf_op jit(solution)/shard_map/experts/pallas_call | solution.py:221
  19.8 14.0 %all_to_all.5 = bf16[32,8,512]{2,1,0:T(8,128)(2,1)S(1)} all-to-all(bf16[32,8,512]{2,1,0:T(8,128)(2,1)S(1)} %bitcast.4), channel_id=1, replica_groups=mesh['expert'=8,'hidden'=4] {'expert','hidden'}, dimensions={0} | all-to-all | bytes 524288 | tf_op jit(solution)/shard_map/all_to_all | solution.py:231
  33.8 0.0 copy-done.3
  33.8 0.0 copy-done.5
  33.8 1.6 %tokens_back.1 = bf16[1,196,1024]{2,1,0:T(8,128)(2,1)} custom-call(bf16[256,512]{1,0:T(8,128)(2,1)S(1)} %bitcast.3, f32[16,1024]{1,0:T(8,128)S(1)} %copy-done.3, bf16[1,196,1024]{2,1,0:T(8,128)(2,1)S(1)} %get-tuple-element.17.tok_ref, bf16[1,196,1024]{2,1,0:T(8,128)(2,1)S(1)} %get-tuple-element.18.grad_ref, ...), custom_call_target="tpu_custom_call" | custom-call | tf_op jit(solution)/shard_map/tokens_back/pallas_call | solution.py:242
  (4 shorter events, 0.0 us)
Async XLA Ops:
  0.0 2.0 %copy-start.8 = (bf16[4,196,1024]{2,0,1:T(4,128)(2,1)S(1)}, bf16[4,196,1024]{2,0,1:T(4,128)(2,1)}, u32[]{:S(2)}) copy-start(bf16[4,196,1024]{2,0,1:T(4,128)(2,1)} %param.16) | copy-start | bytes 4816900
  2.0 0.8 %copy-start.4 = (bf16[1024,16]{0,1:T(8,128)(2,1)S(1)}, bf16[1024,16]{0,1:T(8,128)(2,1)}, u32[]{:S(2)}) copy-start(bf16[1024,16]{0,1:T(8,128)(2,1)} %param.11) | copy-start | bytes 98308
  2.0 0.8 %copy-start.7 = (bf16[128,128]{1,0:T(8,128)(2,1)S(1)}, bf16[128,128]{1,0:T(8,128)(2,1)}, u32[]{:S(2)}) copy-start(bf16[128,128]{1,0:T(8,128)(2,1)} %constant.6.clone.perm_ref) | copy-start | bytes 98308
  2.8 12.7 %copy-start = (bf16[2,1024,1024]{2,1,0:T(8,128)(2,1)S(1)}, bf16[2,1024,1024]{2,1,0:T(8,128)(2,1)}, u32[]{:S(2)}) copy-start(bf16[2,1024,1024]{2,1,0:T(8,128)(2,1)} %win_ref.1) | copy-start | bytes 12582916
  2.8 12.7 %copy-start.1 = (bf16[2,1024,1024]{2,1,0:T(8,128)(2,1)S(1)}, bf16[2,1024,1024]{2,1,0:T(8,128)(2,1)}, u32[]{:S(2)}) copy-start(bf16[2,1024,1024]{2,1,0:T(8,128)(2,1)} %wout_ref.1) | copy-start | bytes 12582916
  2.8 12.7 %copy-start.2 = (bf16[256,256]{1,0:T(8,128)(2,1)S(1)}, bf16[256,256]{1,0:T(8,128)(2,1)}, u32[]{:S(2)}) copy-start(bf16[256,256]{1,0:T(8,128)(2,1)} %constant.7.clone.t_ref) | copy-start | bytes 393220
  2.8 12.7 %copy-start.6 = (f32[2,1024]{1,0:T(2,128)S(1)}, f32[2,1024]{1,0:T(2,128)}, u32[]{:S(2)}) copy-start(f32[2,1024]{1,0:T(2,128)} %bin_ref.1) | copy-start | bytes 24580
  4.5 5.4 %collective-permute-start = (bf16[32,1024]{1,0:T(8,128)(2,1)S(1)}, bf16[32,1024]{1,0:T(8,128)(2,1)S(1)}, u32[]{:S(2)}, u32[]{:S(2)}) collective-permute-start(bf16[32,1024]{1,0:T(8,128)(2,1)S(1)} %get-tuple-element.14), channel_id=1, source_target_pairs={{0,8},{4,12},{8,0},{12,4},{16,24},{20,28},{24,16},{28,20},{1,9},{5... | collective-permute-start | bytes 196616 | tf_op jit(solution)/shard_map/ppermute | solution.py:212
  7.5 4.3 %collective-permute-start.1 = (bf16[32,1024]{1,0:T(8,128)(2,1)S(1)}, bf16[32,1024]{1,0:T(8,128)(2,1)S(1)}, u32[]{:S(2)}, u32[]{:S(2)}) collective-permute-start(bf16[32,1024]{1,0:T(8,128)(2,1)S(1)} %get-tuple-element.15), channel_id=1, source_target_pairs={{0,16},{4,20},{8,24},{12,28},{16,0},{20,4},{24,8},{28,12},{1,17},{... | collective-permute-start | bytes 196616 | tf_op jit(solution)/shard_map/ppermute | solution.py:212
  9.0 5.2 %collective-permute-start.2 = (bf16[32,1024]{1,0:T(8,128)(2,1)S(1)}, bf16[32,1024]{1,0:T(8,128)(2,1)S(1)}, u32[]{:S(2)}, u32[]{:S(2)}) collective-permute-start(bf16[32,1024]{1,0:T(8,128)(2,1)S(1)} %get-tuple-element.16), channel_id=1, source_target_pairs={{0,24},{4,28},{8,16},{12,20},{16,8},{20,12},{24,0},{28,4},{1,25},{... | collective-permute-start | bytes 196616 | tf_op jit(solution)/shard_map/ppermute | solution.py:212
  9.0 5.2 %collective-permute-start.3 = (bf16[16,1024]{1,0:T(8,128)(2,1)S(1)}, bf16[16,1024]{1,0:T(8,128)(2,1)S(1)}, u32[]{:S(2)}, u32[]{:S(2)}) collective-permute-start(bf16[16,1024]{1,0:T(8,128)(2,1)S(1)} %slice.12), channel_id=1, source_target_pairs={{0,4},{4,0},{8,12},{12,8},{16,20},{20,16},{24,28},{28,24},{1,5},{5... | collective-permute-start | bytes 98312 | tf_op jit(solution)/shard_map/ppermute | solution.py:215
  9.9 4.4 %collective-permute-start.4 = (bf16[16,1024]{1,0:T(8,128)(2,1)S(1)}, bf16[16,1024]{1,0:T(8,128)(2,1)S(1)}, u32[]{:S(2)}, u32[]{:S(2)}) collective-permute-start(bf16[16,1024]{1,0:T(8,128)(2,1)S(1)} %slice.16), channel_id=1, source_target_pairs={{0,4},{4,0},{8,12},{12,8},{16,20},{20,16},{24,28},{28,24},{1,5},{5... | collective-permute-start | bytes 98312 | tf_op jit(solution)/shard_map/ppermute | solution.py:215
  11.8 2.5 %collective-permute-start.5 = (bf16[16,1024]{1,0:T(8,128)(2,1)S(1)}, bf16[16,1024]{1,0:T(8,128)(2,1)S(1)}, u32[]{:S(2)}, u32[]{:S(2)}) collective-permute-start(bf16[16,1024]{1,0:T(8,128)(2,1)S(1)} %slice.17), channel_id=1, source_target_pairs={{0,4},{4,0},{8,12},{12,8},{16,20},{20,16},{24,28},{28,24},{1,5},{5... | collective-permute-start | bytes 98312 | tf_op jit(solution)/shard_map/ppermute | solution.py:215
  14.2 19.6 %copy-start.3 = (f32[16,1024]{1,0:T(8,128)S(1)}, f32[16,1024]{1,0:T(8,128)}, u32[]{:S(2)}) copy-start(f32[16,1024]{1,0:T(8,128)} %bias_ref.1) | copy-start | bytes 196612
  14.2 19.6 %copy-start.5 = (bf16[64,256]{1,0:T(8,128)(2,1)S(1)}, bf16[64,256]{1,0:T(8,128)(2,1)}, u32[]{:S(2)}) copy-start(bf16[64,256]{1,0:T(8,128)(2,1)} %constant.8.clone.sel_ref) | copy-start | bytes 98308
  14.2 1.3 %collective-permute-start.6 = (bf16[16,1024]{1,0:T(8,128)(2,1)S(1)}, bf16[16,1024]{1,0:T(8,128)(2,1)S(1)}, u32[]{:S(2)}, u32[]{:S(2)}) collective-permute-start(bf16[16,1024]{1,0:T(8,128)(2,1)S(1)} %slice.18), channel_id=1, source_target_pairs={{0,4},{4,0},{8,12},{12,8},{16,20},{20,16},{24,28},{28,24},{1,5},{5... | collective-permute-start | bytes 98312 | tf_op jit(solution)/shard_map/ppermute | solution.py:215
